TPU v7x, 32 devices: a whole 2x2x4 slice. The times are simulated.
32 devices in a mesh: dp: 4 (over y, x), group: 8 (over z, core).
Axes of the slice: x: 2, y: 2, z: 4, core: 2. Of those that a mesh axis runs over, the one named last changes fastest.
Arguments:
- hidden_in: bfloat16 [4, 2048, 2048], P('dp', 'group'), may hold values from -6 to 6
- cotangent: bfloat16 [4, 2048, 2048], P('dp', 'group'), may hold values from -6 to 6
- segment_ids: int32 [4, 2048], P('dp'), may hold values from 0 to 3, never falling along the last dimension, each value on 1 to 1024 neighbouring positions
- weight_in: bfloat16 [32, 448, 2048], P(('dp', 'group')), may hold values from -0.125 to 0.125
- weight_back: bfloat16 [32, 320, 2048], P(('dp', 'group')), may hold values from -1 to 1
- moment_in: float32 [32, 448, 2048], P(('dp', 'group')), may hold values from -112 to 112
- moment_back: float32 [32, 320, 2048], P(('dp', 'group')), may hold values from -160 to 160
- norm_gain: float32 [2048], replicated, may hold values from 0.5 to 1.5
- norm_shift: float32 [2048], replicated, may hold values from -1.75 to 1.75
- bias_in: float32 [14336], replicated, may hold values from -3 to 3
- bias_out: float32 [2048], replicated, may hold values from -3 to 3
- vector_moment: float32 [20480], replicated, may hold values from -256 to 256
Outputs:
- block_out: bfloat16 [4, 2048, 2048], P('dp', 'group')
- grad_hidden: float32 [4, 2048, 2048], P('dp', 'group')
- grad_in: float32 [32, 448, 2048], P(('dp', 'group'))
- grad_back: float32 [32, 320, 2048], P(('dp', 'group'))
- moment_in_new: float32 [32, 448, 2048], P(('dp', 'group'))
- moment_back_new: float32 [32, 320, 2048], P(('dp', 'group'))
- step_in: float32 [32, 448, 2048], P(('dp', 'group'))
- step_back: float32 [32, 320, 2048], P(('dp', 'group'))
- vector_grad: float32 [20480], replicated
- vector_moment_new: float32 [20480], replicated
- vector_step: float32 [20480], replicated
- bias_out_grad: float32 [2048], replicated
Inputs may be any that keep to these rules, and one draw needn't show every extreme that they name: `segment_ids`: in each pack the numbers never fall; every sequence has 1 to 1024 tokens and one has exactly 1024.
All inputs are finite; a program needn't handle non-finite values.
Results may differ from a plain program's by a relative error of at most 0.04.
Values may be sent and summed in bfloat16 or wider, within the bound.
No kernel may reach another device: no remote copies, remote signals or barrier semaphores. Data moves between devices by JAX's collectives and lax.ppermute only.
A program may use at most 832 MiB of HBM per device.

v0:
```python
import math

import jax
import jax.numpy as jnp
from jax import lax
from jax.sharding import PartitionSpec as P

HEADS = 32
HEAD = 64
ROT = 32
FF = 8192
NS_ITERS = 5


NEG = -1e30
NS_A = 3.4445
NS_B = -4.775
NS_C = 2.0315
MOMENTUM = 0.95


def positions(segments):
    index_all = jnp.arange(segments.shape[0], dtype=jnp.int32)
    previous = jnp.concatenate([jnp.full((1,), -1, jnp.int32), segments[:-1]])
    starts = jnp.where(segments != previous, index_all, 0)
    return index_all - lax.cummax(starts, axis=0)


def rotary_tables(position):
    half_rot = ROT // 2
    freq = jnp.exp(jnp.arange(half_rot, dtype=jnp.float32) * (-2.0 * math.log(10000.0) / ROT))
    angle = position.astype(jnp.float32)[:, None] * freq[None, :]
    return (jnp.cos(angle)[:, None, :], jnp.sin(angle)[:, None, :])


def rotate(values, cos_tab, sin_tab):
    half_rot = ROT // 2
    first = values[..., :half_rot]
    second = values[..., half_rot:ROT]
    return jnp.concatenate(
        [first * cos_tab - second * sin_tab, second * cos_tab + first * sin_tab, values[..., ROT:]],
        axis=-1,
    )


def gelu_tanh(values):
    inner = 0.7978845608028654 * (values + 0.044715 * values * values * values)
    return 0.5 * values * (1.0 + jnp.tanh(inner))


def layer_norm(values, gain, shift):
    centre = values - jnp.mean(values, axis=-1, keepdims=True)
    spread = jnp.mean(centre * centre, axis=-1, keepdims=True)
    return centre * lax.rsqrt(spread + 1e-05) * gain + shift


def heads_of(values):
    return values.reshape(values.shape[0], HEADS, HEAD)


def block_scores(query_low, key_part):
    return jnp.einsum(
        "qhe,khe->hqk", heads_of(query_low), heads_of(key_part), preferred_element_type=jnp.float32
    ) * HEAD ** (-0.5)


def shards(
    hidden_in,
    cotangent,
    segment_ids,
    weight_in,
    weight_back,
    moment_in,
    moment_back,
    norm_gain,
    norm_shift,
    bias_in,
    bias_out,
    vector_moment,
):
    model_width = hidden_in.shape[2]
    tokens = hidden_in.shape[1]
    pack_len = segment_ids.shape[1]
    data_count = lax.axis_size("dp")
    group_count = lax.axis_size("group")
    devices = data_count * group_count
    qkv_rows = 3 * model_width // devices
    ff_rows = FF // devices
    out_rows = model_width // devices
    in_rows = weight_in.shape[1]
    back_rows = weight_back.shape[1]
    offset = lax.axis_index("group") * tokens
    contract_last = (((1,), (1,)), ((), ()))
    contract_first = (((0,), (0,)), ((), ()))
    x_float = hidden_in[0].astype(jnp.float32)
    normed, norm_pull = jax.vjp(layer_norm, x_float, norm_gain, norm_shift)
    normed_low = normed.astype(jnp.bfloat16)
    whole_in, whole_back = (
        lax.all_gather(weight_in, ("dp", "group"), axis=0, tiled=True),
        lax.all_gather(weight_back, ("dp", "group"), axis=0, tiled=True),
    )
    flat_in = whole_in.reshape(devices * in_rows, model_width)
    flat_back = whole_back.reshape(devices * back_rows, model_width)
    pre_mixed = lax.dot_general(
        normed_low, flat_in, contract_last, preferred_element_type=jnp.float32
    )
    pre_parts = pre_mixed.reshape(tokens, devices, in_rows)
    pre_qkv = (
        pre_parts[:, :, :qkv_rows].reshape(tokens, 3 * model_width) + bias_in[: 3 * model_width]
    )
    pre_up = pre_parts[:, :, qkv_rows:].reshape(tokens, FF) + bias_in[3 * model_width :]
    seg_pack = segment_ids[0]
    pos_pack = positions(seg_pack)
    pos_own = lax.dynamic_slice_in_dim(pos_pack, offset, tokens)
    seg_own = lax.dynamic_slice_in_dim(seg_pack, offset, tokens)
    cos_tab, sin_tab = rotary_tables(pos_own)

    def rotate_both(query_part, key_part):
        return (rotate(query_part, cos_tab, sin_tab), rotate(key_part, cos_tab, sin_tab))

    (rot_query, rot_keys), rotary_pull = jax.vjp(
        rotate_both,
        heads_of(pre_qkv[:, :model_width]),
        heads_of(pre_qkv[:, model_width : 2 * model_width]),
    )
    query_low = rot_query.reshape(tokens, model_width).astype(jnp.bfloat16)
    key_low = rot_keys.reshape(tokens, model_width).astype(jnp.bfloat16)
    value_low = pre_qkv[:, 2 * model_width :].astype(jnp.bfloat16)
    keys_all, values_all = (
        lax.all_gather(key_low, "group", axis=0, tiled=True),
        lax.all_gather(value_low, "group", axis=0, tiled=True),
    )
    key_block = min(512, pack_len)
    block_count = pack_len // key_block
    query_index = offset + jnp.arange(tokens, dtype=jnp.int32)
    index_pack = jnp.arange(pack_len, dtype=jnp.int32)
    stacked = (
        keys_all.reshape(block_count, key_block, model_width),
        values_all.reshape(block_count, key_block, model_width),
        seg_pack.reshape(block_count, key_block),
        index_pack.reshape(block_count, key_block),
    )

    def allowed_of(seg_part, index_part):
        return (seg_own[:, None] == seg_part[None, :]) & (
            index_part[None, :] <= query_index[:, None]
        )

    def max_step(running, block_item):
        key_part, value_part, seg_part, index_part = block_item
        allowed = allowed_of(seg_part, index_part)

        def max_compute(state):
            scores = jnp.where(allowed[None], block_scores(query_low, key_part), NEG)
            row_max = jnp.maximum(state[0], jnp.max(scores, axis=-1))
            row_total = state[1] * jnp.exp(state[0] - row_max) + jnp.sum(
                jnp.exp(scores - row_max[..., None]), axis=-1
            )
            return (row_max, row_total)

        return (lax.cond(jnp.any(allowed), max_compute, lambda state: state, running), None)

    start_state = (
        jnp.full((HEADS, tokens), NEG, jnp.float32),
        jnp.zeros((HEADS, tokens), jnp.float32),
    )
    (row_max, row_total), _ = lax.scan(max_step, start_state, stacked)
    log_total = row_max + jnp.log(row_total)

    def probability_of(key_part, allowed):
        return jnp.where(
            allowed[None], jnp.exp(block_scores(query_low, key_part) - log_total[..., None]), 0.0
        )

    def out_step(running, block_item):
        key_part, value_part, seg_part, index_part = block_item
        allowed = allowed_of(seg_part, index_part)

        def out_compute(state):
            prob_low = probability_of(key_part, allowed).astype(jnp.bfloat16)
            return state + jnp.einsum(
                "hqk,khe->qhe", prob_low, heads_of(value_part), preferred_element_type=jnp.float32
            )

        return (lax.cond(jnp.any(allowed), out_compute, lambda state: state, running), None)

    attended, _ = lax.scan(out_step, jnp.zeros((tokens, HEADS, HEAD), jnp.float32), stacked)
    attended_low = attended.reshape(tokens, model_width).astype(jnp.bfloat16)
    activated_low = gelu_tanh(pre_up).astype(jnp.bfloat16)
    back_in = jnp.concatenate(
        [
            attended_low.reshape(tokens, devices, out_rows),
            activated_low.reshape(tokens, devices, ff_rows),
        ],
        axis=2,
    ).reshape(tokens, devices * back_rows)
    branch_sum = jnp.dot(back_in, flat_back, preferred_element_type=jnp.float32)
    block_out = (x_float + branch_sum + bias_out).astype(jnp.bfloat16)
    grad_y = cotangent[0]
    grad_back_in = lax.dot_general(
        grad_y, flat_back, contract_last, preferred_element_type=jnp.float32
    )
    grad_parts = grad_back_in.reshape(tokens, devices, back_rows)
    grad_attended = grad_parts[:, :, :out_rows].reshape(tokens, model_width).astype(jnp.bfloat16)
    grad_activated = grad_parts[:, :, out_rows:].reshape(tokens, FF)
    _, gelu_pull = jax.vjp(gelu_tanh, pre_up)
    grad_pre_up = gelu_pull(grad_activated)[0]
    grad_heads = heads_of(grad_attended)

    def delta_step(running, block_item):
        key_part, value_part, seg_part, index_part = block_item
        allowed = allowed_of(seg_part, index_part)

        def delta_compute(state):
            grad_prob = jnp.einsum(
                "qhe,khe->hqk", grad_heads, heads_of(value_part), preferred_element_type=jnp.float32
            )
            return state + jnp.sum(probability_of(key_part, allowed) * grad_prob, axis=-1)

        return (lax.cond(jnp.any(allowed), delta_compute, lambda state: state, running), None)

    delta, _ = lax.scan(delta_step, jnp.zeros((HEADS, tokens), jnp.float32), stacked)

    def score_grads(key_part, value_part, allowed):
        probability = probability_of(key_part, allowed)
        grad_prob = jnp.einsum(
            "qhe,khe->hqk", grad_heads, heads_of(value_part), preferred_element_type=jnp.float32
        )
        return (probability, (probability * (grad_prob - delta[..., None])).astype(jnp.bfloat16))

    def query_step(running, block_item):
        key_part, value_part, seg_part, index_part = block_item
        allowed = allowed_of(seg_part, index_part)

        def query_compute(state):
            probability, grad_scores = score_grads(key_part, value_part, allowed)
            return state + jnp.einsum(
                "hqk,khe->qhe", grad_scores, heads_of(key_part), preferred_element_type=jnp.float32
            )

        return (lax.cond(jnp.any(allowed), query_compute, lambda state: state, running), None)

    grad_query, _ = lax.scan(query_step, jnp.zeros((tokens, HEADS, HEAD), jnp.float32), stacked)
    grad_query = grad_query * HEAD ** (-0.5)
    query_heads = heads_of(query_low)
    sub_rows = math.gcd(tokens * lax.axis_size("group"), 512)
    part_count = tokens * lax.axis_size("group") // sub_rows

    def one_part(part_index):
        begin = part_index * sub_rows
        key_part = lax.dynamic_slice_in_dim(keys_all, begin, sub_rows)
        value_part = lax.dynamic_slice_in_dim(values_all, begin, sub_rows)
        seg_part = lax.dynamic_slice_in_dim(seg_pack, begin, sub_rows)
        index_part = begin + jnp.arange(sub_rows, dtype=jnp.int32)
        allowed = allowed_of(seg_part, index_part)

        def one_compute(unused):
            probability, grad_scores = score_grads(key_part, value_part, allowed)
            grad_value = jnp.einsum(
                "hqk,qhe->khe",
                probability.astype(jnp.bfloat16),
                grad_heads,
                preferred_element_type=jnp.float32,
            )
            grad_key = jnp.einsum(
                "hqk,qhe->khe", grad_scores, query_heads, preferred_element_type=jnp.float32
            ) * HEAD ** (-0.5)
            return jnp.concatenate(
                [
                    grad_key.reshape(sub_rows, model_width),
                    grad_value.reshape(sub_rows, model_width),
                ],
                axis=1,
            )

        empty = jnp.zeros((sub_rows, 2 * model_width), jnp.float32)
        return lax.cond(jnp.any(allowed), one_compute, lambda unused: empty, 0)

    key_grads = lax.psum_scatter(
        lax.map(one_part, jnp.arange(part_count))
        .reshape(tokens * lax.axis_size("group"), 2 * model_width)
        .astype(jnp.bfloat16),
        "group",
        scatter_dimension=0,
        tiled=True,
    ).astype(jnp.float32)
    grad_q_pre, grad_k_pre = rotary_pull((grad_query, heads_of(key_grads[:, :model_width])))
    grad_qkv = jnp.concatenate(
        [
            grad_q_pre.reshape(tokens, model_width),
            grad_k_pre.reshape(tokens, model_width),
            key_grads[:, model_width:],
        ],
        axis=1,
    )
    grad_pre_mixed = (
        jnp.concatenate(
            [
                grad_qkv.reshape(tokens, devices, qkv_rows),
                grad_pre_up.reshape(tokens, devices, ff_rows),
            ],
            axis=2,
        )
        .reshape(tokens, devices * in_rows)
        .astype(jnp.bfloat16)
    )
    grad_normed = jnp.dot(grad_pre_mixed, flat_in, preferred_element_type=jnp.float32)
    grad_x_norm, grad_gain, grad_shift = norm_pull(grad_normed)
    grad_y_float = grad_y.astype(jnp.float32)
    grad_hidden = grad_y_float + grad_x_norm
    ones_row = jnp.ones((1, tokens), jnp.bfloat16)
    bias_sums = jnp.dot(ones_row, grad_pre_mixed, preferred_element_type=jnp.float32).reshape(
        devices, in_rows
    )
    grad_bias_in = jnp.concatenate(
        [bias_sums[:, :qkv_rows].reshape(-1), bias_sums[:, qkv_rows:].reshape(-1)]
    )
    grad_bias_out = jnp.sum(grad_y_float, axis=0)
    rows_dev = in_rows + back_rows
    mixed_parts = grad_pre_mixed.reshape(tokens, devices, in_rows)
    back_parts = back_in.reshape(tokens, devices, back_rows)
    term_in = jnp.einsum("tki,td->kid", mixed_parts, normed_low, preferred_element_type=jnp.float32)
    term_back = jnp.einsum("tki,td->kid", back_parts, grad_y, preferred_element_type=jnp.float32)
    own_grads = lax.psum_scatter(
        jnp.concatenate([term_in, term_back], axis=1).reshape(
            rows_dev * lax.axis_size(("dp", "group")), model_width
        ),
        ("dp", "group"),
        scatter_dimension=0,
        tiled=True,
    )
    grad_in = own_grads[:in_rows][None]
    grad_back = own_grads[in_rows:][None]
    moment_in_new = MOMENTUM * moment_in + grad_in
    moment_back_new = MOMENTUM * moment_back + grad_back
    part_qkv = moment_in_new[0, :qkv_rows]
    part_up = moment_in_new[0, qkv_rows:]
    part_out = moment_back_new[0, :out_rows]
    part_down = moment_back_new[0, out_rows:]
    squares = jnp.stack(
        [
            jnp.sum(part_qkv * part_qkv),
            jnp.sum(part_up * part_up),
            jnp.sum(part_out * part_out),
            jnp.sum(part_down * part_down),
        ]
    )
    vector_local = jnp.concatenate([grad_gain, grad_shift, grad_bias_in, grad_bias_out])
    vector_grad, square_sums = lax.psum((vector_local, squares), ("dp", "group"))
    norms = jnp.sqrt(square_sums) + 1e-07

    def scaled_slot(matrix_part, matrix_index):
        scaled = (matrix_part / norms[matrix_index]).astype(jnp.bfloat16)
        scaled = jnp.pad(scaled, ((0, ff_rows - matrix_part.shape[0]), (0, 0)))
        return scaled[None]

    unused_slots = jnp.zeros((data_count - 4, ff_rows, model_width), jnp.bfloat16)
    send_slots = jnp.concatenate(
        [
            scaled_slot(part_qkv, 0),
            scaled_slot(part_up, 1),
            scaled_slot(part_out, 2),
            scaled_slot(part_down, 3),
            unused_slots,
        ],
        axis=0,
    )
    owned = lax.all_to_all(send_slots, "dp", split_axis=0, concat_axis=0, tiled=True)
    current = owned.reshape(data_count * ff_rows, model_width)
    for iteration in range(NS_ITERS):
        partial_gram = lax.dot_general(
            current, current, contract_first, preferred_element_type=jnp.float32
        )
        gram_part = lax.psum_scatter(
            partial_gram.astype(jnp.bfloat16), "group", scatter_dimension=0, tiled=True
        )
        gram_full = lax.all_gather(gram_part, "group", axis=0, tiled=True)
        poly_rows = (
            NS_B * gram_part.astype(jnp.float32)
            + NS_C * jnp.dot(gram_part, gram_full, preferred_element_type=jnp.float32)
        ).astype(jnp.bfloat16)
        poly_full = lax.all_gather(poly_rows, "group", axis=0, tiled=True)
        current = (
            NS_A * current.astype(jnp.float32)
            + jnp.dot(current, poly_full, preferred_element_type=jnp.float32)
        ).astype(jnp.bfloat16)
    returned = lax.all_to_all(
        current.reshape(data_count, ff_rows, model_width),
        "dp",
        split_axis=0,
        concat_axis=0,
        tiled=True,
    )

    def matrix_rows(matrix_index, row_count):
        return returned[matrix_index, :row_count].astype(jnp.float32)

    scale_qkv = math.sqrt(3.0 * model_width)
    scale_ff = math.sqrt(1.0 * FF)
    scale_out = math.sqrt(1.0 * model_width)
    step_in = jnp.concatenate(
        [-scale_qkv * matrix_rows(0, qkv_rows), -scale_ff * matrix_rows(1, ff_rows)], axis=0
    )[None]
    step_back = jnp.concatenate(
        [-scale_out * matrix_rows(2, out_rows), -scale_ff * matrix_rows(3, ff_rows)], axis=0
    )[None]
    total_tokens = tokens * devices
    bias_out_grad = vector_grad[vector_grad.shape[0] - model_width :]
    vector_moment_new = MOMENTUM * vector_moment + vector_grad
    vector_step = -(0.2 / math.sqrt(total_tokens)) * vector_moment_new
    return (
        block_out[None],
        grad_hidden[None],
        grad_in,
        grad_back,
        moment_in_new,
        moment_back_new,
        step_in,
        step_back,
        vector_grad,
        vector_moment_new,
        vector_step,
        bias_out_grad,
    )


def solution(mesh):
    in_specs = (
        P("dp", "group", None),
        P("dp", "group", None),
        P("dp", None),
        P(("dp", "group"), None, None),
        P(("dp", "group"), None, None),
        P(("dp", "group"), None, None),
        P(("dp", "group"), None, None),
        P(),
        P(),
        P(),
        P(),
        P(),
    )
    out_specs = (
        P("dp", "group", None),
        P("dp", "group", None),
        P(("dp", "group"), None, None),
        P(("dp", "group"), None, None),
        P(("dp", "group"), None, None),
        P(("dp", "group"), None, None),
        P(("dp", "group"), None, None),
        P(("dp", "group"), None, None),
        P(),
        P(),
        P(),
        P(),
    )
    return jax.shard_map(shards, mesh=mesh, in_specs=in_specs, out_specs=out_specs, check_vma=False)
```

profile of v0, /device:TPU:1, one launch (start us, length us, event | category | flops | bytes accessed | tf_op | source)
XLA Modules:
  0.0 4646.1 jit_solution(18318952346816722356)
XLA Ops:
  12.9 316.6 %all-gather.15.cloned.1.call-done = bf16[32,448,2048]{2,1,0:T(8,128)(2,1)} async-done(((bf16[1,448,2048]{2,1,0:T(8,128)(2,1)}), bf16[32,448,2048]{2,1,0:T(8,128)(2,1)}) %all-gather.15.cloned.1.call-update) | async-done | bytes 58720272 | tf_op jit(solution)/shard_map/all_gather | solution.py:99
  329.5 29.1 fusion.77
  371.2 194.6 %all-gather.21.cloned.1.call-done = bf16[32,320,2048]{2,1,0:T(8,128)(2,1)} async-done(((bf16[1,320,2048]{2,1,0:T(8,128)(2,1)}), bf16[32,320,2048]{2,1,0:T(8,128)(2,1)}) %all-gather.21.cloned.1.call-update) | async-done | bytes 41943056 | tf_op jit(solution)/shard_map/all_gather | solution.py:100
  565.8 18.8 fusion.83
  590.2 58.4 %all-gather.17.cloned.1.call-done = bf16[2048,2048]{0,1:T(8,128)(2,1)} async-done(((bf16[256,2048]{0,1:T(8,128)(2,1)}), bf16[2048,2048]{0,1:T(8,128)(2,1)}) %all-gather.17.cloned.1.call-update) | async-done | bytes 8388624 | tf_op jit(solution)/shard_map/all_gather | solution.py:130
  648.7 7.4 copy.117
  656.1 25.0 while.66
  657.6 18.8 conditional.15
  667.0 9.4 exponential_reduce_fusion
  681.1 50.3 %all-gather.19.cloned.1.call-done = bf16[2048,2048]{0,1:T(8,128)(2,1)} async-done(((bf16[256,2048]{0,1:T(8,128)(2,1)}), bf16[2048,2048]{0,1:T(8,128)(2,1)}) %all-gather.19.cloned.1.call-update) | async-done | bytes 8388624 | tf_op jit(solution)/shard_map/all_gather | solution.py:131
  731.4 7.5 copy.116
  738.9 17.9 while.68
  740.9 11.3 conditional.17
  757.5 105.0 %while.70 = (s32[]{:T(128)}, bf16[4,512,4096]{2,1,0:T(8,128)(2,1)}, s32[256]{0:T(256)S(1)}, s32[4]{0:T(128)S(1)}, s32[2048]{0:T(1024)}, /*index=5*/bf16[2048,204...) while((s32[]{:T(128)}, bf16[4,512,4096]{2,1,0:T(8,128)(2,1)}, ...), condition=%wide.region_31.32_spmd.clone, body=%wide.region_27.31_spmd.clone.sunk | while | flops 2200437504 | bytes 105362784 | solution.py:280
  761.0 39.5 conditional.19
  766.0 8.2 fusion.113
  774.2 11.6 broadcast_multiply_fusion
  785.9 10.7 fusion.22
  862.5 22.5 copy.83
  885.9 7.8 fusion.39
  893.7 11.4 fusion.36
  906.7 18.4 while.67
  908.2 12.3 conditional.16
  912.0 8.4 bitcast_add_fusion
  929.4 29.9 while.69
  931.1 23.5 conditional.18
  935.0 8.1 fusion.112
  943.1 11.6 bitcast_add_fusion.1
  962.8 31.0 fusion.42
  993.8 151.4 %reduce-scatter.8.cloned.1.call-done = bf16[256,4096]{0,1:T(8,128)(2,1)} async-done(((bf16[2048,4096]{0,1:T(8,128)(2,1)}), bf16[256,4096]{0,1:T(8,128)(2,1)}) %reduce-scatter.8.cloned.1.call-update) | async-done | bytes 2097168 | tf_op jit(solution)/shard_map/reduce_scatter | solution.py:279
  1150.8 41.3 fusion.80
  1192.1 131.9 %pad_maximum_fusion = f32[32,768,2048]{2,1,0:T(8,128)} fusion(f32[32,320,2048]{2,1,0:T(8,128)} %fusion.42, f32[32,448,2048]{2,1,0:T(8,128)} %fusion.80), kind=kLoop, calls=%fused_computation.70 | loop fusion | flops 50331648 | bytes 402653184 | tf_op jit(solution)/shard_map/concatenate | solution.py:325
  1324.1 1614.4 %reduce-scatter.10.cloned.1.call-done = f32[768,2048]{1,0:T(8,128)} async-done(((f32[24576,2048]{1,0:T(8,128)}), f32[768,2048]{1,0:T(8,128)}) %reduce-scatter.10.cloned.1.call-update) | async-done | bytes 6291472 | tf_op jit(solution)/shard_map/reduce_scatter | solution.py:324
  2954.5 37.7 psum.14
  2998.5 48.8 %all_to_all.10 = bf16[4,256,2048]{2,1,0:T(8,128)(2,1)S(1)} all-to-all(bf16[4,256,2048]{2,1,0:T(8,128)(2,1)S(1)} %pad_maximum_fusion.3), channel_id=1, replica_groups=mesh['dp'=4,'group'=8] {'dp'}, dimensions={0} | all-to-all | bytes 8388608 | tf_op jit(solution)/shard_map/all_to_all | solution.py:368
  3049.3 11.5 bitcast_convert_fusion
  3060.9 88.4 %reduce-scatter.12.cloned.1.call-done = bf16[256,2048]{1,0:T(8,128)(2,1)} async-done(((bf16[2048,2048]{1,0:T(8,128)(2,1)}), bf16[256,2048]{1,0:T(8,128)(2,1)}) %reduce-scatter.12.cloned.1.call-update) | async-done | bytes 1048592 | tf_op jit(solution)/shard_map/reduce_scatter | solution.py:374
  3149.4 84.5 %all-gather.23.cloned.1.call-done = bf16[2048,2048]{1,0:T(8,128)(2,1)} async-done(((bf16[256,2048]{1,0:T(8,128)(2,1)}), bf16[2048,2048]{1,0:T(8,128)(2,1)}) %all-gather.23.cloned.1.call-update) | async-done | bytes 8388624 | tf_op jit(solution)/shard_map/all_gather | solution.py:377
  3241.3 80.7 %all-gather.25.cloned.1.call-done = bf16[2048,2048]{1,0:T(8,128)(2,1)} async-done(((bf16[256,2048]{1,0:T(8,128)(2,1)}), bf16[2048,2048]{1,0:T(8,128)(2,1)}) %all-gather.25.cloned.1.call-update) | async-done | bytes 8388624 | tf_op jit(solution)/shard_map/all_gather | solution.py:382
  3322.0 13.3 add_convert_fusion.4
  3337.3 11.5 convolution_convert_fusion.3
  3348.9 85.7 %reduce-scatter.14.cloned.1.call-done = bf16[256,2048]{1,0:T(8,128)(2,1)} async-done(((bf16[2048,2048]{1,0:T(8,128)(2,1)}), bf16[256,2048]{1,0:T(8,128)(2,1)}) %reduce-scatter.14.cloned.1.call-update) | async-done | bytes 1048592 | tf_op jit(solution)/shard_map/reduce_scatter | solution.py:374
  3434.7 84.6 %all-gather.27.cloned.1.call-done = bf16[2048,2048]{1,0:T(8,128)(2,1)} async-done(((bf16[256,2048]{1,0:T(8,128)(2,1)}), bf16[2048,2048]{1,0:T(8,128)(2,1)}) %all-gather.27.cloned.1.call-update) | async-done | bytes 8388624 | tf_op jit(solution)/shard_map/all_gather | solution.py:377
  3526.6 80.7 %all-gather.29.cloned.1.call-done = bf16[2048,2048]{1,0:T(8,128)(2,1)} async-done(((bf16[256,2048]{1,0:T(8,128)(2,1)}), bf16[2048,2048]{1,0:T(8,128)(2,1)}) %all-gather.29.cloned.1.call-update) | async-done | bytes 8388624 | tf_op jit(solution)/shard_map/all_gather | solution.py:382
  3607.3 13.3 add_convert_fusion.3
  3622.7 11.5 convolution_convert_fusion.2
  3634.3 85.7 %reduce-scatter.16.cloned.1.call-done = bf16[256,2048]{1,0:T(8,128)(2,1)} async-done(((bf16[2048,2048]{1,0:T(8,128)(2,1)}), bf16[256,2048]{1,0:T(8,128)(2,1)}) %reduce-scatter.16.cloned.1.call-update) | async-done | bytes 1048592 | tf_op jit(solution)/shard_map/reduce_scatter | solution.py:374
  3720.0 84.4 %all-gather.31.cloned.1.call-done = bf16[2048,2048]{1,0:T(8,128)(2,1)} async-done(((bf16[256,2048]{1,0:T(8,128)(2,1)}), bf16[2048,2048]{1,0:T(8,128)(2,1)}) %all-gather.31.cloned.1.call-update) | async-done | bytes 8388624 | tf_op jit(solution)/shard_map/all_gather | solution.py:377
  3811.8 80.7 %all-gather.33.cloned.1.call-done = bf16[2048,2048]{1,0:T(8,128)(2,1)} async-done(((bf16[256,2048]{1,0:T(8,128)(2,1)}), bf16[2048,2048]{1,0:T(8,128)(2,1)}) %all-gather.33.cloned.1.call-update) | async-done | bytes 8388624 | tf_op jit(solution)/shard_map/all_gather | solution.py:382
  3892.5 13.5 add_convert_fusion.2
  3908.1 11.5 convolution_convert_fusion.1
  3919.6 85.7 %reduce-scatter.18.cloned.1.call-done = bf16[256,2048]{1,0:T(8,128)(2,1)} async-done(((bf16[2048,2048]{1,0:T(8,128)(2,1)}), bf16[256,2048]{1,0:T(8,128)(2,1)}) %reduce-scatter.18.cloned.1.call-update) | async-done | bytes 1048592 | tf_op jit(solution)/shard_map/reduce_scatter | solution.py:374
  4005.4 84.4 %all-gather.35.cloned.1.call-done = bf16[2048,2048]{1,0:T(8,128)(2,1)} async-done(((bf16[256,2048]{1,0:T(8,128)(2,1)}), bf16[2048,2048]{1,0:T(8,128)(2,1)}) %all-gather.35.cloned.1.call-update) | async-done | bytes 8388624 | tf_op jit(solution)/shard_map/all_gather | solution.py:377
  4097.2 80.7 %all-gather.37.cloned.1.call-done = bf16[2048,2048]{1,0:T(8,128)(2,1)} async-done(((bf16[256,2048]{1,0:T(8,128)(2,1)}), bf16[2048,2048]{1,0:T(8,128)(2,1)}) %all-gather.37.cloned.1.call-update) | async-done | bytes 8388624 | tf_op jit(solution)/shard_map/all_gather | solution.py:382
  4177.9 13.3 add_convert_fusion.1
  4193.2 11.5 convolution_convert_fusion
  4204.8 85.7 %reduce-scatter.20.cloned.1.call-done = bf16[256,2048]{1,0:T(8,128)(2,1)} async-done(((bf16[2048,2048]{1,0:T(8,128)(2,1)}), bf16[256,2048]{1,0:T(8,128)(2,1)}) %reduce-scatter.20.cloned.1.call-update) | async-done | bytes 1048592 | tf_op jit(solution)/shard_map/reduce_scatter | solution.py:374
  4290.5 84.4 %all-gather.39.cloned.1.call-done = bf16[2048,2048]{1,0:T(8,128)(2,1)} async-done(((bf16[256,2048]{1,0:T(8,128)(2,1)}), bf16[2048,2048]{1,0:T(8,128)(2,1)}) %all-gather.39.cloned.1.call-update) | async-done | bytes 8388624 | tf_op jit(solution)/shard_map/all_gather | solution.py:377
  4374.9 7.3 fusion.58
  4387.8 26.4 fusion.103
  4415.3 47.7 %all-gather.41.cloned.1.call-done = bf16[2048,2048]{1,0:T(8,128)(2,1)} async-done(((bf16[256,2048]{1,0:T(8,128)(2,1)}), bf16[2048,2048]{1,0:T(8,128)(2,1)}) %all-gather.41.cloned.1.call-update) | async-done | bytes 8388624 | tf_op jit(solution)/shard_map/all_gather | solution.py:382
  4463.0 14.4 add_convert_fusion
  4486.7 21.2 fusion.63
  4507.9 119.3 %all-reduce.10.cloned.1.call-done = f32[20480]{0:T(1024)} async-done(((f32[20480]{0:T(1024)}), f32[20480]{0:T(1024)}) %all-reduce.10.cloned.1.call-update) | async-done | bytes 81936 | tf_op jit(solution)/shard_map/psum | solution.py:349
  (339 shorter events, 248.1 us)
Async XLA Ops:
  7.2 4.6 copy-start.3
  7.2 322.3 %copy-start.27 = (f32[2048]{0:T(1024)S(1)}, f32[2048]{0:T(1024)}, u32[]{:S(2)}) copy-start(f32[2048]{0:T(1024)} %param.39) | copy-start | bytes 24580
  7.2 322.3 %copy-start.38 = (f32[2048]{0:T(1024)S(1)}, f32[2048]{0:T(1024)}, u32[]{:S(2)}) copy-start(f32[2048]{0:T(1024)} %param.40) | copy-start | bytes 24580
  7.2 322.3 %all-gather.15.cloned.1.call-start = ((), (), s32[]{:S(2)}) async-start(), calls=%async_computation.9 | async-start | bytes 60555264 | tf_op jit(solution)/shard_map/all_gather | solution.py:99
  7.9 557.9 %all-gather.21.cloned.1.call-start = ((), (), s32[]{:S(2)}) async-start(), calls=%async_computation.12 | async-start | bytes 43253760 | tf_op jit(solution)/shard_map/all_gather | solution.py:100
  8.7 640.0 %all-gather.17.cloned.1.call-start = ((), (), s32[]{:S(2)}) async-start(), calls=%async_computation.10 | async-start | bytes 9437184 | tf_op jit(solution)/shard_map/all_gather | solution.py:130
  11.7 346.8 %copy-start.30 = (f32[256]{0:T(256)}, f32[256]{0:T(256)S(1)}, u32[]{:S(2)}) copy-start(f32[256]{0:T(256)S(1)} %broadcast_multiply_fusion.3) | copy-start | bytes 3076
  12.8 345.8 %copy-start.33 = (f32[256]{0:T(256)}, f32[256]{0:T(256)S(1)}, u32[]{:S(2)}) copy-start(f32[256]{0:T(256)S(1)} %fusion.97) | copy-start | bytes 3076
  12.9 575.0 %copy-start.20 = (f32[256,16]{0,1:T(8,128)}, f32[256,16]{0,1:T(8,128)S(1)}, u32[]{:S(2)}) copy-start(f32[256,16]{0,1:T(8,128)S(1)} %get-tuple-element.1091) | copy-start | bytes 49156
  12.9 575.0 %copy-start.22 = (f32[256,16]{0,1:T(8,128)}, f32[256,16]{0,1:T(8,128)S(1)}, u32[]{:S(2)}) copy-start(f32[256,16]{0,1:T(8,128)S(1)} %get-tuple-element.1092) | copy-start | bytes 49156
  358.6 2.8 slice-start
  358.6 2.8 slice-start.2
  362.4 3.3 copy-start.7
  365.8 4.8 copy-start.24
  367.0 364.4 %all-gather.19.cloned.1.call-start = ((), (), s32[]{:S(2)}) async-start(), calls=%async_computation.11 | async-start | bytes 9437184 | tf_op jit(solution)/shard_map/all_gather | solution.py:131
  369.8 775.4 %reduce-scatter.8.cloned.1.call-start = ((), (), s32[]{:S(2)}) async-start(), calls=%async_computation.13 | async-start | bytes 18874368 | tf_op jit(solution)/shard_map/reduce_scatter | solution.py:279
  584.6 5.6 copy-start.9
  785.9 10.7 copy-start
  885.1 2053.4 %reduce-scatter.10.cloned.1.call-start = ((), (), s32[]{:S(2)}) async-start(), calls=%async_computation.14 | async-start | bytes 207618048 | tf_op jit(solution)/shard_map/reduce_scatter | solution.py:324
  893.7 13.0 copy-start.17
  893.7 13.0 copy-start.19
  959.3 3.0 copy-start.8
  959.3 3.5 copy-start.11
  993.8 152.8 %copy-start.21 = (f32[256,16]{0,1:T(8,128)S(1)}, f32[256,16]{0,1:T(8,128)}, u32[]{:S(2)}) copy-start(f32[256,16]{0,1:T(8,128)} %copy-done.20) | copy-start | bytes 49156
  993.8 152.8 %copy-start.23 = (f32[256,16]{0,1:T(8,128)S(1)}, f32[256,16]{0,1:T(8,128)}, u32[]{:S(2)}) copy-start(f32[256,16]{0,1:T(8,128)} %copy-done.22) | copy-start | bytes 49156
  1148.1 2.7 copy-start.4
  1148.1 2.7 copy-start.28
  1148.1 2.7 copy-start.31
  1148.2 2.6 copy-start.34
  1148.2 2.6 copy-start.39
  1324.1 1825.2 %reduce-scatter.12.cloned.1.call-start = ((), (), s32[]{:S(2)}) async-start(), calls=%async_computation.15 | async-start | bytes 9437184 | tf_op jit(solution)/shard_map/reduce_scatter | solution.py:374
  2938.5 6.7 copy-start.10
  2938.5 7.3 copy-start.14
  2943.3 52.9 %copy-start.6 = (f32[1,320,2048]{2,1,0:T(8,128)}, f32[1,320,2048]{2,1,0:T(8,128)S(1)}, u32[]{:S(2)}) copy-start(f32[1,320,2048]{2,1,0:T(8,128)S(1)} %get-tuple-element.1673) | copy-start | bytes 7864324
  2993.5 3.6 copy-start.2
  3047.3 2.1 copy-start.12
  3060.9 173.0 %all-gather.23.cloned.1.call-start = ((), (), s32[]{:S(2)}) async-start(), calls=%async_computation.16 | async-start | bytes 9437184 | tf_op jit(solution)/shard_map/all_gather | solution.py:377
  3149.3 172.7 %all-gather.25.cloned.1.call-start = ((), (), s32[]{:S(2)}) async-start(), calls=%async_computation.17 | async-start | bytes 9437184 | tf_op jit(solution)/shard_map/all_gather | solution.py:382
  3241.3 193.3 %reduce-scatter.14.cloned.1.call-start = ((), (), s32[]{:S(2)}) async-start(), calls=%async_computation.18 | async-start | bytes 9437184 | tf_op jit(solution)/shard_map/reduce_scatter | solution.py:374
  3335.3 2.1 copy-start.42
  3348.9 170.4 %all-gather.27.cloned.1.call-start = ((), (), s32[]{:S(2)}) async-start(), calls=%async_computation.19 | async-start | bytes 9437184 | tf_op jit(solution)/shard_map/all_gather | solution.py:377
  3434.6 172.7 %all-gather.29.cloned.1.call-start = ((), (), s32[]{:S(2)}) async-start(), calls=%async_computation.20 | async-start | bytes 9437184 | tf_op jit(solution)/shard_map/all_gather | solution.py:382
  3526.6 193.4 %reduce-scatter.16.cloned.1.call-start = ((), (), s32[]{:S(2)}) async-start(), calls=%async_computation.21 | async-start | bytes 9437184 | tf_op jit(solution)/shard_map/reduce_scatter | solution.py:374
  3620.6 2.1 copy-start.43
  3634.2 170.2 %all-gather.31.cloned.1.call-start = ((), (), s32[]{:S(2)}) async-start(), calls=%async_computation.22 | async-start | bytes 9437184 | tf_op jit(solution)/shard_map/all_gather | solution.py:377
  3720.0 172.5 %all-gather.33.cloned.1.call-start = ((), (), s32[]{:S(2)}) async-start(), calls=%async_computation.23 | async-start | bytes 9437184 | tf_op jit(solution)/shard_map/all_gather | solution.py:382
  3811.7 193.6 %reduce-scatter.18.cloned.1.call-start = ((), (), s32[]{:S(2)}) async-start(), calls=%async_computation.24 | async-start | bytes 9437184 | tf_op jit(solution)/shard_map/reduce_scatter | solution.py:374
  3906.0 2.1 copy-start.44
  3919.6 170.2 %all-gather.35.cloned.1.call-start = ((), (), s32[]{:S(2)}) async-start(), calls=%async_computation.25 | async-start | bytes 9437184 | tf_op jit(solution)/shard_map/all_gather | solution.py:377
  4005.3 172.5 %all-gather.37.cloned.1.call-start = ((), (), s32[]{:S(2)}) async-start(), calls=%async_computation.26 | async-start | bytes 9437184 | tf_op jit(solution)/shard_map/all_gather | solution.py:382
  4097.1 193.3 %reduce-scatter.20.cloned.1.call-start = ((), (), s32[]{:S(2)}) async-start(), calls=%async_computation.27 | async-start | bytes 9437184 | tf_op jit(solution)/shard_map/reduce_scatter | solution.py:374
  4191.1 2.1 copy-start.41
  4204.7 170.2 %all-gather.39.cloned.1.call-start = ((), (), s32[]{:S(2)}) async-start(), calls=%async_computation.28 | async-start | bytes 9437184 | tf_op jit(solution)/shard_map/all_gather | solution.py:377
  4290.5 172.5 %all-gather.41.cloned.1.call-start = ((), (), s32[]{:S(2)}) async-start(), calls=%async_computation.29 | async-start | bytes 9437184 | tf_op jit(solution)/shard_map/all_gather | solution.py:382
  4382.2 5.6 copy-start.5
  4382.2 5.6 copy-start.29
  4382.3 5.6 copy-start.32
  4387.8 26.4 copy-start.37
  4387.8 26.5 copy-start.35
  4477.4 152.7 %all-to-all-start.1 = ((bf16[4,256,2048]{2,1,0:T(8,128)(2,1)}), bf16[4,256,2048]{2,1,0:T(8,128)(2,1)}, u32[]{:S(2)}, u32[]{:S(2)}) async-start(bf16[4,256,2048]{2,1,0:T(8,128)(2,1)} %bitcast.365), calls=%async_computation.8 | async-start | bytes 8388608 | tf_op jit(solution)/shard_map/all_to_all | solution.py:387
  4482.3 4.4 copy-start.40
  4482.3 144.9 %all-reduce.10.cloned.1.call-start = ((), (), s32[]{:S(2)}) async-start(), calls=%async_computation.30 | async-start | bytes 163840 | tf_op jit(solution)/shard_map/psum | solution.py:349
  4486.6 141.9 %copy-start.26 = (f32[20480]{0:T(1024)S(1)}, f32[20480]{0:T(1024)}, u32[]{:S(2)}) copy-start(f32[20480]{0:T(1024)} %param.43) | copy-start | bytes 245764
  4636.0 2.3 copy-start.15
  (8 other events, 7.5 us)
Sparse Core Ops, SparseCore 0:
  10.9 318.5 all-gather.14
  332.4 233.3 all-gather.20
  568.0 80.6 all-gather.16
  650.7 80.6 all-gather.18
  885.2 259.9 reduce-scatter.7
  1324.2 1614.2 reduce-scatter.9
  3061.0 88.2 reduce-scatter.11
  3150.9 82.9 all-gather.22
  3241.4 80.5 all-gather.24
  3349.0 85.5 reduce-scatter.13
  3436.2 82.9 all-gather.26
  3526.7 80.5 all-gather.28
  3634.3 85.5 reduce-scatter.15
  3721.4 82.9 all-gather.30
  3811.9 80.5 all-gather.32
  3919.7 85.5 reduce-scatter.17
  4006.8 82.9 all-gather.34
  4097.2 80.5 all-gather.36
  4204.8 85.5 reduce-scatter.19
  4291.9 82.9 all-gather.38
  4382.4 80.5 all-gather.40
  4489.3 137.8 all-reduce.9
where the time goes:
time: 4650 us
  waiting for transfers between devices  3730 us (80%)
  matrix products  410 us (9%)
  other arithmetic  232 us (5%)
  local copies, waits for them, and re-layouts  149 us (3%)
  blocking collectives  86.5 us (2%)
    reduce_scatter x1, waiting for transfers between devices, shards(): lax.psum_scatter(jnp.concatenate([term_in, term_back], axis=1).reshape(ro...  1610 us
    reduce_scatter x5, waiting for transfers between devices, shards(): lax.psum_scatter(partial_gram.astype(jnp.bfloat16), 'group', scatter_dime...  431 us
    all_gather x5, waiting for transfers between devices, shards(): gram_full = lax.all_gather(gram_part, 'group', axis=0, tiled=True)  422 us
    all_gather x5, waiting for transfers between devices, shards(): poly_full = lax.all_gather(poly_rows, 'group', axis=0, tiled=True)  370 us
    all_gather x1, waiting for transfers between devices, shards(): lax.all_gather(weight_in, ('dp', 'group'), axis=0, tiled=True)  317 us
    all_gather x1, waiting for transfers between devices, shards(): lax.all_gather(weight_back, ('dp', 'group'), axis=0, tiled=True)  195 us
    reduce_scatter x1, waiting for transfers between devices, shards(): lax.psum_scatter(lax.map(one_part, jnp.arange(part_count)).reshape(tokens...  151 us
    concatenate x1, other arithmetic, shards(): jnp.concatenate([term_in, term_back], axis=1)  132 us
  transfers between devices with their start and end apart: 23, of which 22 were waited for; matrix products, arithmetic and copies ran while one was open for 6% of the time, Pallas kernels for 0%

commit v1 on v0

v1 whole, which is shorter than its diff:
```python
import functools
import math

import jax
import jax.numpy as jnp
from jax import lax
from jax.experimental import pallas as pl
from jax.experimental.pallas import tpu as pltpu
from jax.sharding import PartitionSpec as P

HEADS = 32
HEAD = 64
ROT = 32
FF = 8192
SEQ_MAX = 1024
NEG = -1e30
NS_A = 3.4445
NS_B = -4.775
NS_C = 2.0315
MOMENTUM = 0.95
F32 = jnp.float32
BF16 = jnp.bfloat16
CHUNK = 256
PANEL = 512
VMEM_BYTES = 61 * 2**20


def positions(segments):
    index_all = jnp.arange(segments.shape[0], dtype=jnp.int32)
    previous = jnp.concatenate([jnp.full((1,), -1, jnp.int32), segments[:-1]])
    starts = jnp.where(segments != previous, index_all, 0)
    return index_all - lax.cummax(starts, axis=0)


def gelu_tanh(values):
    inner = 0.7978845608028654 * (values + 0.044715 * values * values * values)
    return 0.5 * values * (1.0 + jnp.tanh(inner))


def rotary_lanes(position, heads):
    half_rot = ROT // 2
    freq = jnp.exp(jnp.arange(half_rot, dtype=F32) * (-2.0 * math.log(10000.0) / ROT))
    angle = position.astype(F32)[:, None] * freq[None, :]
    cos, sin = jnp.cos(angle), jnp.sin(angle)
    rest = (position.shape[0], HEAD - ROT)
    cos_head = jnp.concatenate([cos, cos, jnp.ones(rest, F32)], axis=1)
    sin_head = jnp.concatenate([-sin, sin, jnp.zeros(rest, F32)], axis=1)
    return jnp.tile(cos_head, (1, heads)), jnp.tile(sin_head, (1, heads))


def after(values, *others):
    return pl.pallas_call(
        lambda *refs: None,
        out_shape=jax.ShapeDtypeStruct(values.shape, values.dtype),
        in_specs=[pl.BlockSpec(memory_space=pl.ANY)] * (1 + len(others)),
        out_specs=pl.BlockSpec(memory_space=pl.ANY),
        input_output_aliases={0: 0},
        name="after",
    )(values, *others)


def rows_at(index, size):
    return pl.ds(pl.multiple_of(index * size, size), size)


def attention_body(
    first_ref, pre_ref, grad_ref, start_ref, cos_ref, sin_ref, att_ref, out_ref, q_s, k_s, v_s, dk_s, dv_s, o_s, dq_s
):
    pack_len, width = grad_ref.shape
    heads = width // HEAD
    blocks = pack_len // CHUNK
    lane = lax.broadcasted_iota(jnp.int32, (CHUNK, width), 1)
    low_half = lane % HEAD < ROT // 2
    head_of = lane // HEAD

    def turn(values, rows, sign):
        swapped = jnp.where(
            low_half, pltpu.roll(values, width - ROT // 2, 1), pltpu.roll(values, ROT // 2, 1)
        )
        return values * cos_ref[rows, :] + (sign * sin_ref[rows, :]) * swapped

    def prepare(block, carry):
        rows = rows_at(block, CHUNK)
        query = turn(pre_ref[rows, :width], rows, 1.0).astype(BF16)
        q_s[rows, :] = (query.astype(F32) * HEAD ** (-0.5)).astype(BF16)
        k_s[rows, :] = turn(pre_ref[rows, width : 2 * width], rows, 1.0).astype(BF16)
        v_s[rows, :] = pre_ref[rows, 2 * width :].astype(BF16)
        dk_s[rows, :] = jnp.zeros((CHUNK, width), F32)
        dv_s[rows, :] = jnp.zeros((CHUNK, width), F32)
        return carry

    lax.fori_loop(0, blocks, prepare, 0)
    over_last = (((1,), (1,)), ((), ()))
    over_first = (((0,), (0,)), ((), ()))

    def window(block, count):
        rows = rows_at(block, CHUNK)
        span = pl.ds(pl.multiple_of((block + 1 - count) * CHUNK, CHUNK), count * CHUNK)
        shape = (CHUNK, count * CHUNK)
        column = (block + 1 - count) * CHUNK + lax.broadcasted_iota(jnp.int32, shape, 1)
        row = block * CHUNK + lax.broadcasted_iota(jnp.int32, shape, 0)
        allowed = (column >= start_ref[rows, :]) & (column <= row)
        o_s[...] = jnp.zeros((CHUNK, width), F32)
        dq_s[...] = jnp.zeros((CHUNK, width), F32)

        def one_head(head, carry):
            mine = head_of == head
            query = jnp.where(mine, q_s[rows, :], jnp.zeros((), BF16))
            grad = jnp.where(mine, grad_ref[rows, :], jnp.zeros((), BF16))
            keys, values = k_s[span, :], v_s[span, :]
            scores = lax.dot_general(query, keys, over_last, preferred_element_type=F32)
            scores = jnp.where(allowed, scores, NEG)
            prob = jnp.exp(scores - jnp.max(scores, axis=1, keepdims=True))
            prob = prob * (1.0 / jnp.sum(prob, axis=1, keepdims=True))
            prob_low = prob.astype(BF16)
            grad_prob = lax.dot_general(grad, values, over_last, preferred_element_type=F32)
            delta = jnp.sum(prob * grad_prob, axis=1, keepdims=True)
            grad_scores = (prob * (grad_prob - delta)).astype(BF16)
            o_s[...] += jnp.where(mine, jnp.dot(prob_low, values, preferred_element_type=F32), 0.0)
            dq_s[...] += jnp.where(mine, jnp.dot(grad_scores, keys, preferred_element_type=F32), 0.0)
            dk_s[span, :] += lax.dot_general(
                grad_scores, query, over_first, preferred_element_type=F32
            )
            dv_s[span, :] += lax.dot_general(prob_low, grad, over_first, preferred_element_type=F32)
            return carry

        lax.fori_loop(0, heads, one_head, 0)
        att_ref[rows, :] = o_s[...].astype(BF16)
        out_ref[rows, :width] = turn(dq_s[...] * HEAD ** (-0.5), rows, -1.0).astype(BF16)

    def one_block(block, carry):
        used = block + 1 - first_ref[block]
        for count in range(1, min(blocks, -(-(SEQ_MAX - 1) // CHUNK) + 1) + 1):
            pl.when(used == count)(functools.partial(window, block, count))
        return carry

    lax.fori_loop(0, blocks, one_block, 0)

    def finish(block, carry):
        rows = rows_at(block, CHUNK)
        out_ref[rows, width : 2 * width] = turn(dk_s[rows, :], rows, -1.0).astype(BF16)
        out_ref[rows, 2 * width :] = dv_s[rows, :].astype(BF16)
        return carry

    lax.fori_loop(0, blocks, finish, 0)


def attention(pre_qkv, grad_attended, position, part, width):
    pack_len = grad_attended.shape[0]
    start = jnp.arange(pack_len, dtype=jnp.int32) - position
    first = start[::CHUNK] // CHUNK
    cos_tab, sin_tab = rotary_lanes(position, width // HEAD)
    whole = pl.BlockSpec(memory_space=pltpu.VMEM)
    pairs = pack_len * SEQ_MAX * (width // HEAD)
    return pl.pallas_call(
        attention_body,
        grid=(1,),
        out_shape=(
            jax.ShapeDtypeStruct((pack_len, width), BF16),
            jax.ShapeDtypeStruct((pack_len, 3 * width), BF16),
        ),
        in_specs=[
            pl.BlockSpec(memory_space=pltpu.SMEM),
            pl.BlockSpec((pack_len, 3 * width), lambda step: (0, part), memory_space=pltpu.VMEM),
            pl.BlockSpec((pack_len, width), lambda step: (0, part), memory_space=pltpu.VMEM),
            whole,
            whole,
            whole,
        ],
        out_specs=(whole, whole),
        scratch_shapes=[pltpu.VMEM((pack_len, width), BF16)] * 3
        + [pltpu.VMEM((pack_len, width), F32)] * 2
        + [pltpu.VMEM((CHUNK, width), F32)] * 2,
        compiler_params=pltpu.CompilerParams(vmem_limit_bytes=VMEM_BYTES),
        cost_estimate=pl.CostEstimate(
            flops=pairs * 10 * HEAD * 4, bytes_accessed=16 * pack_len * width, transcendentals=pairs
        ),
        name="attention",
    )(first, pre_qkv, grad_attended, start[:, None], cos_tab, sin_tab)


def tri(index):
    return index * (index + 1) // 2


def packed_rows(size):
    return tri(size // CHUNK) * CHUNK


def panels(size):
    for panel in range(size // PANEL):
        yield panel, (panel + 1) * PANEL, slice(panel * PANEL, (panel + 1) * PANEL)


def symmetric(lhs, rhs, size, epilogue):
    for panel, height, columns in panels(size):
        epilogue(
            panel, height, columns, jnp.dot(lhs[:height, :], rhs[:, columns], preferred_element_type=F32)
        )


def put_mirrored(ref, height, columns, values):
    ref[:height, columns] = values
    if height > PANEL:
        ref[columns, : height - PANEL] = values[: height - PANEL, :].T


def gram_packed(x, xt_ref, size, packed_ref):
    depth = x.shape[0]
    for block in range(depth // CHUNK):
        part = slice(block * CHUNK, (block + 1) * CHUNK)
        xt_ref[:, part] = x[part, :].T
    for panel, height, columns in panels(size):
        product = jnp.dot(xt_ref[:height, :depth], x[:, columns], preferred_element_type=F32).astype(BF16)
        for half in range(PANEL // CHUNK):
            column = panel * (PANEL // CHUNK) + half
            rows = (column + 1) * CHUNK
            packed_ref[tri(column) * CHUNK : tri(column) * CHUNK + rows, :] = product[
                :rows, half * CHUNK : (half + 1) * CHUNK
            ]


def gram_body(x_ref, before_ref, packed_ref, xt_s):
    gram_packed(x_ref, xt_s, x_ref.shape[1], packed_ref)


def unpack(packed_ref, size, scale, exact_s, low_s):
    per_panel = PANEL // CHUNK
    for column in range(size // CHUNK):
        rows = (column + 1) * CHUNK
        at = tri(column) * CHUNK
        panel, half = column // per_panel, column % per_panel
        base = tri(panel) * PANEL
        lanes = slice(half * CHUNK, (half + 1) * CHUNK)
        cols = slice(column * CHUNK, (column + 1) * CHUNK)
        values = packed_ref[at : at + rows, :].astype(F32) * scale
        exact_s[base : base + rows, lanes] = values
        low = values.astype(BF16)
        low_s[:rows, cols] = low
        if column:
            low_s[cols, : rows - CHUNK] = low[: rows - CHUNK, :].T
        for other in range(half):
            left = panel * per_panel + other
            exact_s[base + column * CHUNK : base + rows, other * CHUNK : (other + 1) * CHUNK] = values[
                left * CHUNK : (left + 1) * CHUNK, :
            ].T


def iterate(x_s, exact_s, low_s, poly_s, mix_s, size, count):
    def one(step, carry):
        source, target = step % 2, (step + 1) % 2

        def poly_end(panel, height, columns, product):
            at = tri(panel) * PANEL
            values = NS_B * exact_s[at : at + height, :] + NS_C * product
            put_mirrored(poly_s, height, columns, values.astype(BF16))

        symmetric(low_s, low_s, size, poly_end)

        def x_columns(panel, inner):
            columns = rows_at(panel, PANEL)
            product = jnp.dot(x_s[source], poly_s[:, columns], preferred_element_type=F32)
            x_s[target, :, columns] = (NS_A * x_s[source, :, columns].astype(F32) + product).astype(BF16)
            return inner

        lax.fori_loop(0, size // PANEL, x_columns, 0)

        @pl.when(step < count - 1)
        def next_gram():
            def mix_end(panel, height, columns, product):
                at = tri(panel) * PANEL
                exact_s[at : at + height, :] = (NS_A * NS_A) * exact_s[at : at + height, :] + (
                    2.0 * NS_A
                ) * product
                put_mirrored(mix_s, height, columns, product.astype(BF16))

            symmetric(low_s, poly_s, size, mix_end)

            def gram_end(panel, height, columns, product):
                at = tri(panel) * PANEL
                values = exact_s[at : at + height, :] + product
                exact_s[at : at + height, :] = values
                put_mirrored(low_s, height, columns, values.astype(BF16))

            symmetric(mix_s, poly_s, size, gram_end)

        return carry

    lax.fori_loop(0, count, one, 0)


def first_body(count, packed_ref, x_ref, x_out, packed_out, x_s, exact_s, low_s, poly_s, mix_s, packed_s, sems):
    size = x_ref.shape[1]
    load_x = pltpu.make_async_copy(x_ref, x_s.at[0], sems.at[0])
    load_packed = pltpu.make_async_copy(packed_ref, packed_s, sems.at[1])
    load_x.start()
    load_packed.start()
    load_packed.wait()
    trace = jnp.zeros((1, 1), F32)
    eye = lax.broadcasted_iota(jnp.int32, (CHUNK, CHUNK), 0) == lax.broadcasted_iota(
        jnp.int32, (CHUNK, CHUNK), 1
    )
    for column in range(size // CHUNK):
        at = tri(column) * CHUNK + column * CHUNK
        block = jnp.where(eye, packed_s[at : at + CHUNK, :].astype(F32), 0.0)
        trace = trace + jnp.sum(jnp.sum(block, axis=1, keepdims=True), axis=0, keepdims=True)
    inverse = 1.0 / (jnp.sqrt(trace) + 1e-7)
    unpack(packed_s, size, inverse * inverse, exact_s, low_s)
    load_x.wait()
    iterate(x_s, exact_s, low_s, poly_s, mix_s, size, count)
    depth = x_ref.shape[0]

    def scale_rows(block, carry):
        rows = rows_at(block, CHUNK)
        x_s[count % 2, rows, :] = (x_s[count % 2, rows, :].astype(F32) * inverse).astype(BF16)
        return carry

    lax.fori_loop(0, depth // CHUNK, scale_rows, 0)
    store_x = pltpu.make_async_copy(x_s.at[count % 2], x_out, sems.at[0])
    store_x.start()
    gram_packed(x_s.at[count % 2], poly_s, size, packed_s)
    store_packed = pltpu.make_async_copy(packed_s, packed_out, sems.at[1])
    store_packed.start()
    store_x.wait()
    store_packed.wait()


def second_body(count, packed_ref, x_ref, x_out, x_s, exact_s, low_s, poly_s, mix_s, packed_s, sems):
    size = x_ref.shape[1]
    load_x = pltpu.make_async_copy(x_ref, x_s.at[0], sems.at[0])
    load_packed = pltpu.make_async_copy(packed_ref, packed_s, sems.at[1])
    load_x.start()
    load_packed.start()
    load_packed.wait()
    unpack(packed_s, size, 1.0, exact_s, low_s)
    load_x.wait()
    iterate(x_s, exact_s, low_s, poly_s, mix_s, size, count)
    store_x = pltpu.make_async_copy(x_s.at[count % 2], x_out, sems.at[0])
    store_x.start()
    store_x.wait()


def ns_scratch(depth, size):
    return [
        pltpu.VMEM((2, depth, size), BF16),
        pltpu.VMEM((tri(size // PANEL) * PANEL, PANEL), F32),
        pltpu.VMEM((size, size), BF16),
        pltpu.VMEM((size, size), BF16),
        pltpu.VMEM((size, size), BF16),
        pltpu.VMEM((packed_rows(size), CHUNK), BF16),
        pltpu.SemaphoreType.DMA((2,)),
    ]


def orthogonalize(rows, before, before_sum, beside_first, beside_last):
    depth, size = rows.shape
    group_count = lax.axis_size("group")
    packed_shape = jax.ShapeDtypeStruct((packed_rows(size), CHUNK), BF16)
    x_shape = jax.ShapeDtypeStruct((depth, size), BF16)
    vmem = pl.BlockSpec(memory_space=pltpu.VMEM)
    hbm = pl.BlockSpec(memory_space=pl.ANY)
    params = pltpu.CompilerParams(vmem_limit_bytes=VMEM_BYTES)

    def cost(products, x_steps):
        return pl.CostEstimate(
            flops=products * size**3 * 5 // 4 + x_steps * 2 * depth * size * size,
            bytes_accessed=size * size * 4,
            transcendentals=0,
        )

    def summed(packed):
        part = lax.psum_scatter(packed, "group", scatter_dimension=0, tiled=True)
        return lax.all_gather(part, "group", axis=0, tiled=True)

    packed = pl.pallas_call(
        gram_body,
        out_shape=packed_shape,
        in_specs=[vmem, hbm],
        out_specs=vmem,
        scratch_shapes=[pltpu.VMEM((size, depth), BF16)],
        compiler_params=params,
        cost_estimate=cost(0, 1),
        name="gram",
    )(rows, before)
    gathered = summed(after(packed, before_sum))
    first_result = beside_first(gathered)
    half_way, packed = pl.pallas_call(
        functools.partial(first_body, 2),
        out_shape=(x_shape, packed_shape),
        in_specs=[hbm, hbm],
        out_specs=(hbm, hbm),
        scratch_shapes=ns_scratch(depth, size),
        compiler_params=params,
        cost_estimate=cost(4, 3),
        name="first_steps",
    )(gathered, rows)
    gathered = summed(after(packed, first_result))
    last_result = beside_last(first_result, gathered)
    result = pl.pallas_call(
        functools.partial(second_body, 3),
        out_shape=x_shape,
        in_specs=[hbm, hbm],
        out_specs=hbm,
        scratch_shapes=ns_scratch(depth, size),
        compiler_params=params,
        cost_estimate=cost(7, 3),
        name="last_steps",
    )(gathered, half_way)
    return result, last_result


def flip(bit):
    return [(index, index ^ bit) for index in range(4)]


def send(values, bit):
    return lax.ppermute(values, "dp", flip(bit))


def two_by_two():
    return lax.axis_size("dp") == 4


def by_distance(parts):
    if not two_by_two():
        return parts
    me = lax.axis_index("dp")
    return jnp.stack([lax.dynamic_index_in_dim(parts, me ^ r, 0, keepdims=False) for r in range(4)])


def gather_near(own):
    if not two_by_two():
        return lax.all_gather(own, "dp", axis=0, tiled=False)
    return own, send(own, 1), send(own, 2)


def gather_far(near):
    if not two_by_two():
        return near
    own, from_x, from_y = near
    half = own.shape[0] // 2
    first, second = send(from_y[:half], 1), send(from_x[half:], 2)
    return jnp.stack([own, from_x, from_y, jnp.concatenate([first, second], axis=0)])


def came(near):
    return near[1:] if two_by_two() else (near,)


def gather_dp(own):
    return gather_far(gather_near(own))


def scatter_start(parts):
    if not two_by_two():
        return lax.psum_scatter(parts, "dp", scatter_dimension=0, tiled=False).astype(F32)
    half = parts.shape[1] // 2
    terms = parts.reshape(2, 2, parts.shape[1], parts.shape[2])
    left, right = terms[:, :, :half], terms[:, :, half:]
    return terms, send(left[:, 1], 1), send(right[1], 2)


def scatter_next(state, *others):
    if not two_by_two():
        return state
    terms, left_in, right_in = state
    half = terms.shape[2] // 2
    terms = after(terms, *others)
    left, right = terms[:, 0, :half], terms[0, :, half:]
    left_sum = left.astype(F32) + left_in.astype(F32)
    right_sum = right.astype(F32) + right_in.astype(F32)
    return left_sum[0], left_sum[1].astype(BF16), right_sum[0], right_sum[1].astype(BF16)


def scatter_end(state, *others):
    if not two_by_two():
        return state
    left, left_out, right, right_out = state
    left_in, right_in = send(left_out, 2), send(right_out, 1)
    if others:
        left = after(left, *others)
    return jnp.concatenate([left + left_in.astype(F32), right + right_in.astype(F32)], axis=0)


def flying(state):
    return state[1::2] if two_by_two() else (state,)


def owners_start(slots, owners):
    me = lax.axis_index("dp")
    half = slots.shape[1] // 2

    def slot_for(distance):
        picked = slots[0]
        for k, owner in enumerate(owners[1:], 1):
            picked = jnp.where((me ^ distance) == owner, slots[k], picked)
        return picked

    far = slot_for(3)
    first_hop = hop(far[:half], 1, [t ^ 2 for t in owners])
    second_hop = hop(far[half:], 2, [t ^ 1 for t in owners])
    return slot_for(0), hop(slot_for(1), 1, owners), hop(slot_for(2), 2, owners), first_hop, second_hop


def owners_end(state, owners, *others):
    own, from_x, from_y, first_hop, second_hop = state
    if others:
        first_hop = after(first_hop, *others)
    first, second = hop(first_hop, 2, owners), hop(second_hop, 1, owners)
    return jnp.stack([own, from_x, from_y, jnp.concatenate([first, second], axis=0)])


def hop(values, bit, targets):
    return lax.ppermute(values, "dp", [(t ^ bit, t) for t in targets])


def exchange_dp(slots):
    if not two_by_two():
        return lax.all_to_all(slots, "dp", split_axis=0, concat_axis=0, tiled=True)
    half = slots.shape[1] // 2
    first_hop, second_hop = send(slots[3, :half], 1), send(slots[3, half:], 2)
    from_x, from_y = send(slots[1], 1), send(slots[2], 2)
    first, second = send(first_hop, 2), send(second_hop, 1)
    return jnp.stack([slots[0], from_x, from_y, jnp.concatenate([first, second], axis=0)])


def heads_aligned(unit):
    return unit == HEAD and lax.axis_size("group") % 3 != 0


def spread_qkv(own, unit):
    group_count = lax.axis_size("group")
    me = lax.axis_index("group")
    moved = jnp.stack(
        [
            lax.ppermute(
                own[j * unit : (j + 1) * unit], "group", [(g, (3 * g + j) % group_count) for g in range(group_count)]
            )
            for j in range(3)
        ]
    )
    return jnp.concatenate(
        [lax.dynamic_index_in_dim(moved, (me + group_count * i) % 3, 0, keepdims=False) for i in range(3)]
    )


def return_qkv(rows, unit):
    group_count = lax.axis_size("group")
    me = lax.axis_index("group")
    inverse = pow(group_count, -1, 3)
    parts = rows.reshape(3, unit, rows.shape[1])
    return jnp.concatenate(
        [
            lax.ppermute(
                lax.dynamic_index_in_dim(parts, ((j - me) * inverse) % 3, 0, keepdims=False),
                "group",
                [((3 * g + j) % group_count, g) for g in range(group_count)],
            )
            for j in range(3)
        ]
    )


def head_rows(matrix, heads):
    group_count = lax.axis_size("group")
    lead = matrix.shape[:-2]
    split = matrix.reshape(lead + (heads, group_count, HEAD, matrix.shape[-1]))
    picked = lax.dynamic_index_in_dim(split, lax.axis_index("group"), len(lead) + 1, keepdims=False)
    return picked.reshape(lead + (heads * HEAD, matrix.shape[-1]))


def spread_heads(rows, heads):
    group_count = lax.axis_size("group")
    lead = rows.shape[:-2]
    width = rows.shape[-1]
    part = rows.reshape(lead + (heads, 1, HEAD, width))
    empty = jnp.zeros(lead + (heads, group_count, HEAD, width), rows.dtype)
    placed = lax.dynamic_update_slice_in_dim(empty, part, lax.axis_index("group"), len(lead) + 1)
    return placed.reshape(lead + (heads * group_count * HEAD, width))


def shards(
    hidden_in,
    cotangent,
    segment_ids,
    weight_in,
    weight_back,
    moment_in,
    moment_back,
    norm_gain,
    norm_shift,
    bias_in,
    bias_out,
    vector_moment,
):
    model_width = hidden_in.shape[2]
    tokens = hidden_in.shape[1]
    data_count = lax.axis_size("dp")
    group_count = lax.axis_size("group")
    devices = data_count * group_count
    me_group = lax.axis_index("group")
    unit = model_width // devices
    qkv_rows = 3 * unit
    ff_rows = FF // devices
    out_rows = unit
    heads = HEADS // group_count
    width = heads * HEAD
    aligned = heads_aligned(unit)
    everywhere = ("dp", "group")

    def dot(left, right):
        return jnp.dot(left, right, preferred_element_type=F32)

    def dot_last(left, right):
        return lax.dot_general(left, right, (((1,), (1,)), ((), ())), preferred_element_type=F32)

    def dot_first(left, right):
        return lax.dot_general(left, right, (((0,), (0,)), ((), ())), preferred_element_type=F32)

    x_float = hidden_in[0].astype(F32)
    centre = x_float - jnp.mean(x_float, axis=-1, keepdims=True)
    inverse_std = lax.rsqrt(jnp.mean(centre * centre, axis=-1, keepdims=True) + 1e-05)
    x_hat = centre * inverse_std
    normed_low = (x_hat * norm_gain + norm_shift).astype(BF16)
    grad_y = cotangent[0]
    parts = max(1, width // 128)
    lanes = width // parts
    normed_all = lax.all_gather(normed_low, "group", axis=0, tiled=True)
    w_in, w_back = weight_in[0], weight_back[0]
    w_up = gather_dp(w_in[qkv_rows:])
    if aligned:
        near_qkv = gather_near(spread_qkv(w_in[:qkv_rows], unit))
        grad_all = lax.all_gather(after(grad_y, normed_all, w_up, *came(near_qkv)), "group", axis=0, tiled=True)
        w_qkv = by_distance(gather_far(near_qkv))
        all_back = gather_dp(after(w_back, *came(near_qkv)))
        w_out = by_distance(all_back[:, :out_rows]).reshape(width, model_width)
        w_down = all_back[:, out_rows:].reshape(data_count * ff_rows, model_width)
    else:
        grad_all = lax.all_gather(grad_y, "group", axis=0, tiled=True)
        all_qkv = lax.all_gather(w_in[:qkv_rows], everywhere, axis=0, tiled=True)
        w_qkv = head_rows(all_qkv.reshape(3, model_width, model_width), heads)
        w_out = head_rows(lax.all_gather(w_back[:out_rows], everywhere, axis=0, tiled=True), heads)
        w_down = gather_dp(w_back[out_rows:]).reshape(data_count * ff_rows, model_width)
    w_up = w_up.reshape(data_count * ff_rows, model_width)

    def to_parts(rows):
        split = rows.reshape((3, parts, lanes) + rows.shape[1:])
        return jnp.swapaxes(split, 0, 1).reshape(rows.shape)

    def from_parts(rows):
        split = rows.reshape((parts, 3, lanes) + rows.shape[1:])
        return jnp.swapaxes(split, 0, 1).reshape(rows.shape)

    w_qkv = to_parts(w_qkv.reshape(3 * width, model_width))

    bias_up = lax.dynamic_index_in_dim(
        bias_in[3 * model_width :].reshape(data_count, group_count, ff_rows), me_group, 1, keepdims=False
    )
    bias_up = by_distance(bias_up).reshape(data_count * ff_rows)
    bias_qkv = bias_in[: 3 * model_width].reshape(3 * heads, group_count, HEAD)
    bias_qkv = to_parts(lax.dynamic_index_in_dim(bias_qkv, me_group, 1, keepdims=False).reshape(3 * width))
    pre_up = dot_last(normed_all, w_up) + bias_up
    pre_qkv = dot_last(normed_all, w_qkv) + bias_qkv
    activated, gelu_pull = jax.vjp(gelu_tanh, pre_up)
    activated = activated.astype(BF16)
    grad_all = after(grad_all, activated, pre_qkv)

    term_down = dot_first(activated, grad_all).astype(BF16)
    sum_down = scatter_start(term_down.reshape(data_count, ff_rows, model_width))
    grad_pre_up = gelu_pull(dot_last(grad_all, after(w_down, term_down)))[0].astype(BF16)
    term_up = dot_first(grad_pre_up, normed_all).astype(BF16)
    sum_up = scatter_start(term_up.reshape(data_count, ff_rows, model_width))
    grad_attended = dot_last(grad_all, after(w_out, term_up)).astype(BF16)
    sum_down = scatter_next(sum_down, grad_attended)
    grad_w_down = scatter_end(sum_down)

    position = positions(segment_ids[0])
    attended, grad_pre_qkv = [], []
    ready = flying(sum_down)
    for part in range(parts):
        one, one_grad = attention(pre_qkv, after(grad_attended, *ready), position, part, lanes)
        attended.append(one)
        grad_pre_qkv.append(one_grad)
        if part == 0:
            sum_up = scatter_next(sum_up, one)
            ready = flying(sum_up)
        else:
            ready = (one,)
    grad_w_up = scatter_end(sum_up, attended[-1])
    attended = jnp.concatenate(attended, axis=1)
    grad_pre_qkv = jnp.concatenate(grad_pre_qkv, axis=1)

    def slot(rows):
        return jnp.pad(rows.astype(BF16), ((0, ff_rows - rows.shape[0]), (0, 0)))

    moment_up = MOMENTUM * moment_in[0, qkv_rows:] + grad_w_up
    moment_down = MOMENTUM * moment_back[0, out_rows:] + grad_w_down
    early = jnp.stack([slot(moment_up), slot(moment_down)])
    if two_by_two():
        early = owners_start(early, [1, 3])
        term_grad = after(grad_pre_qkv, *early)
    else:
        term_grad = grad_pre_qkv

    term_qkv = from_parts(dot_first(term_grad, normed_all).astype(BF16))
    term_out = dot_first(attended, grad_all).astype(BF16)
    if aligned:
        term_att = by_distance(
            jnp.concatenate(
                [
                    term_qkv.reshape(data_count, qkv_rows, model_width),
                    term_out.reshape(data_count, out_rows, model_width),
                ],
                axis=1,
            )
        )
        sum_att = scatter_start(term_att)
    else:
        term_att = term_qkv

    branch_part = (dot(after(attended, term_att), w_out) + dot(activated, w_down)).astype(BF16)
    branch = lax.psum_scatter(branch_part, "group", scatter_dimension=0, tiled=True)
    block_out = (x_float + branch.astype(F32) + bias_out).astype(BF16)
    if two_by_two():
        early = owners_end(early, [1, 3], branch_part)
    if aligned:
        sum_att = scatter_next(sum_att, branch_part)
        normed_part = dot(after(grad_pre_qkv, *flying(sum_att)), w_qkv)
        own_att = scatter_end(sum_att, normed_part)
        grad_w_qkv = own_att[:qkv_rows].astype(BF16)
        normed_part = (normed_part + dot(after(grad_pre_up, grad_w_qkv), w_up)).astype(BF16)
        grad_w_qkv = return_qkv(grad_w_qkv, unit).astype(F32)
        grad_w_out = own_att[qkv_rows:]
    else:
        normed_part = (dot(after(grad_pre_qkv, branch_part), w_qkv) + dot(grad_pre_up, w_up)).astype(BF16)
        grad_w_qkv = lax.psum_scatter(
            spread_heads(term_qkv.reshape(3, width, model_width), heads).reshape(3 * model_width, model_width),
            everywhere,
            scatter_dimension=0,
            tiled=True,
        ).astype(F32)
        grad_w_out = lax.psum_scatter(
            spread_heads(term_out, heads), everywhere, scatter_dimension=0, tiled=True
        ).astype(F32)
    grad_y_float = grad_y.astype(F32)

    grad_in = jnp.concatenate([grad_w_qkv, grad_w_up], axis=0)[None]
    grad_back = jnp.concatenate([grad_w_out, grad_w_down], axis=0)[None]
    moment_in_new = MOMENTUM * moment_in + grad_in
    moment_back_new = MOMENTUM * moment_back + grad_back
    moment_qkv = MOMENTUM * moment_in[0, :qkv_rows] + grad_w_qkv
    moment_out = MOMENTUM * moment_back[0, :out_rows] + grad_w_out
    if two_by_two():
        late = jnp.stack([moment_qkv.astype(BF16), jnp.pad(moment_out.astype(BF16), ((0, qkv_rows - out_rows), (0, 0)))])
        late = owners_end(owners_start(late, [0, 2]), [0, 2])
        late = jnp.pad(late, ((0, 0), (0, ff_rows - qkv_rows), (0, 0)))
        owned = jnp.where(lax.axis_index("dp") % 2 == 1, early, late)
    else:
        slots = [slot(moment_qkv), early[0], slot(moment_out), early[1]]
        slots = slots + [jnp.zeros_like(early[0])] * (data_count - 4)
        owned = exchange_dp(jnp.stack(slots))

    def sum_normed(gathered):
        return lax.psum_scatter(after(normed_part, gathered), "group", scatter_dimension=0, tiled=True)

    def placed(sums, lead, size):
        empty = jnp.zeros((lead, group_count, size), F32)
        return lax.dynamic_update_slice_in_dim(empty, sums.reshape(lead, 1, size), me_group, 1).reshape(-1)

    def sum_vectors(grad_normed, gathered):
        grad_normed = grad_normed.astype(F32)
        sums_up = jnp.sum(grad_pre_up.astype(F32), axis=0).reshape(data_count, ff_rows)
        vector_local = jnp.concatenate(
            [
                jnp.sum(grad_normed * x_hat, axis=0),
                jnp.sum(grad_normed, axis=0),
                placed(from_parts(jnp.sum(grad_pre_qkv.astype(F32), axis=0)), 3 * heads, HEAD),
                placed(by_distance(sums_up), data_count, ff_rows),
                jnp.sum(grad_y_float, axis=0),
            ]
        )
        return grad_normed, lax.psum(after(vector_local, gathered), everywhere)

    result, (grad_normed, vector_grad) = orthogonalize(
        owned.reshape(data_count * ff_rows, model_width), normed_part, branch, sum_normed, sum_vectors
    )
    result = after(result, vector_grad)
    returned = by_distance(exchange_dp(result.reshape(data_count, ff_rows, model_width)))

    grad_x_hat = grad_normed * norm_gain
    grad_hidden = grad_y_float + inverse_std * (
        grad_x_hat
        - jnp.mean(grad_x_hat, axis=-1, keepdims=True)
        - x_hat * jnp.mean(grad_x_hat * x_hat, axis=-1, keepdims=True)
    )

    def matrix_rows(matrix_index, row_count, scale):
        return -scale * returned[matrix_index, :row_count].astype(F32)

    scale_ff = math.sqrt(1.0 * FF)
    step_in = jnp.concatenate(
        [matrix_rows(0, qkv_rows, math.sqrt(3.0 * model_width)), matrix_rows(1, ff_rows, scale_ff)], axis=0
    )[None]
    step_back = jnp.concatenate(
        [matrix_rows(2, out_rows, math.sqrt(1.0 * model_width)), matrix_rows(3, ff_rows, scale_ff)], axis=0
    )[None]
    bias_out_grad = vector_grad[vector_grad.shape[0] - model_width :]
    vector_moment_new = MOMENTUM * vector_moment + vector_grad
    vector_step = -(0.2 / math.sqrt(tokens * devices)) * vector_moment_new
    return (
        block_out[None],
        grad_hidden[None],
        grad_in,
        grad_back,
        moment_in_new,
        moment_back_new,
        step_in,
        step_back,
        vector_grad,
        vector_moment_new,
        vector_step,
        bias_out_grad,
    )


def solution(mesh):
    tokens_spec = P("dp", "group", None)
    blocks_spec = P(("dp", "group"), None, None)
    in_specs = (
        (tokens_spec, tokens_spec, P("dp", None))
        + (blocks_spec,) * 4
        + (P(),) * 5
    )
    out_specs = (tokens_spec, tokens_spec) + (blocks_spec,) * 6 + (P(),) * 4
    return jax.shard_map(shards, mesh=mesh, in_specs=in_specs, out_specs=out_specs, check_vma=False)
```

time: 4650 us -> 1090 us (0.23)
  waiting for transfers between devices: 3730 us -> 399 us
  Pallas kernels: 0 us -> 300 us
  matrix products: 410 us -> 144 us
  other arithmetic: 232 us -> 73.4 us
  blocking collectives: 86.5 us -> 0 us
  local copies, waits for them, and re-layouts: 149 us -> 65.9 us
  starting transfers between devices: 5.96 us -> 80.8 us
    reduce_scatter x7 -> x4, waiting for transfers between devices: 2200 us -> 107 us  [the longest x2 107 us: summed(): part = lax.psum_scatter(packed, 'group', scatter_dimension=0, tiled=True)]
    all_gather x14 -> x4, waiting for transfers between devices: 1410 us -> 128 us  [the longest x2 98.6 us: summed(): return lax.all_gather(part, 'group', axis=0, tiled=True)]
    pallas_call x0 -> x27, Pallas kernels: none -> 300 us  [the longest x1 137 us: orthogonalize(): pl.pallas_call(functools.partial(second_body, 3), out_shape=x_shape, in_s...]
    dot_general x31 -> x12, matrix products: 410 us -> 144 us  [the longest x4 52.9 us: dot(): return jnp.dot(left, right, preferred_element_type=F32)]
    ppermute x0 -> x48, waiting for transfers between devices: none -> 163 us  [the longest x30 94.8 us: send(): return lax.ppermute(values, 'dp', flip(bit))]
    concatenate x4 -> x3, other arithmetic: 135 us -> 0.78 us  [the longest x1 0.57 us: shards(): jnp.concatenate([term_qkv.reshape(data_count, qkv_rows, model_width), ter...]
    psum x1, waiting for transfers between devices: 119 us -> 0.02 us  [sum_vectors(): return (grad_normed, lax.psum(after(vector_local, gathered), everywhere))]
    ppermute x0 -> x48, starting transfers between devices: none -> 80 us  [the longest x12 26.6 us: hop(): return lax.ppermute(values, 'dp', [(t ^ bit, t) for t in targets])]
  transfers between devices with their start and end apart: 23 -> 57, of which waited for: 22 -> 23; matrix products, arithmetic and copies ran while one was open for 6% -> 20% of each run, Pallas kernels for 0% -> 28%
where the time goes in v1:
time: 1090 us; the launch traced here: 1080 us
  waiting for transfers between devices  399 us (37%)
  Pallas kernels  300 us (28%)
  matrix products  144 us (13%)
  starting transfers between devices  80.8 us (7%)
  other arithmetic  73.4 us (7%)
  local copies, waits for them, and re-layouts  65.9 us (6%)
  between operations  15.8 us (1%)
    pallas_call x1, Pallas kernels, orthogonalize(): pl.pallas_call(functools.partial(second_body, 3), out_shape=x_shape, in_s...  137 us
    reduce_scatter x2, waiting for transfers between devices, summed(): part = lax.psum_scatter(packed, 'group', scatter_dimension=0, tiled=True)  107 us
    pallas_call x1, Pallas kernels, orthogonalize(): pl.pallas_call(functools.partial(first_body, 2), out_shape=(x_shape, pack...  101 us
    all_gather x2, waiting for transfers between devices, summed(): return lax.all_gather(part, 'group', axis=0, tiled=True)  98.6 us
    ppermute x30, waiting for transfers between devices, send(): return lax.ppermute(values, 'dp', flip(bit))  94.8 us
    dot_general x4, matrix products, dot(): return jnp.dot(left, right, preferred_element_type=F32)  52.9 us
    pallas_call x2, Pallas kernels, attention(): pl.pallas_call(attention_body, grid=(1,), out_shape=(jax.ShapeDtypeStruct...  52.6 us
    dot_general x4, matrix products, dot_last(): lax.dot_general(left, right, (((1,), (1,)), ((), ())), preferred_element_...  50.2 us
  transfers between devices with their start and end apart: 57, of which 23 were waited for; matrix products, arithmetic and copies ran while one was open for 20% of the time, Pallas kernels for 28%

profile of v1, /device:TPU:1, one launch (start us, length us, event | category | flops | bytes accessed | tf_op | source)
XLA Modules:
  0.0 1078.9 jit_solution(5606820224810460836)
XLA Ops:
  7.3 2.6 copy.137
  12.7 2.5 fusion.73
  19.6 3.2 collective-permute-start
  23.8 3.3 collective-permute-start.2
  27.2 3.9 collective-permute-done
  31.1 10.6 collective-permute-done.1
  41.7 16.0 %collective-permute-done.2 = bf16[64,2048]{1,0:T(8,128)(2,1)} collective-permute-done((bf16[64,2048]{1,0:T(8,128)(2,1)S(1)}, bf16[64,2048]{1,0:T(8,128)(2,1)}, u32[]{:S(2)}, u32[]{:S(2)}) %collective-permute-start.2) | collective-permute-done | bytes 262176 | tf_op jit(solution)/shard_map/ppermute | solution.py:536
  65.0 2.3 collective-permute-done.9
  69.1 3.4 pad_maximum_fusion.3.refs_2_
  72.5 3.3 collective-permute-done.3.refs_3_.refs_1_
  77.4 29.9 %all-gather.5.cloned.1.call-done.refs_1_ = bf16[2048,2048]{1,0:T(8,128)(2,1)} async-done(((bf16[256,2048]{1,0:T(8,128)(2,1)}), bf16[2048,2048]{1,0:T(8,128)(2,1)}) %all-gather.5.cloned.1.call-update) | async-done | bytes 8388624 | tf_op jit(solution)/shard_map/all_gather | solution.py:628
  111.0 2.6 copy.86.cos_ref
  114.7 2.7 copy.87.sin_ref
  121.9 2.3 subtract_subtract_fusion.start_ref
  124.2 24.0 %collective-permute-done.6 = bf16[96,2048]{1,0:T(8,128)(2,1)S(1)} collective-permute-done((bf16[96,2048]{1,0:T(8,128)(2,1)S(1)}, bf16[96,2048]{1,0:T(8,128)(2,1)S(1)}, u32[]{:S(2)}, u32[]{:S(2)}) %collective-permute-start.6) | collective-permute-done | bytes 393248 | tf_op jit(solution)/shard_map/ppermute | solution.py:417
  154.5 9.0 collective-permute-done.13
  167.3 2.3 pad_maximum_fusion
  170.9 13.6 %fusion.11 = (bf16[2048,1024]{1,0:T(8,128)(2,1)S(1)}, f32[2048,1024]{1,0:T(8,128)}) fusion(f32[1024]{0:T(1024)S(1)} %bitcast.364, bf16[2048,2048]{1,0:T(8,128)(2,1)S(1)} %bitcast.337, bf16[1024,2048]{1,0:T(8,128)(2,1)S(1)} %bitcast.329), kind=kOutput, calls=%fused_computation.19 | convolution fusion | flops 8610906112 | bytes 25169920 | tf_op jit(solution)/shard_map/dot_general | solution.py:615
  184.5 11.7 %fusion.77 = f32[2048,2048]{1,0:T(8,128)} fusion(bf16[2048,1024]{1,0:T(8,128)(2,1)S(1)} %get-tuple-element.110.refs_1_, bf16[1024,2048]{1,0:T(8,128)(2,1)S(1)} %bitcast.325), kind=kOutput, calls=%fused_computation.243 | convolution fusion | flops 8589934592 | bytes 25165824 | tf_op jit(solution)/shard_map/dot_general | solution.py:612
  196.2 8.8 broadcast_add_fusion.refs_2_.pre_ref
  205.0 12.7 %convolution_convert_fusion.1.refs_1_ = bf16[1024,2048]{1,0:T(8,128)(2,1)S(1)} fusion(bf16[2048,1024]{1,0:T(8,128)(2,1)} %copy-done.46, bf16[2048,2048]{1,0:T(8,128)(2,1)} %after.23), kind=kOutput, calls=%fused_computation.40 | convolution fusion | flops 8592031744 | bytes 16777216 | tf_op jit(solution)/shard_map/dot_general | solution.py:618
  223.3 20.9 %convert_reduce_fusion = (f32[1024]{0:T(1024)}, bf16[2048,1024]{1,0:T(8,128)(2,1)S(1)}) fusion(f32[2048,1024]{1,0:T(8,128)} %get-tuple-element.111, f32[1024]{0:T(1024)S(1)} %bitcast.365, bf16[2048,2048]{1,0:T(8,128)(2,1)} %after.23, bf16[1024,2048]{1,0:T(8,128)(2,1)} %after.25), kind=kOutput, calls=%fused_computation.17 | convolution fusion | flops 8646556672 | bytes 25174016 | tf_op jit(solution)/shard_map/dot_general | solution.py:615
  246.1 13.3 %convolution_convert_fusion.refs_1_ = bf16[1024,2048]{1,0:T(8,128)(2,1)} fusion(bf16[2048,1024]{1,0:T(8,128)(2,1)S(1)} %get-tuple-element.31.refs_0_, bf16[2048,2048]{1,0:T(8,128)(2,1)} %all-gather.5.cloned.1.call-done.refs_1_), kind=kOutput, calls=%fused_computation.39 | convolution fusion | flops 8592031744 | bytes 16777216 | tf_op jit(solution)/shard_map/dot_general | solution.py:618
  259.4 7.0 convolution_convert_fusion.4.refs_1_.refs_0_
  272.6 2.3 convert_add_fusion.5
  280.3 26.2 %attention.2 = (bf16[2048,128]{1,0:T(8,128)(2,1)}, bf16[2048,384]{1,0:T(8,128)(2,1)}) custom-call(s32[8]{0:T(128)} %and_select_fusion.first_ref, f32[2048,768]{1,0:T(8,128)} %broadcast_add_fusion.refs_2_.pre_ref, bf16[2048,256]{1,0:T(8,128)(2,1)} %after.28.grad_ref, s32[2048,1]{1,0:T(8,128)} %subtract_subtract_fusion.start_ref, f32[2048,128]{1,0:T(8,128)} %copy.86.cos_ref, ...), custom_call_target="tpu_custom_call" | custom-call | flops 10737418240 | bytes 4194304 | tf_op jit(solution)/shard_map/attention/pallas_call | solution.py:155
  308.4 3.0 convert_add_fusion.3
  314.6 26.4 %attention.3 = (bf16[2048,128]{1,0:T(8,128)(2,1)}, bf16[2048,384]{1,0:T(8,128)(2,1)}) custom-call(s32[8]{0:T(128)} %and_select_fusion.first_ref, f32[2048,768]{1,0:T(8,128)} %broadcast_add_fusion.refs_2_.pre_ref, bf16[2048,256]{1,0:T(8,128)(2,1)} %after.30.grad_ref, s32[2048,1]{1,0:T(8,128)} %subtract_subtract_fusion.start_ref, f32[2048,128]{1,0:T(8,128)} %copy.86.cos_ref, ...), custom_call_target="tpu_custom_call" | custom-call | flops 10737418240 | bytes 4194304 | tf_op jit(solution)/shard_map/attention/pallas_call | solution.py:155
  358.3 5.4 collective-permute-start.23
  363.8 2.3 collective-permute-start.26
  368.2 4.5 convolution_convert_fusion.3
  374.1 17.6 %collective-permute-done.25.refs_4_.refs_0_ = bf16[128,2048]{1,0:T(8,128)(2,1)} collective-permute-done((bf16[128,2048]{1,0:T(8,128)(2,1)S(1)}, bf16[128,2048]{1,0:T(8,128)(2,1)}, u32[]{:S(2)}, u32[]{:S(2)}) %collective-permute-start.25) | collective-permute-done | bytes 524320 | tf_op jit(solution)/shard_map/ppermute | solution.py:514
  391.7 10.6 convolution_convert_fusion.2
  404.0 2.3 pad_maximum_fusion.4.refs_1_
  406.4 12.1 %add_convert_fusion.1.refs_1_ = bf16[2048,2048]{1,0:T(8,128)(2,1)} fusion(f32[2048,2048]{1,0:T(8,128)} %fusion.77, bf16[2048,256]{1,0:T(8,128)(2,1)} %after.33, bf16[256,2048]{1,0:T(8,128)(2,1)} %bitcast.335), kind=kOutput, calls=%fused_computation.1 | convolution fusion | flops 2155872256 | bytes 27262976 | tf_op jit(solution)/shard_map/dot_general | solution.py:612
  418.6 2.3 slice_bitcast_fusion.3
  420.9 2.3 slice_bitcast_fusion.5
  423.2 2.3 collective-permute-start.27
  426.0 2.7 collective-permute-start.32
  430.1 13.4 %collective-permute-done.27 = bf16[2,128,2048]{2,1,0:T(8,128)(2,1)} collective-permute-done((bf16[2,128,2048]{2,1,0:T(8,128)(2,1)}, bf16[2,128,2048]{2,1,0:T(8,128)(2,1)}, u32[]{:S(2)}, u32[]{:S(2)}) %collective-permute-start.27) | collective-permute-done | bytes 1048608 | tf_op jit(solution)/shard_map/ppermute | solution.py:417
  444.5 3.1 convert_add_fusion.1
  451.4 12.7 %fusion.78.refs_1_ = f32[2048,2048]{1,0:T(8,128)} fusion(bf16[2048,768]{1,0:T(8,128)(2,1)} %after.35, bf16[768,2048]{1,0:T(8,128)(2,1)} %bitcast.347), kind=kOutput, calls=%fused_computation.244 | convolution fusion | flops 6442450944 | bytes 23068672 | tf_op jit(solution)/shard_map/dot_general | solution.py:612
  471.2 4.3 collective-permute-start.35
  475.6 14.5 %collective-permute-start.34 = (bf16[64,2048]{1,0:T(8,128)(2,1)S(1)}, bf16[64,2048]{1,0:T(8,128)(2,1)S(1)}, u32[]{:S(2)}, u32[]{:S(2)}) collective-permute-start(bf16[64,2048]{1,0:T(8,128)(2,1)S(1)} %get-tuple-element.93), channel_id=1, source_target_pairs={{1,0},{4,1},{7,2},{2,3},{5,4},{0,5},{3,6},{6,7},{9,8},{12,9},{15,1... | collective-permute-start | bytes 786440 | tf_op jit(solution)/shard_map/ppermute | solution.py:554
  491.0 14.7 %collective-permute-done.34 = bf16[64,2048]{1,0:T(8,128)(2,1)S(1)} collective-permute-done((bf16[64,2048]{1,0:T(8,128)(2,1)S(1)}, bf16[64,2048]{1,0:T(8,128)(2,1)S(1)}, u32[]{:S(2)}, u32[]{:S(2)}) %collective-permute-start.34) | collective-permute-done | bytes 262176 | tf_op jit(solution)/shard_map/ppermute | solution.py:554
  513.9 2.3 maximum_bitcast_fusion.6
  517.5 2.7 collective-permute-start.37
  520.2 2.9 collective-permute-start.39
  524.4 16.4 %add_convert_fusion.before_ref.refs_0_ = bf16[2048,2048]{1,0:T(8,128)(2,1)} fusion(f32[2048,2048]{1,0:T(8,128)} %fusion.78.refs_1_, bf16[2048,1024]{1,0:T(8,128)(2,1)} %after.37, bf16[1024,2048]{1,0:T(8,128)(2,1)} %bitcast.328), kind=kOutput, calls=%fused_computation | convolution fusion | flops 8598323200 | bytes 33554432 | tf_op jit(solution)/shard_map/dot_general | solution.py:612
  540.8 4.3 collective-permute-done.39
  545.2 5.0 fusion.15
  550.2 10.1 gram.1.refs_0_
  560.3 55.9 %reduce-scatter.7.cloned.1.call-done = bf16[1152,256]{1,0:T(8,128)(2,1)} async-done(((bf16[9216,256]{1,0:T(8,128)(2,1)}), bf16[1152,256]{1,0:T(8,128)(2,1)}) %reduce-scatter.7.cloned.1.call-update) | async-done | bytes 589840 | tf_op jit(solution)/shard_map/reduce_scatter | solution.py:372
  616.2 54.1 %all-gather.9.cloned.1.call-done.refs_1_.packed_ref = bf16[9216,256]{1,0:T(8,128)(2,1)} async-done(((bf16[1152,256]{1,0:T(8,128)(2,1)}), bf16[9216,256]{1,0:T(8,128)(2,1)}) %all-gather.9.cloned.1.call-update) | async-done | bytes 4718608 | tf_op jit(solution)/shard_map/all_gather | solution.py:373
  670.8 100.6 %first_steps.1 = (bf16[1024,2048]{1,0:T(8,128)(2,1)}, bf16[9216,256]{1,0:T(8,128)(2,1)}) custom-call(bf16[9216,256]{1,0:T(8,128)(2,1)} %all-gather.9.cloned.1.call-done.refs_1_.packed_ref, bf16[1024,2048]{1,0:T(8,128)(2,1)} %bitcast.343), custom_call_target="tpu_custom_call" | custom-call | flops 68719476736 | bytes 16777216 | tf_op jit(solution)/shard_map/first_steps/pallas_call | solution.py:387
  771.5 51.3 %reduce-scatter.11.cloned.1.call-done = bf16[1152,256]{1,0:T(8,128)(2,1)} async-done(((bf16[9216,256]{1,0:T(8,128)(2,1)}), bf16[1152,256]{1,0:T(8,128)(2,1)}) %reduce-scatter.11.cloned.1.call-update) | async-done | bytes 589840 | tf_op jit(solution)/shard_map/reduce_scatter | solution.py:372
  823.4 5.0 multiply_add_fusion.2
  829.6 3.0 convert_reduce_fusion.3
  832.7 44.5 %all-gather.11.cloned.1.call-done.packed_ref.refs_1_ = bf16[9216,256]{1,0:T(8,128)(2,1)} async-done(((bf16[1152,256]{1,0:T(8,128)(2,1)}), bf16[9216,256]{1,0:T(8,128)(2,1)}) %all-gather.11.cloned.1.call-update) | async-done | bytes 4718608 | tf_op jit(solution)/shard_map/all_gather | solution.py:373
  877.2 136.6 %last_steps.1.refs_0_ = bf16[1024,2048]{1,0:T(8,128)(2,1)} custom-call(bf16[9216,256]{1,0:T(8,128)(2,1)} %all-gather.11.cloned.1.call-done.packed_ref.refs_1_, bf16[1024,2048]{1,0:T(8,128)(2,1)} %get-tuple-element.23.x_ref), custom_call_target="tpu_custom_call" | custom-call | flops 100931731456 | bytes 16777216 | tf_op jit(solution)/shard_map/last_steps/pallas_call | solution.py:399
  1021.2 3.8 multiply_add_fusion.1
  1025.6 5.9 collective-permute-done.44
  1034.5 31.5 %collective-permute-done.45 = bf16[128,2048]{1,0:T(8,128)(2,1)S(1)} collective-permute-done((bf16[128,2048]{1,0:T(8,128)(2,1)S(1)}, bf16[128,2048]{1,0:T(8,128)(2,1)S(1)}, u32[]{:S(2)}, u32[]{:S(2)}) %collective-permute-start.45) | collective-permute-done | bytes 524320 | tf_op jit(solution)/shard_map/ppermute | solution.py:417
  1069.1 2.3 maximum_bitcast_fusion.1
  (396 shorter events, 128.4 us)
Async XLA Ops:
  7.2 100.1 %all-gather.5.cloned.1.call-start = ((), (), s32[]{:S(2)}) async-start(), calls=%async_computation.4 | async-start | bytes 9437184 | tf_op jit(solution)/shard_map/all_gather | solution.py:628
  12.7 192.3 %all-gather.7.cloned.1.call-start = ((), (), s32[]{:S(2)}) async-start(), calls=%async_computation.5 | async-start | bytes 9437184 | tf_op jit(solution)/shard_map/all_gather | solution.py:633
  15.2 43.6 %collective-permute-start.8 = (bf16[256,2048]{1,0:T(8,128)(2,1)}, bf16[256,2048]{1,0:T(8,128)(2,1)S(1)}, u32[]{:S(2)}, u32[]{:S(2)}) collective-permute-start(bf16[256,2048]{1,0:T(8,128)(2,1)} %get-tuple-element.73), channel_id=1, source_target_pairs={{0,16},{8,24},{16,0},{24,8},{1,17},{9,25},{17,1},{25,9},{2,18},{10... | collective-permute-start | bytes 3145736 | tf_op jit(solution)/shard_map/ppermute | solution.py:417
  17.2 41.7 %collective-permute-start.7 = (bf16[256,2048]{1,0:T(8,128)(2,1)}, bf16[256,2048]{1,0:T(8,128)(2,1)}, u32[]{:S(2)}, u32[]{:S(2)}) collective-permute-start(bf16[256,2048]{1,0:T(8,128)(2,1)} %get-tuple-element.73), channel_id=1, source_target_pairs={{0,8},{8,0},{16,24},{24,16},{1,9},{9,1},{17,25},{25,17},{2,10},{10... | collective-permute-start | bytes 3145736 | tf_op jit(solution)/shard_map/ppermute | solution.py:417
  19.6 11.5 %collective-permute-start = (bf16[64,2048]{1,0:T(8,128)(2,1)S(1)}, bf16[64,2048]{1,0:T(8,128)(2,1)S(1)}, u32[]{:S(2)}, u32[]{:S(2)}) collective-permute-start(bf16[64,2048]{1,0:T(8,128)(2,1)S(1)} %get-tuple-element.69), channel_id=1, source_target_pairs={{0,0},{1,3},{2,6},{3,1},{4,4},{5,7},{6,2},{7,5},{8,8},{9,11},{10,1... | collective-permute-start | bytes 786440 | tf_op jit(solution)/shard_map/ppermute | solution.py:536
  22.8 18.9 %collective-permute-start.1 = (bf16[64,2048]{1,0:T(8,128)(2,1)S(1)}, bf16[64,2048]{1,0:T(8,128)(2,1)S(1)}, u32[]{:S(2)}, u32[]{:S(2)}) collective-permute-start(bf16[64,2048]{1,0:T(8,128)(2,1)S(1)} %get-tuple-element.70), channel_id=1, source_target_pairs={{0,1},{1,4},{2,7},{3,2},{4,5},{5,0},{6,3},{7,6},{8,9},{9,12},{10,1... | collective-permute-start | bytes 786440 | tf_op jit(solution)/shard_map/ppermute | solution.py:536
  23.8 34.0 %collective-permute-start.2 = (bf16[64,2048]{1,0:T(8,128)(2,1)S(1)}, bf16[64,2048]{1,0:T(8,128)(2,1)}, u32[]{:S(2)}, u32[]{:S(2)}) collective-permute-start(bf16[64,2048]{1,0:T(8,128)(2,1)S(1)} %get-tuple-element.71), channel_id=1, source_target_pairs={{0,2},{1,5},{2,0},{3,3},{4,6},{5,1},{6,4},{7,7},{8,10},{9,13},{10,... | collective-permute-start | bytes 786440 | tf_op jit(solution)/shard_map/ppermute | solution.py:536
  58.9 8.5 collective-permute-start.9
  60.5 8.5 collective-permute-start.10
  61.7 14.1 %collective-permute-start.3 = (bf16[192,2048]{1,0:T(8,128)(2,1)S(1)}, bf16[192,2048]{1,0:T(8,128)(2,1)S(1)}, u32[]{:S(2)}, u32[]{:S(2)}) collective-permute-start(bf16[192,2048]{1,0:T(8,128)(2,1)S(1)} %get-tuple-element.95), channel_id=1, source_target_pairs={{0,8},{8,0},{16,24},{24,16},{1,9},{9,1},{17,25},{25,17},{2,10},{10... | collective-permute-start | bytes 2359304 | tf_op jit(solution)/shard_map/ppermute | solution.py:417
  62.6 14.8 %collective-permute-start.4 = (bf16[192,2048]{1,0:T(8,128)(2,1)S(1)}, bf16[192,2048]{1,0:T(8,128)(2,1)S(1)}, u32[]{:S(2)}, u32[]{:S(2)}) collective-permute-start(bf16[192,2048]{1,0:T(8,128)(2,1)S(1)} %get-tuple-element.95), channel_id=1, source_target_pairs={{0,16},{8,24},{16,0},{24,8},{1,17},{9,25},{17,1},{25,9},{2,18},{10... | collective-permute-start | bytes 2359304 | tf_op jit(solution)/shard_map/ppermute | solution.py:417
  72.5 35.1 %copy-start.61 = (s32[1,2048]{1,0:T(1,128)S(1)}, s32[1,2048]{1,0:T(1,128)}, u32[]{:S(2)}) copy-start(s32[1,2048]{1,0:T(1,128)} %param.14) | copy-start | bytes 24580
  72.5 35.8 %slice-start.4 = ((f32[14336]{0:T(1024)}), f32[6144]{0:T(1024)S(1)}, s32[]{:S(2)}) async-start(f32[14336]{0:T(1024)} %param.21), calls=%async_computation.17 | async-start | bytes 49152 | tf_op jit(solution)/shard_map/slice | solution.py:660
  72.5 36.1 %slice-start.5 = ((f32[14336]{0:T(1024)}), f32[8192]{0:T(1024)S(1)}, s32[]{:S(2)}) async-start(f32[14336]{0:T(1024)} %param.21), calls=%async_computation.18 | async-start | bytes 65536 | tf_op jit(solution)/shard_map/slice | solution.py:657
  107.3 452.9 %reduce-scatter.5.cloned.1.call-start = ((), (), s32[]{:S(2)}) async-start(), calls=%async_computation.6 | async-start | bytes 9437184 | tf_op jit(solution)/shard_map/reduce_scatter | solution.py:722
  109.2 39.0 %collective-permute-start.12 = (bf16[320,2048]{1,0:T(8,128)(2,1)}, bf16[320,2048]{1,0:T(8,128)(2,1)S(1)}, u32[]{:S(2)}, u32[]{:S(2)}) collective-permute-start(bf16[320,2048]{1,0:T(8,128)(2,1)} %after.24), channel_id=1, source_target_pairs={{0,16},{8,24},{16,0},{24,8},{1,17},{9,25},{17,1},{25,9},{2,18},{10... | collective-permute-start | bytes 3932168 | tf_op jit(solution)/shard_map/ppermute | solution.py:417
  109.5 39.1 %collective-permute-start.11 = (bf16[320,2048]{1,0:T(8,128)(2,1)}, bf16[320,2048]{1,0:T(8,128)(2,1)}, u32[]{:S(2)}, u32[]{:S(2)}) collective-permute-start(bf16[320,2048]{1,0:T(8,128)(2,1)} %after.24), channel_id=1, source_target_pairs={{0,8},{8,0},{16,24},{24,16},{1,9},{9,1},{17,25},{25,17},{2,10},{10... | collective-permute-start | bytes 3932168 | tf_op jit(solution)/shard_map/ppermute | solution.py:417
  119.2 28.9 %collective-permute-start.6 = (bf16[96,2048]{1,0:T(8,128)(2,1)S(1)}, bf16[96,2048]{1,0:T(8,128)(2,1)S(1)}, u32[]{:S(2)}, u32[]{:S(2)}) collective-permute-start(bf16[96,2048]{1,0:T(8,128)(2,1)S(1)} %slice.314), channel_id=1, source_target_pairs={{0,16},{8,24},{16,0},{24,8},{1,17},{9,25},{17,1},{25,9},{2,18},{10... | collective-permute-start | bytes 1179656 | tf_op jit(solution)/shard_map/ppermute | solution.py:417
  120.6 27.5 %collective-permute-start.5 = (bf16[96,2048]{1,0:T(8,128)(2,1)S(1)}, bf16[96,2048]{1,0:T(8,128)(2,1)S(1)}, u32[]{:S(2)}, u32[]{:S(2)}) collective-permute-start(bf16[96,2048]{1,0:T(8,128)(2,1)S(1)} %slice.313), channel_id=1, source_target_pairs={{0,8},{8,0},{16,24},{24,16},{1,9},{9,1},{17,25},{25,17},{2,10},{10... | collective-permute-start | bytes 1179656 | tf_op jit(solution)/shard_map/ppermute | solution.py:417
  148.3 15.2 %collective-permute-start.13 = (bf16[160,2048]{1,0:T(8,128)(2,1)S(1)}, bf16[160,2048]{1,0:T(8,128)(2,1)S(1)}, u32[]{:S(2)}, u32[]{:S(2)}) collective-permute-start(bf16[160,2048]{1,0:T(8,128)(2,1)S(1)} %slice.317), channel_id=1, source_target_pairs={{0,8},{8,0},{16,24},{24,16},{1,9},{9,1},{17,25},{25,17},{2,10},{10... | collective-permute-start | bytes 1966088 | tf_op jit(solution)/shard_map/ppermute | solution.py:417
  149.7 14.9 %collective-permute-start.14 = (bf16[160,2048]{1,0:T(8,128)(2,1)S(1)}, bf16[160,2048]{1,0:T(8,128)(2,1)S(1)}, u32[]{:S(2)}, u32[]{:S(2)}) collective-permute-start(bf16[160,2048]{1,0:T(8,128)(2,1)S(1)} %slice.318), channel_id=1, source_target_pairs={{0,16},{8,24},{16,0},{24,8},{1,17},{9,25},{17,1},{25,9},{2,18},{10... | collective-permute-start | bytes 1966088 | tf_op jit(solution)/shard_map/ppermute | solution.py:417
  221.0 51.6 %collective-permute-start.15 = (bf16[2,128,2048]{2,1,0:T(8,128)(2,1)}, bf16[2,128,2048]{2,1,0:T(8,128)(2,1)}, u32[]{:S(2)}, u32[]{:S(2)}) collective-permute-start(bf16[2,128,2048]{2,1,0:T(8,128)(2,1)} %slice_bitcast_fusion.17), channel_id=1, source_target_pairs={{0,8},{8,0},{16,24},{24,16},{1,9},{9,1},{17,25},{25,17},{2,10},{10... | collective-permute-start | bytes 3145736 | tf_op jit(solution)/shard_map/ppermute | solution.py:417
  222.2 50.4 %collective-permute-start.16 = (bf16[2,128,2048]{2,1,0:T(8,128)(2,1)}, bf16[2,128,2048]{2,1,0:T(8,128)(2,1)}, u32[]{:S(2)}, u32[]{:S(2)}) collective-permute-start(bf16[2,128,2048]{2,1,0:T(8,128)(2,1)} %slice_bitcast_fusion.15), channel_id=1, source_target_pairs={{0,16},{8,24},{16,0},{24,8},{1,17},{9,25},{17,1},{25,9},{2,18},{10... | collective-permute-start | bytes 3145736 | tf_op jit(solution)/shard_map/ppermute | solution.py:417
  270.5 37.9 %collective-permute-start.17 = (bf16[2,128,2048]{2,1,0:T(8,128)(2,1)S(1)}, bf16[2,128,2048]{2,1,0:T(8,128)(2,1)}, u32[]{:S(2)}, u32[]{:S(2)}) collective-permute-start(bf16[2,128,2048]{2,1,0:T(8,128)(2,1)S(1)} %slice_bitcast_fusion.13), channel_id=1, source_target_pairs={{0,8},{8,0},{16,24},{24,16},{1,9},{9,1},{17,25},{25,17},{2,10},{10... | collective-permute-start | bytes 3145736 | tf_op jit(solution)/shard_map/ppermute | solution.py:417
  272.2 36.2 %collective-permute-start.18 = (bf16[2,128,2048]{2,1,0:T(8,128)(2,1)S(1)}, bf16[2,128,2048]{2,1,0:T(8,128)(2,1)}, u32[]{:S(2)}, u32[]{:S(2)}) collective-permute-start(bf16[2,128,2048]{2,1,0:T(8,128)(2,1)S(1)} %slice_bitcast_fusion.11), channel_id=1, source_target_pairs={{0,16},{8,24},{16,0},{24,8},{1,17},{9,25},{17,1},{25,9},{2,18},{10... | collective-permute-start | bytes 3145736 | tf_op jit(solution)/shard_map/ppermute | solution.py:417
  278.0 69.3 %collective-permute-start.19 = (bf16[128,2048]{1,0:T(8,128)(2,1)}, bf16[128,2048]{1,0:T(8,128)(2,1)}, u32[]{:S(2)}, u32[]{:S(2)}) collective-permute-start(bf16[128,2048]{1,0:T(8,128)(2,1)} %fusion.51.refs_1_), channel_id=1, source_target_pairs={{0,16},{8,24},{16,0},{24,8},{1,17},{9,25},{17,1},{25,9},{2,18},{10... | collective-permute-start | bytes 1572872 | tf_op jit(solution)/shard_map/ppermute | solution.py:417
  279.1 69.9 %collective-permute-start.20 = (bf16[128,2048]{1,0:T(8,128)(2,1)}, bf16[128,2048]{1,0:T(8,128)(2,1)}, u32[]{:S(2)}, u32[]{:S(2)}) collective-permute-start(bf16[128,2048]{1,0:T(8,128)(2,1)} %fusion.52.refs_2_), channel_id=1, source_target_pairs={{0,8},{8,0},{16,24},{24,16},{1,9},{9,1},{17,25},{25,17},{2,10},{10... | collective-permute-start | bytes 1572872 | tf_op jit(solution)/shard_map/ppermute | solution.py:417
  314.4 38.3 %collective-permute-start.21 = (bf16[128,2048]{1,0:T(8,128)(2,1)}, bf16[128,2048]{1,0:T(8,128)(2,1)}, u32[]{:S(2)}, u32[]{:S(2)}) collective-permute-start(bf16[128,2048]{1,0:T(8,128)(2,1)} %fusion.53.refs_1_), channel_id=1, source_target_pairs={{0,16},{8,24},{16,0},{24,8},{1,17},{9,25},{17,1},{25,9},{2,18},{10... | collective-permute-start | bytes 1572872 | tf_op jit(solution)/shard_map/ppermute | solution.py:417
  314.4 36.4 %collective-permute-start.22 = (bf16[128,2048]{1,0:T(8,128)(2,1)}, bf16[128,2048]{1,0:T(8,128)(2,1)}, u32[]{:S(2)}, u32[]{:S(2)}) collective-permute-start(bf16[128,2048]{1,0:T(8,128)(2,1)} %fusion.54.refs_2_), channel_id=1, source_target_pairs={{0,8},{8,0},{16,24},{24,16},{1,9},{9,1},{17,25},{25,17},{2,10},{10... | collective-permute-start | bytes 1572872 | tf_op jit(solution)/shard_map/ppermute | solution.py:417
  356.7 35.0 %collective-permute-start.24 = (bf16[256,2048]{1,0:T(8,128)(2,1)S(1)}, bf16[256,2048]{1,0:T(8,128)(2,1)}, u32[]{:S(2)}, u32[]{:S(2)}) collective-permute-start(bf16[256,2048]{1,0:T(8,128)(2,1)S(1)} %get-tuple-element.66), channel_id=1, source_target_pairs={{24,8},{8,24},{25,9},{9,25},{26,10},{10,26},{27,11},{11,27},{28,12... | collective-permute-start | bytes 3145736 | tf_op jit(solution)/shard_map/ppermute | solution.py:514
  358.3 33.3 %collective-permute-start.23 = (bf16[256,2048]{1,0:T(8,128)(2,1)S(1)}, bf16[256,2048]{1,0:T(8,128)(2,1)}, u32[]{:S(2)}, u32[]{:S(2)}) collective-permute-start(bf16[256,2048]{1,0:T(8,128)(2,1)S(1)} %get-tuple-element.67), channel_id=1, source_target_pairs={{0,8},{16,24},{1,9},{17,25},{2,10},{18,26},{3,11},{19,27},{4,12},{... | collective-permute-start | bytes 3145736 | tf_op jit(solution)/shard_map/ppermute | solution.py:514
  363.8 10.3 collective-permute-start.26
  366.1 25.5 %collective-permute-start.25 = (bf16[128,2048]{1,0:T(8,128)(2,1)S(1)}, bf16[128,2048]{1,0:T(8,128)(2,1)}, u32[]{:S(2)}, u32[]{:S(2)}) collective-permute-start(bf16[128,2048]{1,0:T(8,128)(2,1)S(1)} %get-tuple-element.83), channel_id=1, source_target_pairs={{16,24},{0,8},{17,25},{1,9},{18,26},{2,10},{19,27},{3,11},{20,28},... | collective-permute-start | bytes 1572872 | tf_op jit(solution)/shard_map/ppermute | solution.py:514
  418.5 197.6 %reduce-scatter.7.cloned.1.call-start = ((), (), s32[]{:S(2)}) async-start(), calls=%async_computation.7 | async-start | bytes 5308416 | tf_op jit(solution)/shard_map/reduce_scatter | solution.py:372
  423.2 20.4 %collective-permute-start.27 = (bf16[2,128,2048]{2,1,0:T(8,128)(2,1)}, bf16[2,128,2048]{2,1,0:T(8,128)(2,1)}, u32[]{:S(2)}, u32[]{:S(2)}) collective-permute-start(bf16[2,128,2048]{2,1,0:T(8,128)(2,1)} %slice_bitcast_fusion.5), channel_id=1, source_target_pairs={{0,8},{8,0},{16,24},{24,16},{1,9},{9,1},{17,25},{25,17},{2,10},{10... | collective-permute-start | bytes 3145736 | tf_op jit(solution)/shard_map/ppermute | solution.py:417
  425.5 19.0 %collective-permute-start.28 = (bf16[2,128,2048]{2,1,0:T(8,128)(2,1)}, bf16[2,128,2048]{2,1,0:T(8,128)(2,1)}, u32[]{:S(2)}, u32[]{:S(2)}) collective-permute-start(bf16[2,128,2048]{2,1,0:T(8,128)(2,1)} %slice_bitcast_fusion.3), channel_id=1, source_target_pairs={{0,16},{8,24},{16,0},{24,8},{1,17},{9,25},{17,1},{25,9},{2,18},{10... | collective-permute-start | bytes 3145736 | tf_op jit(solution)/shard_map/ppermute | solution.py:417
  426.0 87.9 %collective-permute-start.32 = (bf16[128,2048]{1,0:T(8,128)(2,1)}, bf16[128,2048]{1,0:T(8,128)(2,1)}, u32[]{:S(2)}, u32[]{:S(2)}) collective-permute-start(bf16[128,2048]{1,0:T(8,128)(2,1)} %copy-done.56), channel_id=1, source_target_pairs={{0,8},{16,24},{1,9},{17,25},{2,10},{18,26},{3,11},{19,27},{4,12},{... | collective-permute-start | bytes 1572872 | tf_op jit(solution)/shard_map/ppermute | solution.py:514
  428.7 85.2 %collective-permute-start.31 = (bf16[128,2048]{1,0:T(8,128)(2,1)}, bf16[128,2048]{1,0:T(8,128)(2,1)}, u32[]{:S(2)}, u32[]{:S(2)}) collective-permute-start(bf16[128,2048]{1,0:T(8,128)(2,1)} %after.38), channel_id=1, source_target_pairs={{24,8},{8,24},{25,9},{9,25},{26,10},{10,26},{27,11},{11,27},{28,12... | collective-permute-start | bytes 1572872 | tf_op jit(solution)/shard_map/ppermute | solution.py:514
  449.7 15.4 %collective-permute-start.29 = (bf16[128,2048]{1,0:T(8,128)(2,1)}, bf16[128,2048]{1,0:T(8,128)(2,1)}, u32[]{:S(2)}, u32[]{:S(2)}) collective-permute-start(bf16[128,2048]{1,0:T(8,128)(2,1)} %fusion.55.refs_1_), channel_id=1, source_target_pairs={{0,16},{8,24},{16,0},{24,8},{1,17},{9,25},{17,1},{25,9},{2,18},{10... | collective-permute-start | bytes 1572872 | tf_op jit(solution)/shard_map/ppermute | solution.py:417
  451.1 15.5 %collective-permute-start.30 = (bf16[128,2048]{1,0:T(8,128)(2,1)}, bf16[128,2048]{1,0:T(8,128)(2,1)}, u32[]{:S(2)}, u32[]{:S(2)}) collective-permute-start(bf16[128,2048]{1,0:T(8,128)(2,1)} %fusion.56.refs_2_), channel_id=1, source_target_pairs={{0,8},{8,0},{16,24},{24,16},{1,9},{9,1},{17,25},{25,17},{2,10},{10... | collective-permute-start | bytes 1572872 | tf_op jit(solution)/shard_map/ppermute | solution.py:417
  468.2 37.5 %copy-start.6 = (f32[1,448,2048]{2,1,0:T(8,128)S(1)}, f32[1,448,2048]{2,1,0:T(8,128)}, u32[]{:S(2)}) copy-start(f32[1,448,2048]{2,1,0:T(8,128)} %param.17) | copy-start | bytes 11010052
  469.2 21.8 %collective-permute-start.33 = (bf16[64,2048]{1,0:T(8,128)(2,1)S(1)}, bf16[64,2048]{1,0:T(8,128)(2,1)S(1)}, u32[]{:S(2)}, u32[]{:S(2)}) collective-permute-start(bf16[64,2048]{1,0:T(8,128)(2,1)S(1)} %get-tuple-element.91), channel_id=1, source_target_pairs={{0,0},{3,1},{6,2},{1,3},{4,4},{7,5},{2,6},{5,7},{8,8},{11,9},{14,1... | collective-permute-start | bytes 786440 | tf_op jit(solution)/shard_map/ppermute | solution.py:554
  471.2 19.7 %collective-permute-start.35 = (bf16[64,2048]{1,0:T(8,128)(2,1)S(1)}, bf16[64,2048]{1,0:T(8,128)(2,1)S(1)}, u32[]{:S(2)}, u32[]{:S(2)}) collective-permute-start(bf16[64,2048]{1,0:T(8,128)(2,1)S(1)} %get-tuple-element.92), channel_id=1, source_target_pairs={{2,0},{5,1},{0,2},{3,3},{6,4},{1,5},{4,6},{7,7},{10,8},{13,9},{8,1... | collective-permute-start | bytes 786440 | tf_op jit(solution)/shard_map/ppermute | solution.py:554
  475.6 30.1 %collective-permute-start.34 = (bf16[64,2048]{1,0:T(8,128)(2,1)S(1)}, bf16[64,2048]{1,0:T(8,128)(2,1)S(1)}, u32[]{:S(2)}, u32[]{:S(2)}) collective-permute-start(bf16[64,2048]{1,0:T(8,128)(2,1)S(1)} %get-tuple-element.93), channel_id=1, source_target_pairs={{1,0},{4,1},{7,2},{2,3},{5,4},{0,5},{3,6},{6,7},{9,8},{12,9},{15,1... | collective-permute-start | bytes 786440 | tf_op jit(solution)/shard_map/ppermute | solution.py:554
  509.1 11.1 %collective-permute-start.38 = (bf16[96,2048]{1,0:T(8,128)(2,1)S(1)}, bf16[96,2048]{1,0:T(8,128)(2,1)}, u32[]{:S(2)}, u32[]{:S(2)}) collective-permute-start(bf16[96,2048]{1,0:T(8,128)(2,1)S(1)} %get-tuple-element.89), channel_id=1, source_target_pairs={{24,16},{8,0},{25,17},{9,1},{26,18},{10,2},{27,19},{11,3},{28,20},... | collective-permute-start | bytes 1179656 | tf_op jit(solution)/shard_map/ppermute | solution.py:514
  510.5 12.6 %collective-permute-start.40 = (bf16[96,2048]{1,0:T(8,128)(2,1)S(1)}, bf16[96,2048]{1,0:T(8,128)(2,1)}, u32[]{:S(2)}, u32[]{:S(2)}) collective-permute-start(bf16[96,2048]{1,0:T(8,128)(2,1)S(1)} %get-tuple-element.90), channel_id=1, source_target_pairs={{24,8},{8,24},{25,9},{9,25},{26,10},{10,26},{27,11},{11,27},{28,12... | collective-permute-start | bytes 1179656 | tf_op jit(solution)/shard_map/ppermute | solution.py:514
  516.2 29.0 %collective-permute-start.36 = (bf16[192,2048]{1,0:T(8,128)(2,1)}, bf16[192,2048]{1,0:T(8,128)(2,1)S(1)}, u32[]{:S(2)}, u32[]{:S(2)}) collective-permute-start(bf16[192,2048]{1,0:T(8,128)(2,1)} %get-tuple-element.79), channel_id=1, source_target_pairs={{8,0},{24,16},{9,1},{25,17},{10,2},{26,18},{11,3},{27,19},{12,4},{... | collective-permute-start | bytes 2359304 | tf_op jit(solution)/shard_map/ppermute | solution.py:514
  517.5 27.7 %collective-permute-start.37 = (bf16[192,2048]{1,0:T(8,128)(2,1)}, bf16[192,2048]{1,0:T(8,128)(2,1)S(1)}, u32[]{:S(2)}, u32[]{:S(2)}) collective-permute-start(bf16[192,2048]{1,0:T(8,128)(2,1)} %get-tuple-element.80), channel_id=1, source_target_pairs={{16,0},{0,16},{17,1},{1,17},{18,2},{2,18},{19,3},{3,19},{20,4},{4,... | collective-permute-start | bytes 2359304 | tf_op jit(solution)/shard_map/ppermute | solution.py:514
  520.2 24.9 %collective-permute-start.39 = (bf16[96,2048]{1,0:T(8,128)(2,1)}, bf16[96,2048]{1,0:T(8,128)(2,1)S(1)}, u32[]{:S(2)}, u32[]{:S(2)}) collective-permute-start(bf16[96,2048]{1,0:T(8,128)(2,1)} %collective-permute-done.38), channel_id=1, source_target_pairs={{16,0},{0,16},{17,1},{1,17},{18,2},{2,18},{19,3},{3,19},{20,4},{4,... | collective-permute-start | bytes 1179656 | tf_op jit(solution)/shard_map/ppermute | solution.py:514
  523.1 22.0 %collective-permute-start.41 = (bf16[96,2048]{1,0:T(8,128)(2,1)}, bf16[96,2048]{1,0:T(8,128)(2,1)S(1)}, u32[]{:S(2)}, u32[]{:S(2)}) collective-permute-start(bf16[96,2048]{1,0:T(8,128)(2,1)} %collective-permute-done.40), channel_id=1, source_target_pairs={{8,0},{24,16},{9,1},{25,17},{10,2},{26,18},{11,3},{27,19},{12,4},{... | collective-permute-start | bytes 1179656 | tf_op jit(solution)/shard_map/ppermute | solution.py:514
  560.3 110.1 %all-gather.9.cloned.1.call-start = ((), (), s32[]{:S(2)}) async-start(), calls=%async_computation.8 | async-start | bytes 5308416 | tf_op jit(solution)/shard_map/all_gather | solution.py:373
  616.2 155.2 %reduce-scatter.9.cloned.1.call-start = ((), (), s32[]{:S(2)}) async-start(), calls=%async_computation.9 | async-start | bytes 9437184 | tf_op jit(solution)/shard_map/reduce_scatter | solution.py:764
  670.3 152.5 %reduce-scatter.11.cloned.1.call-start = ((), (), s32[]{:S(2)}) async-start(), calls=%async_computation.10 | async-start | bytes 5308416 | tf_op jit(solution)/shard_map/reduce_scatter | solution.py:372
  771.4 51.5 %copy-start.69 = (f32[1024]{0:T(1024)S(1)}, f32[1024]{0:T(1024)}, u32[]{:S(2)}) copy-start(f32[1024]{0:T(1024)} %get-tuple-element.30) | copy-start | bytes 12292
  771.5 51.7 %copy-start.64 = (f32[768]{0:T(1024)S(1)}, f32[768]{0:T(1024)}, u32[]{:S(2)}) copy-start(f32[768]{0:T(1024)} %convert_reduce_fusion.1) | copy-start | bytes 9220
  771.5 105.7 %all-gather.11.cloned.1.call-start = ((), (), s32[]{:S(2)}) async-start(), calls=%async_computation.11 | async-start | bytes 5308416 | tf_op jit(solution)/shard_map/all_gather | solution.py:373
  822.9 190.9 %all-reduce.4.cloned.1.call-start = ((), (), s32[]{:S(2)}) async-start(), calls=%async_computation.12 | async-start | bytes 163840 | tf_op jit(solution)/shard_map/psum | solution.py:782
  832.7 44.5 %copy-start.57 = (f32[20480]{0:T(1024)}, f32[20480]{0:T(1024)S(1)}, u32[]{:S(2)}) copy-start(f32[20480]{0:T(1024)S(1)} %constant_dynamic-update-slice_fusion.5.refs_0_) | copy-start | bytes 245764
  1018.2 13.3 %collective-permute-start.44 = (bf16[128,2048]{1,0:T(8,128)(2,1)S(1)}, bf16[128,2048]{1,0:T(8,128)(2,1)S(1)}, u32[]{:S(2)}, u32[]{:S(2)}) collective-permute-start(bf16[128,2048]{1,0:T(8,128)(2,1)S(1)} %get-tuple-element.50), channel_id=1, source_target_pairs={{0,8},{8,0},{16,24},{24,16},{1,9},{9,1},{17,25},{25,17},{2,10},{10... | collective-permute-start | bytes 1572872 | tf_op jit(solution)/shard_map/ppermute | solution.py:417
  1019.4 13.3 %collective-permute-start.46 = (bf16[128,2048]{1,0:T(8,128)(2,1)S(1)}, bf16[128,2048]{1,0:T(8,128)(2,1)S(1)}, u32[]{:S(2)}, u32[]{:S(2)}) collective-permute-start(bf16[128,2048]{1,0:T(8,128)(2,1)S(1)} %get-tuple-element.51), channel_id=1, source_target_pairs={{0,16},{8,24},{16,0},{24,8},{1,17},{9,25},{17,1},{25,9},{2,18},{10... | collective-permute-start | bytes 1572872 | tf_op jit(solution)/shard_map/ppermute | solution.py:417
  1020.6 45.5 %collective-permute-start.43 = (bf16[256,2048]{1,0:T(8,128)(2,1)S(1)}, bf16[256,2048]{1,0:T(8,128)(2,1)S(1)}, u32[]{:S(2)}, u32[]{:S(2)}) collective-permute-start(bf16[256,2048]{1,0:T(8,128)(2,1)S(1)} %get-tuple-element.48), channel_id=1, source_target_pairs={{0,16},{8,24},{16,0},{24,8},{1,17},{9,25},{17,1},{25,9},{2,18},{10... | collective-permute-start | bytes 3145736 | tf_op jit(solution)/shard_map/ppermute | solution.py:417
  1020.9 45.3 %collective-permute-start.42 = (bf16[256,2048]{1,0:T(8,128)(2,1)S(1)}, bf16[256,2048]{1,0:T(8,128)(2,1)S(1)}, u32[]{:S(2)}, u32[]{:S(2)}) collective-permute-start(bf16[256,2048]{1,0:T(8,128)(2,1)S(1)} %get-tuple-element.49), channel_id=1, source_target_pairs={{0,8},{8,0},{16,24},{24,16},{1,9},{9,1},{17,25},{25,17},{2,10},{10... | collective-permute-start | bytes 3145736 | tf_op jit(solution)/shard_map/ppermute | solution.py:417
  1031.5 34.6 %collective-permute-start.45 = (bf16[128,2048]{1,0:T(8,128)(2,1)S(1)}, bf16[128,2048]{1,0:T(8,128)(2,1)S(1)}, u32[]{:S(2)}, u32[]{:S(2)}) collective-permute-start(bf16[128,2048]{1,0:T(8,128)(2,1)S(1)} %collective-permute-done.44), channel_id=1, source_target_pairs={{0,16},{8,24},{16,0},{24,8},{1,17},{9,25},{17,1},{25,9},{2,18},{10... | collective-permute-start | bytes 1572872 | tf_op jit(solution)/shard_map/ppermute | solution.py:417
  1032.7 33.4 %collective-permute-start.47 = (bf16[128,2048]{1,0:T(8,128)(2,1)S(1)}, bf16[128,2048]{1,0:T(8,128)(2,1)S(1)}, u32[]{:S(2)}, u32[]{:S(2)}) collective-permute-start(bf16[128,2048]{1,0:T(8,128)(2,1)S(1)} %collective-permute-done.46), channel_id=1, source_target_pairs={{0,8},{8,0},{16,24},{24,16},{1,9},{9,1},{17,25},{25,17},{2,10},{10... | collective-permute-start | bytes 1572872 | tf_op jit(solution)/shard_map/ppermute | solution.py:417
  (69 other events, 510.7 us)
Sparse Core Ops, SparseCore 0:
  12.8 94.4 all-gather.4
  109.5 81.6 all-gather.6
  418.6 104.6 reduce-scatter.4
  560.4 55.7 reduce-scatter.6
  617.6 52.6 all-gather.8
  672.5 85.8 reduce-scatter.8
  771.6 51.2 reduce-scatter.10
  824.5 52.6 all-gather.10
  883.3 118.7 all-reduce.3

commit v2 on v1

--- a/solution.py
+++ b/solution.py
@@ -23,6 +23,7 @@
 CHUNK = 256
 PANEL = 512
 VMEM_BYTES = 61 * 2**20
+MATMUL_BYTES = 60 * 2**20
 
 
 def positions(segments):
@@ -32,9 +33,12 @@
     return index_all - lax.cummax(starts, axis=0)
 
 
-def gelu_tanh(values):
-    inner = 0.7978845608028654 * (values + 0.044715 * values * values * values)
-    return 0.5 * values * (1.0 + jnp.tanh(inner))
+def gelu_and_slope(values):
+    square = values * values
+    bent = jnp.tanh(0.7978845608028654 * (values + 0.044715 * values * square))
+    inner_slope = 0.7978845608028654 * (1.0 + 3.0 * 0.044715 * square)
+    half = 0.5 * (1.0 + bent)
+    return values * half, half + 0.5 * values * (1.0 - bent * bent) * inner_slope
 
 
 def rotary_lanes(position, heads):
@@ -57,6 +61,178 @@
         input_output_aliases={0: 0},
         name="after",
     )(values, *others)
+
+
+def over(left, right, axes):
+    return lax.dot_general(left, right, (axes, ((), ())), preferred_element_type=F32)
+
+
+NOTHING = pl.CostEstimate(flops=0, bytes_accessed=0, transcendentals=0)
+ROWS = ((1,), (1,))
+TOKENS = ((0,), (0,))
+
+
+def by_rows(body, blocked, whole, outs, rows, name):
+    steps = blocked[0].shape[0] // rows
+    return pl.pallas_call(
+        body,
+        grid=(steps,),
+        in_specs=[pl.BlockSpec((rows, one.shape[1]), lambda step: (step, 0)) for one in blocked]
+        + [
+            pl.BlockSpec(one.shape, lambda step, rank=one.ndim: (0,) * rank, pipeline_mode=pl.Buffered(1))
+            for one in whole
+        ],
+        out_specs=tuple(pl.BlockSpec((rows, width), lambda step: (step, 0)) for width, _ in outs),
+        out_shape=tuple(jax.ShapeDtypeStruct((steps * rows, width), dtype) for width, dtype in outs),
+        compiler_params=pltpu.CompilerParams(vmem_limit_bytes=MATMUL_BYTES),
+        cost_estimate=NOTHING,
+        name=name,
+    )(*blocked, *whole)
+
+
+def by_columns(body, whole, blocked, outs, columns, name, scratch=(), scalar=None):
+    steps = blocked[0].shape[1] // columns
+    return pl.pallas_call(
+        body,
+        grid=(steps,),
+        in_specs=([] if scalar is None else [pl.BlockSpec(memory_space=pltpu.SMEM)])
+        + [pl.BlockSpec(one.shape, lambda step: (0, 0), pipeline_mode=pl.Buffered(1)) for one in whole]
+        + [pl.BlockSpec((one.shape[0], columns), lambda step: (0, step)) for one in blocked],
+        out_specs=tuple(pl.BlockSpec((rows, columns), lambda step: (0, step)) for rows, _ in outs),
+        out_shape=tuple(jax.ShapeDtypeStruct((rows, steps * columns), dtype) for rows, dtype in outs),
+        scratch_shapes=list(scratch),
+        compiler_params=pltpu.CompilerParams(vmem_limit_bytes=MATMUL_BYTES),
+        cost_estimate=NOTHING,
+        name=name,
+    )(*([] if scalar is None else [scalar]), *whole, *blocked)
+
+
+def in_vmem(body, ins, others, outs, name, scalar=None):
+    vmem = pl.BlockSpec(memory_space=pltpu.VMEM)
+    first = [] if scalar is None else [pl.BlockSpec(memory_space=pltpu.SMEM)]
+    return pl.pallas_call(
+        body,
+        in_specs=first + [vmem] * len(ins) + [pl.BlockSpec(memory_space=pl.ANY)] * len(others),
+        out_specs=[vmem] * len(outs),
+        out_shape=[jax.ShapeDtypeStruct(shape, dtype) for shape, dtype in outs],
+        compiler_params=pltpu.CompilerParams(vmem_limit_bytes=MATMUL_BYTES),
+        cost_estimate=NOTHING,
+        name=name,
+    )(*([] if scalar is None else [scalar]), *ins, *others)
+
+
+def up_forward(normed, w_up, bias):
+    def body(x_ref, w_ref, b_ref, act_ref, slope_ref):
+        act, slope = gelu_and_slope(over(x_ref[...], w_ref[...], ROWS) + b_ref[...])
+        act_ref[...] = act.astype(BF16)
+        slope_ref[...] = slope.astype(BF16)
+
+    units = w_up.shape[0]
+    return by_rows(body, [normed], [w_up, bias[None]], [(units, BF16), (units, BF16)], 256, "up_forward")
+
+
+def up_backward(grad, slope, w_down):
+    def body(g_ref, s_ref, w_ref, out_ref):
+        out_ref[...] = (over(g_ref[...], w_ref[...], ROWS) * s_ref[...].astype(F32)).astype(BF16)
+
+    return by_rows(body, [grad, slope], [w_down], [(w_down.shape[0], BF16)], 512, "up_backward")[0]
+
+
+def project(x, w, bias, dtype, name):
+    def body(x_ref, w_ref, b_ref, out_ref):
+        out_ref[...] = (over(x_ref[...], w_ref[...], ROWS) + b_ref[...]).astype(dtype)
+
+    return by_rows(body, [x], [w, bias[None]], [(w.shape[0], dtype)], 512, name)[0]
+
+
+def weight_grad(left, right, name, split=False):
+    tokens, rows = left.shape
+    quarter = rows // 8 if split else rows
+
+    def body(l_ref, r_ref, *refs):
+        t_s = refs[-1]
+
+        @pl.when(pl.program_id(0) == 0)
+        def turn_over():
+            for block in range(0, tokens, 256):
+                t_s[:, block : block + 256] = l_ref[block : block + 256, :].T
+
+        product = jnp.dot(t_s[...], r_ref[...], preferred_element_type=F32).astype(BF16)
+        if not split:
+            refs[0][...] = product
+            return
+        for block in range(4):
+            for half in range(2):
+                y, x = block // 2, block % 2
+                sent, at = (x, y) if half == 0 else (y, x)
+                source = (2 * block + half) * quarter
+                refs[2 * half + 1 - sent][at * quarter : (at + 1) * quarter, :] = product[source : source + quarter, :]
+
+    scratch = [pltpu.VMEM((rows, tokens), BF16)]
+    outs = [(2 * quarter, BF16)] * 4 if split else [(rows, BF16)]
+    results = by_columns(body, [left], [right], outs, 512, name, scratch)
+    return results if split else results[0]
+
+
+def weight_grads_plus(left, right, other_left, other_right, moment, other_moment, part, heads):
+    tokens = left.shape[0]
+    rows, other_rows = left.shape[1], other_left.shape[1]
+    half, other_half = rows // 2, other_rows // 2
+    per_part = other_rows // HEAD
+    me = lax.axis_index("dp").astype(jnp.int32).reshape(1)
+
+    def body(
+        me_ref, l_ref, o_ref, r_ref, q_ref, m_ref, n_ref, out_ref, other_ref, sent_x, kept_x, sent_y, kept_y, t_s, f_s, g_s
+    ):
+        @pl.when(pl.program_id(0) == 0)
+        def turn_over():
+            for block in range(0, tokens, 256):
+                t_s[:rows, block : block + 256] = l_ref[block : block + 256, :].T
+                t_s[rows:, block : block + 256] = o_ref[block : block + 256, :].T
+
+        f_s[...] = jnp.dot(t_s[:rows, :], r_ref[...], preferred_element_type=F32)
+        out_ref[...] = f_s[...].astype(BF16)
+        g_s[...] = jnp.dot(t_s[rows:, :], q_ref[...], preferred_element_type=F32)
+        other_ref[...] = g_s[...].astype(BF16)
+        for i in range(3):
+            chunk = 3 * me_ref[0] + i
+            kind, head = chunk // heads, chunk % heads
+
+            @pl.when(head // per_part == part)
+            def add_qkv(i=i, kind=kind, head=head):
+                at = pl.ds(pl.multiple_of(kind * other_rows + (head % per_part) * HEAD, HEAD), HEAD)
+                f_s[at, :] += m_ref[i * HEAD : (i + 1) * HEAD, :]
+
+        @pl.when(me_ref[0] // per_part == part)
+        def add_out():
+            at = pl.ds(pl.multiple_of((me_ref[0] % per_part) * HEAD, HEAD), HEAD)
+            g_s[at, :] += n_ref[...]
+
+        full, other = f_s[...].astype(BF16), g_s[...].astype(BF16)
+        nothing = jnp.zeros((half - other_half, other.shape[1]), BF16)
+        for at, (sent, kept, mine) in enumerate(
+            ((sent_x, kept_x, (me_ref[0] & 1) == 1), (sent_y, kept_y, (me_ref[0] & 2) == 0))
+        ):
+            first = full[at * half : (at + 1) * half]
+            second = jnp.concatenate([other[at * other_half : (at + 1) * other_half], nothing], axis=0)
+            sent[...] = jnp.where(mine, second, first)
+            kept[...] = jnp.where(mine, first, second)
+
+    columns = 512
+    return by_columns(
+        body,
+        [left, other_left],
+        [right, other_right, moment, other_moment],
+        [(rows, BF16), (other_rows, BF16)] + [(half, BF16)] * 4,
+        columns,
+        "weight_grads_plus",
+        [
+            pltpu.VMEM((rows + other_rows, tokens), BF16),
+            pltpu.VMEM((rows, columns), F32),
+            pltpu.VMEM((other_rows, columns), F32),
+        ],
+        me,
+    )
 
 
 def rows_at(index, size):
@@ -145,13 +321,9 @@
     lax.fori_loop(0, blocks, finish, 0)
 
 
-def attention(pre_qkv, grad_attended, position, part, width):
+def attention(pre_qkv, grad_attended, tables, part, width):
     pack_len = grad_attended.shape[0]
-    start = jnp.arange(pack_len, dtype=jnp.int32) - position
-    first = start[::CHUNK] // CHUNK
-    cos_tab, sin_tab = rotary_lanes(position, width // HEAD)
     whole = pl.BlockSpec(memory_space=pltpu.VMEM)
-    pairs = pack_len * SEQ_MAX * (width // HEAD)
     return pl.pallas_call(
         attention_body,
         grid=(1,),
@@ -172,11 +344,9 @@
         + [pltpu.VMEM((pack_len, width), F32)] * 2
         + [pltpu.VMEM((CHUNK, width), F32)] * 2,
         compiler_params=pltpu.CompilerParams(vmem_limit_bytes=VMEM_BYTES),
-        cost_estimate=pl.CostEstimate(
-            flops=pairs * 10 * HEAD * 4, bytes_accessed=16 * pack_len * width, transcendentals=pairs
-        ),
+        cost_estimate=NOTHING,
         name="attention",
-    )(first, pre_qkv, grad_attended, start[:, None], cos_tab, sin_tab)
+    )(tables[0], pre_qkv, grad_attended, *tables[1:])
 
 
 def tri(index):
@@ -220,7 +390,31 @@
             ]
 
 
-def gram_body(x_ref, before_ref, packed_ref, xt_s):
+def gram_body(x_ref, packed_ref, xt_s):
+    gram_packed(x_ref, xt_s, x_ref.shape[1], packed_ref)
+
+
+def owned_gram_body(me_ref, *refs):
+    early, late, (x_ref, packed_ref, xt_s) = refs[:5], refs[5:13], refs[13:]
+    pieces = [late[at : at + 2] for at in range(0, 8, 2)]
+    block = early[0].shape[0]
+
+    @pl.when((me_ref[0] == 0) | (me_ref[0] == 3))
+    def from_early():
+        at = 0
+        for one in early:
+            x_ref[at : at + one.shape[0], :] = one[...]
+            at += one.shape[0]
+
+    for owner, share in ((1, 1), (2, 3)):
+
+        @pl.when(me_ref[0] == owner)
+        def from_late(share=share):
+            rows = pieces[0][0].shape[0] // share
+            for at, (total, got) in enumerate(pieces):
+                x_ref[at * rows : (at + 1) * rows, :] = (total[:rows, :] + got[:rows, :].astype(F32)).astype(BF16)
+            x_ref[4 * rows :, :] = jnp.zeros((4 * (block - rows), x_ref.shape[1]), BF16)
+
     gram_packed(x_ref, xt_s, x_ref.shape[1], packed_ref)
 
 
@@ -325,7 +519,8 @@
     store_packed.wait()
 
 
-def second_body(count, packed_ref, x_ref, x_out, x_s, exact_s, low_s, poly_s, mix_s, packed_s, sems):
+def second_body(count, from_ref, packed_ref, x_ref, *refs):
+    outs, (x_s, exact_s, low_s, poly_s, mix_s, packed_s, sems, out_sems) = refs[:-8], refs[-8:]
     size = x_ref.shape[1]
     load_x = pltpu.make_async_copy(x_ref, x_s.at[0], sems.at[0])
     load_packed = pltpu.make_async_copy(packed_ref, packed_s, sems.at[1])
@@ -335,9 +530,20 @@
     unpack(packed_s, size, 1.0, exact_s, low_s)
     load_x.wait()
     iterate(x_s, exact_s, low_s, poly_s, mix_s, size, count)
-    store_x = pltpu.make_async_copy(x_s.at[count % 2], x_out, sems.at[0])
-    store_x.start()
-    store_x.wait()
+    stores = []
+    for out in outs:
+        unit = x_ref.shape[0] // out_sems.shape[0]
+        for at in range(0, out.shape[0], unit):
+            source = pl.ds(pl.multiple_of(from_ref[len(stores)], unit), unit)
+            stores.append(
+                pltpu.make_async_copy(
+                    x_s.at[count % 2, source, :], out.at[at : at + unit, :], out_sems.at[len(stores)]
+                )
+            )
+    for store in stores:
+        store.start()
+    for store in stores:
+        store.wait()
 
 
 def ns_scratch(depth, size):
@@ -352,38 +558,49 @@
     ]
 
 
-def orthogonalize(rows, before, before_sum, beside_first, beside_last):
+def first_gram(rows, early=(), late=()):
+    depth, size = rows
+    vmem = pl.BlockSpec(memory_space=pltpu.VMEM)
+    shapes = (jax.ShapeDtypeStruct((depth, size), BF16), jax.ShapeDtypeStruct((packed_rows(size), CHUNK), BF16))
+    me = lax.axis_index("dp").astype(jnp.int32).reshape(1)
+    return pl.pallas_call(
+        owned_gram_body,
+        out_shape=shapes,
+        in_specs=[pl.BlockSpec(memory_space=pltpu.SMEM)] + [vmem] * (len(early) + len(late)),
+        out_specs=(vmem, vmem),
+        scratch_shapes=[pltpu.VMEM((size, depth), BF16)],
+        compiler_params=pltpu.CompilerParams(vmem_limit_bytes=VMEM_BYTES),
+        cost_estimate=NOTHING,
+        name="gram",
+    )(me, *early, *late)
+
+
+def orthogonalize(rows, packed, source_rows, pieces, after_gram, beside_first, after_first_steps, after_first, beside_last):
     depth, size = rows.shape
-    group_count = lax.axis_size("group")
     packed_shape = jax.ShapeDtypeStruct((packed_rows(size), CHUNK), BF16)
     x_shape = jax.ShapeDtypeStruct((depth, size), BF16)
     vmem = pl.BlockSpec(memory_space=pltpu.VMEM)
     hbm = pl.BlockSpec(memory_space=pl.ANY)
     params = pltpu.CompilerParams(vmem_limit_bytes=VMEM_BYTES)
 
-    def cost(products, x_steps):
-        return pl.CostEstimate(
-            flops=products * size**3 * 5 // 4 + x_steps * 2 * depth * size * size,
-            bytes_accessed=size * size * 4,
-            transcendentals=0,
-        )
-
-    def summed(packed):
+    def gram_sum(packed, meanwhile):
         part = lax.psum_scatter(packed, "group", scatter_dimension=0, tiled=True)
-        return lax.all_gather(part, "group", axis=0, tiled=True)
-
-    packed = pl.pallas_call(
-        gram_body,
-        out_shape=packed_shape,
-        in_specs=[vmem, hbm],
-        out_specs=vmem,
-        scratch_shapes=[pltpu.VMEM((size, depth), BF16)],
-        compiler_params=params,
-        cost_estimate=cost(0, 1),
-        name="gram",
-    )(rows, before)
-    gathered = summed(after(packed, before_sum))
-    first_result = beside_first(gathered)
+        return lax.all_gather(after(part, *jax.tree.leaves(meanwhile)), "group", axis=0, tiled=True)
+
+    if packed is None:
+        packed = pl.pallas_call(
+            gram_body,
+            out_shape=packed_shape,
+            in_specs=[vmem],
+            out_specs=vmem,
+            scratch_shapes=[pltpu.VMEM((size, depth), BF16)],
+            compiler_params=params,
+            cost_estimate=NOTHING,
+            name="gram",
+        )(rows)
+    meanwhile = after_gram(packed)
+    gathered = gram_sum(packed, meanwhile)
+    first = beside_first(gathered, meanwhile)
     half_way, packed = pl.pallas_call(
         functools.partial(first_body, 2),
         out_shape=(x_shape, packed_shape),
@@ -391,137 +608,148 @@
         out_specs=(hbm, hbm),
         scratch_shapes=ns_scratch(depth, size),
         compiler_params=params,
-        cost_estimate=cost(4, 3),
+        cost_estimate=NOTHING,
         name="first_steps",
     )(gathered, rows)
-    gathered = summed(after(packed, first_result))
-    last_result = beside_last(first_result, gathered)
-    result = pl.pallas_call(
+    first = after_first_steps(first, packed)
+    packed = after(packed, *first)
+    meanwhile = after_first(packed, first)
+    gathered = gram_sum(packed, meanwhile)
+    last = beside_last(gathered)
+    results = pl.pallas_call(
         functools.partial(second_body, 3),
-        out_shape=x_shape,
-        in_specs=[hbm, hbm],
-        out_specs=hbm,
-        scratch_shapes=ns_scratch(depth, size),
+        out_shape=[jax.ShapeDtypeStruct((piece, size), BF16) for piece in pieces],
+        in_specs=[pl.BlockSpec(memory_space=pltpu.SMEM), hbm, hbm],
+        out_specs=[hbm] * len(pieces),
+        scratch_shapes=ns_scratch(depth, size) + [pltpu.SemaphoreType.DMA((source_rows.shape[0],))],
         compiler_params=params,
-        cost_estimate=cost(7, 3),
+        cost_estimate=NOTHING,
         name="last_steps",
-    )(gathered, half_way)
-    return result, last_result
-
-
-def flip(bit):
-    return [(index, index ^ bit) for index in range(4)]
-
-
-def send(values, bit):
-    return lax.ppermute(values, "dp", flip(bit))
+    )(source_rows, gathered, half_way)
+    return results, first, meanwhile, last
 
 
 def two_by_two():
     return lax.axis_size("dp") == 4
 
 
+def hop(values, bit, targets=range(4)):
+    return lax.ppermute(values, "dp", [(t ^ bit, t) for t in targets])
+
+
 def by_distance(parts):
-    if not two_by_two():
-        return parts
     me = lax.axis_index("dp")
     return jnp.stack([lax.dynamic_index_in_dim(parts, me ^ r, 0, keepdims=False) for r in range(4)])
 
 
 def gather_near(own):
-    if not two_by_two():
-        return lax.all_gather(own, "dp", axis=0, tiled=False)
-    return own, send(own, 1), send(own, 2)
+    return own, hop(own, 1), hop(own, 2)
 
 
 def gather_far(near):
-    if not two_by_two():
-        return near
     own, from_x, from_y = near
     half = own.shape[0] // 2
-    first, second = send(from_y[:half], 1), send(from_x[half:], 2)
+    first, second = hop(from_y[:half], 1), hop(from_x[half:], 2)
     return jnp.stack([own, from_x, from_y, jnp.concatenate([first, second], axis=0)])
 
 
-def came(near):
-    return near[1:] if two_by_two() else (near,)
-
-
-def gather_dp(own):
-    return gather_far(gather_near(own))
-
-
-def scatter_start(parts):
-    if not two_by_two():
-        return lax.psum_scatter(parts, "dp", scatter_dimension=0, tiled=False).astype(F32)
-    half = parts.shape[1] // 2
-    terms = parts.reshape(2, 2, parts.shape[1], parts.shape[2])
-    left, right = terms[:, :, :half], terms[:, :, half:]
-    return terms, send(left[:, 1], 1), send(right[1], 2)
+def reduce_start(sent_x, kept_x, sent_y, kept_y):
+    return kept_x, hop(sent_x, 1), kept_y, hop(sent_y, 2)
+
+
+def reduce_next(state, *others):
+    def body(*refs):
+        outs = refs[4 + len(others) :]
+        for k in range(2):
+            total = refs[2 * k][...].astype(F32) + refs[2 * k + 1][...].astype(F32)
+            outs[2 * k][...] = total
+            outs[2 * k + 1][...] = total.astype(BF16)
+
+    shapes = [(state[0].shape, dtype) for dtype in (F32, BF16)] * 2
+    total_x, out_x, total_y, out_y = in_vmem(body, state, others, shapes, "reduce_next")
+    return (total_x, hop(out_x, 2, [1, 2]), total_y, hop(out_y, 1, [1, 2])), (out_x, out_y)
+
+
+def scatter_start(split):
+    left_out, left, right_out, right = split
+    return left, hop(left_out, 1), right, hop(right_out, 2)
 
 
 def scatter_next(state, *others):
-    if not two_by_two():
-        return state
-    terms, left_in, right_in = state
-    half = terms.shape[2] // 2
-    terms = after(terms, *others)
-    left, right = terms[:, 0, :half], terms[0, :, half:]
-    left_sum = left.astype(F32) + left_in.astype(F32)
-    right_sum = right.astype(F32) + right_in.astype(F32)
-    return left_sum[0], left_sum[1].astype(BF16), right_sum[0], right_sum[1].astype(BF16)
-
-
-def scatter_end(state, *others):
-    if not two_by_two():
-        return state
-    left, left_out, right, right_out = state
-    left_in, right_in = send(left_out, 2), send(right_out, 1)
-    if others:
-        left = after(left, *others)
+    half = state[0].shape[0] // 2
+
+    def body(*refs):
+        outs = refs[4 + len(others) :]
+        for k in range(2):
+            total = refs[2 * k][...].astype(F32) + refs[2 * k + 1][...].astype(F32)
+            outs[2 * k][...] = total[:half]
+            outs[2 * k + 1][...] = total[half:].astype(BF16)
+
+    shapes = [((half, state[0].shape[1]), dtype) for dtype in (F32, BF16)] * 2
+    left, left_out, right, right_out = in_vmem(body, state, others, shapes, "scatter_next")
+    return (left, hop(left_out, 2), right, hop(right_out, 1)), (left_out, right_out)
+
+
+def scatter_end(state):
+    left, left_in, right, right_in = state
     return jnp.concatenate([left + left_in.astype(F32), right + right_in.astype(F32)], axis=0)
 
 
-def flying(state):
-    return state[1::2] if two_by_two() else (state,)
-
-
-def owners_start(slots, owners):
-    me = lax.axis_index("dp")
-    half = slots.shape[1] // 2
-
-    def slot_for(distance):
-        picked = slots[0]
-        for k, owner in enumerate(owners[1:], 1):
-            picked = jnp.where((me ^ distance) == owner, slots[k], picked)
-        return picked
-
-    far = slot_for(3)
-    first_hop = hop(far[:half], 1, [t ^ 2 for t in owners])
-    second_hop = hop(far[half:], 2, [t ^ 1 for t in owners])
-    return slot_for(0), hop(slot_for(1), 1, owners), hop(slot_for(2), 2, owners), first_hop, second_hop
+def scatter_momentum(state, moment, *others):
+    rows, width = moment.shape
+    half = rows // 2
+
+    def body(*refs):
+        left, left_in, right, right_in, moment_ref = refs[:5]
+        own, full = refs[5 + len(others) :]
+        for at, (one, got) in ((0, (left, left_in)), (half, (right, right_in))):
+            total = one[...] + got[...].astype(F32)
+            own[at : at + half, :] = total
+            full[at : at + half, :] = (total + moment_ref[at : at + half, :]).astype(BF16)
+
+    shapes = [((rows, width), F32), ((rows, width), BF16)]
+    return in_vmem(body, [*state, moment], others, shapes, "momentum")
+
+
+def owners_start(slots, owners, *others):
+    rows, width = slots[0].shape
+    half = rows // 2
+    me = lax.axis_index("dp").astype(jnp.int32).reshape(1)
+
+    def body(me_ref, first_ref, second_ref, *refs):
+        outs = refs[len(others) :]
+        for r in range(4):
+            picked = jnp.where((me_ref[0] ^ r) == owners[0], first_ref[...], second_ref[...])
+            if r < 3:
+                outs[r][...] = picked
+            else:
+                outs[3][...], outs[4][...] = picked[:half], picked[half:]
+
+    shapes = [((rows, width), BF16)] * 3 + [((half, width), BF16)] * 2
+    own, to_x, to_y, first_hop, second_hop = sent = in_vmem(body, slots, others, shapes, "to_owners", me)
+    first_hop, second_hop = hop(first_hop, 1, [t ^ 2 for t in owners]), hop(second_hop, 2, [t ^ 1 for t in owners])
+    return (own, hop(to_x, 1, owners), hop(to_y, 2, owners), first_hop, second_hop), sent[1:]
 
 
 def owners_end(state, owners, *others):
     own, from_x, from_y, first_hop, second_hop = state
-    if others:
-        first_hop = after(first_hop, *others)
-    first, second = hop(first_hop, 2, owners), hop(second_hop, 1, owners)
+    return own, from_x, from_y, hop(after(first_hop, *others), 2, owners), hop(second_hop, 1, owners)
+
+
+def exchange_dp(own, to_x, to_y, first_hop, second_hop):
+    first_hop, second_hop = hop(first_hop, 1), hop(second_hop, 2)
+    from_x, from_y = hop(to_x, 1), hop(to_y, 2)
+    first, second = hop(first_hop, 2), hop(second_hop, 1)
     return jnp.stack([own, from_x, from_y, jnp.concatenate([first, second], axis=0)])
 
 
-def hop(values, bit, targets):
-    return lax.ppermute(values, "dp", [(t ^ bit, t) for t in targets])
-
-
-def exchange_dp(slots):
-    if not two_by_two():
-        return lax.all_to_all(slots, "dp", split_axis=0, concat_axis=0, tiled=True)
-    half = slots.shape[1] // 2
-    first_hop, second_hop = send(slots[3, :half], 1), send(slots[3, half:], 2)
-    from_x, from_y = send(slots[1], 1), send(slots[2], 2)
-    first, second = send(first_hop, 2), send(second_hop, 1)
-    return jnp.stack([slots[0], from_x, from_y, jnp.concatenate([first, second], axis=0)])
+def butterfly(values):
+    for axis in ("group", "dp"):
+        size, bit = lax.axis_size(axis), 1
+        while bit < size:
+            values = values + lax.ppermute(values, axis, [(i, i ^ bit) for i in range(size)])
+            bit *= 2
+    return values
 
 
 def heads_aligned(unit):
@@ -599,13 +827,14 @@
     group_count = lax.axis_size("group")
     devices = data_count * group_count
     me_group = lax.axis_index("group")
+    me = lax.axis_index("dp")
     unit = model_width // devices
     qkv_rows = 3 * unit
     ff_rows = FF // devices
     out_rows = unit
     heads = HEADS // group_count
     width = heads * HEAD
-    aligned = heads_aligned(unit)
+    fast = heads_aligned(unit) and two_by_two()
     everywhere = ("dp", "group")
 
     def dot(left, right):
@@ -625,114 +854,110 @@
     grad_y = cotangent[0]
     parts = max(1, width // 128)
     lanes = width // parts
+    w_in, w_back = weight_in[0], weight_back[0]
+    m_in, m_back = MOMENTUM * moment_in[0], MOMENTUM * moment_back[0]
+    position = positions(segment_ids[0])
+    start = jnp.arange(position.shape[0], dtype=jnp.int32) - position
+    tables = (start[::CHUNK] // CHUNK, start[:, None]) + rotary_lanes(position, lanes // HEAD)
+    grad_y_float = grad_y.astype(F32)
+
+    def to_parts(rows):
+        split = rows.reshape((3, parts, lanes) + rows.shape[1:])
+        return jnp.swapaxes(split, 0, 1).reshape(rows.shape)
+
+    def from_parts(rows):
+        split = rows.reshape((parts, 3, lanes) + rows.shape[1:])
+        return jnp.swapaxes(split, 0, 1).reshape(rows.shape)
+
     normed_all = lax.all_gather(normed_low, "group", axis=0, tiled=True)
-    w_in, w_back = weight_in[0], weight_back[0]
-    w_up = gather_dp(w_in[qkv_rows:])
-    if aligned:
+    if fast:
+        w_up = gather_far(gather_near(w_in[qkv_rows:]))
         near_qkv = gather_near(spread_qkv(w_in[:qkv_rows], unit))
-        grad_all = lax.all_gather(after(grad_y, normed_all, w_up, *came(near_qkv)), "group", axis=0, tiled=True)
-        w_qkv = by_distance(gather_far(near_qkv))
-        all_back = gather_dp(after(w_back, *came(near_qkv)))
+        grad_all = lax.all_gather(after(grad_y, normed_all, w_up, *near_qkv[1:], *tables), "group", axis=0, tiled=True)
+    else:
+        grad_all = lax.all_gather(grad_y, "group", axis=0, tiled=True)
+        w_up = lax.all_gather(w_in[qkv_rows:], "dp", axis=0, tiled=True)
+    w_up = w_up.reshape(data_count * ff_rows, model_width)
+
+    bias_up = lax.dynamic_index_in_dim(
+        bias_in[3 * model_width :].reshape(data_count, group_count, ff_rows), me_group, 1, keepdims=False
+    )
+    bias_up = (by_distance(bias_up) if fast else bias_up).reshape(data_count * ff_rows)
+    bias_qkv = bias_in[: 3 * model_width].reshape(3 * heads, group_count, HEAD)
+    bias_qkv = to_parts(lax.dynamic_index_in_dim(bias_qkv, me_group, 1, keepdims=False).reshape(3 * width))
+    activated, slope = up_forward(normed_all, w_up, bias_up)
+    if fast:
+        near_back = gather_near(after(w_back, *near_qkv[1:]))
+        own, from_x, from_y = near_qkv
+        w_qkv = by_distance(gather_far((own, after(from_x, activated), from_y)))
+        own, from_x, from_y = near_back
+        all_back = gather_far((own, after(from_x, activated), from_y))
         w_out = by_distance(all_back[:, :out_rows]).reshape(width, model_width)
         w_down = all_back[:, out_rows:].reshape(data_count * ff_rows, model_width)
     else:
-        grad_all = lax.all_gather(grad_y, "group", axis=0, tiled=True)
         all_qkv = lax.all_gather(w_in[:qkv_rows], everywhere, axis=0, tiled=True)
         w_qkv = head_rows(all_qkv.reshape(3, model_width, model_width), heads)
         w_out = head_rows(lax.all_gather(w_back[:out_rows], everywhere, axis=0, tiled=True), heads)
-        w_down = gather_dp(w_back[out_rows:]).reshape(data_count * ff_rows, model_width)
-    w_up = w_up.reshape(data_count * ff_rows, model_width)
-
-    def to_parts(rows):
-        split = rows.reshape((3, parts, lanes) + rows.shape[1:])
-        return jnp.swapaxes(split, 0, 1).reshape(rows.shape)
-
-    def from_parts(rows):
-        split = rows.reshape((parts, 3, lanes) + rows.shape[1:])
-        return jnp.swapaxes(split, 0, 1).reshape(rows.shape)
-
+        w_down = lax.all_gather(w_back[out_rows:], "dp", axis=0, tiled=True)
     w_qkv = to_parts(w_qkv.reshape(3 * width, model_width))
-
-    bias_up = lax.dynamic_index_in_dim(
-        bias_in[3 * model_width :].reshape(data_count, group_count, ff_rows), me_group, 1, keepdims=False
-    )
-    bias_up = by_distance(bias_up).reshape(data_count * ff_rows)
-    bias_qkv = bias_in[: 3 * model_width].reshape(3 * heads, group_count, HEAD)
-    bias_qkv = to_parts(lax.dynamic_index_in_dim(bias_qkv, me_group, 1, keepdims=False).reshape(3 * width))
-    pre_up = dot_last(normed_all, w_up) + bias_up
-    pre_qkv = dot_last(normed_all, w_qkv) + bias_qkv
-    activated, gelu_pull = jax.vjp(gelu_tanh, pre_up)
-    activated = activated.astype(BF16)
-    grad_all = after(grad_all, activated, pre_qkv)
-
-    term_down = dot_first(activated, grad_all).astype(BF16)
-    sum_down = scatter_start(term_down.reshape(data_count, ff_rows, model_width))
-    grad_pre_up = gelu_pull(dot_last(grad_all, after(w_down, term_down)))[0].astype(BF16)
-    term_up = dot_first(grad_pre_up, normed_all).astype(BF16)
-    sum_up = scatter_start(term_up.reshape(data_count, ff_rows, model_width))
-    grad_attended = dot_last(grad_all, after(w_out, term_up)).astype(BF16)
-    sum_down = scatter_next(sum_down, grad_attended)
-    grad_w_down = scatter_end(sum_down)
-
-    position = positions(segment_ids[0])
-    attended, grad_pre_qkv = [], []
-    ready = flying(sum_down)
+    pre_qkv = project(normed_all, w_qkv, bias_qkv, F32, "project_qkv")
+    grad_all = after(grad_all, activated, slope, pre_qkv, w_down, w_out)
+
+    term_down = weight_grad(activated, grad_all, "grad_down", fast)
+    if fast:
+        m_qkv = spread_qkv(after(m_in[:qkv_rows], term_down[0]), unit)
+        sum_down = scatter_start(term_down)
+        slope = after(slope, *term_down)
+    grad_pre_up = up_backward(grad_all, slope, w_down)
+    term_up = weight_grad(grad_pre_up, normed_all, "grad_up", fast)
+    late_w_out = w_out
+    if fast:
+        sum_up = scatter_start(term_up)
+        sum_down, flying = scatter_next(sum_down, *term_up)
+        late_w_out = after(w_out, *flying)
+    grad_attended = project(grad_all, late_w_out, jnp.zeros((width,), F32), BF16, "project_grad")
+    ready = ()
+
+    attended, grad_pre_qkv, term_qkv, term_out, sum_att = [], [], [], [], []
     for part in range(parts):
-        one, one_grad = attention(pre_qkv, after(grad_attended, *ready), position, part, lanes)
+        one, one_grad = attention(pre_qkv, after(grad_attended, *ready), tables, part, lanes)
         attended.append(one)
         grad_pre_qkv.append(one_grad)
+        if not fast:
+            ready = (one,)
+            term_qkv.append(dot_first(one_grad, normed_all).astype(BF16))
+            term_out.append(dot_first(one, grad_all).astype(BF16))
+            continue
         if part == 0:
-            sum_up = scatter_next(sum_up, one)
-            ready = flying(sum_up)
-        else:
-            ready = (one,)
-    grad_w_up = scatter_end(sum_up, attended[-1])
-    attended = jnp.concatenate(attended, axis=1)
-    grad_pre_qkv = jnp.concatenate(grad_pre_qkv, axis=1)
-
-    def slot(rows):
-        return jnp.pad(rows.astype(BF16), ((0, ff_rows - rows.shape[0]), (0, 0)))
-
-    moment_up = MOMENTUM * moment_in[0, qkv_rows:] + grad_w_up
-    moment_down = MOMENTUM * moment_back[0, out_rows:] + grad_w_down
-    early = jnp.stack([slot(moment_up), slot(moment_down)])
-    if two_by_two():
-        early = owners_start(early, [1, 3])
-        term_grad = after(grad_pre_qkv, *early)
+            sum_up, flying = scatter_next(sum_up, one)
+            own_down, full_down = scatter_momentum(sum_down, m_back[out_rows:], one)
+            one_grad = after(one_grad, full_down, *flying)
+        one_qkv, one_out, *split = weight_grads_plus(
+            one_grad,
+            normed_all,
+            one,
+            grad_all,
+            m_qkv,
+            m_back[:out_rows],
+            part,
+            heads,
+        )
+        sum_att.append(reduce_start(*split))
+        if part == 0:
+            own_up, full_up = scatter_momentum(sum_up, m_in[qkv_rows:], split[0])
+            early, ready = owners_start([full_up, full_down], [0, 3])
+        term_qkv.append(one_qkv)
+        term_out.append(one_out)
+
+    if fast:
+        first_half, flying = reduce_next(sum_att[0], split[0])
+        early = owners_end(early, [0, 3], *flying)
+        second_half, flying = reduce_next(sum_att[1], *flying)
+        owned, packed = first_gram((data_count * ff_rows, model_width), early, (*first_half, *second_half))
     else:
-        term_grad = grad_pre_qkv
-
-    term_qkv = from_parts(dot_first(term_grad, normed_all).astype(BF16))
-    term_out = dot_first(attended, grad_all).astype(BF16)
-    if aligned:
-        term_att = by_distance(
-            jnp.concatenate(
-                [
-                    term_qkv.reshape(data_count, qkv_rows, model_width),
-                    term_out.reshape(data_count, out_rows, model_width),
-                ],
-                axis=1,
-            )
-        )
-        sum_att = scatter_start(term_att)
-    else:
-        term_att = term_qkv
-
-    branch_part = (dot(after(attended, term_att), w_out) + dot(activated, w_down)).astype(BF16)
-    branch = lax.psum_scatter(branch_part, "group", scatter_dimension=0, tiled=True)
-    block_out = (x_float + branch.astype(F32) + bias_out).astype(BF16)
-    if two_by_two():
-        early = owners_end(early, [1, 3], branch_part)
-    if aligned:
-        sum_att = scatter_next(sum_att, branch_part)
-        normed_part = dot(after(grad_pre_qkv, *flying(sum_att)), w_qkv)
-        own_att = scatter_end(sum_att, normed_part)
-        grad_w_qkv = own_att[:qkv_rows].astype(BF16)
-        normed_part = (normed_part + dot(after(grad_pre_up, grad_w_qkv), w_up)).astype(BF16)
-        grad_w_qkv = return_qkv(grad_w_qkv, unit).astype(F32)
-        grad_w_out = own_att[qkv_rows:]
-    else:
-        normed_part = (dot(after(grad_pre_qkv, branch_part), w_qkv) + dot(grad_pre_up, w_up)).astype(BF16)
+        packed = None
+        term_qkv = from_parts(jnp.concatenate(term_qkv))
+        term_out = jnp.concatenate(term_out)
         grad_w_qkv = lax.psum_scatter(
             spread_heads(term_qkv.reshape(3, width, model_width), heads).reshape(3 * model_width, model_width),
             everywhere,
@@ -742,67 +967,115 @@
         grad_w_out = lax.psum_scatter(
             spread_heads(term_out, heads), everywhere, scatter_dimension=0, tiled=True
         ).astype(F32)
-    grad_y_float = grad_y.astype(F32)
-
-    grad_in = jnp.concatenate([grad_w_qkv, grad_w_up], axis=0)[None]
-    grad_back = jnp.concatenate([grad_w_out, grad_w_down], axis=0)[None]
-    moment_in_new = MOMENTUM * moment_in + grad_in
-    moment_back_new = MOMENTUM * moment_back + grad_back
-    moment_qkv = MOMENTUM * moment_in[0, :qkv_rows] + grad_w_qkv
-    moment_out = MOMENTUM * moment_back[0, :out_rows] + grad_w_out
-    if two_by_two():
-        late = jnp.stack([moment_qkv.astype(BF16), jnp.pad(moment_out.astype(BF16), ((0, qkv_rows - out_rows), (0, 0)))])
-        late = owners_end(owners_start(late, [0, 2]), [0, 2])
-        late = jnp.pad(late, ((0, 0), (0, ff_rows - qkv_rows), (0, 0)))
-        owned = jnp.where(lax.axis_index("dp") % 2 == 1, early, late)
-    else:
-        slots = [slot(moment_qkv), early[0], slot(moment_out), early[1]]
-        slots = slots + [jnp.zeros_like(early[0])] * (data_count - 4)
-        owned = exchange_dp(jnp.stack(slots))
-
-    def sum_normed(gathered):
-        return lax.psum_scatter(after(normed_part, gathered), "group", scatter_dimension=0, tiled=True)
-
-    def placed(sums, lead, size):
-        empty = jnp.zeros((lead, group_count, size), F32)
-        return lax.dynamic_update_slice_in_dim(empty, sums.reshape(lead, 1, size), me_group, 1).reshape(-1)
-
-    def sum_vectors(grad_normed, gathered):
-        grad_normed = grad_normed.astype(F32)
-        sums_up = jnp.sum(grad_pre_up.astype(F32), axis=0).reshape(data_count, ff_rows)
+        own_up = lax.psum_scatter(term_up, "dp", scatter_dimension=0, tiled=True).astype(F32)
+        own_down = lax.psum_scatter(term_down, "dp", scatter_dimension=0, tiled=True).astype(F32)
+        slots = [m_in[qkv_rows:] + own_up, m_in[:qkv_rows] + grad_w_qkv, m_back[:out_rows] + grad_w_out]
+        slots = slots + [m_back[out_rows:] + own_down] + [jnp.zeros((0, model_width))] * (data_count - 4)
+        slots = [jnp.pad(rows.astype(BF16), ((0, ff_rows - rows.shape[0]), (0, 0))) for rows in slots]
+        owned = lax.all_to_all(jnp.stack(slots), "dp", split_axis=0, concat_axis=0, tiled=True)
+        owned = owned.reshape(data_count * ff_rows, model_width)
+
+    def after_gram(packed):
+        late_qkv, late_up = jnp.concatenate(grad_pre_qkv, axis=1), after(grad_pre_up, packed)
+        late_qkv = after(late_qkv, packed)
+        late_attended = after(jnp.concatenate(attended, axis=1), packed)
+        normed_part = dot(late_qkv, w_qkv) + dot(late_up, w_up)
+        branch_part = dot(late_attended, w_out) + dot(after(activated, packed), w_down)
+        split = ()
+        if fast:
+            terms = [from_parts(jnp.concatenate(term_qkv)), jnp.concatenate(term_out)]
+            terms = [after(one, packed).reshape(data_count, -1, model_width) for one in terms]
+            terms = by_distance(jnp.concatenate(terms, axis=1)).reshape(2, 2, 2, unit * 2, model_width)
+            split = terms[:, 1, 0], terms[:, 0, 0], terms[1, :, 1], terms[0, :, 1]
+            split = [one.reshape(4 * unit, model_width) for one in split]
+        return normed_part.astype(BF16), branch_part.astype(BF16), late_qkv, late_up, split
+
+    kept = []
+
+    def beside_first(gathered, meanwhile):
+        kept.extend(meanwhile[1:])
+        if fast:
+            split = [after(one, gathered) for one in kept[3]]
+            kept.append(scatter_start(split))
+        return (lax.psum_scatter(after(meanwhile[0], gathered), "group", scatter_dimension=0, tiled=True),)
+
+    def after_first_steps(first, packed):
+        if not fast:
+            return first
+        state, flying = scatter_next(kept[4], packed)
+        kept.append(state)
+        return first + flying
+
+    def after_first(packed, first):
+        grad_normed = first[0].astype(F32)
+        grad_x_hat = grad_normed * norm_gain
+        grad_hidden = grad_y_float + inverse_std * (
+            grad_x_hat
+            - jnp.mean(grad_x_hat, axis=-1, keepdims=True)
+            - x_hat * jnp.mean(grad_x_hat * x_hat, axis=-1, keepdims=True)
+        )
+        if fast:
+            own = scatter_end(kept[5])
+            own_qkv = return_qkv(own[:qkv_rows].astype(BF16), unit).astype(F32)
+            own_out = own[qkv_rows:]
+        else:
+            own_qkv, own_out = grad_w_qkv, grad_w_out
+        grad_in = jnp.concatenate([own_qkv, own_up])
+        grad_back = jnp.concatenate([own_out, own_down])
+        sums_up = jnp.sum(kept[2].astype(F32), axis=0).reshape(data_count, ff_rows)
+        sums_qkv = jnp.sum(kept[1].astype(F32), axis=0)
         vector_local = jnp.concatenate(
             [
                 jnp.sum(grad_normed * x_hat, axis=0),
                 jnp.sum(grad_normed, axis=0),
-                placed(from_parts(jnp.sum(grad_pre_qkv.astype(F32), axis=0)), 3 * heads, HEAD),
-                placed(by_distance(sums_up), data_count, ff_rows),
+                placed(from_parts(sums_qkv), 3 * heads, HEAD),
+                placed(by_distance(sums_up) if fast else sums_up, data_count, ff_rows),
                 jnp.sum(grad_y_float, axis=0),
             ]
         )
-        return grad_normed, lax.psum(after(vector_local, gathered), everywhere)
-
-    result, (grad_normed, vector_grad) = orthogonalize(
-        owned.reshape(data_count * ff_rows, model_width), normed_part, branch, sum_normed, sum_vectors
+        vector_grad = butterfly(vector_local)
+        return grad_hidden, grad_in, grad_back, m_in + grad_in, m_back + grad_back, vector_grad
+
+    def beside_last(gathered):
+        return (lax.psum_scatter(after(kept[0], gathered), "group", scatter_dimension=0, tiled=True),)
+
+    def placed(sums, lead, size):
+        empty = jnp.zeros((lead, group_count, size), F32)
+        return lax.dynamic_update_slice_in_dim(empty, sums.reshape(lead, 1, size), me_group, 1).reshape(-1)
+
+    if fast:
+        distance, run = jnp.divmod(jnp.arange(4 * ff_rows // unit), ff_rows // unit)
+        holder = me ^ distance
+        kind, head = jnp.divmod(3 * holder + jnp.minimum(run, 2), heads)
+        per_part = heads // parts
+        of_qkv = (head // per_part) * 3 * lanes + kind * lanes + (head % per_part) * HEAD
+        source_rows = jnp.where(me == 1, of_qkv, jnp.where(me == 2, holder * unit, distance * ff_rows + run * unit))
+        pieces = [ff_rows] * 3 + [ff_rows // 2] * 2
+    else:
+        source_rows = jnp.arange(0, data_count * ff_rows, ff_rows)
+        pieces = [data_count * ff_rows]
+    results, _, meanwhile, (branch,) = orthogonalize(
+        owned, packed, source_rows.astype(jnp.int32), pieces, after_gram, beside_first, after_first_steps, after_first, beside_last
     )
-    result = after(result, vector_grad)
-    returned = by_distance(exchange_dp(result.reshape(data_count, ff_rows, model_width)))
-
-    grad_x_hat = grad_normed * norm_gain
-    grad_hidden = grad_y_float + inverse_std * (
-        grad_x_hat
-        - jnp.mean(grad_x_hat, axis=-1, keepdims=True)
-        - x_hat * jnp.mean(grad_x_hat * x_hat, axis=-1, keepdims=True)
-    )
-
-    def matrix_rows(matrix_index, row_count, scale):
-        return -scale * returned[matrix_index, :row_count].astype(F32)
+    grad_hidden, grad_in, grad_back, moment_in_new, moment_back_new, vector_grad = meanwhile
+    block_out = (x_float + branch.astype(F32) + bias_out).astype(BF16)
+    if fast:
+        returned = by_distance(exchange_dp(*results))
+        o_qkv = return_qkv(returned[1, :qkv_rows], unit)
+    else:
+        result = results[0].reshape(data_count, ff_rows, model_width)
+        returned = lax.all_to_all(result, "dp", split_axis=0, concat_axis=0, tiled=True)
+        o_qkv = returned[1, :qkv_rows]
+
+    def step_of(rows, scale):
+        return -scale * rows.astype(F32)
 
     scale_ff = math.sqrt(1.0 * FF)
     step_in = jnp.concatenate(
-        [matrix_rows(0, qkv_rows, math.sqrt(3.0 * model_width)), matrix_rows(1, ff_rows, scale_ff)], axis=0
+        [step_of(o_qkv, math.sqrt(3.0 * model_width)), step_of(returned[0], scale_ff)], axis=0
     )[None]
     step_back = jnp.concatenate(
-        [matrix_rows(2, out_rows, math.sqrt(1.0 * model_width)), matrix_rows(3, ff_rows, scale_ff)], axis=0
+        [step_of(returned[2, :out_rows], math.sqrt(1.0 * model_width)), step_of(returned[3], scale_ff)], axis=0
     )[None]
     bias_out_grad = vector_grad[vector_grad.shape[0] - model_width :]
     vector_moment_new = MOMENTUM * vector_moment + vector_grad
@@ -810,10 +1083,10 @@
     return (
         block_out[None],
         grad_hidden[None],
-        grad_in,
-        grad_back,
-        moment_in_new,
-        moment_back_new,
+        grad_in[None],
+        grad_back[None],
+        moment_in_new[None],
+        moment_back_new[None],
         step_in,
         step_back,
         vector_grad,

time: 1090 us -> 1030 us (0.945)
  Pallas kernels: 300 us -> 422 us
  matrix products: 144 us -> 48.6 us
  waiting for transfers between devices: 399 us -> 314 us
    pallas_call x2 -> x18, Pallas kernels: 147 us -> 271 us  [the longest x1 119 us: orthogonalize(): pl.pallas_call(functools.partial(second_body, 3), out_shape=[jax.ShapeDty...]
    reduce_scatter x4, waiting for transfers between devices: 107 us -> 0.01 us  [the longest x2 0.01 us: gram_sum(): part = lax.psum_scatter(packed, 'group', scatter_dimension=0, tiled=True)]
    dot_general x8 -> x0, matrix products: 91.3 us -> none  [the longest x4 50.2 us: dot_last(): lax.dot_general(left, right, (((1,), (1,)), ((), ())), preferred_element_...]
    ppermute x12 -> x44, waiting for transfers between devices: 23.2 us -> 95.3 us  [hop(): return lax.ppermute(values, 'dp', [(t ^ bit, t) for t in targets])]
    ppermute x30 -> x5, waiting for transfers between devices: 94.8 us -> 26.6 us  [butterfly(): lax.ppermute(values, axis, [(i, i ^ bit) for i in range(size)])]
    all_gather x3, waiting for transfers between devices: 98.6 us -> 131 us  [the longest x2 114 us: gram_sum(): lax.all_gather(after(part, *jax.tree.leaves(meanwhile)), 'group', axis=0,...]
    ppermute x12 -> x44, starting transfers between devices: 26.6 us -> 53.3 us  [hop(): return lax.ppermute(values, 'dp', [(t ^ bit, t) for t in targets])]
    ppermute x30 -> x5, starting transfers between devices: 25 us -> 7.89 us  [butterfly(): lax.ppermute(values, axis, [(i, i ^ bit) for i in range(size)])]
  transfers between devices with their start and end apart: 57 -> 69, of which waited for: 23 -> 27; matrix products, arithmetic and copies ran while one was open for 20% -> 16% of each run, Pallas kernels for 28% -> 39%
where the time goes in v2:
time: 1030 us; the launch traced here: 1020 us
  Pallas kernels  422 us (41%)
  waiting for transfers between devices  314 us (30%)
  starting transfers between devices  91.3 us (9%)
  other arithmetic  71 us (7%)
  local copies, waits for them, and re-layouts  58.1 us (6%)
  matrix products  48.6 us (5%)
  between operations  15.8 us (2%)
    pallas_call x1, Pallas kernels, orthogonalize(): pl.pallas_call(functools.partial(second_body, 3), out_shape=[jax.ShapeDty...  119 us
    all_gather x2, waiting for transfers between devices, gram_sum(): lax.all_gather(after(part, *jax.tree.leaves(meanwhile)), 'group', axis=0,...  114 us
    pallas_call x1, Pallas kernels, orthogonalize(): pl.pallas_call(functools.partial(first_body, 2), out_shape=(x_shape, pack...  98.2 us
    ppermute x44, waiting for transfers between devices, hop(): return lax.ppermute(values, 'dp', [(t ^ bit, t) for t in targets])  95.3 us
    pallas_call x4, Pallas kernels, by_columns(): pl.pallas_call(body, grid=(steps,), in_specs=([] if scalar is None else [...  54.3 us
    ppermute x44, starting transfers between devices, hop(): return lax.ppermute(values, 'dp', [(t ^ bit, t) for t in targets])  53.3 us
    pallas_call x2, Pallas kernels, attention(): pl.pallas_call(attention_body, grid=(1,), out_shape=(jax.ShapeDtypeStruct...  52.2 us
    pallas_call x4, Pallas kernels, by_rows(): pl.pallas_call(body, grid=(steps,), in_specs=[pl.BlockSpec((rows, one.sha...  51.3 us
  transfers between devices with their start and end apart: 69, of which 27 were waited for; matrix products, arithmetic and copies ran while one was open for 16% of the time, Pallas kernels for 39%

profile of v2, /device:TPU:1, one launch (start us, length us, event | category | flops | bytes accessed | tf_op | source)
XLA Modules:
  0.0 1020.3 jit_solution(609515880854182307)
XLA Ops:
  19.6 3.2 collective-permute-start
  36.1 6.3 collective-permute-done.1
  42.4 16.0 %collective-permute-done.2 = bf16[64,2048]{1,0:T(8,128)(2,1)} collective-permute-done((bf16[64,2048]{1,0:T(8,128)(2,1)}, bf16[64,2048]{1,0:T(8,128)(2,1)}, u32[]{:S(2)}, u32[]{:S(2)}) %collective-permute-start.2) | collective-permute-done | bytes 262176 | tf_op jit(solution)/shard_map/ppermute | solution.py:764
  65.4 2.7 collective-permute-done.6
  69.5 3.4 pad_maximum_fusion.1.refs_2_
  72.9 3.5 collective-permute-done.3.refs_0_.refs_3_.refs_1_
  77.9 29.6 %all-gather.5.cloned.1.call-done.x_ref.refs_1_.r_ref = bf16[2048,2048]{1,0:T(8,128)(2,1)} async-done(((bf16[256,2048]{1,0:T(8,128)(2,1)}), bf16[2048,2048]{1,0:T(8,128)(2,1)}) %all-gather.5.cloned.1.call-update) | async-done | bytes 8388624 | tf_op jit(solution)/shard_map/all_gather | solution.py:872
  113.1 4.5 broadcast_multiply_fusion
  120.3 18.7 %up_forward.1 = (bf16[2048,1024]{1,0:T(8,128)(2,1)}, bf16[2048,1024]{1,0:T(8,128)(2,1)}) custom-call(bf16[2048,2048]{1,0:T(8,128)(2,1)} %all-gather.5.cloned.1.call-done.x_ref.refs_1_.r_ref, bf16[1024,2048]{1,0:T(8,128)(2,1)} %bitcast.204, f32[1,1024]{1,0:T(1,128)} %bitcast.255), custom_call_target="tpu_custom_call" | custom-call | tf_op jit(solution)/shard_map/up_forward/pallas_call | solution.py:77
  142.1 2.7 slice_bitcast_fusion.2.refs_0_
  156.2 11.6 %project_qkv.1.refs_3_.pre_ref = f32[2048,768]{1,0:T(8,128)} custom-call(bf16[2048,2048]{1,0:T(8,128)(2,1)} %all-gather.5.cloned.1.call-done.x_ref.refs_1_.r_ref, bf16[768,2048]{1,0:T(8,128)(2,1)} %bitcast.223, f32[1,768]{1,0:T(1,128)} %broadcast_in_dim_reshape.7.b_ref), custom_call_target="tpu_custom_call" | custom-call | tf_op jit(solution)/shard_map/project_qkv/pallas_call | solution.py:77
  174.1 17.2 %all-gather.7.cloned.1.call-done.refs_0_ = bf16[2048,2048]{1,0:T(8,128)(2,1)} async-done(((bf16[256,2048]{1,0:T(8,128)(2,1)}), bf16[2048,2048]{1,0:T(8,128)(2,1)}) %all-gather.7.cloned.1.call-update) | async-done | bytes 8388624 | tf_op jit(solution)/shard_map/all_gather | solution.py:876
  191.3 14.3 %grad_down.1 = (bf16[256,2048]{1,0:T(8,128)(2,1)}, bf16[256,2048]{1,0:T(8,128)(2,1)}, bf16[256,2048]{1,0:T(8,128)(2,1)}, bf16[256,2048]{1,0:T(8,128)(2,1)}) custom-call(bf16[2048,1024]{1,0:T(8,128)(2,1)} %get-tuple-element.82.refs_1_.l_ref.refs_0_, bf16[2048,2048]{1,0:T(8,128)(2,1)} %after.31.r_ref.g_ref.x_ref.q_ref), custom_call_target="tpu_custom_call" | custom-call | tf_op jit(solution)/shard_map/grad_down/pallas_call | solution.py:95
  206.8 2.7 fusion.40
  211.4 2.7 collective-permute-start.25
  214.1 4.0 collective-permute-start.24
  220.9 14.3 %up_backward.1.l_ref.refs_0_ = bf16[2048,1024]{1,0:T(8,128)(2,1)} custom-call(bf16[2048,2048]{1,0:T(8,128)(2,1)} %after.31.r_ref.g_ref.x_ref.q_ref, bf16[2048,1024]{1,0:T(8,128)(2,1)} %after.32.s_ref, bf16[1024,2048]{1,0:T(8,128)(2,1)} %bitcast.202), custom_call_target="tpu_custom_call" | custom-call | tf_op jit(solution)/shard_map/up_backward/pallas_call | solution.py:77
  235.2 14.4 %grad_up.1 = (bf16[256,2048]{1,0:T(8,128)(2,1)}, bf16[256,2048]{1,0:T(8,128)(2,1)}, bf16[256,2048]{1,0:T(8,128)(2,1)}, bf16[256,2048]{1,0:T(8,128)(2,1)}) custom-call(bf16[2048,1024]{1,0:T(8,128)(2,1)} %up_backward.1.l_ref.refs_0_, bf16[2048,2048]{1,0:T(8,128)(2,1)} %all-gather.5.cloned.1.call-done.x_ref.refs_1_.r_ref), custom_call_target="tpu_custom_call" | custom-call | tf_op jit(solution)/shard_map/grad_up/pallas_call | solution.py:95
  253.6 3.9 scatter_next.3
  261.9 6.7 project_grad.1.refs_0_
  270.8 26.3 %attention.2 = (bf16[2048,128]{1,0:T(8,128)(2,1)}, bf16[2048,384]{1,0:T(8,128)(2,1)}) custom-call(s32[8]{0:T(128)} %and_select_fusion.6.refs_5_.first_ref, f32[2048,768]{1,0:T(8,128)} %project_qkv.1.refs_3_.pre_ref, bf16[2048,256]{1,0:T(8,128)(2,1)} %after.34.grad_ref, s32[2048,1]{1,0:T(8,128)} %subtract_subtract_fusion.refs_6_.start_ref, ...), custom_call_target="tpu_custom_call" | custom-call | tf_op jit(solution)/shard_map/attention/pallas_call | solution.py:327
  297.1 4.1 scatter_next.4
  303.3 4.5 momentum.2
  307.9 12.9 %weight_grads_plus.2 = (bf16[384,2048]{1,0:T(8,128)(2,1)}, bf16[128,2048]{1,0:T(8,128)(2,1)}, bf16[192,2048]{1,0:T(8,128)(2,1)}, bf16[192,2048]{1,0:T(8,128)(2,1...) custom-call(s32[1]{0:T(128)} %bitcast.42.me_ref, bf16[2048,384]{1,0:T(8,128)(2,1)} %after.35.l_ref, ...), custom_call_target="tpu_custom_call" | custom-call | tf_op jit(solution)/shard_map/weight_grads_plus/pallas_call | solution.py:95
  325.2 4.5 momentum.3
  329.8 3.7 to_owners.1
  333.4 2.8 collective-permute-start.32
  336.2 26.0 %attention.3 = (bf16[2048,128]{1,0:T(8,128)(2,1)}, bf16[2048,384]{1,0:T(8,128)(2,1)}) custom-call(s32[8]{0:T(128)} %and_select_fusion.6.refs_5_.first_ref, f32[2048,768]{1,0:T(8,128)} %project_qkv.1.refs_3_.pre_ref, bf16[2048,256]{1,0:T(8,128)(2,1)} %after.37.grad_ref, s32[2048,1]{1,0:T(8,128)} %subtract_subtract_fusion.refs_6_.start_ref, ...), custom_call_target="tpu_custom_call" | custom-call | tf_op jit(solution)/shard_map/attention/pallas_call | solution.py:327
  362.2 12.7 %weight_grads_plus.3 = (bf16[384,2048]{1,0:T(8,128)(2,1)}, bf16[128,2048]{1,0:T(8,128)(2,1)}, bf16[192,2048]{1,0:T(8,128)(2,1)}, bf16[192,2048]{1,0:T(8,128)(2,1...) custom-call(s32[1]{0:T(128)} %bitcast.42.me_ref, bf16[2048,384]{1,0:T(8,128)(2,1)} %get-tuple-element.114.l_ref, ...), custom_call_target="tpu_custom_call" | custom-call | tf_op jit(solution)/shard_map/weight_grads_plus/pallas_call | solution.py:95
  376.2 3.0 collective-permute-start.36
  380.6 5.2 collective-permute-start.28
  385.7 6.3 collective-permute-done.37.refs_3_
  393.4 4.2 reduce_next.2
  397.6 18.8 %collective-permute-done.36.refs_1_ = bf16[192,2048]{1,0:T(8,128)(2,1)} collective-permute-done((bf16[192,2048]{1,0:T(8,128)(2,1)}, bf16[192,2048]{1,0:T(8,128)(2,1)}, u32[]{:S(2)}, u32[]{:S(2)}) %collective-permute-start.36) | collective-permute-done | bytes 786464 | tf_op jit(solution)/shard_map/ppermute | solution.py:637
  418.7 4.2 reduce_next.3
  425.1 2.6 collective-permute-done.33.refs_4_
  436.6 3.6 pad_maximum_fusion.8
  440.2 6.4 collective-permute-done.31.refs_3_
  446.7 5.8 collective-permute-done.39.refs_12_
  452.5 13.2 %gram.1 = (bf16[1024,2048]{1,0:T(8,128)(2,1)}, bf16[9216,256]{1,0:T(8,128)(2,1)}) custom-call(s32[1]{0:T(128)} %bitcast.42.me_ref, bf16[256,2048]{1,0:T(8,128)(2,1)} %get-tuple-element.110.refs_0_, bf16[256,2048]{1,0:T(8,128)(2,1)} %collective-permute-done.26.refs_1_, bf16[256,2048]{1,0:T(8,128)(2,1)} %collective-permute-done.27.refs_2_, ...), custom_call_target="tpu_custom_call" | custom-call | tf_op jit(solution)/shard_map/gram/pallas_call | solution.py:566
  479.3 11.7 %fusion.41 = f32[2048,2048]{1,0:T(8,128)} fusion(bf16[2048,1024]{1,0:T(8,128)(2,1)S(1)} %copy-done.1, bf16[1024,2048]{1,0:T(8,128)(2,1)S(1)} %bitcast.203), kind=kOutput, calls=%fused_computation.185 | convolution fusion | flops 8589934592 | bytes 25165824 | tf_op jit(solution)/shard_map/dot_general | solution.py:841
  491.0 11.9 %add_convert_fusion.1.refs_2_.refs_0_ = bf16[2048,2048]{1,0:T(8,128)(2,1)} fusion(f32[2048,2048]{1,0:T(8,128)} %fusion.41, bf16[2048,256]{1,0:T(8,128)(2,1)S(1)} %copy-done.24, bf16[256,2048]{1,0:T(8,128)(2,1)S(1)} %bitcast.219), kind=kOutput, calls=%fused_computation.1 | convolution fusion | flops 2155872256 | bytes 27262976 | tf_op jit(solution)/shard_map/dot_general | solution.py:841
  502.8 11.7 %fusion.42 = f32[2048,2048]{1,0:T(8,128)} fusion(bf16[2048,1024]{1,0:T(8,128)(2,1)S(1)} %copy-done, bf16[1024,2048]{1,0:T(8,128)(2,1)S(1)} %bitcast.205), kind=kOutput, calls=%fused_computation.186 | convolution fusion | flops 8589934592 | bytes 25165824 | tf_op jit(solution)/shard_map/dot_general | solution.py:841
  514.5 13.3 %add_convert_fusion.refs_1_.refs_0_ = bf16[2048,2048]{1,0:T(8,128)(2,1)} fusion(f32[2048,2048]{1,0:T(8,128)} %fusion.42, bf16[2048,768]{1,0:T(8,128)(2,1)S(1)} %copy-done.2, bf16[768,2048]{1,0:T(8,128)(2,1)} %bitcast.224), kind=kOutput, calls=%fused_computation | convolution fusion | flops 6450839552 | bytes 31457280 | tf_op jit(solution)/shard_map/dot_general | solution.py:841
  527.9 59.5 %all-gather.9.cloned.1.call-done.packed_ref.refs_1_ = bf16[9216,256]{1,0:T(8,128)(2,1)} async-done(((bf16[1152,256]{1,0:T(8,128)(2,1)}), bf16[9216,256]{1,0:T(8,128)(2,1)}) %all-gather.9.cloned.1.call-update) | async-done | bytes 4718608 | tf_op jit(solution)/shard_map/all_gather | solution.py:588
  590.4 98.2 %first_steps.1 = (bf16[1024,2048]{1,0:T(8,128)(2,1)}, bf16[9216,256]{1,0:T(8,128)(2,1)}) custom-call(bf16[9216,256]{1,0:T(8,128)(2,1)} %all-gather.9.cloned.1.call-done.packed_ref.refs_1_, bf16[1024,2048]{1,0:T(8,128)(2,1)} %get-tuple-element.132.x_ref), custom_call_target="tpu_custom_call" | custom-call | tf_op jit(solution)/shard_map/first_steps/pallas_call | solution.py:604
  690.0 3.9 scatter_next.5
  695.3 2.9 convert_reduce_fusion
  700.3 7.3 collective-permute-done.42
  709.2 2.8 collective-permute-done.43
  719.4 3.0 collective-permute-start.46
  724.2 20.3 %collective-permute-done.48 = f32[20480]{0:T(1024)S(1)} collective-permute-done((f32[20480]{0:T(1024)S(1)}, f32[20480]{0:T(1024)S(1)}, u32[]{:S(2)}, u32[]{:S(2)}) %collective-permute-start.48) | collective-permute-done | bytes 81952 | tf_op jit(solution)/shard_map/ppermute | solution.py:750
  744.6 4.7 collective-permute-start.49
  749.3 3.9 fusion.34
  753.1 3.6 collective-permute-done.49
  757.8 2.7 collective-permute-done.50
  760.9 5.2 fusion.35
  766.8 54.3 %all-gather.11.cloned.1.call-done.refs_1_.packed_ref = bf16[9216,256]{1,0:T(8,128)(2,1)} async-done(((bf16[1152,256]{1,0:T(8,128)(2,1)}), bf16[9216,256]{1,0:T(8,128)(2,1)}) %all-gather.11.cloned.1.call-update) | async-done | bytes 4718608 | tf_op jit(solution)/shard_map/all_gather | solution.py:588
  821.7 119.3 %last_steps.1 = (bf16[256,2048]{1,0:T(8,128)(2,1)}, bf16[256,2048]{1,0:T(8,128)(2,1)}, bf16[256,2048]{1,0:T(8,128)(2,1)}, bf16[128,2048]{1,0:T(8,128)(2,1)}, bf16[128,2048]{1,0:T(8,128)(2,1)}) custom-call(s32[16]{0:T(128)} %broadcast_select_fusion.1.from_ref, bf16[9216,256]{1,0:T(8,128)(2,1)} %all-gather.11.cloned.1.call-done.refs_1_.packed_ref, ...), custom_call_target="tpu_custom_call" | custom-call | tf_op jit(solution)/shard_map/last_steps/pallas_call | solution.py:619
  943.4 4.6 maximum_add_fusion.1
  948.8 5.8 collective-permute-done.54
  960.8 28.3 %collective-permute-done.55 = bf16[128,2048]{1,0:T(8,128)(2,1)S(1)} collective-permute-done((bf16[128,2048]{1,0:T(8,128)(2,1)S(1)}, bf16[128,2048]{1,0:T(8,128)(2,1)S(1)}, u32[]{:S(2)}, u32[]{:S(2)}) %collective-permute-start.55) | collective-permute-done | bytes 524320 | tf_op jit(solution)/shard_map/ppermute | solution.py:637
  991.8 3.0 collective-permute-start.60
  999.0 7.9 collective-permute-done.60
  (399 shorter events, 161.5 us)
Async XLA Ops:
  7.2 100.3 %all-gather.5.cloned.1.call-start = ((), (), s32[]{:S(2)}) async-start(), calls=%async_computation.4 | async-start | bytes 9437184 | tf_op jit(solution)/shard_map/all_gather | solution.py:872
  12.7 178.6 %all-gather.7.cloned.1.call-start = ((), (), s32[]{:S(2)}) async-start(), calls=%async_computation.5 | async-start | bytes 9437184 | tf_op jit(solution)/shard_map/all_gather | solution.py:876
  14.3 45.1 %collective-permute-start.5 = (bf16[256,2048]{1,0:T(8,128)(2,1)}, bf16[256,2048]{1,0:T(8,128)(2,1)S(1)}, u32[]{:S(2)}, u32[]{:S(2)}) collective-permute-start(bf16[256,2048]{1,0:T(8,128)(2,1)} %get-tuple-element.185), channel_id=1, source_target_pairs={{16,0},{24,8},{0,16},{8,24},{17,1},{25,9},{1,17},{9,25},{18,2},{26... | collective-permute-start | bytes 3145736 | tf_op jit(solution)/shard_map/ppermute | solution.py:637
  16.4 43.2 %collective-permute-start.4 = (bf16[256,2048]{1,0:T(8,128)(2,1)}, bf16[256,2048]{1,0:T(8,128)(2,1)}, u32[]{:S(2)}, u32[]{:S(2)}) collective-permute-start(bf16[256,2048]{1,0:T(8,128)(2,1)} %get-tuple-element.185), channel_id=1, source_target_pairs={{8,0},{0,8},{24,16},{16,24},{9,1},{1,9},{25,17},{17,25},{10,2},{2,... | collective-permute-start | bytes 3145736 | tf_op jit(solution)/shard_map/ppermute | solution.py:637
  19.6 16.5 %collective-permute-start = (bf16[64,2048]{1,0:T(8,128)(2,1)}, bf16[64,2048]{1,0:T(8,128)(2,1)S(1)}, u32[]{:S(2)}, u32[]{:S(2)}) collective-permute-start(bf16[64,2048]{1,0:T(8,128)(2,1)} %get-tuple-element.181), channel_id=1, source_target_pairs={{0,0},{1,3},{2,6},{3,1},{4,4},{5,7},{6,2},{7,5},{8,8},{9,11},{10,1... | collective-permute-start | bytes 786440 | tf_op jit(solution)/shard_map/ppermute | solution.py:764
  22.8 19.6 %collective-permute-start.1 = (bf16[64,2048]{1,0:T(8,128)(2,1)}, bf16[64,2048]{1,0:T(8,128)(2,1)}, u32[]{:S(2)}, u32[]{:S(2)}) collective-permute-start(bf16[64,2048]{1,0:T(8,128)(2,1)} %get-tuple-element.182), channel_id=1, source_target_pairs={{0,1},{1,4},{2,7},{3,2},{4,5},{5,0},{6,3},{7,6},{8,9},{9,12},{10,1... | collective-permute-start | bytes 786440 | tf_op jit(solution)/shard_map/ppermute | solution.py:764
  24.6 33.7 %collective-permute-start.2 = (bf16[64,2048]{1,0:T(8,128)(2,1)}, bf16[64,2048]{1,0:T(8,128)(2,1)}, u32[]{:S(2)}, u32[]{:S(2)}) collective-permute-start(bf16[64,2048]{1,0:T(8,128)(2,1)} %get-tuple-element.183), channel_id=1, source_target_pairs={{0,2},{1,5},{2,0},{3,3},{4,6},{5,1},{6,4},{7,7},{8,10},{9,13},{10,... | collective-permute-start | bytes 786440 | tf_op jit(solution)/shard_map/ppermute | solution.py:764
  62.1 14.3 %collective-permute-start.3 = (bf16[192,2048]{1,0:T(8,128)(2,1)S(1)}, bf16[192,2048]{1,0:T(8,128)(2,1)S(1)}, u32[]{:S(2)}, u32[]{:S(2)}) collective-permute-start(bf16[192,2048]{1,0:T(8,128)(2,1)S(1)} %get-tuple-element.207), channel_id=1, source_target_pairs={{8,0},{0,8},{24,16},{16,24},{9,1},{1,9},{25,17},{17,25},{10,2},{2,... | collective-permute-start | bytes 2359304 | tf_op jit(solution)/shard_map/ppermute | solution.py:637
  63.3 14.5 %collective-permute-start.8 = (bf16[192,2048]{1,0:T(8,128)(2,1)S(1)}, bf16[192,2048]{1,0:T(8,128)(2,1)}, u32[]{:S(2)}, u32[]{:S(2)}) collective-permute-start(bf16[192,2048]{1,0:T(8,128)(2,1)S(1)} %get-tuple-element.207), channel_id=1, source_target_pairs={{16,0},{24,8},{0,16},{8,24},{17,1},{25,9},{1,17},{9,25},{18,2},{26... | collective-permute-start | bytes 2359304 | tf_op jit(solution)/shard_map/ppermute | solution.py:637
  107.5 420.3 %reduce-scatter.5.cloned.1.call-start = ((), (), s32[]{:S(2)}) async-start(), calls=%async_computation.6 | async-start | bytes 5308416 | tf_op jit(solution)/shard_map/reduce_scatter | solution.py:587
  110.9 33.8 %collective-permute-start.12 = (bf16[320,2048]{1,0:T(8,128)(2,1)}, bf16[320,2048]{1,0:T(8,128)(2,1)S(1)}, u32[]{:S(2)}, u32[]{:S(2)}) collective-permute-start(bf16[320,2048]{1,0:T(8,128)(2,1)} %after.29), channel_id=1, source_target_pairs={{16,0},{24,8},{0,16},{8,24},{17,1},{25,9},{1,17},{9,25},{18,2},{26... | collective-permute-start | bytes 3932168 | tf_op jit(solution)/shard_map/ppermute | solution.py:637
  111.2 34.8 %collective-permute-start.11 = (bf16[320,2048]{1,0:T(8,128)(2,1)}, bf16[320,2048]{1,0:T(8,128)(2,1)S(1)}, u32[]{:S(2)}, u32[]{:S(2)}) collective-permute-start(bf16[320,2048]{1,0:T(8,128)(2,1)} %after.29), channel_id=1, source_target_pairs={{8,0},{0,8},{24,16},{16,24},{9,1},{1,9},{25,17},{17,25},{10,2},{2,... | collective-permute-start | bytes 3932168 | tf_op jit(solution)/shard_map/ppermute | solution.py:637
  119.4 30.4 %collective-permute-start.9 = (bf16[96,2048]{1,0:T(8,128)(2,1)}, bf16[96,2048]{1,0:T(8,128)(2,1)}, u32[]{:S(2)}, u32[]{:S(2)}) collective-permute-start(bf16[96,2048]{1,0:T(8,128)(2,1)} %slice.203), channel_id=1, source_target_pairs={{8,0},{0,8},{24,16},{16,24},{9,1},{1,9},{25,17},{17,25},{10,2},{2,... | collective-permute-start | bytes 1179656 | tf_op jit(solution)/shard_map/ppermute | solution.py:637
  140.8 9.8 collective-permute-start.10
  145.7 22.1 %collective-permute-start.13 = (bf16[160,2048]{1,0:T(8,128)(2,1)}, bf16[160,2048]{1,0:T(8,128)(2,1)S(1)}, u32[]{:S(2)}, u32[]{:S(2)}) collective-permute-start(bf16[160,2048]{1,0:T(8,128)(2,1)} %slice.205), channel_id=1, source_target_pairs={{8,0},{0,8},{24,16},{16,24},{9,1},{1,9},{25,17},{17,25},{10,2},{2,... | collective-permute-start | bytes 1966088 | tf_op jit(solution)/shard_map/ppermute | solution.py:637
  148.3 19.5 %collective-permute-start.14 = (bf16[160,2048]{1,0:T(8,128)(2,1)S(1)}, bf16[160,2048]{1,0:T(8,128)(2,1)S(1)}, u32[]{:S(2)}, u32[]{:S(2)}) collective-permute-start(bf16[160,2048]{1,0:T(8,128)(2,1)S(1)} %slice.206), channel_id=1, source_target_pairs={{16,0},{24,8},{0,16},{8,24},{17,1},{25,9},{1,17},{9,25},{18,2},{26... | collective-permute-start | bytes 1966088 | tf_op jit(solution)/shard_map/ppermute | solution.py:637
  205.6 48.1 %collective-permute-start.15 = (bf16[256,2048]{1,0:T(8,128)(2,1)}, bf16[256,2048]{1,0:T(8,128)(2,1)}, u32[]{:S(2)}, u32[]{:S(2)}) collective-permute-start(bf16[256,2048]{1,0:T(8,128)(2,1)} %get-tuple-element.85.refs_1_), channel_id=1, source_target_pairs={{8,0},{0,8},{24,16},{16,24},{9,1},{1,9},{25,17},{17,25},{10,2},{2,... | collective-permute-start | bytes 3145736 | tf_op jit(solution)/shard_map/ppermute | solution.py:637
  209.5 40.1 %collective-permute-start.23 = (f32[64,2048]{1,0:T(8,128)}, f32[64,2048]{1,0:T(8,128)}, u32[]{:S(2)}, u32[]{:S(2)}) collective-permute-start(f32[64,2048]{1,0:T(8,128)} %get-tuple-element.189), channel_id=1, source_target_pairs={{0,0},{1,3},{2,6},{3,1},{4,4},{5,7},{6,2},{7,5},{8,8},{9,11},{10,1... | collective-permute-start | bytes 1572872 | tf_op jit(solution)/shard_map/ppermute | solution.py:764
  211.4 38.5 %collective-permute-start.25 = (f32[64,2048]{1,0:T(8,128)}, f32[64,2048]{1,0:T(8,128)}, u32[]{:S(2)}, u32[]{:S(2)}) collective-permute-start(f32[64,2048]{1,0:T(8,128)} %get-tuple-element.190), channel_id=1, source_target_pairs={{0,2},{1,5},{2,0},{3,3},{4,6},{5,1},{6,4},{7,7},{8,10},{9,13},{10,... | collective-permute-start | bytes 1572872 | tf_op jit(solution)/shard_map/ppermute | solution.py:764
  214.1 37.9 %collective-permute-start.24 = (f32[64,2048]{1,0:T(8,128)}, f32[64,2048]{1,0:T(8,128)}, u32[]{:S(2)}, u32[]{:S(2)}) collective-permute-start(f32[64,2048]{1,0:T(8,128)} %get-tuple-element.191), channel_id=1, source_target_pairs={{0,1},{1,4},{2,7},{3,2},{4,5},{5,0},{6,3},{7,6},{8,9},{9,12},{10,1... | collective-permute-start | bytes 1572872 | tf_op jit(solution)/shard_map/ppermute | solution.py:764
  218.2 35.4 %collective-permute-start.16 = (bf16[256,2048]{1,0:T(8,128)(2,1)}, bf16[256,2048]{1,0:T(8,128)(2,1)}, u32[]{:S(2)}, u32[]{:S(2)}) collective-permute-start(bf16[256,2048]{1,0:T(8,128)(2,1)} %get-tuple-element.87.refs_3_), channel_id=1, source_target_pairs={{16,0},{24,8},{0,16},{8,24},{17,1},{25,9},{1,17},{9,25},{18,2},{26... | collective-permute-start | bytes 3145736 | tf_op jit(solution)/shard_map/ppermute | solution.py:637
  249.6 47.4 %collective-permute-start.17 = (bf16[256,2048]{1,0:T(8,128)(2,1)}, bf16[256,2048]{1,0:T(8,128)(2,1)}, u32[]{:S(2)}, u32[]{:S(2)}) collective-permute-start(bf16[256,2048]{1,0:T(8,128)(2,1)} %get-tuple-element.88.refs_4_), channel_id=1, source_target_pairs={{8,0},{0,8},{24,16},{16,24},{9,1},{1,9},{25,17},{17,25},{10,2},{2,... | collective-permute-start | bytes 3145736 | tf_op jit(solution)/shard_map/ppermute | solution.py:637
  250.0 47.1 %collective-permute-start.18 = (bf16[256,2048]{1,0:T(8,128)(2,1)}, bf16[256,2048]{1,0:T(8,128)(2,1)}, u32[]{:S(2)}, u32[]{:S(2)}) collective-permute-start(bf16[256,2048]{1,0:T(8,128)(2,1)} %get-tuple-element.90.refs_6_), channel_id=1, source_target_pairs={{16,0},{24,8},{0,16},{8,24},{17,1},{25,9},{1,17},{9,25},{18,2},{26... | collective-permute-start | bytes 3145736 | tf_op jit(solution)/shard_map/ppermute | solution.py:637
  257.6 44.8 %collective-permute-start.21 = (bf16[128,2048]{1,0:T(8,128)(2,1)}, bf16[128,2048]{1,0:T(8,128)(2,1)S(1)}, u32[]{:S(2)}, u32[]{:S(2)}) collective-permute-start(bf16[128,2048]{1,0:T(8,128)(2,1)} %get-tuple-element.92.refs_1_), channel_id=1, source_target_pairs={{16,0},{24,8},{0,16},{8,24},{17,1},{25,9},{1,17},{9,25},{18,2},{26... | collective-permute-start | bytes 1572872 | tf_op jit(solution)/shard_map/ppermute | solution.py:637
  258.7 43.6 %collective-permute-start.22 = (bf16[128,2048]{1,0:T(8,128)(2,1)}, bf16[128,2048]{1,0:T(8,128)(2,1)S(1)}, u32[]{:S(2)}, u32[]{:S(2)}) collective-permute-start(bf16[128,2048]{1,0:T(8,128)(2,1)} %get-tuple-element.93.refs_2_), channel_id=1, source_target_pairs={{8,0},{0,8},{24,16},{16,24},{9,1},{1,9},{25,17},{17,25},{10,2},{2,... | collective-permute-start | bytes 1572872 | tf_op jit(solution)/shard_map/ppermute | solution.py:637
  301.2 24.1 %collective-permute-start.19 = (bf16[128,2048]{1,0:T(8,128)(2,1)}, bf16[128,2048]{1,0:T(8,128)(2,1)}, u32[]{:S(2)}, u32[]{:S(2)}) collective-permute-start(bf16[128,2048]{1,0:T(8,128)(2,1)} %get-tuple-element.96.refs_2_), channel_id=1, source_target_pairs={{16,0},{24,8},{0,16},{8,24},{17,1},{25,9},{1,17},{9,25},{18,2},{26... | collective-permute-start | bytes 1572872 | tf_op jit(solution)/shard_map/ppermute | solution.py:637
  301.2 24.1 %collective-permute-start.20 = (bf16[128,2048]{1,0:T(8,128)(2,1)}, bf16[128,2048]{1,0:T(8,128)(2,1)}, u32[]{:S(2)}, u32[]{:S(2)}) collective-permute-start(bf16[128,2048]{1,0:T(8,128)(2,1)} %get-tuple-element.98.refs_3_), channel_id=1, source_target_pairs={{8,0},{0,8},{24,16},{16,24},{9,1},{1,9},{25,17},{17,25},{10,2},{2,... | collective-permute-start | bytes 1572872 | tf_op jit(solution)/shard_map/ppermute | solution.py:637
  320.8 58.5 %collective-permute-start.30 = (bf16[192,2048]{1,0:T(8,128)(2,1)}, bf16[192,2048]{1,0:T(8,128)(2,1)}, u32[]{:S(2)}, u32[]{:S(2)}) collective-permute-start(bf16[192,2048]{1,0:T(8,128)(2,1)} %get-tuple-element.113), channel_id=1, source_target_pairs={{16,0},{24,8},{0,16},{8,24},{17,1},{25,9},{1,17},{9,25},{18,2},{26... | collective-permute-start | bytes 2359304 | tf_op jit(solution)/shard_map/ppermute | solution.py:637
  323.8 56.8 %collective-permute-start.29 = (bf16[192,2048]{1,0:T(8,128)(2,1)}, bf16[192,2048]{1,0:T(8,128)(2,1)S(1)}, u32[]{:S(2)}, u32[]{:S(2)}) collective-permute-start(bf16[192,2048]{1,0:T(8,128)(2,1)} %get-tuple-element.103.refs_5_), channel_id=1, source_target_pairs={{8,0},{0,8},{24,16},{16,24},{9,1},{1,9},{25,17},{17,25},{10,2},{2,... | collective-permute-start | bytes 2359304 | tf_op jit(solution)/shard_map/ppermute | solution.py:637
  333.4 42.7 %collective-permute-start.32 = (bf16[128,2048]{1,0:T(8,128)(2,1)}, bf16[128,2048]{1,0:T(8,128)(2,1)}, u32[]{:S(2)}, u32[]{:S(2)}) collective-permute-start(bf16[128,2048]{1,0:T(8,128)(2,1)} %get-tuple-element.108.refs_4_), channel_id=1, source_target_pairs={{24,8},{0,16},{25,9},{1,17},{26,10},{2,18},{27,11},{3,19},{28,12},... | collective-permute-start | bytes 1572872 | tf_op jit(solution)/shard_map/ppermute | solution.py:637
  374.8 17.3 %collective-permute-start.37 = (bf16[192,2048]{1,0:T(8,128)(2,1)}, bf16[192,2048]{1,0:T(8,128)(2,1)}, u32[]{:S(2)}, u32[]{:S(2)}) collective-permute-start(bf16[192,2048]{1,0:T(8,128)(2,1)} %get-tuple-element.122), channel_id=1, source_target_pairs={{16,0},{24,8},{0,16},{8,24},{17,1},{25,9},{1,17},{9,25},{18,2},{26... | collective-permute-start | bytes 2359304 | tf_op jit(solution)/shard_map/ppermute | solution.py:637
  374.9 55.0 %collective-permute-start.26 = (bf16[256,2048]{1,0:T(8,128)(2,1)}, bf16[256,2048]{1,0:T(8,128)(2,1)}, u32[]{:S(2)}, u32[]{:S(2)}) collective-permute-start(bf16[256,2048]{1,0:T(8,128)(2,1)} %get-tuple-element.105.refs_1_), channel_id=1, source_target_pairs={{8,0},{16,24},{9,1},{17,25},{10,2},{18,26},{11,3},{19,27},{12,4},{... | collective-permute-start | bytes 3145736 | tf_op jit(solution)/shard_map/ppermute | solution.py:637
  376.2 40.3 %collective-permute-start.36 = (bf16[192,2048]{1,0:T(8,128)(2,1)}, bf16[192,2048]{1,0:T(8,128)(2,1)}, u32[]{:S(2)}, u32[]{:S(2)}) collective-permute-start(bf16[192,2048]{1,0:T(8,128)(2,1)} %get-tuple-element.115.refs_4_), channel_id=1, source_target_pairs={{8,0},{0,8},{24,16},{16,24},{9,1},{1,9},{25,17},{17,25},{10,2},{2,... | collective-permute-start | bytes 2359304 | tf_op jit(solution)/shard_map/ppermute | solution.py:637
  379.2 54.8 %collective-permute-start.27 = (bf16[256,2048]{1,0:T(8,128)(2,1)}, bf16[256,2048]{1,0:T(8,128)(2,1)}, u32[]{:S(2)}, u32[]{:S(2)}) collective-permute-start(bf16[256,2048]{1,0:T(8,128)(2,1)} %get-tuple-element.106.refs_2_), channel_id=1, source_target_pairs={{16,0},{8,24},{17,1},{9,25},{18,2},{10,26},{19,3},{11,27},{20,4},{... | collective-permute-start | bytes 3145736 | tf_op jit(solution)/shard_map/ppermute | solution.py:637
  380.6 42.3 %collective-permute-start.28 = (bf16[128,2048]{1,0:T(8,128)(2,1)}, bf16[128,2048]{1,0:T(8,128)(2,1)}, u32[]{:S(2)}, u32[]{:S(2)}) collective-permute-start(bf16[128,2048]{1,0:T(8,128)(2,1)} %get-tuple-element.107.refs_3_), channel_id=1, source_target_pairs={{24,16},{0,8},{25,17},{1,9},{26,18},{2,10},{27,19},{3,11},{28,20},... | collective-permute-start | bytes 1572872 | tf_op jit(solution)/shard_map/ppermute | solution.py:637
  392.1 35.6 %collective-permute-start.33 = (bf16[128,2048]{1,0:T(8,128)(2,1)}, bf16[128,2048]{1,0:T(8,128)(2,1)}, u32[]{:S(2)}, u32[]{:S(2)}) collective-permute-start(bf16[128,2048]{1,0:T(8,128)(2,1)} %collective-permute-done.32), channel_id=1, source_target_pairs={{8,0},{16,24},{9,1},{17,25},{10,2},{18,26},{11,3},{19,27},{12,4},{... | collective-permute-start | bytes 1572872 | tf_op jit(solution)/shard_map/ppermute | solution.py:637
  416.5 30.1 %collective-permute-start.34 = (bf16[192,2048]{1,0:T(8,128)(2,1)}, bf16[192,2048]{1,0:T(8,128)(2,1)}, u32[]{:S(2)}, u32[]{:S(2)}) collective-permute-start(bf16[192,2048]{1,0:T(8,128)(2,1)} %get-tuple-element.116.refs_1_.refs_4_), channel_id=1, source_target_pairs={{24,8},{0,16},{25,9},{1,17},{26,10},{2,18},{27,11},{3,19},{28,12},... | collective-permute-start | bytes 2359304 | tf_op jit(solution)/shard_map/ppermute | solution.py:637
  422.9 23.7 %collective-permute-start.35 = (bf16[192,2048]{1,0:T(8,128)(2,1)S(1)}, bf16[192,2048]{1,0:T(8,128)(2,1)}, u32[]{:S(2)}, u32[]{:S(2)}) collective-permute-start(bf16[192,2048]{1,0:T(8,128)(2,1)S(1)} %copy-done.36), channel_id=1, source_target_pairs={{0,8},{24,16},{1,9},{25,17},{2,10},{26,18},{3,11},{27,19},{4,12},{... | collective-permute-start | bytes 2359304 | tf_op jit(solution)/shard_map/ppermute | solution.py:637
  427.7 19.0 %collective-permute-start.38 = (bf16[192,2048]{1,0:T(8,128)(2,1)}, bf16[192,2048]{1,0:T(8,128)(2,1)}, u32[]{:S(2)}, u32[]{:S(2)}) collective-permute-start(bf16[192,2048]{1,0:T(8,128)(2,1)} %get-tuple-element.124), channel_id=1, source_target_pairs={{24,8},{0,16},{25,9},{1,17},{26,10},{2,18},{27,11},{3,19},{28,12},... | collective-permute-start | bytes 2359304 | tf_op jit(solution)/shard_map/ppermute | solution.py:637
  429.9 22.7 %collective-permute-start.39 = (bf16[192,2048]{1,0:T(8,128)(2,1)}, bf16[192,2048]{1,0:T(8,128)(2,1)}, u32[]{:S(2)}, u32[]{:S(2)}) collective-permute-start(bf16[192,2048]{1,0:T(8,128)(2,1)} %get-tuple-element.126), channel_id=1, source_target_pairs={{0,8},{24,16},{1,9},{25,17},{2,10},{26,18},{3,11},{27,19},{4,12},{... | collective-permute-start | bytes 2359304 | tf_op jit(solution)/shard_map/ppermute | solution.py:637
  434.0 12.6 %collective-permute-start.31 = (bf16[128,2048]{1,0:T(8,128)(2,1)}, bf16[128,2048]{1,0:T(8,128)(2,1)S(1)}, u32[]{:S(2)}, u32[]{:S(2)}) collective-permute-start(bf16[128,2048]{1,0:T(8,128)(2,1)} %after.38), channel_id=1, source_target_pairs={{16,0},{8,24},{17,1},{9,25},{18,2},{10,26},{19,3},{11,27},{20,4},{... | collective-permute-start | bytes 1572872 | tf_op jit(solution)/shard_map/ppermute | solution.py:637
  465.8 121.6 %all-gather.9.cloned.1.call-start = ((), (), s32[]{:S(2)}) async-start(), calls=%async_computation.7 | async-start | bytes 5308416 | tf_op jit(solution)/shard_map/all_gather | solution.py:588
  527.9 166.0 %reduce-scatter.7.cloned.1.call-start = ((), (), s32[]{:S(2)}) async-start(), calls=%async_computation.8 | async-start | bytes 9437184 | tf_op jit(solution)/shard_map/reduce_scatter | solution.py:1000
  587.4 179.3 %reduce-scatter.9.cloned.1.call-start = ((), (), s32[]{:S(2)}) async-start(), calls=%async_computation.9 | async-start | bytes 5308416 | tf_op jit(solution)/shard_map/reduce_scatter | solution.py:587
  587.9 100.7 %collective-permute-start.40 = (bf16[256,2048]{1,0:T(8,128)(2,1)}, bf16[256,2048]{1,0:T(8,128)(2,1)S(1)}, u32[]{:S(2)}, u32[]{:S(2)}) collective-permute-start(bf16[256,2048]{1,0:T(8,128)(2,1)} %after.48), channel_id=1, source_target_pairs={{8,0},{0,8},{24,16},{16,24},{9,1},{1,9},{25,17},{17,25},{10,2},{2,... | collective-permute-start | bytes 3145736 | tf_op jit(solution)/shard_map/ppermute | solution.py:637
  589.2 99.5 %collective-permute-start.41 = (bf16[256,2048]{1,0:T(8,128)(2,1)}, bf16[256,2048]{1,0:T(8,128)(2,1)S(1)}, u32[]{:S(2)}, u32[]{:S(2)}) collective-permute-start(bf16[256,2048]{1,0:T(8,128)(2,1)} %after.50), channel_id=1, source_target_pairs={{16,0},{24,8},{0,16},{8,24},{17,1},{25,9},{1,17},{9,25},{18,2},{26... | collective-permute-start | bytes 3145736 | tf_op jit(solution)/shard_map/ppermute | solution.py:637
  693.9 127.2 %all-gather.11.cloned.1.call-start = ((), (), s32[]{:S(2)}) async-start(), calls=%async_computation.10 | async-start | bytes 5308416 | tf_op jit(solution)/shard_map/all_gather | solution.py:588
  694.1 13.6 %collective-permute-start.42 = (bf16[128,2048]{1,0:T(8,128)(2,1)}, bf16[128,2048]{1,0:T(8,128)(2,1)}, u32[]{:S(2)}, u32[]{:S(2)}) collective-permute-start(bf16[128,2048]{1,0:T(8,128)(2,1)} %get-tuple-element.134.refs_2_), channel_id=1, source_target_pairs={{16,0},{24,8},{0,16},{8,24},{17,1},{25,9},{1,17},{9,25},{18,2},{26... | collective-permute-start | bytes 1572872 | tf_op jit(solution)/shard_map/ppermute | solution.py:637
  698.8 13.3 %collective-permute-start.43 = (bf16[128,2048]{1,0:T(8,128)(2,1)}, bf16[128,2048]{1,0:T(8,128)(2,1)S(1)}, u32[]{:S(2)}, u32[]{:S(2)}) collective-permute-start(bf16[128,2048]{1,0:T(8,128)(2,1)} %get-tuple-element.135.refs_3_), channel_id=1, source_target_pairs={{8,0},{0,8},{24,16},{16,24},{9,1},{1,9},{25,17},{17,25},{10,2},{2,... | collective-permute-start | bytes 1572872 | tf_op jit(solution)/shard_map/ppermute | solution.py:637
  717.4 40.2 %collective-permute-start.44 = (bf16[64,2048]{1,0:T(8,128)(2,1)S(1)}, bf16[64,2048]{1,0:T(8,128)(2,1)S(1)}, u32[]{:S(2)}, u32[]{:S(2)}) collective-permute-start(bf16[64,2048]{1,0:T(8,128)(2,1)S(1)} %get-tuple-element.203), channel_id=1, source_target_pairs={{0,0},{3,1},{6,2},{1,3},{4,4},{7,5},{2,6},{5,7},{8,8},{11,9},{14,1... | collective-permute-start | bytes 786440 | tf_op jit(solution)/shard_map/ppermute | solution.py:782
  719.4 38.3 %collective-permute-start.46 = (bf16[64,2048]{1,0:T(8,128)(2,1)S(1)}, bf16[64,2048]{1,0:T(8,128)(2,1)S(1)}, u32[]{:S(2)}, u32[]{:S(2)}) collective-permute-start(bf16[64,2048]{1,0:T(8,128)(2,1)S(1)} %get-tuple-element.204), channel_id=1, source_target_pairs={{2,0},{5,1},{0,2},{3,3},{6,4},{1,5},{4,6},{7,7},{10,8},{13,9},{8,1... | collective-permute-start | bytes 786440 | tf_op jit(solution)/shard_map/ppermute | solution.py:782
  722.4 35.3 %collective-permute-start.45 = (bf16[64,2048]{1,0:T(8,128)(2,1)S(1)}, bf16[64,2048]{1,0:T(8,128)(2,1)S(1)}, u32[]{:S(2)}, u32[]{:S(2)}) collective-permute-start(bf16[64,2048]{1,0:T(8,128)(2,1)S(1)} %get-tuple-element.205), channel_id=1, source_target_pairs={{1,0},{4,1},{7,2},{2,3},{5,4},{0,5},{3,6},{6,7},{9,8},{12,9},{15,1... | collective-permute-start | bytes 786440 | tf_op jit(solution)/shard_map/ppermute | solution.py:782
  723.5 21.0 %collective-permute-start.48 = (f32[20480]{0:T(1024)S(1)}, f32[20480]{0:T(1024)S(1)}, u32[]{:S(2)}, u32[]{:S(2)}) collective-permute-start(f32[20480]{0:T(1024)S(1)} %add.251), channel_id=1, source_target_pairs={{0,2},{1,3},{2,0},{3,1},{4,6},{5,7},{6,4},{7,5},{8,10},{9,11},{10,... | collective-permute-start | bytes 245768 | tf_op jit(solution)/shard_map/ppermute | solution.py:750
  744.6 12.1 %collective-permute-start.49 = (f32[20480]{0:T(1024)S(1)}, f32[20480]{0:T(1024)S(1)}, u32[]{:S(2)}, u32[]{:S(2)}) collective-permute-start(f32[20480]{0:T(1024)S(1)} %add.252), channel_id=1, source_target_pairs={{0,4},{1,5},{2,6},{3,7},{4,0},{5,1},{6,2},{7,3},{8,12},{9,13},{10,... | collective-permute-start | bytes 245768 | tf_op jit(solution)/shard_map/ppermute | solution.py:750
  766.8 243.7 %reduce-scatter.11.cloned.1.call-start = ((), (), s32[]{:S(2)}) async-start(), calls=%async_computation.11 | async-start | bytes 9437184 | tf_op jit(solution)/shard_map/reduce_scatter | solution.py:1040
  941.0 13.6 %collective-permute-start.54 = (bf16[128,2048]{1,0:T(8,128)(2,1)}, bf16[128,2048]{1,0:T(8,128)(2,1)S(1)}, u32[]{:S(2)}, u32[]{:S(2)}) collective-permute-start(bf16[128,2048]{1,0:T(8,128)(2,1)} %get-tuple-element.148), channel_id=1, source_target_pairs={{8,0},{0,8},{24,16},{16,24},{9,1},{1,9},{25,17},{17,25},{10,2},{2,... | collective-permute-start | bytes 1572872 | tf_op jit(solution)/shard_map/ppermute | solution.py:637
  942.2 13.5 %collective-permute-start.56 = (bf16[128,2048]{1,0:T(8,128)(2,1)}, bf16[128,2048]{1,0:T(8,128)(2,1)S(1)}, u32[]{:S(2)}, u32[]{:S(2)}) collective-permute-start(bf16[128,2048]{1,0:T(8,128)(2,1)} %get-tuple-element.149), channel_id=1, source_target_pairs={{16,0},{24,8},{0,16},{8,24},{17,1},{25,9},{1,17},{9,25},{18,2},{26... | collective-permute-start | bytes 1572872 | tf_op jit(solution)/shard_map/ppermute | solution.py:637
  948.0 41.1 %collective-permute-start.52 = (bf16[256,2048]{1,0:T(8,128)(2,1)S(1)}, bf16[256,2048]{1,0:T(8,128)(2,1)S(1)}, u32[]{:S(2)}, u32[]{:S(2)}) collective-permute-start(bf16[256,2048]{1,0:T(8,128)(2,1)S(1)} %copy-done.61), channel_id=1, source_target_pairs={{8,0},{0,8},{24,16},{16,24},{9,1},{1,9},{25,17},{17,25},{10,2},{2,... | collective-permute-start | bytes 3145736 | tf_op jit(solution)/shard_map/ppermute | solution.py:637
  948.3 40.8 %collective-permute-start.53 = (bf16[256,2048]{1,0:T(8,128)(2,1)S(1)}, bf16[256,2048]{1,0:T(8,128)(2,1)S(1)}, u32[]{:S(2)}, u32[]{:S(2)}) collective-permute-start(bf16[256,2048]{1,0:T(8,128)(2,1)S(1)} %copy-done.60), channel_id=1, source_target_pairs={{16,0},{24,8},{0,16},{8,24},{17,1},{25,9},{1,17},{9,25},{18,2},{26... | collective-permute-start | bytes 3145736 | tf_op jit(solution)/shard_map/ppermute | solution.py:637
  954.5 34.6 %collective-permute-start.55 = (bf16[128,2048]{1,0:T(8,128)(2,1)S(1)}, bf16[128,2048]{1,0:T(8,128)(2,1)S(1)}, u32[]{:S(2)}, u32[]{:S(2)}) collective-permute-start(bf16[128,2048]{1,0:T(8,128)(2,1)S(1)} %collective-permute-done.54), channel_id=1, source_target_pairs={{16,0},{24,8},{0,16},{8,24},{17,1},{25,9},{1,17},{9,25},{18,2},{26... | collective-permute-start | bytes 1572872 | tf_op jit(solution)/shard_map/ppermute | solution.py:637
  955.7 33.4 %collective-permute-start.57 = (bf16[128,2048]{1,0:T(8,128)(2,1)S(1)}, bf16[128,2048]{1,0:T(8,128)(2,1)S(1)}, u32[]{:S(2)}, u32[]{:S(2)}) collective-permute-start(bf16[128,2048]{1,0:T(8,128)(2,1)S(1)} %collective-permute-done.56), channel_id=1, source_target_pairs={{8,0},{0,8},{24,16},{16,24},{9,1},{1,9},{25,17},{17,25},{10,2},{2,... | collective-permute-start | bytes 1572872 | tf_op jit(solution)/shard_map/ppermute | solution.py:637
  989.9 9.1 collective-permute-start.58
  991.8 15.1 %collective-permute-start.60 = (bf16[64,2048]{1,0:T(8,128)(2,1)S(1)}, bf16[64,2048]{1,0:T(8,128)(2,1)S(1)}, u32[]{:S(2)}, u32[]{:S(2)}) collective-permute-start(bf16[64,2048]{1,0:T(8,128)(2,1)S(1)} %get-tuple-element.201), channel_id=1, source_target_pairs={{2,0},{5,1},{0,2},{3,3},{6,4},{1,5},{4,6},{7,7},{10,8},{13,9},{8,1... | collective-permute-start | bytes 786440 | tf_op jit(solution)/shard_map/ppermute | solution.py:782
  994.8 13.2 %collective-permute-start.59 = (bf16[64,2048]{1,0:T(8,128)(2,1)S(1)}, bf16[64,2048]{1,0:T(8,128)(2,1)S(1)}, u32[]{:S(2)}, u32[]{:S(2)}) collective-permute-start(bf16[64,2048]{1,0:T(8,128)(2,1)S(1)} %get-tuple-element.202), channel_id=1, source_target_pairs={{1,0},{4,1},{7,2},{2,3},{5,4},{0,5},{3,6},{6,7},{9,8},{12,9},{15,1... | collective-permute-start | bytes 786440 | tf_op jit(solution)/shard_map/ppermute | solution.py:782
  (69 other events, 599.0 us)
Sparse Core Ops, SparseCore 0:
  12.8 94.6 all-gather.4
  109.6 81.5 all-gather.6
  465.9 59.5 reduce-scatter.4
  528.0 59.3 all-gather.8
  589.5 85.8 reduce-scatter.6
  694.1 65.9 reduce-scatter.8
  766.9 54.1 all-gather.10
  823.4 85.8 reduce-scatter.10

commit v3 on v2

--- a/solution.py
+++ b/solution.py
@@ -240,7 +240,7 @@
 
 
 def attention_body(
-    first_ref, pre_ref, grad_ref, start_ref, cos_ref, sin_ref, att_ref, out_ref, q_s, k_s, v_s, dk_s, dv_s, o_s, dq_s
+    first_ref, pre_ref, grad_ref, start_ref, cos_ref, sin_ref, att_ref, out_ref, q_s, k_s, v_s, dk_s, dv_s
 ):
     pack_len, width = grad_ref.shape
     heads = width // HEAD
@@ -276,33 +276,34 @@
         column = (block + 1 - count) * CHUNK + lax.broadcasted_iota(jnp.int32, shape, 1)
         row = block * CHUNK + lax.broadcasted_iota(jnp.int32, shape, 0)
         allowed = (column >= start_ref[rows, :]) & (column <= row)
-        o_s[...] = jnp.zeros((CHUNK, width), F32)
-        dq_s[...] = jnp.zeros((CHUNK, width), F32)
-
-        def one_head(head, carry):
-            mine = head_of == head
-            query = jnp.where(mine, q_s[rows, :], jnp.zeros((), BF16))
-            grad = jnp.where(mine, grad_ref[rows, :], jnp.zeros((), BF16))
-            keys, values = k_s[span, :], v_s[span, :]
-            scores = lax.dot_general(query, keys, over_last, preferred_element_type=F32)
-            scores = jnp.where(allowed, scores, NEG)
-            prob = jnp.exp(scores - jnp.max(scores, axis=1, keepdims=True))
-            prob = prob * (1.0 / jnp.sum(prob, axis=1, keepdims=True))
-            prob_low = prob.astype(BF16)
-            grad_prob = lax.dot_general(grad, values, over_last, preferred_element_type=F32)
-            delta = jnp.sum(prob * grad_prob, axis=1, keepdims=True)
-            grad_scores = (prob * (grad_prob - delta)).astype(BF16)
-            o_s[...] += jnp.where(mine, jnp.dot(prob_low, values, preferred_element_type=F32), 0.0)
-            dq_s[...] += jnp.where(mine, jnp.dot(grad_scores, keys, preferred_element_type=F32), 0.0)
-            dk_s[span, :] += lax.dot_general(
-                grad_scores, query, over_first, preferred_element_type=F32
+        allowed = jnp.concatenate([allowed] * heads, axis=0)
+
+        def one_by_one(values):
+            return jnp.concatenate(
+                [jnp.where(head_of == head, values, jnp.zeros((), BF16)) for head in range(heads)], axis=0
             )
-            dv_s[span, :] += lax.dot_general(prob_low, grad, over_first, preferred_element_type=F32)
-            return carry
-
-        lax.fori_loop(0, heads, one_head, 0)
-        att_ref[rows, :] = o_s[...].astype(BF16)
-        out_ref[rows, :width] = turn(dq_s[...] * HEAD ** (-0.5), rows, -1.0).astype(BF16)
+
+        def side_by_side(values):
+            total = values[:CHUNK]
+            for head in range(1, heads):
+                total = jnp.where(head_of == head, values[head * CHUNK : (head + 1) * CHUNK], total)
+            return total
+
+        query, grad = one_by_one(q_s[rows, :]), one_by_one(grad_ref[rows, :])
+        keys, values = k_s[span, :], v_s[span, :]
+        scores = lax.dot_general(query, keys, over_last, preferred_element_type=F32)
+        scores = jnp.where(allowed, scores, NEG)
+        prob = jnp.exp(scores - jnp.max(scores, axis=1, keepdims=True))
+        prob = prob * (1.0 / jnp.sum(prob, axis=1, keepdims=True))
+        prob_low = prob.astype(BF16)
+        grad_prob = lax.dot_general(grad, values, over_last, preferred_element_type=F32)
+        delta = jnp.sum(prob * grad_prob, axis=1, keepdims=True)
+        grad_scores = (prob * (grad_prob - delta)).astype(BF16)
+        dk_s[span, :] += lax.dot_general(grad_scores, query, over_first, preferred_element_type=F32)
+        dv_s[span, :] += lax.dot_general(prob_low, grad, over_first, preferred_element_type=F32)
+        att_ref[rows, :] = side_by_side(jnp.dot(prob_low, values, preferred_element_type=F32)).astype(BF16)
+        grad_query = side_by_side(jnp.dot(grad_scores, keys, preferred_element_type=F32))
+        out_ref[rows, :width] = turn(grad_query * HEAD ** (-0.5), rows, -1.0).astype(BF16)
 
     def one_block(block, carry):
         used = block + 1 - first_ref[block]
@@ -341,8 +342,7 @@
         ],
         out_specs=(whole, whole),
         scratch_shapes=[pltpu.VMEM((pack_len, width), BF16)] * 3
-        + [pltpu.VMEM((pack_len, width), F32)] * 2
-        + [pltpu.VMEM((CHUNK, width), F32)] * 2,
+        + [pltpu.VMEM((pack_len, width), F32)] * 2,
         compiler_params=pltpu.CompilerParams(vmem_limit_bytes=VMEM_BYTES),
         cost_estimate=NOTHING,
         name="attention",
@@ -690,8 +690,10 @@
     return (left, hop(left_out, 2), right, hop(right_out, 1)), (left_out, right_out)
 
 
-def scatter_end(state):
+def scatter_end(state, *others):
     left, left_in, right, right_in = state
+    if others:
+        left, right = after(left, *others), after(right, *others)
     return jnp.concatenate([left + left_in.astype(F32), right + right_in.astype(F32)], axis=0)
 
 
@@ -889,9 +891,9 @@
     if fast:
         near_back = gather_near(after(w_back, *near_qkv[1:]))
         own, from_x, from_y = near_qkv
-        w_qkv = by_distance(gather_far((own, after(from_x, activated), from_y)))
+        w_qkv = by_distance(gather_far((own, after(from_x, activated), after(from_y, activated))))
         own, from_x, from_y = near_back
-        all_back = gather_far((own, after(from_x, activated), from_y))
+        all_back = gather_far((own, after(from_x, activated), after(from_y, activated)))
         w_out = by_distance(all_back[:, :out_rows]).reshape(width, model_width)
         w_down = all_back[:, out_rows:].reshape(data_count * ff_rows, model_width)
     else:
@@ -901,12 +903,13 @@
         w_down = lax.all_gather(w_back[out_rows:], "dp", axis=0, tiled=True)
     w_qkv = to_parts(w_qkv.reshape(3 * width, model_width))
     pre_qkv = project(normed_all, w_qkv, bias_qkv, F32, "project_qkv")
-    grad_all = after(grad_all, activated, slope, pre_qkv, w_down, w_out)
+    branch_up = dot(activated, w_down)
+    grad_all = after(grad_all, activated, slope, pre_qkv, w_down, w_out, branch_up)
 
     term_down = weight_grad(activated, grad_all, "grad_down", fast)
     if fast:
+        sum_down = scatter_start(term_down)
         m_qkv = spread_qkv(after(m_in[:qkv_rows], term_down[0]), unit)
-        sum_down = scatter_start(term_down)
         slope = after(slope, *term_down)
     grad_pre_up = up_backward(grad_all, slope, w_down)
     term_up = weight_grad(grad_pre_up, normed_all, "grad_up", fast)
@@ -932,6 +935,9 @@
             sum_up, flying = scatter_next(sum_up, one)
             own_down, full_down = scatter_momentum(sum_down, m_back[out_rows:], one)
             one_grad = after(one_grad, full_down, *flying)
+        else:
+            first_half, flying = reduce_next(sum_att[0], one)
+            one_grad = after(one_grad, *flying)
         one_qkv, one_out, *split = weight_grads_plus(
             one_grad,
             normed_all,
@@ -950,9 +956,8 @@
         term_out.append(one_out)
 
     if fast:
-        first_half, flying = reduce_next(sum_att[0], split[0])
-        early = owners_end(early, [0, 3], *flying)
-        second_half, flying = reduce_next(sum_att[1], *flying)
+        early = owners_end(early, [0, 3], split[0])
+        second_half, _ = reduce_next(sum_att[1])
         owned, packed = first_gram((data_count * ff_rows, model_width), early, (*first_half, *second_half))
     else:
         packed = None
@@ -978,9 +983,7 @@
     def after_gram(packed):
         late_qkv, late_up = jnp.concatenate(grad_pre_qkv, axis=1), after(grad_pre_up, packed)
         late_qkv = after(late_qkv, packed)
-        late_attended = after(jnp.concatenate(attended, axis=1), packed)
         normed_part = dot(late_qkv, w_qkv) + dot(late_up, w_up)
-        branch_part = dot(late_attended, w_out) + dot(after(activated, packed), w_down)
         split = ()
         if fast:
             terms = [from_parts(jnp.concatenate(term_qkv)), jnp.concatenate(term_out)]
@@ -988,9 +991,11 @@
             terms = by_distance(jnp.concatenate(terms, axis=1)).reshape(2, 2, 2, unit * 2, model_width)
             split = terms[:, 1, 0], terms[:, 0, 0], terms[1, :, 1], terms[0, :, 1]
             split = [one.reshape(4 * unit, model_width) for one in split]
-        return normed_part.astype(BF16), branch_part.astype(BF16), late_qkv, late_up, split
-
-    kept = []
+        branch_part = dot(after(attended_all, packed), w_out) + branch_up
+        return normed_part.astype(BF16), late_qkv, late_up, split, branch_part.astype(BF16)
+
+    kept = [None]
+    attended_all = jnp.concatenate(attended, axis=1)
 
     def beside_first(gathered, meanwhile):
         kept.extend(meanwhile[1:])
@@ -1002,7 +1007,7 @@
     def after_first_steps(first, packed):
         if not fast:
             return first
-        state, flying = scatter_next(kept[4], packed)
+        state, flying = scatter_next(kept[5], packed)
         kept.append(state)
         return first + flying
 
@@ -1015,13 +1020,14 @@
             - x_hat * jnp.mean(grad_x_hat * x_hat, axis=-1, keepdims=True)
         )
         if fast:
-            own = scatter_end(kept[5])
+            own = scatter_end(kept[6])
             own_qkv = return_qkv(own[:qkv_rows].astype(BF16), unit).astype(F32)
             own_out = own[qkv_rows:]
         else:
             own_qkv, own_out = grad_w_qkv, grad_w_out
         grad_in = jnp.concatenate([own_qkv, own_up])
         grad_back = jnp.concatenate([own_out, own_down])
+        grads = grad_in, grad_back, m_in + grad_in, m_back + grad_back
         sums_up = jnp.sum(kept[2].astype(F32), axis=0).reshape(data_count, ff_rows)
         sums_qkv = jnp.sum(kept[1].astype(F32), axis=0)
         vector_local = jnp.concatenate(
@@ -1034,10 +1040,10 @@
             ]
         )
         vector_grad = butterfly(vector_local)
-        return grad_hidden, grad_in, grad_back, m_in + grad_in, m_back + grad_back, vector_grad
+        return grad_hidden, vector_grad, *grads
 
     def beside_last(gathered):
-        return (lax.psum_scatter(after(kept[0], gathered), "group", scatter_dimension=0, tiled=True),)
+        return (lax.psum_scatter(after(kept[4], gathered), "group", scatter_dimension=0, tiled=True),)
 
     def placed(sums, lead, size):
         empty = jnp.zeros((lead, group_count, size), F32)
@@ -1057,7 +1063,7 @@
     results, _, meanwhile, (branch,) = orthogonalize(
         owned, packed, source_rows.astype(jnp.int32), pieces, after_gram, beside_first, after_first_steps, after_first, beside_last
     )
-    grad_hidden, grad_in, grad_back, moment_in_new, moment_back_new, vector_grad = meanwhile
+    grad_hidden, vector_grad, grad_in, grad_back, moment_in_new, moment_back_new = meanwhile
     block_out = (x_float + branch.astype(F32) + bias_out).astype(BF16)
     if fast:
         returned = by_distance(exchange_dp(*results))

time: 1030 us -> 1010 us (0.981)
  waiting for transfers between devices: 314 us -> 291 us
    ppermute x44, waiting for transfers between devices: 95.3 us -> 110 us  [hop(): return lax.ppermute(values, 'dp', [(t ^ bit, t) for t in targets])]
    all_gather x1, waiting for transfers between devices: 17.2 us -> 2.2 us  [shards(): lax.all_gather(after(grad_y, normed_all, w_up, *near_qkv[1:], *tables), '...]
    pallas_call x2, Pallas kernels: 52.2 us -> 40.6 us  [attention(): pl.pallas_call(attention_body, grid=(1,), out_shape=(jax.ShapeDtypeStruct...]
    unnamed x135 -> x145, local copies, waits for them, and re-layouts: 20 us -> 26.8 us
  transfers between devices with their start and end apart: 69 -> 69, of which waited for: 27 -> 26; matrix products, arithmetic and copies ran while one was open for 16% -> 16% of each run, Pallas kernels for 39% -> 37%
where the time goes in v3:
time: 1010 us; the launch traced here: 1000 us
  Pallas kernels  420 us (42%)
  waiting for transfers between devices  291 us (29%)
  starting transfers between devices  96.2 us (10%)
  other arithmetic  68.9 us (7%)
  local copies, waits for them, and re-layouts  64.2 us (6%)
  matrix products  48.7 us (5%)
  between operations  15.8 us (2%)
    pallas_call x1, Pallas kernels, orthogonalize(): pl.pallas_call(functools.partial(second_body, 3), out_shape=[jax.ShapeDty...  119 us
    ppermute x44, waiting for transfers between devices, hop(): return lax.ppermute(values, 'dp', [(t ^ bit, t) for t in targets])  110 us
    pallas_call x1, Pallas kernels, orthogonalize(): pl.pallas_call(functools.partial(first_body, 2), out_shape=(x_shape, pack...  107 us
    all_gather x2, waiting for transfers between devices, gram_sum(): lax.all_gather(after(part, *jax.tree.leaves(meanwhile)), 'group', axis=0,...  107 us
    ppermute x44, starting transfers between devices, hop(): return lax.ppermute(values, 'dp', [(t ^ bit, t) for t in targets])  57.7 us
    pallas_call x4, Pallas kernels, by_columns(): pl.pallas_call(body, grid=(steps,), in_specs=([] if scalar is None else [...  54.9 us
    pallas_call x4, Pallas kernels, by_rows(): pl.pallas_call(body, grid=(steps,), in_specs=[pl.BlockSpec((rows, one.sha...  51.3 us
    dot_general x4, matrix products, dot(): return jnp.dot(left, right, preferred_element_type=F32)  48.7 us
  transfers between devices with their start and end apart: 69, of which 26 were waited for; matrix products, arithmetic and copies ran while one was open for 16% of the time, Pallas kernels for 37%

profile of v3, /device:TPU:1, one launch (start us, length us, event | category | flops | bytes accessed | tf_op | source)
XLA Modules:
  0.0 1004.9 jit_solution(10797281258721868311)
XLA Ops:
  7.3 2.6 copy.126
  19.6 4.2 collective-permute-start.2
  25.7 4.4 collective-permute-start.1
  38.9 11.8 %collective-permute-done = bf16[64,2048]{1,0:T(8,128)(2,1)} collective-permute-done((bf16[64,2048]{1,0:T(8,128)(2,1)}, bf16[64,2048]{1,0:T(8,128)(2,1)}, u32[]{:S(2)}, u32[]{:S(2)}) %collective-permute-start) | collective-permute-done | bytes 262176 | tf_op jit(solution)/shard_map/ppermute | solution.py:766
  59.3 8.3 collective-permute-done.6
  69.1 3.3 pad_maximum_fusion.1.refs_2_
  72.5 10.9 %collective-permute-done.3.refs_0_.refs_3_.refs_1_ = bf16[192,2048]{1,0:T(8,128)(2,1)} collective-permute-done((bf16[192,2048]{1,0:T(8,128)(2,1)S(1)}, bf16[192,2048]{1,0:T(8,128)(2,1)}, u32[]{:S(2)}, u32[]{:S(2)}) %collective-permute-start.3) | collective-permute-done | bytes 786464 | tf_op jit(solution)/shard_map/ppermute | solution.py:637
  84.8 21.3 %all-gather.5.cloned.1.call-done.x_ref.refs_1_.r_ref = bf16[2048,2048]{1,0:T(8,128)(2,1)} async-done(((bf16[256,2048]{1,0:T(8,128)(2,1)}), bf16[2048,2048]{1,0:T(8,128)(2,1)}) %all-gather.5.cloned.1.call-update) | async-done | bytes 8388624 | tf_op jit(solution)/shard_map/all_gather | solution.py:874
  113.0 4.9 broadcast_multiply_fusion
  117.9 18.7 %up_forward.1 = (bf16[2048,1024]{1,0:T(8,128)(2,1)}, bf16[2048,1024]{1,0:T(8,128)(2,1)}) custom-call(bf16[2048,2048]{1,0:T(8,128)(2,1)} %all-gather.5.cloned.1.call-done.x_ref.refs_1_.r_ref, bf16[1024,2048]{1,0:T(8,128)(2,1)} %bitcast.204, f32[1,1024]{1,0:T(1,128)} %bitcast.255), custom_call_target="tpu_custom_call" | custom-call | tf_op jit(solution)/shard_map/up_forward/pallas_call | solution.py:77
  141.5 2.7 slice_bitcast_fusion.2.refs_0_
  156.8 11.6 %project_qkv.1.refs_3_.pre_ref = f32[2048,768]{1,0:T(8,128)} custom-call(bf16[2048,2048]{1,0:T(8,128)(2,1)} %all-gather.5.cloned.1.call-done.x_ref.refs_1_.r_ref, bf16[768,2048]{1,0:T(8,128)(2,1)} %bitcast.225, f32[1,768]{1,0:T(1,128)} %broadcast_in_dim_reshape.7.b_ref), custom_call_target="tpu_custom_call" | custom-call | tf_op jit(solution)/shard_map/project_qkv/pallas_call | solution.py:77
  175.7 11.7 %fusion.41.refs_6_ = f32[2048,2048]{1,0:T(8,128)} fusion(bf16[2048,1024]{1,0:T(8,128)(2,1)S(1)} %copy-done, bf16[1024,2048]{1,0:T(8,128)(2,1)S(1)} %bitcast.201), kind=kOutput, calls=%fused_computation.185 | convolution fusion | flops 8589934592 | bytes 25165824 | tf_op jit(solution)/shard_map/dot_general | solution.py:843
  189.6 14.3 %grad_down.1 = (bf16[256,2048]{1,0:T(8,128)(2,1)}, bf16[256,2048]{1,0:T(8,128)(2,1)}, bf16[256,2048]{1,0:T(8,128)(2,1)}, bf16[256,2048]{1,0:T(8,128)(2,1)}) custom-call(bf16[2048,1024]{1,0:T(8,128)(2,1)} %get-tuple-element.82.refs_1_.l_ref, bf16[2048,2048]{1,0:T(8,128)(2,1)} %after.35.r_ref.g_ref.x_ref.q_ref), custom_call_target="tpu_custom_call" | custom-call | tf_op jit(solution)/shard_map/grad_down/pallas_call | solution.py:95
  205.1 2.7 fusion.40
  209.8 6.6 collective-permute-start.24
  221.2 14.3 %up_backward.1.l_ref.refs_0_ = bf16[2048,1024]{1,0:T(8,128)(2,1)} custom-call(bf16[2048,2048]{1,0:T(8,128)(2,1)} %after.35.r_ref.g_ref.x_ref.q_ref, bf16[2048,1024]{1,0:T(8,128)(2,1)} %after.36.s_ref, bf16[1024,2048]{1,0:T(8,128)(2,1)} %bitcast.203), custom_call_target="tpu_custom_call" | custom-call | tf_op jit(solution)/shard_map/up_backward/pallas_call | solution.py:77
  235.5 14.5 %grad_up.1 = (bf16[256,2048]{1,0:T(8,128)(2,1)}, bf16[256,2048]{1,0:T(8,128)(2,1)}, bf16[256,2048]{1,0:T(8,128)(2,1)}, bf16[256,2048]{1,0:T(8,128)(2,1)}) custom-call(bf16[2048,1024]{1,0:T(8,128)(2,1)} %up_backward.1.l_ref.refs_0_, bf16[2048,2048]{1,0:T(8,128)(2,1)} %all-gather.5.cloned.1.call-done.x_ref.refs_1_.r_ref), custom_call_target="tpu_custom_call" | custom-call | tf_op jit(solution)/shard_map/grad_up/pallas_call | solution.py:95
  254.6 4.0 scatter_next.3
  262.2 6.7 project_grad.1.refs_0_
  271.2 20.2 %attention.2 = (bf16[2048,128]{1,0:T(8,128)(2,1)}, bf16[2048,384]{1,0:T(8,128)(2,1)}) custom-call(s32[8]{0:T(128)} %and_select_fusion.6.refs_5_.first_ref, f32[2048,768]{1,0:T(8,128)} %project_qkv.1.refs_3_.pre_ref, bf16[2048,256]{1,0:T(8,128)(2,1)} %after.38.grad_ref, s32[2048,1]{1,0:T(8,128)} %subtract_subtract_fusion.refs_6_.start_ref, ...), custom_call_target="tpu_custom_call" | custom-call | tf_op jit(solution)/shard_map/attention/pallas_call | solution.py:328
  291.4 2.7 copy.100.refs_0_
  294.1 4.0 scatter_next.4
  302.5 4.5 momentum.2
  307.1 13.0 %weight_grads_plus.2 = (bf16[384,2048]{1,0:T(8,128)(2,1)}, bf16[128,2048]{1,0:T(8,128)(2,1)}, bf16[192,2048]{1,0:T(8,128)(2,1)}, bf16[192,2048]{1,0:T(8,128)(2,1...) custom-call(s32[1]{0:T(128)} %bitcast.42.me_ref, bf16[2048,384]{1,0:T(8,128)(2,1)} %after.39.l_ref, ...), custom_call_target="tpu_custom_call" | custom-call | tf_op jit(solution)/shard_map/weight_grads_plus/pallas_call | solution.py:95
  321.9 4.5 momentum.3
  326.4 3.6 to_owners.1
  330.0 20.3 %attention.3 = (bf16[2048,128]{1,0:T(8,128)(2,1)}, bf16[2048,384]{1,0:T(8,128)(2,1)}) custom-call(s32[8]{0:T(128)} %and_select_fusion.6.refs_5_.first_ref, f32[2048,768]{1,0:T(8,128)} %project_qkv.1.refs_3_.pre_ref, bf16[2048,256]{1,0:T(8,128)(2,1)} %after.41.grad_ref, s32[2048,1]{1,0:T(8,128)} %subtract_subtract_fusion.refs_6_.start_ref, ...), custom_call_target="tpu_custom_call" | custom-call | tf_op jit(solution)/shard_map/attention/pallas_call | solution.py:328
  350.3 3.3 pad_maximum_fusion.7.refs_0_
  353.7 4.2 reduce_next.2
  357.9 13.1 %weight_grads_plus.3 = (bf16[384,2048]{1,0:T(8,128)(2,1)}, bf16[128,2048]{1,0:T(8,128)(2,1)}, bf16[192,2048]{1,0:T(8,128)(2,1)}, bf16[192,2048]{1,0:T(8,128)(2,1...) custom-call(s32[1]{0:T(128)} %bitcast.42.me_ref, bf16[2048,384]{1,0:T(8,128)(2,1)} %after.42.l_ref, ...), custom_call_target="tpu_custom_call" | custom-call | tf_op jit(solution)/shard_map/weight_grads_plus/pallas_call | solution.py:95
  373.1 5.8 collective-permute-start.32
  381.6 7.3 collective-permute-done.32
  388.9 3.5 collective-permute-start.28
  393.7 12.1 %collective-permute-done.37.refs_3_ = bf16[192,2048]{1,0:T(8,128)(2,1)} collective-permute-done((bf16[192,2048]{1,0:T(8,128)(2,1)}, bf16[192,2048]{1,0:T(8,128)(2,1)}, u32[]{:S(2)}, u32[]{:S(2)}) %collective-permute-start.37) | collective-permute-done | bytes 786464 | tf_op jit(solution)/shard_map/ppermute | solution.py:637
  405.8 5.0 collective-permute-start.34
  410.7 4.2 reduce_next.3
  417.1 7.8 collective-permute-done.33.refs_4_
  424.9 4.6 collective-permute-start.38
  432.1 12.7 %collective-permute-done.31.refs_3_ = bf16[128,2048]{1,0:T(8,128)(2,1)S(1)} collective-permute-done((bf16[128,2048]{1,0:T(8,128)(2,1)}, bf16[128,2048]{1,0:T(8,128)(2,1)S(1)}, u32[]{:S(2)}, u32[]{:S(2)}) %collective-permute-start.31) | collective-permute-done | bytes 524320 | tf_op jit(solution)/shard_map/ppermute | solution.py:637
  444.8 3.8 collective-permute-done.39.refs_12_
  449.5 13.0 %gram.1 = (bf16[1024,2048]{1,0:T(8,128)(2,1)}, bf16[9216,256]{1,0:T(8,128)(2,1)}) custom-call(s32[1]{0:T(128)} %bitcast.42.me_ref, bf16[256,2048]{1,0:T(8,128)(2,1)} %get-tuple-element.110.refs_0_, bf16[256,2048]{1,0:T(8,128)(2,1)} %copy-done.46, bf16[256,2048]{1,0:T(8,128)(2,1)} %collective-permute-done.27.refs_2_, bf16[128,2048]{1,0:T(8,128)(2,1)} %copy-done.54, ...), custom_call_target="tpu_custom_call" | custom-call | tf_op jit(solution)/shard_map/gram/pallas_call | solution.py:566
  477.4 11.9 %add_convert_fusion.1.refs_8_.refs_0_ = bf16[2048,2048]{1,0:T(8,128)(2,1)} fusion(f32[2048,2048]{1,0:T(8,128)} %fusion.41.refs_6_, bf16[2048,256]{1,0:T(8,128)(2,1)S(1)} %copy-done.25, bf16[256,2048]{1,0:T(8,128)(2,1)S(1)} %bitcast.219), kind=kOutput, calls=%fused_computation.1 | convolution fusion | flops 2155872256 | bytes 27262976 | tf_op jit(solution)/shard_map/dot_general | solution.py:843
  489.3 11.7 %fusion.42 = f32[2048,2048]{1,0:T(8,128)} fusion(bf16[2048,1024]{1,0:T(8,128)(2,1)S(1)} %copy-done.1, bf16[1024,2048]{1,0:T(8,128)(2,1)S(1)} %bitcast.205), kind=kOutput, calls=%fused_computation.186 | convolution fusion | flops 8589934592 | bytes 25165824 | tf_op jit(solution)/shard_map/dot_general | solution.py:843
  501.0 13.4 %add_convert_fusion.refs_1_.refs_0_ = bf16[2048,2048]{1,0:T(8,128)(2,1)} fusion(f32[2048,2048]{1,0:T(8,128)} %fusion.42, bf16[2048,768]{1,0:T(8,128)(2,1)S(1)} %copy-done.2, bf16[768,2048]{1,0:T(8,128)(2,1)} %bitcast.226), kind=kOutput, calls=%fused_computation | convolution fusion | flops 6450839552 | bytes 31457280 | tf_op jit(solution)/shard_map/dot_general | solution.py:843
  514.4 3.7 reduce-scatter.5.cloned.1.call-done.refs_0_
  518.1 54.1 %all-gather.9.cloned.1.call-done.packed_ref.refs_1_ = bf16[9216,256]{1,0:T(8,128)(2,1)} async-done(((bf16[1152,256]{1,0:T(8,128)(2,1)}), bf16[9216,256]{1,0:T(8,128)(2,1)}) %all-gather.9.cloned.1.call-update) | async-done | bytes 4718608 | tf_op jit(solution)/shard_map/all_gather | solution.py:588
  574.7 107.5 %first_steps.1 = (bf16[1024,2048]{1,0:T(8,128)(2,1)}, bf16[9216,256]{1,0:T(8,128)(2,1)}) custom-call(bf16[9216,256]{1,0:T(8,128)(2,1)} %all-gather.9.cloned.1.call-done.packed_ref.refs_1_, bf16[1024,2048]{1,0:T(8,128)(2,1)} %get-tuple-element.132.x_ref), custom_call_target="tpu_custom_call" | custom-call | tf_op jit(solution)/shard_map/first_steps/pallas_call | solution.py:604
  683.6 4.0 scatter_next.5
  688.0 3.1 convert_reduce_fusion
  692.3 8.3 collective-permute-done.48
  711.5 3.3 collective-permute-start.49
  714.9 3.3 collective-permute-start.51
  719.7 3.9 fusion.34
  723.6 19.7 %collective-permute-done.44 = f32[20480]{0:T(1024)S(1)} collective-permute-done((f32[20480]{0:T(1024)S(1)}, f32[20480]{0:T(1024)S(1)}, u32[]{:S(2)}, u32[]{:S(2)}) %collective-permute-start.44) | collective-permute-done | bytes 81952 | tf_op jit(solution)/shard_map/ppermute | solution.py:752
  744.5 3.3 collective-permute-done.45
  748.1 5.2 fusion.35
  754.1 52.6 %all-gather.11.cloned.1.call-done.refs_1_.packed_ref = bf16[9216,256]{1,0:T(8,128)(2,1)} async-done(((bf16[1152,256]{1,0:T(8,128)(2,1)}), bf16[9216,256]{1,0:T(8,128)(2,1)}) %all-gather.11.cloned.1.call-update) | async-done | bytes 4718608 | tf_op jit(solution)/shard_map/all_gather | solution.py:588
  807.3 119.3 %last_steps.1 = (bf16[256,2048]{1,0:T(8,128)(2,1)}, bf16[256,2048]{1,0:T(8,128)(2,1)}, bf16[256,2048]{1,0:T(8,128)(2,1)}, bf16[128,2048]{1,0:T(8,128)(2,1)}, bf16[128,2048]{1,0:T(8,128)(2,1)}) custom-call(s32[16]{0:T(128)} %broadcast_select_fusion.1.from_ref, bf16[9216,256]{1,0:T(8,128)(2,1)} %all-gather.11.cloned.1.call-done.refs_1_.packed_ref, ...), custom_call_target="tpu_custom_call" | custom-call | tf_op jit(solution)/shard_map/last_steps/pallas_call | solution.py:619
  929.0 4.6 maximum_add_fusion.1
  934.3 5.7 collective-permute-done.54
  946.4 28.3 %collective-permute-done.55 = bf16[128,2048]{1,0:T(8,128)(2,1)S(1)} collective-permute-done((bf16[128,2048]{1,0:T(8,128)(2,1)S(1)}, bf16[128,2048]{1,0:T(8,128)(2,1)S(1)}, u32[]{:S(2)}, u32[]{:S(2)}) %collective-permute-start.55) | collective-permute-done | bytes 524320 | tf_op jit(solution)/shard_map/ppermute | solution.py:637
  977.6 2.9 collective-permute-start.60
  985.2 6.2 collective-permute-done.59
  (411 shorter events, 160.4 us)
Async XLA Ops:
  7.2 98.9 %all-gather.5.cloned.1.call-start = ((), (), s32[]{:S(2)}) async-start(), calls=%async_computation.4 | async-start | bytes 9437184 | tf_op jit(solution)/shard_map/all_gather | solution.py:874
  12.7 176.9 %all-gather.7.cloned.1.call-start = ((), (), s32[]{:S(2)}) async-start(), calls=%async_computation.5 | async-start | bytes 9437184 | tf_op jit(solution)/shard_map/all_gather | solution.py:878
  14.3 39.1 %collective-permute-start.5 = (bf16[256,2048]{1,0:T(8,128)(2,1)}, bf16[256,2048]{1,0:T(8,128)(2,1)S(1)}, u32[]{:S(2)}, u32[]{:S(2)}) collective-permute-start(bf16[256,2048]{1,0:T(8,128)(2,1)} %get-tuple-element.185), channel_id=1, source_target_pairs={{16,0},{24,8},{0,16},{8,24},{17,1},{25,9},{1,17},{9,25},{18,2},{26... | collective-permute-start | bytes 3145736 | tf_op jit(solution)/shard_map/ppermute | solution.py:637
  16.4 37.2 %collective-permute-start.4 = (bf16[256,2048]{1,0:T(8,128)(2,1)}, bf16[256,2048]{1,0:T(8,128)(2,1)}, u32[]{:S(2)}, u32[]{:S(2)}) collective-permute-start(bf16[256,2048]{1,0:T(8,128)(2,1)} %get-tuple-element.185), channel_id=1, source_target_pairs={{8,0},{0,8},{24,16},{16,24},{9,1},{1,9},{25,17},{17,25},{10,2},{2,... | collective-permute-start | bytes 3145736 | tf_op jit(solution)/shard_map/ppermute | solution.py:637
  19.6 19.3 %collective-permute-start.2 = (bf16[64,2048]{1,0:T(8,128)(2,1)}, bf16[64,2048]{1,0:T(8,128)(2,1)S(1)}, u32[]{:S(2)}, u32[]{:S(2)}) collective-permute-start(bf16[64,2048]{1,0:T(8,128)(2,1)} %get-tuple-element.183), channel_id=1, source_target_pairs={{0,2},{1,5},{2,0},{3,3},{4,6},{5,1},{6,4},{7,7},{8,10},{9,13},{10,... | collective-permute-start | bytes 786440 | tf_op jit(solution)/shard_map/ppermute | solution.py:766
  23.8 27.0 %collective-permute-start = (bf16[64,2048]{1,0:T(8,128)(2,1)}, bf16[64,2048]{1,0:T(8,128)(2,1)}, u32[]{:S(2)}, u32[]{:S(2)}) collective-permute-start(bf16[64,2048]{1,0:T(8,128)(2,1)} %get-tuple-element.181), channel_id=1, source_target_pairs={{0,0},{1,3},{2,6},{3,1},{4,4},{5,7},{6,2},{7,5},{8,8},{9,11},{10,1... | collective-permute-start | bytes 786440 | tf_op jit(solution)/shard_map/ppermute | solution.py:766
  25.7 26.6 %collective-permute-start.1 = (bf16[64,2048]{1,0:T(8,128)(2,1)}, bf16[64,2048]{1,0:T(8,128)(2,1)}, u32[]{:S(2)}, u32[]{:S(2)}) collective-permute-start(bf16[64,2048]{1,0:T(8,128)(2,1)} %get-tuple-element.182), channel_id=1, source_target_pairs={{0,1},{1,4},{2,7},{3,2},{4,5},{5,0},{6,3},{7,6},{8,9},{9,12},{10,1... | collective-permute-start | bytes 786440 | tf_op jit(solution)/shard_map/ppermute | solution.py:766
  53.5 14.1 %collective-permute-start.6 = (bf16[128,2048]{1,0:T(8,128)(2,1)S(1)}, bf16[128,2048]{1,0:T(8,128)(2,1)S(1)}, u32[]{:S(2)}, u32[]{:S(2)}) collective-permute-start(bf16[128,2048]{1,0:T(8,128)(2,1)S(1)} %slice.201), channel_id=1, source_target_pairs={{8,0},{0,8},{24,16},{16,24},{9,1},{1,9},{25,17},{17,25},{10,2},{2,... | collective-permute-start | bytes 1572872 | tf_op jit(solution)/shard_map/ppermute | solution.py:637
  54.9 14.1 %collective-permute-start.7 = (bf16[128,2048]{1,0:T(8,128)(2,1)S(1)}, bf16[128,2048]{1,0:T(8,128)(2,1)S(1)}, u32[]{:S(2)}, u32[]{:S(2)}) collective-permute-start(bf16[128,2048]{1,0:T(8,128)(2,1)S(1)} %slice.202), channel_id=1, source_target_pairs={{16,0},{24,8},{0,16},{8,24},{17,1},{25,9},{1,17},{9,25},{18,2},{26... | collective-permute-start | bytes 1572872 | tf_op jit(solution)/shard_map/ppermute | solution.py:637
  56.1 27.3 %collective-permute-start.3 = (bf16[192,2048]{1,0:T(8,128)(2,1)S(1)}, bf16[192,2048]{1,0:T(8,128)(2,1)}, u32[]{:S(2)}, u32[]{:S(2)}) collective-permute-start(bf16[192,2048]{1,0:T(8,128)(2,1)S(1)} %get-tuple-element.207), channel_id=1, source_target_pairs={{8,0},{0,8},{24,16},{16,24},{9,1},{1,9},{25,17},{17,25},{10,2},{2,... | collective-permute-start | bytes 2359304 | tf_op jit(solution)/shard_map/ppermute | solution.py:637
  57.3 27.5 %collective-permute-start.8 = (bf16[192,2048]{1,0:T(8,128)(2,1)S(1)}, bf16[192,2048]{1,0:T(8,128)(2,1)S(1)}, u32[]{:S(2)}, u32[]{:S(2)}) collective-permute-start(bf16[192,2048]{1,0:T(8,128)(2,1)S(1)} %get-tuple-element.207), channel_id=1, source_target_pairs={{16,0},{24,8},{0,16},{8,24},{17,1},{25,9},{1,17},{9,25},{18,2},{26... | collective-permute-start | bytes 2359304 | tf_op jit(solution)/shard_map/ppermute | solution.py:637
  106.2 411.9 %reduce-scatter.5.cloned.1.call-start = ((), (), s32[]{:S(2)}) async-start(), calls=%async_computation.6 | async-start | bytes 5308416 | tf_op jit(solution)/shard_map/reduce_scatter | solution.py:587
  109.6 34.6 %collective-permute-start.12 = (bf16[320,2048]{1,0:T(8,128)(2,1)}, bf16[320,2048]{1,0:T(8,128)(2,1)S(1)}, u32[]{:S(2)}, u32[]{:S(2)}) collective-permute-start(bf16[320,2048]{1,0:T(8,128)(2,1)} %after.32), channel_id=1, source_target_pairs={{16,0},{24,8},{0,16},{8,24},{17,1},{25,9},{1,17},{9,25},{18,2},{26... | collective-permute-start | bytes 3932168 | tf_op jit(solution)/shard_map/ppermute | solution.py:637
  110.4 36.7 %collective-permute-start.11 = (bf16[320,2048]{1,0:T(8,128)(2,1)}, bf16[320,2048]{1,0:T(8,128)(2,1)S(1)}, u32[]{:S(2)}, u32[]{:S(2)}) collective-permute-start(bf16[320,2048]{1,0:T(8,128)(2,1)} %after.32), channel_id=1, source_target_pairs={{8,0},{0,8},{24,16},{16,24},{9,1},{1,9},{25,17},{17,25},{10,2},{2,... | collective-permute-start | bytes 3932168 | tf_op jit(solution)/shard_map/ppermute | solution.py:637
  138.4 12.9 %collective-permute-start.10 = (bf16[96,2048]{1,0:T(8,128)(2,1)}, bf16[96,2048]{1,0:T(8,128)(2,1)}, u32[]{:S(2)}, u32[]{:S(2)}) collective-permute-start(bf16[96,2048]{1,0:T(8,128)(2,1)} %slice.204), channel_id=1, source_target_pairs={{16,0},{24,8},{0,16},{8,24},{17,1},{25,9},{1,17},{9,25},{18,2},{26... | collective-permute-start | bytes 1179656 | tf_op jit(solution)/shard_map/ppermute | solution.py:637
  140.7 10.6 %collective-permute-start.9 = (bf16[96,2048]{1,0:T(8,128)(2,1)}, bf16[96,2048]{1,0:T(8,128)(2,1)}, u32[]{:S(2)}, u32[]{:S(2)}) collective-permute-start(bf16[96,2048]{1,0:T(8,128)(2,1)} %slice.203), channel_id=1, source_target_pairs={{8,0},{0,8},{24,16},{16,24},{9,1},{1,9},{25,17},{17,25},{10,2},{2,... | collective-permute-start | bytes 1179656 | tf_op jit(solution)/shard_map/ppermute | solution.py:637
  146.4 22.0 %collective-permute-start.13 = (bf16[160,2048]{1,0:T(8,128)(2,1)S(1)}, bf16[160,2048]{1,0:T(8,128)(2,1)S(1)}, u32[]{:S(2)}, u32[]{:S(2)}) collective-permute-start(bf16[160,2048]{1,0:T(8,128)(2,1)S(1)} %slice.205), channel_id=1, source_target_pairs={{8,0},{0,8},{24,16},{16,24},{9,1},{1,9},{25,17},{17,25},{10,2},{2,... | collective-permute-start | bytes 1966088 | tf_op jit(solution)/shard_map/ppermute | solution.py:637
  150.3 18.1 %collective-permute-start.14 = (bf16[160,2048]{1,0:T(8,128)(2,1)}, bf16[160,2048]{1,0:T(8,128)(2,1)S(1)}, u32[]{:S(2)}, u32[]{:S(2)}) collective-permute-start(bf16[160,2048]{1,0:T(8,128)(2,1)} %slice.206), channel_id=1, source_target_pairs={{16,0},{24,8},{0,16},{8,24},{17,1},{25,9},{1,17},{9,25},{18,2},{26... | collective-permute-start | bytes 1966088 | tf_op jit(solution)/shard_map/ppermute | solution.py:637
  203.9 50.6 %collective-permute-start.15 = (bf16[256,2048]{1,0:T(8,128)(2,1)}, bf16[256,2048]{1,0:T(8,128)(2,1)}, u32[]{:S(2)}, u32[]{:S(2)}) collective-permute-start(bf16[256,2048]{1,0:T(8,128)(2,1)} %get-tuple-element.85.refs_1_), channel_id=1, source_target_pairs={{8,0},{0,8},{24,16},{16,24},{9,1},{1,9},{25,17},{17,25},{10,2},{2,... | collective-permute-start | bytes 3145736 | tf_op jit(solution)/shard_map/ppermute | solution.py:637
  207.9 42.1 %collective-permute-start.23 = (f32[64,2048]{1,0:T(8,128)}, f32[64,2048]{1,0:T(8,128)}, u32[]{:S(2)}, u32[]{:S(2)}) collective-permute-start(f32[64,2048]{1,0:T(8,128)} %get-tuple-element.189), channel_id=1, source_target_pairs={{0,0},{1,3},{2,6},{3,1},{4,4},{5,7},{6,2},{7,5},{8,8},{9,11},{10,1... | collective-permute-start | bytes 1572872 | tf_op jit(solution)/shard_map/ppermute | solution.py:766
  209.8 40.7 %collective-permute-start.24 = (f32[64,2048]{1,0:T(8,128)}, f32[64,2048]{1,0:T(8,128)}, u32[]{:S(2)}, u32[]{:S(2)}) collective-permute-start(f32[64,2048]{1,0:T(8,128)} %get-tuple-element.191), channel_id=1, source_target_pairs={{0,1},{1,4},{2,7},{3,2},{4,5},{5,0},{6,3},{7,6},{8,9},{9,12},{10,1... | collective-permute-start | bytes 1572872 | tf_op jit(solution)/shard_map/ppermute | solution.py:766
  216.4 36.6 %collective-permute-start.25 = (f32[64,2048]{1,0:T(8,128)}, f32[64,2048]{1,0:T(8,128)}, u32[]{:S(2)}, u32[]{:S(2)}) collective-permute-start(f32[64,2048]{1,0:T(8,128)} %get-tuple-element.190), channel_id=1, source_target_pairs={{0,2},{1,5},{2,0},{3,3},{4,6},{5,1},{6,4},{7,7},{8,10},{9,13},{10,... | collective-permute-start | bytes 1572872 | tf_op jit(solution)/shard_map/ppermute | solution.py:766
  218.8 35.8 %collective-permute-start.16 = (bf16[256,2048]{1,0:T(8,128)(2,1)}, bf16[256,2048]{1,0:T(8,128)(2,1)}, u32[]{:S(2)}, u32[]{:S(2)}) collective-permute-start(bf16[256,2048]{1,0:T(8,128)(2,1)} %get-tuple-element.87.refs_3_), channel_id=1, source_target_pairs={{16,0},{24,8},{0,16},{8,24},{17,1},{25,9},{1,17},{9,25},{18,2},{26... | collective-permute-start | bytes 3145736 | tf_op jit(solution)/shard_map/ppermute | solution.py:637
  250.0 44.2 %collective-permute-start.17 = (bf16[256,2048]{1,0:T(8,128)(2,1)}, bf16[256,2048]{1,0:T(8,128)(2,1)}, u32[]{:S(2)}, u32[]{:S(2)}) collective-permute-start(bf16[256,2048]{1,0:T(8,128)(2,1)} %get-tuple-element.88.refs_4_), channel_id=1, source_target_pairs={{8,0},{0,8},{24,16},{16,24},{9,1},{1,9},{25,17},{17,25},{10,2},{2,... | collective-permute-start | bytes 3145736 | tf_op jit(solution)/shard_map/ppermute | solution.py:637
  250.5 43.6 %collective-permute-start.18 = (bf16[256,2048]{1,0:T(8,128)(2,1)}, bf16[256,2048]{1,0:T(8,128)(2,1)}, u32[]{:S(2)}, u32[]{:S(2)}) collective-permute-start(bf16[256,2048]{1,0:T(8,128)(2,1)} %get-tuple-element.90.refs_6_), channel_id=1, source_target_pairs={{16,0},{24,8},{0,16},{8,24},{17,1},{25,9},{1,17},{9,25},{18,2},{26... | collective-permute-start | bytes 3145736 | tf_op jit(solution)/shard_map/ppermute | solution.py:637
  258.5 43.0 %collective-permute-start.21 = (bf16[128,2048]{1,0:T(8,128)(2,1)}, bf16[128,2048]{1,0:T(8,128)(2,1)S(1)}, u32[]{:S(2)}, u32[]{:S(2)}) collective-permute-start(bf16[128,2048]{1,0:T(8,128)(2,1)} %get-tuple-element.92.refs_1_), channel_id=1, source_target_pairs={{16,0},{24,8},{0,16},{8,24},{17,1},{25,9},{1,17},{9,25},{18,2},{26... | collective-permute-start | bytes 1572872 | tf_op jit(solution)/shard_map/ppermute | solution.py:637
  259.3 42.2 %collective-permute-start.22 = (bf16[128,2048]{1,0:T(8,128)(2,1)}, bf16[128,2048]{1,0:T(8,128)(2,1)S(1)}, u32[]{:S(2)}, u32[]{:S(2)}) collective-permute-start(bf16[128,2048]{1,0:T(8,128)(2,1)} %get-tuple-element.93.refs_2_), channel_id=1, source_target_pairs={{8,0},{0,8},{24,16},{16,24},{9,1},{1,9},{25,17},{17,25},{10,2},{2,... | collective-permute-start | bytes 1572872 | tf_op jit(solution)/shard_map/ppermute | solution.py:637
  298.1 23.7 %collective-permute-start.19 = (bf16[128,2048]{1,0:T(8,128)(2,1)}, bf16[128,2048]{1,0:T(8,128)(2,1)}, u32[]{:S(2)}, u32[]{:S(2)}) collective-permute-start(bf16[128,2048]{1,0:T(8,128)(2,1)} %get-tuple-element.96.refs_2_), channel_id=1, source_target_pairs={{16,0},{24,8},{0,16},{8,24},{17,1},{25,9},{1,17},{9,25},{18,2},{26... | collective-permute-start | bytes 1572872 | tf_op jit(solution)/shard_map/ppermute | solution.py:637
  299.4 22.4 %collective-permute-start.20 = (bf16[128,2048]{1,0:T(8,128)(2,1)}, bf16[128,2048]{1,0:T(8,128)(2,1)}, u32[]{:S(2)}, u32[]{:S(2)}) collective-permute-start(bf16[128,2048]{1,0:T(8,128)(2,1)} %get-tuple-element.98.refs_3_), channel_id=1, source_target_pairs={{8,0},{0,8},{24,16},{16,24},{9,1},{1,9},{25,17},{17,25},{10,2},{2,... | collective-permute-start | bytes 1572872 | tf_op jit(solution)/shard_map/ppermute | solution.py:637
  320.1 33.5 %collective-permute-start.29 = (bf16[192,2048]{1,0:T(8,128)(2,1)}, bf16[192,2048]{1,0:T(8,128)(2,1)}, u32[]{:S(2)}, u32[]{:S(2)}) collective-permute-start(bf16[192,2048]{1,0:T(8,128)(2,1)} %get-tuple-element.103.refs_5_), channel_id=1, source_target_pairs={{8,0},{0,8},{24,16},{16,24},{9,1},{1,9},{25,17},{17,25},{10,2},{2,... | collective-permute-start | bytes 2359304 | tf_op jit(solution)/shard_map/ppermute | solution.py:637
  320.2 33.5 %collective-permute-start.30 = (bf16[192,2048]{1,0:T(8,128)(2,1)}, bf16[192,2048]{1,0:T(8,128)(2,1)}, u32[]{:S(2)}, u32[]{:S(2)}) collective-permute-start(bf16[192,2048]{1,0:T(8,128)(2,1)} %get-tuple-element.114), channel_id=1, source_target_pairs={{16,0},{24,8},{0,16},{8,24},{17,1},{25,9},{1,17},{9,25},{18,2},{26... | collective-permute-start | bytes 2359304 | tf_op jit(solution)/shard_map/ppermute | solution.py:637
  371.0 21.4 %collective-permute-start.36 = (bf16[192,2048]{1,0:T(8,128)(2,1)}, bf16[192,2048]{1,0:T(8,128)(2,1)}, u32[]{:S(2)}, u32[]{:S(2)}) collective-permute-start(bf16[192,2048]{1,0:T(8,128)(2,1)} %get-tuple-element.117.refs_1_), channel_id=1, source_target_pairs={{8,0},{0,8},{24,16},{16,24},{9,1},{1,9},{25,17},{17,25},{10,2},{2,... | collective-permute-start | bytes 2359304 | tf_op jit(solution)/shard_map/ppermute | solution.py:637
  373.1 15.8 %collective-permute-start.32 = (bf16[128,2048]{1,0:T(8,128)(2,1)}, bf16[128,2048]{1,0:T(8,128)(2,1)}, u32[]{:S(2)}, u32[]{:S(2)}) collective-permute-start(bf16[128,2048]{1,0:T(8,128)(2,1)} %get-tuple-element.108.refs_4_), channel_id=1, source_target_pairs={{24,8},{0,16},{25,9},{1,17},{26,10},{2,18},{27,11},{3,19},{28,12},... | collective-permute-start | bytes 1572872 | tf_op jit(solution)/shard_map/ppermute | solution.py:637
  378.9 50.6 %collective-permute-start.26 = (bf16[256,2048]{1,0:T(8,128)(2,1)S(1)}, bf16[256,2048]{1,0:T(8,128)(2,1)S(1)}, u32[]{:S(2)}, u32[]{:S(2)}) collective-permute-start(bf16[256,2048]{1,0:T(8,128)(2,1)S(1)} %copy-done.42), channel_id=1, source_target_pairs={{8,0},{16,24},{9,1},{17,25},{10,2},{18,26},{11,3},{19,27},{12,4},{... | collective-permute-start | bytes 3145736 | tf_op jit(solution)/shard_map/ppermute | solution.py:637
  380.2 25.6 %collective-permute-start.37 = (bf16[192,2048]{1,0:T(8,128)(2,1)}, bf16[192,2048]{1,0:T(8,128)(2,1)}, u32[]{:S(2)}, u32[]{:S(2)}) collective-permute-start(bf16[192,2048]{1,0:T(8,128)(2,1)} %get-tuple-element.122), channel_id=1, source_target_pairs={{16,0},{24,8},{0,16},{8,24},{17,1},{25,9},{1,17},{9,25},{18,2},{26... | collective-permute-start | bytes 2359304 | tf_op jit(solution)/shard_map/ppermute | solution.py:637
  380.3 50.5 %collective-permute-start.27 = (bf16[256,2048]{1,0:T(8,128)(2,1)S(1)}, bf16[256,2048]{1,0:T(8,128)(2,1)}, u32[]{:S(2)}, u32[]{:S(2)}) collective-permute-start(bf16[256,2048]{1,0:T(8,128)(2,1)S(1)} %copy-done.41), channel_id=1, source_target_pairs={{16,0},{8,24},{17,1},{9,25},{18,2},{10,26},{19,3},{11,27},{20,4},{... | collective-permute-start | bytes 3145736 | tf_op jit(solution)/shard_map/ppermute | solution.py:637
  388.9 26.1 %collective-permute-start.28 = (bf16[128,2048]{1,0:T(8,128)(2,1)S(1)}, bf16[128,2048]{1,0:T(8,128)(2,1)}, u32[]{:S(2)}, u32[]{:S(2)}) collective-permute-start(bf16[128,2048]{1,0:T(8,128)(2,1)S(1)} %copy-done.49), channel_id=1, source_target_pairs={{24,16},{0,8},{25,17},{1,9},{26,18},{2,10},{27,19},{3,11},{28,20},... | collective-permute-start | bytes 1572872 | tf_op jit(solution)/shard_map/ppermute | solution.py:637
  392.4 32.5 %collective-permute-start.33 = (bf16[128,2048]{1,0:T(8,128)(2,1)}, bf16[128,2048]{1,0:T(8,128)(2,1)}, u32[]{:S(2)}, u32[]{:S(2)}) collective-permute-start(bf16[128,2048]{1,0:T(8,128)(2,1)} %collective-permute-done.32), channel_id=1, source_target_pairs={{8,0},{16,24},{9,1},{17,25},{10,2},{18,26},{11,3},{19,27},{12,4},{... | collective-permute-start | bytes 1572872 | tf_op jit(solution)/shard_map/ppermute | solution.py:637
  405.8 39.0 %collective-permute-start.34 = (bf16[192,2048]{1,0:T(8,128)(2,1)}, bf16[192,2048]{1,0:T(8,128)(2,1)}, u32[]{:S(2)}, u32[]{:S(2)}) collective-permute-start(bf16[192,2048]{1,0:T(8,128)(2,1)} %get-tuple-element.115.refs_1_), channel_id=1, source_target_pairs={{24,8},{0,16},{25,9},{1,17},{26,10},{2,18},{27,11},{3,19},{28,12},... | collective-permute-start | bytes 2359304 | tf_op jit(solution)/shard_map/ppermute | solution.py:637
  415.0 29.8 %collective-permute-start.35 = (bf16[192,2048]{1,0:T(8,128)(2,1)}, bf16[192,2048]{1,0:T(8,128)(2,1)}, u32[]{:S(2)}, u32[]{:S(2)}) collective-permute-start(bf16[192,2048]{1,0:T(8,128)(2,1)} %get-tuple-element.116.refs_2_), channel_id=1, source_target_pairs={{0,8},{24,16},{1,9},{25,17},{2,10},{26,18},{3,11},{27,19},{4,12},{... | collective-permute-start | bytes 2359304 | tf_op jit(solution)/shard_map/ppermute | solution.py:637
  424.9 19.9 %collective-permute-start.38 = (bf16[192,2048]{1,0:T(8,128)(2,1)}, bf16[192,2048]{1,0:T(8,128)(2,1)}, u32[]{:S(2)}, u32[]{:S(2)}) collective-permute-start(bf16[192,2048]{1,0:T(8,128)(2,1)} %get-tuple-element.124), channel_id=1, source_target_pairs={{24,8},{0,16},{25,9},{1,17},{26,10},{2,18},{27,11},{3,19},{28,12},... | collective-permute-start | bytes 2359304 | tf_op jit(solution)/shard_map/ppermute | solution.py:637
  429.5 19.2 %collective-permute-start.39 = (bf16[192,2048]{1,0:T(8,128)(2,1)}, bf16[192,2048]{1,0:T(8,128)(2,1)S(1)}, u32[]{:S(2)}, u32[]{:S(2)}) collective-permute-start(bf16[192,2048]{1,0:T(8,128)(2,1)} %get-tuple-element.126), channel_id=1, source_target_pairs={{0,8},{24,16},{1,9},{25,17},{2,10},{26,18},{3,11},{27,19},{4,12},{... | collective-permute-start | bytes 2359304 | tf_op jit(solution)/shard_map/ppermute | solution.py:637
  430.8 14.0 %collective-permute-start.31 = (bf16[128,2048]{1,0:T(8,128)(2,1)}, bf16[128,2048]{1,0:T(8,128)(2,1)S(1)}, u32[]{:S(2)}, u32[]{:S(2)}) collective-permute-start(bf16[128,2048]{1,0:T(8,128)(2,1)} %after.43), channel_id=1, source_target_pairs={{16,0},{8,24},{17,1},{9,25},{18,2},{10,26},{19,3},{11,27},{20,4},{... | collective-permute-start | bytes 1572872 | tf_op jit(solution)/shard_map/ppermute | solution.py:637
  462.5 109.7 %all-gather.9.cloned.1.call-start = ((), (), s32[]{:S(2)}) async-start(), calls=%async_computation.7 | async-start | bytes 5308416 | tf_op jit(solution)/shard_map/all_gather | solution.py:588
  518.1 169.4 %reduce-scatter.7.cloned.1.call-start = ((), (), s32[]{:S(2)}) async-start(), calls=%async_computation.8 | async-start | bytes 9437184 | tf_op jit(solution)/shard_map/reduce_scatter | solution.py:1005
  572.2 181.8 %reduce-scatter.9.cloned.1.call-start = ((), (), s32[]{:S(2)}) async-start(), calls=%async_computation.9 | async-start | bytes 5308416 | tf_op jit(solution)/shard_map/reduce_scatter | solution.py:587
  572.3 109.9 %collective-permute-start.41 = (bf16[256,2048]{1,0:T(8,128)(2,1)}, bf16[256,2048]{1,0:T(8,128)(2,1)S(1)}, u32[]{:S(2)}, u32[]{:S(2)}) collective-permute-start(bf16[256,2048]{1,0:T(8,128)(2,1)} %after.54), channel_id=1, source_target_pairs={{16,0},{24,8},{0,16},{8,24},{17,1},{25,9},{1,17},{9,25},{18,2},{26... | collective-permute-start | bytes 3145736 | tf_op jit(solution)/shard_map/ppermute | solution.py:637
  573.6 108.7 %collective-permute-start.40 = (bf16[256,2048]{1,0:T(8,128)(2,1)}, bf16[256,2048]{1,0:T(8,128)(2,1)S(1)}, u32[]{:S(2)}, u32[]{:S(2)}) collective-permute-start(bf16[256,2048]{1,0:T(8,128)(2,1)} %after.52), channel_id=1, source_target_pairs={{8,0},{0,8},{24,16},{16,24},{9,1},{1,9},{25,17},{17,25},{10,2},{2,... | collective-permute-start | bytes 3145736 | tf_op jit(solution)/shard_map/ppermute | solution.py:637
  687.6 119.1 %all-gather.11.cloned.1.call-start = ((), (), s32[]{:S(2)}) async-start(), calls=%async_computation.10 | async-start | bytes 5308416 | tf_op jit(solution)/shard_map/all_gather | solution.py:588
  687.7 13.0 %collective-permute-start.48 = (bf16[128,2048]{1,0:T(8,128)(2,1)}, bf16[128,2048]{1,0:T(8,128)(2,1)}, u32[]{:S(2)}, u32[]{:S(2)}) collective-permute-start(bf16[128,2048]{1,0:T(8,128)(2,1)} %get-tuple-element.135.refs_3_), channel_id=1, source_target_pairs={{8,0},{0,8},{24,16},{16,24},{9,1},{1,9},{25,17},{17,25},{10,2},{2,... | collective-permute-start | bytes 1572872 | tf_op jit(solution)/shard_map/ppermute | solution.py:637
  692.0 12.6 %collective-permute-start.47 = (bf16[128,2048]{1,0:T(8,128)(2,1)}, bf16[128,2048]{1,0:T(8,128)(2,1)S(1)}, u32[]{:S(2)}, u32[]{:S(2)}) collective-permute-start(bf16[128,2048]{1,0:T(8,128)(2,1)} %get-tuple-element.134.refs_2_), channel_id=1, source_target_pairs={{16,0},{24,8},{0,16},{8,24},{17,1},{25,9},{1,17},{9,25},{18,2},{26... | collective-permute-start | bytes 1572872 | tf_op jit(solution)/shard_map/ppermute | solution.py:637
  711.5 32.8 %collective-permute-start.49 = (bf16[64,2048]{1,0:T(8,128)(2,1)S(1)}, bf16[64,2048]{1,0:T(8,128)(2,1)S(1)}, u32[]{:S(2)}, u32[]{:S(2)}) collective-permute-start(bf16[64,2048]{1,0:T(8,128)(2,1)S(1)} %get-tuple-element.203), channel_id=1, source_target_pairs={{0,0},{3,1},{6,2},{1,3},{4,4},{7,5},{2,6},{5,7},{8,8},{11,9},{14,1... | collective-permute-start | bytes 786440 | tf_op jit(solution)/shard_map/ppermute | solution.py:784
  714.9 29.5 %collective-permute-start.50 = (bf16[64,2048]{1,0:T(8,128)(2,1)S(1)}, bf16[64,2048]{1,0:T(8,128)(2,1)S(1)}, u32[]{:S(2)}, u32[]{:S(2)}) collective-permute-start(bf16[64,2048]{1,0:T(8,128)(2,1)S(1)} %get-tuple-element.205), channel_id=1, source_target_pairs={{1,0},{4,1},{7,2},{2,3},{5,4},{0,5},{3,6},{6,7},{9,8},{12,9},{15,1... | collective-permute-start | bytes 786440 | tf_op jit(solution)/shard_map/ppermute | solution.py:784
  714.9 29.4 %collective-permute-start.51 = (bf16[64,2048]{1,0:T(8,128)(2,1)S(1)}, bf16[64,2048]{1,0:T(8,128)(2,1)S(1)}, u32[]{:S(2)}, u32[]{:S(2)}) collective-permute-start(bf16[64,2048]{1,0:T(8,128)(2,1)S(1)} %get-tuple-element.204), channel_id=1, source_target_pairs={{2,0},{5,1},{0,2},{3,3},{6,4},{1,5},{4,6},{7,7},{10,8},{13,9},{8,1... | collective-permute-start | bytes 786440 | tf_op jit(solution)/shard_map/ppermute | solution.py:784
  718.2 25.1 %collective-permute-start.44 = (f32[20480]{0:T(1024)S(1)}, f32[20480]{0:T(1024)S(1)}, u32[]{:S(2)}, u32[]{:S(2)}) collective-permute-start(f32[20480]{0:T(1024)S(1)} %add.242), channel_id=1, source_target_pairs={{0,4},{1,5},{2,6},{3,7},{4,0},{5,1},{6,2},{7,3},{8,12},{9,13},{10,... | collective-permute-start | bytes 245768 | tf_op jit(solution)/shard_map/ppermute | solution.py:752
  754.0 241.0 %reduce-scatter.11.cloned.1.call-start = ((), (), s32[]{:S(2)}) async-start(), calls=%async_computation.11 | async-start | bytes 9437184 | tf_op jit(solution)/shard_map/reduce_scatter | solution.py:1046
  926.5 13.5 %collective-permute-start.54 = (bf16[128,2048]{1,0:T(8,128)(2,1)}, bf16[128,2048]{1,0:T(8,128)(2,1)S(1)}, u32[]{:S(2)}, u32[]{:S(2)}) collective-permute-start(bf16[128,2048]{1,0:T(8,128)(2,1)} %get-tuple-element.148), channel_id=1, source_target_pairs={{8,0},{0,8},{24,16},{16,24},{9,1},{1,9},{25,17},{17,25},{10,2},{2,... | collective-permute-start | bytes 1572872 | tf_op jit(solution)/shard_map/ppermute | solution.py:637
  927.8 13.4 %collective-permute-start.56 = (bf16[128,2048]{1,0:T(8,128)(2,1)}, bf16[128,2048]{1,0:T(8,128)(2,1)S(1)}, u32[]{:S(2)}, u32[]{:S(2)}) collective-permute-start(bf16[128,2048]{1,0:T(8,128)(2,1)} %get-tuple-element.149), channel_id=1, source_target_pairs={{16,0},{24,8},{0,16},{8,24},{17,1},{25,9},{1,17},{9,25},{18,2},{26... | collective-permute-start | bytes 1572872 | tf_op jit(solution)/shard_map/ppermute | solution.py:637
  933.6 41.1 %collective-permute-start.52 = (bf16[256,2048]{1,0:T(8,128)(2,1)S(1)}, bf16[256,2048]{1,0:T(8,128)(2,1)S(1)}, u32[]{:S(2)}, u32[]{:S(2)}) collective-permute-start(bf16[256,2048]{1,0:T(8,128)(2,1)S(1)} %copy-done.66), channel_id=1, source_target_pairs={{8,0},{0,8},{24,16},{16,24},{9,1},{1,9},{25,17},{17,25},{10,2},{2,... | collective-permute-start | bytes 3145736 | tf_op jit(solution)/shard_map/ppermute | solution.py:637
  933.9 40.8 %collective-permute-start.53 = (bf16[256,2048]{1,0:T(8,128)(2,1)S(1)}, bf16[256,2048]{1,0:T(8,128)(2,1)S(1)}, u32[]{:S(2)}, u32[]{:S(2)}) collective-permute-start(bf16[256,2048]{1,0:T(8,128)(2,1)S(1)} %copy-done.65), channel_id=1, source_target_pairs={{16,0},{24,8},{0,16},{8,24},{17,1},{25,9},{1,17},{9,25},{18,2},{26... | collective-permute-start | bytes 3145736 | tf_op jit(solution)/shard_map/ppermute | solution.py:637
  940.1 34.6 %collective-permute-start.55 = (bf16[128,2048]{1,0:T(8,128)(2,1)S(1)}, bf16[128,2048]{1,0:T(8,128)(2,1)S(1)}, u32[]{:S(2)}, u32[]{:S(2)}) collective-permute-start(bf16[128,2048]{1,0:T(8,128)(2,1)S(1)} %collective-permute-done.54), channel_id=1, source_target_pairs={{16,0},{24,8},{0,16},{8,24},{17,1},{25,9},{1,17},{9,25},{18,2},{26... | collective-permute-start | bytes 1572872 | tf_op jit(solution)/shard_map/ppermute | solution.py:637
  941.2 33.4 %collective-permute-start.57 = (bf16[128,2048]{1,0:T(8,128)(2,1)S(1)}, bf16[128,2048]{1,0:T(8,128)(2,1)S(1)}, u32[]{:S(2)}, u32[]{:S(2)}) collective-permute-start(bf16[128,2048]{1,0:T(8,128)(2,1)S(1)} %collective-permute-done.56), channel_id=1, source_target_pairs={{8,0},{0,8},{24,16},{16,24},{9,1},{1,9},{25,17},{17,25},{10,2},{2,... | collective-permute-start | bytes 1572872 | tf_op jit(solution)/shard_map/ppermute | solution.py:637
  977.4 14.0 %collective-permute-start.59 = (bf16[64,2048]{1,0:T(8,128)(2,1)S(1)}, bf16[64,2048]{1,0:T(8,128)(2,1)S(1)}, u32[]{:S(2)}, u32[]{:S(2)}) collective-permute-start(bf16[64,2048]{1,0:T(8,128)(2,1)S(1)} %get-tuple-element.202), channel_id=1, source_target_pairs={{1,0},{4,1},{7,2},{2,3},{5,4},{0,5},{3,6},{6,7},{9,8},{12,9},{15,1... | collective-permute-start | bytes 786440 | tf_op jit(solution)/shard_map/ppermute | solution.py:784
  977.6 15.0 %collective-permute-start.60 = (bf16[64,2048]{1,0:T(8,128)(2,1)S(1)}, bf16[64,2048]{1,0:T(8,128)(2,1)S(1)}, u32[]{:S(2)}, u32[]{:S(2)}) collective-permute-start(bf16[64,2048]{1,0:T(8,128)(2,1)S(1)} %get-tuple-element.201), channel_id=1, source_target_pairs={{2,0},{5,1},{0,2},{3,3},{6,4},{1,5},{4,6},{7,7},{10,8},{13,9},{8,1... | collective-permute-start | bytes 786440 | tf_op jit(solution)/shard_map/ppermute | solution.py:784
  (74 other events, 584.9 us)
Sparse Core Ops, SparseCore 0:
  12.8 93.2 all-gather.4
  107.7 81.8 all-gather.6
  462.6 55.3 reduce-scatter.4
  519.5 52.6 all-gather.8
  574.3 85.8 reduce-scatter.6
  687.7 64.7 reduce-scatter.8
  754.1 52.5 all-gather.10
  809.0 85.8 reduce-scatter.10

commit v4 on v3

--- a/solution.py
+++ b/solution.py
@@ -364,15 +364,23 @@
 
 def symmetric(lhs, rhs, size, epilogue):
     for panel, height, columns in panels(size):
+        top = height - CHUNK
         epilogue(
-            panel, height, columns, jnp.dot(lhs[:height, :], rhs[:, columns], preferred_element_type=F32)
+            panel, 0, top, columns, jnp.dot(lhs[:top, :], rhs[:, columns], preferred_element_type=F32)
         )
-
-
-def put_mirrored(ref, height, columns, values):
-    ref[:height, columns] = values
-    if height > PANEL:
-        ref[columns, : height - PANEL] = values[: height - PANEL, :].T
+        right = slice(columns.stop - CHUNK, columns.stop)
+        epilogue(
+            panel, top, height, right, jnp.dot(lhs[top:height, :], rhs[:, right], preferred_element_type=F32)
+        )
+
+
+def put_mirrored(ref, top, height, columns, values):
+    ref[top:height, columns] = values
+    if top == 0:
+        above = height - CHUNK
+        if above:
+            ref[columns, :above] = values[:above, :].T
+        ref[columns.start + CHUNK : columns.stop, above : above + CHUNK] = values[above:, CHUNK:].T
 
 
 def gram_packed(x, xt_ref, size, packed_ref):
@@ -444,10 +452,14 @@
     def one(step, carry):
         source, target = step % 2, (step + 1) % 2
 
-        def poly_end(panel, height, columns, product):
-            at = tri(panel) * PANEL
-            values = NS_B * exact_s[at : at + height, :] + NS_C * product
-            put_mirrored(poly_s, height, columns, values.astype(BF16))
+        def exact_at(panel, top, height, columns):
+            first = columns.start % PANEL
+            lanes = slice(first, first + columns.stop - columns.start)
+            return slice(tri(panel) * PANEL + top, tri(panel) * PANEL + height), lanes
+
+        def poly_end(panel, top, height, columns, product):
+            values = NS_B * exact_s[exact_at(panel, top, height, columns)] + NS_C * product
+            put_mirrored(poly_s, top, height, columns, values.astype(BF16))
 
         symmetric(low_s, low_s, size, poly_end)
 
@@ -461,20 +473,18 @@
 
         @pl.when(step < count - 1)
         def next_gram():
-            def mix_end(panel, height, columns, product):
-                at = tri(panel) * PANEL
-                exact_s[at : at + height, :] = (NS_A * NS_A) * exact_s[at : at + height, :] + (
-                    2.0 * NS_A
-                ) * product
-                put_mirrored(mix_s, height, columns, product.astype(BF16))
+            def mix_end(panel, top, height, columns, product):
+                at = exact_at(panel, top, height, columns)
+                exact_s[at] = (NS_A * NS_A) * exact_s[at] + (2.0 * NS_A) * product
+                put_mirrored(mix_s, top, height, columns, product.astype(BF16))
 
             symmetric(low_s, poly_s, size, mix_end)
 
-            def gram_end(panel, height, columns, product):
-                at = tri(panel) * PANEL
-                values = exact_s[at : at + height, :] + product
-                exact_s[at : at + height, :] = values
-                put_mirrored(low_s, height, columns, values.astype(BF16))
+            def gram_end(panel, top, height, columns, product):
+                at = exact_at(panel, top, height, columns)
+                values = exact_s[at] + product
+                exact_s[at] = values
+                put_mirrored(low_s, top, height, columns, values.astype(BF16))
 
             symmetric(mix_s, poly_s, size, gram_end)
 

time: 1010 us -> 998 us (0.988)
  Pallas kernels: 420 us -> 405 us
  transfers between devices with their start and end apart: 69 -> 69, of which waited for: 26 -> 26; matrix products, arithmetic and copies ran while one was open for 16% -> 16% of each run, Pallas kernels for 37% -> 36%
where the time goes in v4:
time: 998 us; the launch traced here: 993 us
  Pallas kernels  405 us (41%)
  waiting for transfers between devices  290 us (29%)
  starting transfers between devices  99.9 us (10%)
  other arithmetic  68.9 us (7%)
  local copies, waits for them, and re-layouts  64.2 us (6%)
  matrix products  48.7 us (5%)
  between operations  15.8 us (2%)
    pallas_call x1, Pallas kernels, orthogonalize(): pl.pallas_call(functools.partial(second_body, 3), out_shape=[jax.ShapeDty...  109 us
    ppermute x44, waiting for transfers between devices, hop(): return lax.ppermute(values, 'dp', [(t ^ bit, t) for t in targets])  109 us
    all_gather x2, waiting for transfers between devices, gram_sum(): lax.all_gather(after(part, *jax.tree.leaves(meanwhile)), 'group', axis=0,...  107 us
    pallas_call x1, Pallas kernels, orthogonalize(): pl.pallas_call(functools.partial(first_body, 2), out_shape=(x_shape, pack...  102 us
    ppermute x44, starting transfers between devices, hop(): return lax.ppermute(values, 'dp', [(t ^ bit, t) for t in targets])  61.6 us
    pallas_call x4, Pallas kernels, by_columns(): pl.pallas_call(body, grid=(steps,), in_specs=([] if scalar is None else [...  54.9 us
    pallas_call x4, Pallas kernels, by_rows(): pl.pallas_call(body, grid=(steps,), in_specs=[pl.BlockSpec((rows, one.sha...  51.3 us
    dot_general x4, matrix products, dot(): return jnp.dot(left, right, preferred_element_type=F32)  48.7 us
  transfers between devices with their start and end apart: 69, of which 26 were waited for; matrix products, arithmetic and copies ran while one was open for 16% of the time, Pallas kernels for 36%

profile of v4, /device:TPU:1, one launch (start us, length us, event | category | flops | bytes accessed | tf_op | source)
XLA Modules:
  0.0 993.0 jit_solution(16471268984901611155)
XLA Ops:
  19.6 4.2 collective-permute-start.2
  25.7 4.4 collective-permute-start.1
  38.9 11.8 %collective-permute-done = bf16[64,2048]{1,0:T(8,128)(2,1)} collective-permute-done((bf16[64,2048]{1,0:T(8,128)(2,1)}, bf16[64,2048]{1,0:T(8,128)(2,1)}, u32[]{:S(2)}, u32[]{:S(2)}) %collective-permute-start) | collective-permute-done | bytes 262176 | tf_op jit(solution)/shard_map/ppermute | solution.py:776
  59.3 8.3 collective-permute-done.6
  69.1 3.3 pad_maximum_fusion.1.refs_2_
  72.5 10.9 %collective-permute-done.3.refs_0_.refs_3_.refs_1_ = bf16[192,2048]{1,0:T(8,128)(2,1)} collective-permute-done((bf16[192,2048]{1,0:T(8,128)(2,1)S(1)}, bf16[192,2048]{1,0:T(8,128)(2,1)}, u32[]{:S(2)}, u32[]{:S(2)}) %collective-permute-start.3) | collective-permute-done | bytes 786464 | tf_op jit(solution)/shard_map/ppermute | solution.py:647
  84.8 21.3 %all-gather.5.cloned.1.call-done.x_ref.refs_1_.r_ref = bf16[2048,2048]{1,0:T(8,128)(2,1)} async-done(((bf16[256,2048]{1,0:T(8,128)(2,1)}), bf16[2048,2048]{1,0:T(8,128)(2,1)}) %all-gather.5.cloned.1.call-update) | async-done | bytes 8388624 | tf_op jit(solution)/shard_map/all_gather | solution.py:884
  113.0 4.9 broadcast_multiply_fusion
  117.9 18.7 %up_forward.1 = (bf16[2048,1024]{1,0:T(8,128)(2,1)}, bf16[2048,1024]{1,0:T(8,128)(2,1)}) custom-call(bf16[2048,2048]{1,0:T(8,128)(2,1)} %all-gather.5.cloned.1.call-done.x_ref.refs_1_.r_ref, bf16[1024,2048]{1,0:T(8,128)(2,1)} %bitcast.204, f32[1,1024]{1,0:T(1,128)} %bitcast.255), custom_call_target="tpu_custom_call" | custom-call | tf_op jit(solution)/shard_map/up_forward/pallas_call | solution.py:77
  141.5 2.7 slice_bitcast_fusion.2.refs_0_
  156.8 11.6 %project_qkv.1.refs_3_.pre_ref = f32[2048,768]{1,0:T(8,128)} custom-call(bf16[2048,2048]{1,0:T(8,128)(2,1)} %all-gather.5.cloned.1.call-done.x_ref.refs_1_.r_ref, bf16[768,2048]{1,0:T(8,128)(2,1)} %bitcast.225, f32[1,768]{1,0:T(1,128)} %broadcast_in_dim_reshape.7.b_ref), custom_call_target="tpu_custom_call" | custom-call | tf_op jit(solution)/shard_map/project_qkv/pallas_call | solution.py:77
  175.7 11.7 %fusion.41.refs_6_ = f32[2048,2048]{1,0:T(8,128)} fusion(bf16[2048,1024]{1,0:T(8,128)(2,1)S(1)} %copy-done, bf16[1024,2048]{1,0:T(8,128)(2,1)S(1)} %bitcast.201), kind=kOutput, calls=%fused_computation.185 | convolution fusion | flops 8589934592 | bytes 25165824 | tf_op jit(solution)/shard_map/dot_general | solution.py:853
  189.6 14.3 %grad_down.1 = (bf16[256,2048]{1,0:T(8,128)(2,1)}, bf16[256,2048]{1,0:T(8,128)(2,1)}, bf16[256,2048]{1,0:T(8,128)(2,1)}, bf16[256,2048]{1,0:T(8,128)(2,1)}) custom-call(bf16[2048,1024]{1,0:T(8,128)(2,1)} %get-tuple-element.82.refs_1_.l_ref, bf16[2048,2048]{1,0:T(8,128)(2,1)} %after.35.r_ref.g_ref.x_ref.q_ref), custom_call_target="tpu_custom_call" | custom-call | tf_op jit(solution)/shard_map/grad_down/pallas_call | solution.py:95
  205.1 2.7 fusion.40
  209.8 6.6 collective-permute-start.24
  221.2 14.3 %up_backward.1.l_ref.refs_0_ = bf16[2048,1024]{1,0:T(8,128)(2,1)} custom-call(bf16[2048,2048]{1,0:T(8,128)(2,1)} %after.35.r_ref.g_ref.x_ref.q_ref, bf16[2048,1024]{1,0:T(8,128)(2,1)} %after.36.s_ref, bf16[1024,2048]{1,0:T(8,128)(2,1)} %bitcast.203), custom_call_target="tpu_custom_call" | custom-call | tf_op jit(solution)/shard_map/up_backward/pallas_call | solution.py:77
  235.5 14.5 %grad_up.1 = (bf16[256,2048]{1,0:T(8,128)(2,1)}, bf16[256,2048]{1,0:T(8,128)(2,1)}, bf16[256,2048]{1,0:T(8,128)(2,1)}, bf16[256,2048]{1,0:T(8,128)(2,1)}) custom-call(bf16[2048,1024]{1,0:T(8,128)(2,1)} %up_backward.1.l_ref.refs_0_, bf16[2048,2048]{1,0:T(8,128)(2,1)} %all-gather.5.cloned.1.call-done.x_ref.refs_1_.r_ref), custom_call_target="tpu_custom_call" | custom-call | tf_op jit(solution)/shard_map/grad_up/pallas_call | solution.py:95
  254.6 4.0 scatter_next.3
  262.2 6.7 project_grad.1.refs_0_
  271.2 20.9 %attention.2 = (bf16[2048,128]{1,0:T(8,128)(2,1)}, bf16[2048,384]{1,0:T(8,128)(2,1)}) custom-call(s32[8]{0:T(128)} %and_select_fusion.6.refs_5_.first_ref, f32[2048,768]{1,0:T(8,128)} %project_qkv.1.refs_3_.pre_ref, bf16[2048,256]{1,0:T(8,128)(2,1)} %after.38.grad_ref, s32[2048,1]{1,0:T(8,128)} %subtract_subtract_fusion.refs_6_.start_ref, ...), custom_call_target="tpu_custom_call" | custom-call | tf_op jit(solution)/shard_map/attention/pallas_call | solution.py:328
  292.0 2.7 copy.100.refs_0_
  294.8 4.0 scatter_next.4
  299.4 3.8 collective-permute-start.20
  304.3 4.5 momentum.2
  308.9 13.0 %weight_grads_plus.2 = (bf16[384,2048]{1,0:T(8,128)(2,1)}, bf16[128,2048]{1,0:T(8,128)(2,1)}, bf16[192,2048]{1,0:T(8,128)(2,1)}, bf16[192,2048]{1,0:T(8,128)(2,1...) custom-call(s32[1]{0:T(128)} %bitcast.42.me_ref, bf16[2048,384]{1,0:T(8,128)(2,1)} %after.39.l_ref, ...), custom_call_target="tpu_custom_call" | custom-call | tf_op jit(solution)/shard_map/weight_grads_plus/pallas_call | solution.py:95
  323.6 4.5 momentum.3
  328.1 3.6 to_owners.1
  331.8 21.0 %attention.3 = (bf16[2048,128]{1,0:T(8,128)(2,1)}, bf16[2048,384]{1,0:T(8,128)(2,1)}) custom-call(s32[8]{0:T(128)} %and_select_fusion.6.refs_5_.first_ref, f32[2048,768]{1,0:T(8,128)} %project_qkv.1.refs_3_.pre_ref, bf16[2048,256]{1,0:T(8,128)(2,1)} %after.41.grad_ref, s32[2048,1]{1,0:T(8,128)} %subtract_subtract_fusion.refs_6_.start_ref, ...), custom_call_target="tpu_custom_call" | custom-call | tf_op jit(solution)/shard_map/attention/pallas_call | solution.py:328
  352.7 3.3 pad_maximum_fusion.7.refs_0_
  356.0 4.2 reduce_next.2
  360.3 13.1 %weight_grads_plus.3 = (bf16[384,2048]{1,0:T(8,128)(2,1)}, bf16[128,2048]{1,0:T(8,128)(2,1)}, bf16[192,2048]{1,0:T(8,128)(2,1)}, bf16[192,2048]{1,0:T(8,128)(2,1...) custom-call(s32[1]{0:T(128)} %bitcast.42.me_ref, bf16[2048,384]{1,0:T(8,128)(2,1)} %after.42.l_ref, ...), custom_call_target="tpu_custom_call" | custom-call | tf_op jit(solution)/shard_map/weight_grads_plus/pallas_call | solution.py:95
  374.9 7.6 collective-permute-start.32
  385.2 7.3 collective-permute-done.32
  392.5 3.5 collective-permute-start.28
  397.2 12.1 %collective-permute-done.37.refs_3_ = bf16[192,2048]{1,0:T(8,128)(2,1)} collective-permute-done((bf16[192,2048]{1,0:T(8,128)(2,1)}, bf16[192,2048]{1,0:T(8,128)(2,1)}, u32[]{:S(2)}, u32[]{:S(2)}) %collective-permute-start.37) | collective-permute-done | bytes 786464 | tf_op jit(solution)/shard_map/ppermute | solution.py:647
  409.3 5.0 collective-permute-start.34
  414.3 4.2 reduce_next.3
  420.7 6.1 collective-permute-done.33.refs_4_
  426.8 6.2 collective-permute-start.38
  435.7 12.7 %collective-permute-done.31.refs_3_ = bf16[128,2048]{1,0:T(8,128)(2,1)S(1)} collective-permute-done((bf16[128,2048]{1,0:T(8,128)(2,1)}, bf16[128,2048]{1,0:T(8,128)(2,1)S(1)}, u32[]{:S(2)}, u32[]{:S(2)}) %collective-permute-start.31) | collective-permute-done | bytes 524320 | tf_op jit(solution)/shard_map/ppermute | solution.py:647
  448.3 3.8 collective-permute-done.39.refs_12_
  453.1 13.0 %gram.1 = (bf16[1024,2048]{1,0:T(8,128)(2,1)}, bf16[9216,256]{1,0:T(8,128)(2,1)}) custom-call(s32[1]{0:T(128)} %bitcast.42.me_ref, bf16[256,2048]{1,0:T(8,128)(2,1)} %get-tuple-element.110.refs_0_, bf16[256,2048]{1,0:T(8,128)(2,1)} %copy-done.46, bf16[256,2048]{1,0:T(8,128)(2,1)} %collective-permute-done.27.refs_2_, bf16[128,2048]{1,0:T(8,128)(2,1)} %copy-done.54, ...), custom_call_target="tpu_custom_call" | custom-call | tf_op jit(solution)/shard_map/gram/pallas_call | solution.py:576
  481.0 11.9 %add_convert_fusion.1.refs_8_.refs_0_ = bf16[2048,2048]{1,0:T(8,128)(2,1)} fusion(f32[2048,2048]{1,0:T(8,128)} %fusion.41.refs_6_, bf16[2048,256]{1,0:T(8,128)(2,1)S(1)} %copy-done.25, bf16[256,2048]{1,0:T(8,128)(2,1)S(1)} %bitcast.219), kind=kOutput, calls=%fused_computation.1 | convolution fusion | flops 2155872256 | bytes 27262976 | tf_op jit(solution)/shard_map/dot_general | solution.py:853
  492.9 11.7 %fusion.42 = f32[2048,2048]{1,0:T(8,128)} fusion(bf16[2048,1024]{1,0:T(8,128)(2,1)S(1)} %copy-done.1, bf16[1024,2048]{1,0:T(8,128)(2,1)S(1)} %bitcast.205), kind=kOutput, calls=%fused_computation.186 | convolution fusion | flops 8589934592 | bytes 25165824 | tf_op jit(solution)/shard_map/dot_general | solution.py:853
  504.6 13.4 %add_convert_fusion.refs_1_.refs_0_ = bf16[2048,2048]{1,0:T(8,128)(2,1)} fusion(f32[2048,2048]{1,0:T(8,128)} %fusion.42, bf16[2048,768]{1,0:T(8,128)(2,1)S(1)} %copy-done.2, bf16[768,2048]{1,0:T(8,128)(2,1)} %bitcast.226), kind=kOutput, calls=%fused_computation | convolution fusion | flops 6450839552 | bytes 31457280 | tf_op jit(solution)/shard_map/dot_general | solution.py:853
  518.0 3.7 reduce-scatter.5.cloned.1.call-done.refs_0_
  521.7 54.1 %all-gather.9.cloned.1.call-done.packed_ref.refs_1_ = bf16[9216,256]{1,0:T(8,128)(2,1)} async-done(((bf16[1152,256]{1,0:T(8,128)(2,1)}), bf16[9216,256]{1,0:T(8,128)(2,1)}) %all-gather.9.cloned.1.call-update) | async-done | bytes 4718608 | tf_op jit(solution)/shard_map/all_gather | solution.py:598
  578.3 101.8 %first_steps.1 = (bf16[1024,2048]{1,0:T(8,128)(2,1)}, bf16[9216,256]{1,0:T(8,128)(2,1)}) custom-call(bf16[9216,256]{1,0:T(8,128)(2,1)} %all-gather.9.cloned.1.call-done.packed_ref.refs_1_, bf16[1024,2048]{1,0:T(8,128)(2,1)} %get-tuple-element.132.x_ref), custom_call_target="tpu_custom_call" | custom-call | tf_op jit(solution)/shard_map/first_steps/pallas_call | solution.py:614
  681.4 4.0 scatter_next.5
  685.9 3.1 convert_reduce_fusion
  690.2 8.4 collective-permute-done.48
  709.4 3.3 collective-permute-start.49
  712.8 3.3 collective-permute-start.51
  717.6 3.9 fusion.34
  721.4 19.7 %collective-permute-done.44 = f32[20480]{0:T(1024)S(1)} collective-permute-done((f32[20480]{0:T(1024)S(1)}, f32[20480]{0:T(1024)S(1)}, u32[]{:S(2)}, u32[]{:S(2)}) %collective-permute-start.44) | collective-permute-done | bytes 81952 | tf_op jit(solution)/shard_map/ppermute | solution.py:762
  742.4 3.3 collective-permute-done.45
  745.9 5.2 fusion.35
  751.9 52.7 %all-gather.11.cloned.1.call-done.refs_1_.packed_ref = bf16[9216,256]{1,0:T(8,128)(2,1)} async-done(((bf16[1152,256]{1,0:T(8,128)(2,1)}), bf16[9216,256]{1,0:T(8,128)(2,1)}) %all-gather.11.cloned.1.call-update) | async-done | bytes 4718608 | tf_op jit(solution)/shard_map/all_gather | solution.py:598
  805.1 109.3 %last_steps.1 = (bf16[256,2048]{1,0:T(8,128)(2,1)}, bf16[256,2048]{1,0:T(8,128)(2,1)}, bf16[256,2048]{1,0:T(8,128)(2,1)}, bf16[128,2048]{1,0:T(8,128)(2,1)}, bf16[128,2048]{1,0:T(8,128)(2,1)}) custom-call(s32[16]{0:T(128)} %broadcast_select_fusion.1.from_ref, bf16[9216,256]{1,0:T(8,128)(2,1)} %all-gather.11.cloned.1.call-done.refs_1_.packed_ref, ...), custom_call_target="tpu_custom_call" | custom-call | tf_op jit(solution)/shard_map/last_steps/pallas_call | solution.py:629
  916.9 4.6 maximum_add_fusion.1
  922.2 5.7 collective-permute-done.54
  934.1 28.7 %collective-permute-done.55 = bf16[128,2048]{1,0:T(8,128)(2,1)S(1)} collective-permute-done((bf16[128,2048]{1,0:T(8,128)(2,1)S(1)}, bf16[128,2048]{1,0:T(8,128)(2,1)S(1)}, u32[]{:S(2)}, u32[]{:S(2)}) %collective-permute-start.55) | collective-permute-done | bytes 524320 | tf_op jit(solution)/shard_map/ppermute | solution.py:647
  965.6 2.9 collective-permute-start.60
  973.2 6.6 collective-permute-done.59
  (411 shorter events, 159.1 us)
Async XLA Ops:
  7.2 98.9 %all-gather.5.cloned.1.call-start = ((), (), s32[]{:S(2)}) async-start(), calls=%async_computation.4 | async-start | bytes 9437184 | tf_op jit(solution)/shard_map/all_gather | solution.py:884
  12.7 176.9 %all-gather.7.cloned.1.call-start = ((), (), s32[]{:S(2)}) async-start(), calls=%async_computation.5 | async-start | bytes 9437184 | tf_op jit(solution)/shard_map/all_gather | solution.py:888
  14.3 39.1 %collective-permute-start.5 = (bf16[256,2048]{1,0:T(8,128)(2,1)}, bf16[256,2048]{1,0:T(8,128)(2,1)S(1)}, u32[]{:S(2)}, u32[]{:S(2)}) collective-permute-start(bf16[256,2048]{1,0:T(8,128)(2,1)} %get-tuple-element.185), channel_id=1, source_target_pairs={{16,0},{24,8},{0,16},{8,24},{17,1},{25,9},{1,17},{9,25},{18,2},{26... | collective-permute-start | bytes 3145736 | tf_op jit(solution)/shard_map/ppermute | solution.py:647
  16.4 37.2 %collective-permute-start.4 = (bf16[256,2048]{1,0:T(8,128)(2,1)}, bf16[256,2048]{1,0:T(8,128)(2,1)}, u32[]{:S(2)}, u32[]{:S(2)}) collective-permute-start(bf16[256,2048]{1,0:T(8,128)(2,1)} %get-tuple-element.185), channel_id=1, source_target_pairs={{8,0},{0,8},{24,16},{16,24},{9,1},{1,9},{25,17},{17,25},{10,2},{2,... | collective-permute-start | bytes 3145736 | tf_op jit(solution)/shard_map/ppermute | solution.py:647
  19.6 19.3 %collective-permute-start.2 = (bf16[64,2048]{1,0:T(8,128)(2,1)}, bf16[64,2048]{1,0:T(8,128)(2,1)S(1)}, u32[]{:S(2)}, u32[]{:S(2)}) collective-permute-start(bf16[64,2048]{1,0:T(8,128)(2,1)} %get-tuple-element.183), channel_id=1, source_target_pairs={{0,2},{1,5},{2,0},{3,3},{4,6},{5,1},{6,4},{7,7},{8,10},{9,13},{10,... | collective-permute-start | bytes 786440 | tf_op jit(solution)/shard_map/ppermute | solution.py:776
  23.8 27.0 %collective-permute-start = (bf16[64,2048]{1,0:T(8,128)(2,1)}, bf16[64,2048]{1,0:T(8,128)(2,1)}, u32[]{:S(2)}, u32[]{:S(2)}) collective-permute-start(bf16[64,2048]{1,0:T(8,128)(2,1)} %get-tuple-element.181), channel_id=1, source_target_pairs={{0,0},{1,3},{2,6},{3,1},{4,4},{5,7},{6,2},{7,5},{8,8},{9,11},{10,1... | collective-permute-start | bytes 786440 | tf_op jit(solution)/shard_map/ppermute | solution.py:776
  25.7 26.6 %collective-permute-start.1 = (bf16[64,2048]{1,0:T(8,128)(2,1)}, bf16[64,2048]{1,0:T(8,128)(2,1)}, u32[]{:S(2)}, u32[]{:S(2)}) collective-permute-start(bf16[64,2048]{1,0:T(8,128)(2,1)} %get-tuple-element.182), channel_id=1, source_target_pairs={{0,1},{1,4},{2,7},{3,2},{4,5},{5,0},{6,3},{7,6},{8,9},{9,12},{10,1... | collective-permute-start | bytes 786440 | tf_op jit(solution)/shard_map/ppermute | solution.py:776
  53.5 14.1 %collective-permute-start.6 = (bf16[128,2048]{1,0:T(8,128)(2,1)S(1)}, bf16[128,2048]{1,0:T(8,128)(2,1)S(1)}, u32[]{:S(2)}, u32[]{:S(2)}) collective-permute-start(bf16[128,2048]{1,0:T(8,128)(2,1)S(1)} %slice.201), channel_id=1, source_target_pairs={{8,0},{0,8},{24,16},{16,24},{9,1},{1,9},{25,17},{17,25},{10,2},{2,... | collective-permute-start | bytes 1572872 | tf_op jit(solution)/shard_map/ppermute | solution.py:647
  54.9 14.1 %collective-permute-start.7 = (bf16[128,2048]{1,0:T(8,128)(2,1)S(1)}, bf16[128,2048]{1,0:T(8,128)(2,1)S(1)}, u32[]{:S(2)}, u32[]{:S(2)}) collective-permute-start(bf16[128,2048]{1,0:T(8,128)(2,1)S(1)} %slice.202), channel_id=1, source_target_pairs={{16,0},{24,8},{0,16},{8,24},{17,1},{25,9},{1,17},{9,25},{18,2},{26... | collective-permute-start | bytes 1572872 | tf_op jit(solution)/shard_map/ppermute | solution.py:647
  56.1 27.3 %collective-permute-start.3 = (bf16[192,2048]{1,0:T(8,128)(2,1)S(1)}, bf16[192,2048]{1,0:T(8,128)(2,1)}, u32[]{:S(2)}, u32[]{:S(2)}) collective-permute-start(bf16[192,2048]{1,0:T(8,128)(2,1)S(1)} %get-tuple-element.207), channel_id=1, source_target_pairs={{8,0},{0,8},{24,16},{16,24},{9,1},{1,9},{25,17},{17,25},{10,2},{2,... | collective-permute-start | bytes 2359304 | tf_op jit(solution)/shard_map/ppermute | solution.py:647
  57.3 27.5 %collective-permute-start.8 = (bf16[192,2048]{1,0:T(8,128)(2,1)S(1)}, bf16[192,2048]{1,0:T(8,128)(2,1)S(1)}, u32[]{:S(2)}, u32[]{:S(2)}) collective-permute-start(bf16[192,2048]{1,0:T(8,128)(2,1)S(1)} %get-tuple-element.207), channel_id=1, source_target_pairs={{16,0},{24,8},{0,16},{8,24},{17,1},{25,9},{1,17},{9,25},{18,2},{26... | collective-permute-start | bytes 2359304 | tf_op jit(solution)/shard_map/ppermute | solution.py:647
  106.2 415.4 %reduce-scatter.5.cloned.1.call-start = ((), (), s32[]{:S(2)}) async-start(), calls=%async_computation.6 | async-start | bytes 5308416 | tf_op jit(solution)/shard_map/reduce_scatter | solution.py:597
  109.6 34.6 %collective-permute-start.12 = (bf16[320,2048]{1,0:T(8,128)(2,1)}, bf16[320,2048]{1,0:T(8,128)(2,1)S(1)}, u32[]{:S(2)}, u32[]{:S(2)}) collective-permute-start(bf16[320,2048]{1,0:T(8,128)(2,1)} %after.32), channel_id=1, source_target_pairs={{16,0},{24,8},{0,16},{8,24},{17,1},{25,9},{1,17},{9,25},{18,2},{26... | collective-permute-start | bytes 3932168 | tf_op jit(solution)/shard_map/ppermute | solution.py:647
  110.4 36.7 %collective-permute-start.11 = (bf16[320,2048]{1,0:T(8,128)(2,1)}, bf16[320,2048]{1,0:T(8,128)(2,1)S(1)}, u32[]{:S(2)}, u32[]{:S(2)}) collective-permute-start(bf16[320,2048]{1,0:T(8,128)(2,1)} %after.32), channel_id=1, source_target_pairs={{8,0},{0,8},{24,16},{16,24},{9,1},{1,9},{25,17},{17,25},{10,2},{2,... | collective-permute-start | bytes 3932168 | tf_op jit(solution)/shard_map/ppermute | solution.py:647
  138.4 12.9 %collective-permute-start.10 = (bf16[96,2048]{1,0:T(8,128)(2,1)}, bf16[96,2048]{1,0:T(8,128)(2,1)}, u32[]{:S(2)}, u32[]{:S(2)}) collective-permute-start(bf16[96,2048]{1,0:T(8,128)(2,1)} %slice.204), channel_id=1, source_target_pairs={{16,0},{24,8},{0,16},{8,24},{17,1},{25,9},{1,17},{9,25},{18,2},{26... | collective-permute-start | bytes 1179656 | tf_op jit(solution)/shard_map/ppermute | solution.py:647
  140.7 10.6 %collective-permute-start.9 = (bf16[96,2048]{1,0:T(8,128)(2,1)}, bf16[96,2048]{1,0:T(8,128)(2,1)}, u32[]{:S(2)}, u32[]{:S(2)}) collective-permute-start(bf16[96,2048]{1,0:T(8,128)(2,1)} %slice.203), channel_id=1, source_target_pairs={{8,0},{0,8},{24,16},{16,24},{9,1},{1,9},{25,17},{17,25},{10,2},{2,... | collective-permute-start | bytes 1179656 | tf_op jit(solution)/shard_map/ppermute | solution.py:647
  146.4 22.0 %collective-permute-start.13 = (bf16[160,2048]{1,0:T(8,128)(2,1)S(1)}, bf16[160,2048]{1,0:T(8,128)(2,1)S(1)}, u32[]{:S(2)}, u32[]{:S(2)}) collective-permute-start(bf16[160,2048]{1,0:T(8,128)(2,1)S(1)} %slice.205), channel_id=1, source_target_pairs={{8,0},{0,8},{24,16},{16,24},{9,1},{1,9},{25,17},{17,25},{10,2},{2,... | collective-permute-start | bytes 1966088 | tf_op jit(solution)/shard_map/ppermute | solution.py:647
  150.3 18.1 %collective-permute-start.14 = (bf16[160,2048]{1,0:T(8,128)(2,1)}, bf16[160,2048]{1,0:T(8,128)(2,1)S(1)}, u32[]{:S(2)}, u32[]{:S(2)}) collective-permute-start(bf16[160,2048]{1,0:T(8,128)(2,1)} %slice.206), channel_id=1, source_target_pairs={{16,0},{24,8},{0,16},{8,24},{17,1},{25,9},{1,17},{9,25},{18,2},{26... | collective-permute-start | bytes 1966088 | tf_op jit(solution)/shard_map/ppermute | solution.py:647
  203.9 50.6 %collective-permute-start.15 = (bf16[256,2048]{1,0:T(8,128)(2,1)}, bf16[256,2048]{1,0:T(8,128)(2,1)}, u32[]{:S(2)}, u32[]{:S(2)}) collective-permute-start(bf16[256,2048]{1,0:T(8,128)(2,1)} %get-tuple-element.85.refs_1_), channel_id=1, source_target_pairs={{8,0},{0,8},{24,16},{16,24},{9,1},{1,9},{25,17},{17,25},{10,2},{2,... | collective-permute-start | bytes 3145736 | tf_op jit(solution)/shard_map/ppermute | solution.py:647
  207.9 42.1 %collective-permute-start.23 = (f32[64,2048]{1,0:T(8,128)}, f32[64,2048]{1,0:T(8,128)}, u32[]{:S(2)}, u32[]{:S(2)}) collective-permute-start(f32[64,2048]{1,0:T(8,128)} %get-tuple-element.189), channel_id=1, source_target_pairs={{0,0},{1,3},{2,6},{3,1},{4,4},{5,7},{6,2},{7,5},{8,8},{9,11},{10,1... | collective-permute-start | bytes 1572872 | tf_op jit(solution)/shard_map/ppermute | solution.py:776
  209.8 40.7 %collective-permute-start.24 = (f32[64,2048]{1,0:T(8,128)}, f32[64,2048]{1,0:T(8,128)}, u32[]{:S(2)}, u32[]{:S(2)}) collective-permute-start(f32[64,2048]{1,0:T(8,128)} %get-tuple-element.191), channel_id=1, source_target_pairs={{0,1},{1,4},{2,7},{3,2},{4,5},{5,0},{6,3},{7,6},{8,9},{9,12},{10,1... | collective-permute-start | bytes 1572872 | tf_op jit(solution)/shard_map/ppermute | solution.py:776
  216.4 36.6 %collective-permute-start.25 = (f32[64,2048]{1,0:T(8,128)}, f32[64,2048]{1,0:T(8,128)}, u32[]{:S(2)}, u32[]{:S(2)}) collective-permute-start(f32[64,2048]{1,0:T(8,128)} %get-tuple-element.190), channel_id=1, source_target_pairs={{0,2},{1,5},{2,0},{3,3},{4,6},{5,1},{6,4},{7,7},{8,10},{9,13},{10,... | collective-permute-start | bytes 1572872 | tf_op jit(solution)/shard_map/ppermute | solution.py:776
  218.8 35.8 %collective-permute-start.16 = (bf16[256,2048]{1,0:T(8,128)(2,1)}, bf16[256,2048]{1,0:T(8,128)(2,1)}, u32[]{:S(2)}, u32[]{:S(2)}) collective-permute-start(bf16[256,2048]{1,0:T(8,128)(2,1)} %get-tuple-element.87.refs_3_), channel_id=1, source_target_pairs={{16,0},{24,8},{0,16},{8,24},{17,1},{25,9},{1,17},{9,25},{18,2},{26... | collective-permute-start | bytes 3145736 | tf_op jit(solution)/shard_map/ppermute | solution.py:647
  250.0 44.8 %collective-permute-start.17 = (bf16[256,2048]{1,0:T(8,128)(2,1)}, bf16[256,2048]{1,0:T(8,128)(2,1)}, u32[]{:S(2)}, u32[]{:S(2)}) collective-permute-start(bf16[256,2048]{1,0:T(8,128)(2,1)} %get-tuple-element.88.refs_4_), channel_id=1, source_target_pairs={{8,0},{0,8},{24,16},{16,24},{9,1},{1,9},{25,17},{17,25},{10,2},{2,... | collective-permute-start | bytes 3145736 | tf_op jit(solution)/shard_map/ppermute | solution.py:647
  250.5 44.2 %collective-permute-start.18 = (bf16[256,2048]{1,0:T(8,128)(2,1)}, bf16[256,2048]{1,0:T(8,128)(2,1)}, u32[]{:S(2)}, u32[]{:S(2)}) collective-permute-start(bf16[256,2048]{1,0:T(8,128)(2,1)} %get-tuple-element.90.refs_6_), channel_id=1, source_target_pairs={{16,0},{24,8},{0,16},{8,24},{17,1},{25,9},{1,17},{9,25},{18,2},{26... | collective-permute-start | bytes 3145736 | tf_op jit(solution)/shard_map/ppermute | solution.py:647
  258.5 44.7 %collective-permute-start.21 = (bf16[128,2048]{1,0:T(8,128)(2,1)}, bf16[128,2048]{1,0:T(8,128)(2,1)S(1)}, u32[]{:S(2)}, u32[]{:S(2)}) collective-permute-start(bf16[128,2048]{1,0:T(8,128)(2,1)} %get-tuple-element.92.refs_1_), channel_id=1, source_target_pairs={{16,0},{24,8},{0,16},{8,24},{17,1},{25,9},{1,17},{9,25},{18,2},{26... | collective-permute-start | bytes 1572872 | tf_op jit(solution)/shard_map/ppermute | solution.py:647
  259.3 44.0 %collective-permute-start.22 = (bf16[128,2048]{1,0:T(8,128)(2,1)}, bf16[128,2048]{1,0:T(8,128)(2,1)S(1)}, u32[]{:S(2)}, u32[]{:S(2)}) collective-permute-start(bf16[128,2048]{1,0:T(8,128)(2,1)} %get-tuple-element.93.refs_2_), channel_id=1, source_target_pairs={{8,0},{0,8},{24,16},{16,24},{9,1},{1,9},{25,17},{17,25},{10,2},{2,... | collective-permute-start | bytes 1572872 | tf_op jit(solution)/shard_map/ppermute | solution.py:647
  298.7 24.9 %collective-permute-start.19 = (bf16[128,2048]{1,0:T(8,128)(2,1)}, bf16[128,2048]{1,0:T(8,128)(2,1)}, u32[]{:S(2)}, u32[]{:S(2)}) collective-permute-start(bf16[128,2048]{1,0:T(8,128)(2,1)} %get-tuple-element.96.refs_2_), channel_id=1, source_target_pairs={{16,0},{24,8},{0,16},{8,24},{17,1},{25,9},{1,17},{9,25},{18,2},{26... | collective-permute-start | bytes 1572872 | tf_op jit(solution)/shard_map/ppermute | solution.py:647
  299.4 24.2 %collective-permute-start.20 = (bf16[128,2048]{1,0:T(8,128)(2,1)}, bf16[128,2048]{1,0:T(8,128)(2,1)}, u32[]{:S(2)}, u32[]{:S(2)}) collective-permute-start(bf16[128,2048]{1,0:T(8,128)(2,1)} %get-tuple-element.98.refs_3_), channel_id=1, source_target_pairs={{8,0},{0,8},{24,16},{16,24},{9,1},{1,9},{25,17},{17,25},{10,2},{2,... | collective-permute-start | bytes 1572872 | tf_op jit(solution)/shard_map/ppermute | solution.py:647
  321.9 34.1 %collective-permute-start.29 = (bf16[192,2048]{1,0:T(8,128)(2,1)}, bf16[192,2048]{1,0:T(8,128)(2,1)}, u32[]{:S(2)}, u32[]{:S(2)}) collective-permute-start(bf16[192,2048]{1,0:T(8,128)(2,1)} %get-tuple-element.103.refs_5_), channel_id=1, source_target_pairs={{8,0},{0,8},{24,16},{16,24},{9,1},{1,9},{25,17},{17,25},{10,2},{2,... | collective-permute-start | bytes 2359304 | tf_op jit(solution)/shard_map/ppermute | solution.py:647
  322.0 34.1 %collective-permute-start.30 = (bf16[192,2048]{1,0:T(8,128)(2,1)}, bf16[192,2048]{1,0:T(8,128)(2,1)}, u32[]{:S(2)}, u32[]{:S(2)}) collective-permute-start(bf16[192,2048]{1,0:T(8,128)(2,1)} %get-tuple-element.114), channel_id=1, source_target_pairs={{16,0},{24,8},{0,16},{8,24},{17,1},{25,9},{1,17},{9,25},{18,2},{26... | collective-permute-start | bytes 2359304 | tf_op jit(solution)/shard_map/ppermute | solution.py:647
  373.4 22.5 %collective-permute-start.36 = (bf16[192,2048]{1,0:T(8,128)(2,1)}, bf16[192,2048]{1,0:T(8,128)(2,1)}, u32[]{:S(2)}, u32[]{:S(2)}) collective-permute-start(bf16[192,2048]{1,0:T(8,128)(2,1)} %get-tuple-element.117.refs_1_), channel_id=1, source_target_pairs={{8,0},{0,8},{24,16},{16,24},{9,1},{1,9},{25,17},{17,25},{10,2},{2,... | collective-permute-start | bytes 2359304 | tf_op jit(solution)/shard_map/ppermute | solution.py:647
  374.9 17.6 %collective-permute-start.32 = (bf16[128,2048]{1,0:T(8,128)(2,1)}, bf16[128,2048]{1,0:T(8,128)(2,1)}, u32[]{:S(2)}, u32[]{:S(2)}) collective-permute-start(bf16[128,2048]{1,0:T(8,128)(2,1)} %get-tuple-element.108.refs_4_), channel_id=1, source_target_pairs={{24,8},{0,16},{25,9},{1,17},{26,10},{2,18},{27,11},{3,19},{28,12},... | collective-permute-start | bytes 1572872 | tf_op jit(solution)/shard_map/ppermute | solution.py:647
  382.4 50.6 %collective-permute-start.26 = (bf16[256,2048]{1,0:T(8,128)(2,1)S(1)}, bf16[256,2048]{1,0:T(8,128)(2,1)S(1)}, u32[]{:S(2)}, u32[]{:S(2)}) collective-permute-start(bf16[256,2048]{1,0:T(8,128)(2,1)S(1)} %copy-done.42), channel_id=1, source_target_pairs={{8,0},{16,24},{9,1},{17,25},{10,2},{18,26},{11,3},{19,27},{12,4},{... | collective-permute-start | bytes 3145736 | tf_op jit(solution)/shard_map/ppermute | solution.py:647
  383.7 25.6 %collective-permute-start.37 = (bf16[192,2048]{1,0:T(8,128)(2,1)}, bf16[192,2048]{1,0:T(8,128)(2,1)}, u32[]{:S(2)}, u32[]{:S(2)}) collective-permute-start(bf16[192,2048]{1,0:T(8,128)(2,1)} %get-tuple-element.122), channel_id=1, source_target_pairs={{16,0},{24,8},{0,16},{8,24},{17,1},{25,9},{1,17},{9,25},{18,2},{26... | collective-permute-start | bytes 2359304 | tf_op jit(solution)/shard_map/ppermute | solution.py:647
  383.9 50.5 %collective-permute-start.27 = (bf16[256,2048]{1,0:T(8,128)(2,1)S(1)}, bf16[256,2048]{1,0:T(8,128)(2,1)}, u32[]{:S(2)}, u32[]{:S(2)}) collective-permute-start(bf16[256,2048]{1,0:T(8,128)(2,1)S(1)} %copy-done.41), channel_id=1, source_target_pairs={{16,0},{8,24},{17,1},{9,25},{18,2},{10,26},{19,3},{11,27},{20,4},{... | collective-permute-start | bytes 3145736 | tf_op jit(solution)/shard_map/ppermute | solution.py:647
  392.5 26.1 %collective-permute-start.28 = (bf16[128,2048]{1,0:T(8,128)(2,1)S(1)}, bf16[128,2048]{1,0:T(8,128)(2,1)}, u32[]{:S(2)}, u32[]{:S(2)}) collective-permute-start(bf16[128,2048]{1,0:T(8,128)(2,1)S(1)} %copy-done.49), channel_id=1, source_target_pairs={{24,16},{0,8},{25,17},{1,9},{26,18},{2,10},{27,19},{3,11},{28,20},... | collective-permute-start | bytes 1572872 | tf_op jit(solution)/shard_map/ppermute | solution.py:647
  395.9 30.8 %collective-permute-start.33 = (bf16[128,2048]{1,0:T(8,128)(2,1)}, bf16[128,2048]{1,0:T(8,128)(2,1)}, u32[]{:S(2)}, u32[]{:S(2)}) collective-permute-start(bf16[128,2048]{1,0:T(8,128)(2,1)} %collective-permute-done.32), channel_id=1, source_target_pairs={{8,0},{16,24},{9,1},{17,25},{10,2},{18,26},{11,3},{19,27},{12,4},{... | collective-permute-start | bytes 1572872 | tf_op jit(solution)/shard_map/ppermute | solution.py:647
  409.3 39.0 %collective-permute-start.34 = (bf16[192,2048]{1,0:T(8,128)(2,1)}, bf16[192,2048]{1,0:T(8,128)(2,1)}, u32[]{:S(2)}, u32[]{:S(2)}) collective-permute-start(bf16[192,2048]{1,0:T(8,128)(2,1)} %get-tuple-element.115.refs_1_), channel_id=1, source_target_pairs={{24,8},{0,16},{25,9},{1,17},{26,10},{2,18},{27,11},{3,19},{28,12},... | collective-permute-start | bytes 2359304 | tf_op jit(solution)/shard_map/ppermute | solution.py:647
  418.5 29.8 %collective-permute-start.35 = (bf16[192,2048]{1,0:T(8,128)(2,1)}, bf16[192,2048]{1,0:T(8,128)(2,1)}, u32[]{:S(2)}, u32[]{:S(2)}) collective-permute-start(bf16[192,2048]{1,0:T(8,128)(2,1)} %get-tuple-element.116.refs_2_), channel_id=1, source_target_pairs={{0,8},{24,16},{1,9},{25,17},{2,10},{26,18},{3,11},{27,19},{4,12},{... | collective-permute-start | bytes 2359304 | tf_op jit(solution)/shard_map/ppermute | solution.py:647
  426.8 21.5 %collective-permute-start.38 = (bf16[192,2048]{1,0:T(8,128)(2,1)}, bf16[192,2048]{1,0:T(8,128)(2,1)}, u32[]{:S(2)}, u32[]{:S(2)}) collective-permute-start(bf16[192,2048]{1,0:T(8,128)(2,1)} %get-tuple-element.124), channel_id=1, source_target_pairs={{24,8},{0,16},{25,9},{1,17},{26,10},{2,18},{27,11},{3,19},{28,12},... | collective-permute-start | bytes 2359304 | tf_op jit(solution)/shard_map/ppermute | solution.py:647
  433.0 19.2 %collective-permute-start.39 = (bf16[192,2048]{1,0:T(8,128)(2,1)}, bf16[192,2048]{1,0:T(8,128)(2,1)S(1)}, u32[]{:S(2)}, u32[]{:S(2)}) collective-permute-start(bf16[192,2048]{1,0:T(8,128)(2,1)} %get-tuple-element.126), channel_id=1, source_target_pairs={{0,8},{24,16},{1,9},{25,17},{2,10},{26,18},{3,11},{27,19},{4,12},{... | collective-permute-start | bytes 2359304 | tf_op jit(solution)/shard_map/ppermute | solution.py:647
  434.4 14.0 %collective-permute-start.31 = (bf16[128,2048]{1,0:T(8,128)(2,1)}, bf16[128,2048]{1,0:T(8,128)(2,1)S(1)}, u32[]{:S(2)}, u32[]{:S(2)}) collective-permute-start(bf16[128,2048]{1,0:T(8,128)(2,1)} %after.43), channel_id=1, source_target_pairs={{16,0},{8,24},{17,1},{9,25},{18,2},{10,26},{19,3},{11,27},{20,4},{... | collective-permute-start | bytes 1572872 | tf_op jit(solution)/shard_map/ppermute | solution.py:647
  466.1 109.7 %all-gather.9.cloned.1.call-start = ((), (), s32[]{:S(2)}) async-start(), calls=%async_computation.7 | async-start | bytes 5308416 | tf_op jit(solution)/shard_map/all_gather | solution.py:598
  521.6 163.7 %reduce-scatter.7.cloned.1.call-start = ((), (), s32[]{:S(2)}) async-start(), calls=%async_computation.8 | async-start | bytes 9437184 | tf_op jit(solution)/shard_map/reduce_scatter | solution.py:1015
  575.8 176.0 %reduce-scatter.9.cloned.1.call-start = ((), (), s32[]{:S(2)}) async-start(), calls=%async_computation.9 | async-start | bytes 5308416 | tf_op jit(solution)/shard_map/reduce_scatter | solution.py:597
  575.9 104.2 %collective-permute-start.41 = (bf16[256,2048]{1,0:T(8,128)(2,1)}, bf16[256,2048]{1,0:T(8,128)(2,1)S(1)}, u32[]{:S(2)}, u32[]{:S(2)}) collective-permute-start(bf16[256,2048]{1,0:T(8,128)(2,1)} %after.54), channel_id=1, source_target_pairs={{16,0},{24,8},{0,16},{8,24},{17,1},{25,9},{1,17},{9,25},{18,2},{26... | collective-permute-start | bytes 3145736 | tf_op jit(solution)/shard_map/ppermute | solution.py:647
  577.1 103.0 %collective-permute-start.40 = (bf16[256,2048]{1,0:T(8,128)(2,1)}, bf16[256,2048]{1,0:T(8,128)(2,1)S(1)}, u32[]{:S(2)}, u32[]{:S(2)}) collective-permute-start(bf16[256,2048]{1,0:T(8,128)(2,1)} %after.52), channel_id=1, source_target_pairs={{8,0},{0,8},{24,16},{16,24},{9,1},{1,9},{25,17},{17,25},{10,2},{2,... | collective-permute-start | bytes 3145736 | tf_op jit(solution)/shard_map/ppermute | solution.py:647
  685.4 119.1 %all-gather.11.cloned.1.call-start = ((), (), s32[]{:S(2)}) async-start(), calls=%async_computation.10 | async-start | bytes 5308416 | tf_op jit(solution)/shard_map/all_gather | solution.py:598
  685.5 13.0 %collective-permute-start.48 = (bf16[128,2048]{1,0:T(8,128)(2,1)}, bf16[128,2048]{1,0:T(8,128)(2,1)}, u32[]{:S(2)}, u32[]{:S(2)}) collective-permute-start(bf16[128,2048]{1,0:T(8,128)(2,1)} %get-tuple-element.135.refs_3_), channel_id=1, source_target_pairs={{8,0},{0,8},{24,16},{16,24},{9,1},{1,9},{25,17},{17,25},{10,2},{2,... | collective-permute-start | bytes 1572872 | tf_op jit(solution)/shard_map/ppermute | solution.py:647
  689.9 12.6 %collective-permute-start.47 = (bf16[128,2048]{1,0:T(8,128)(2,1)}, bf16[128,2048]{1,0:T(8,128)(2,1)S(1)}, u32[]{:S(2)}, u32[]{:S(2)}) collective-permute-start(bf16[128,2048]{1,0:T(8,128)(2,1)} %get-tuple-element.134.refs_2_), channel_id=1, source_target_pairs={{16,0},{24,8},{0,16},{8,24},{17,1},{25,9},{1,17},{9,25},{18,2},{26... | collective-permute-start | bytes 1572872 | tf_op jit(solution)/shard_map/ppermute | solution.py:647
  709.4 32.8 %collective-permute-start.49 = (bf16[64,2048]{1,0:T(8,128)(2,1)S(1)}, bf16[64,2048]{1,0:T(8,128)(2,1)S(1)}, u32[]{:S(2)}, u32[]{:S(2)}) collective-permute-start(bf16[64,2048]{1,0:T(8,128)(2,1)S(1)} %get-tuple-element.203), channel_id=1, source_target_pairs={{0,0},{3,1},{6,2},{1,3},{4,4},{7,5},{2,6},{5,7},{8,8},{11,9},{14,1... | collective-permute-start | bytes 786440 | tf_op jit(solution)/shard_map/ppermute | solution.py:794
  712.7 29.5 %collective-permute-start.50 = (bf16[64,2048]{1,0:T(8,128)(2,1)S(1)}, bf16[64,2048]{1,0:T(8,128)(2,1)S(1)}, u32[]{:S(2)}, u32[]{:S(2)}) collective-permute-start(bf16[64,2048]{1,0:T(8,128)(2,1)S(1)} %get-tuple-element.205), channel_id=1, source_target_pairs={{1,0},{4,1},{7,2},{2,3},{5,4},{0,5},{3,6},{6,7},{9,8},{12,9},{15,1... | collective-permute-start | bytes 786440 | tf_op jit(solution)/shard_map/ppermute | solution.py:794
  712.8 29.4 %collective-permute-start.51 = (bf16[64,2048]{1,0:T(8,128)(2,1)S(1)}, bf16[64,2048]{1,0:T(8,128)(2,1)S(1)}, u32[]{:S(2)}, u32[]{:S(2)}) collective-permute-start(bf16[64,2048]{1,0:T(8,128)(2,1)S(1)} %get-tuple-element.204), channel_id=1, source_target_pairs={{2,0},{5,1},{0,2},{3,3},{6,4},{1,5},{4,6},{7,7},{10,8},{13,9},{8,1... | collective-permute-start | bytes 786440 | tf_op jit(solution)/shard_map/ppermute | solution.py:794
  716.1 25.1 %collective-permute-start.44 = (f32[20480]{0:T(1024)S(1)}, f32[20480]{0:T(1024)S(1)}, u32[]{:S(2)}, u32[]{:S(2)}) collective-permute-start(f32[20480]{0:T(1024)S(1)} %add.242), channel_id=1, source_target_pairs={{0,4},{1,5},{2,6},{3,7},{4,0},{5,1},{6,2},{7,3},{8,12},{9,13},{10,... | collective-permute-start | bytes 245768 | tf_op jit(solution)/shard_map/ppermute | solution.py:762
  751.8 231.3 %reduce-scatter.11.cloned.1.call-start = ((), (), s32[]{:S(2)}) async-start(), calls=%async_computation.11 | async-start | bytes 9437184 | tf_op jit(solution)/shard_map/reduce_scatter | solution.py:1056
  914.4 13.5 %collective-permute-start.54 = (bf16[128,2048]{1,0:T(8,128)(2,1)}, bf16[128,2048]{1,0:T(8,128)(2,1)S(1)}, u32[]{:S(2)}, u32[]{:S(2)}) collective-permute-start(bf16[128,2048]{1,0:T(8,128)(2,1)} %get-tuple-element.148), channel_id=1, source_target_pairs={{8,0},{0,8},{24,16},{16,24},{9,1},{1,9},{25,17},{17,25},{10,2},{2,... | collective-permute-start | bytes 1572872 | tf_op jit(solution)/shard_map/ppermute | solution.py:647
  915.8 13.3 %collective-permute-start.56 = (bf16[128,2048]{1,0:T(8,128)(2,1)}, bf16[128,2048]{1,0:T(8,128)(2,1)S(1)}, u32[]{:S(2)}, u32[]{:S(2)}) collective-permute-start(bf16[128,2048]{1,0:T(8,128)(2,1)} %get-tuple-element.149), channel_id=1, source_target_pairs={{16,0},{24,8},{0,16},{8,24},{17,1},{25,9},{1,17},{9,25},{18,2},{26... | collective-permute-start | bytes 1572872 | tf_op jit(solution)/shard_map/ppermute | solution.py:647
  921.5 41.4 %collective-permute-start.52 = (bf16[256,2048]{1,0:T(8,128)(2,1)S(1)}, bf16[256,2048]{1,0:T(8,128)(2,1)S(1)}, u32[]{:S(2)}, u32[]{:S(2)}) collective-permute-start(bf16[256,2048]{1,0:T(8,128)(2,1)S(1)} %copy-done.66), channel_id=1, source_target_pairs={{8,0},{0,8},{24,16},{16,24},{9,1},{1,9},{25,17},{17,25},{10,2},{2,... | collective-permute-start | bytes 3145736 | tf_op jit(solution)/shard_map/ppermute | solution.py:647
  921.7 41.1 %collective-permute-start.53 = (bf16[256,2048]{1,0:T(8,128)(2,1)S(1)}, bf16[256,2048]{1,0:T(8,128)(2,1)S(1)}, u32[]{:S(2)}, u32[]{:S(2)}) collective-permute-start(bf16[256,2048]{1,0:T(8,128)(2,1)S(1)} %copy-done.65), channel_id=1, source_target_pairs={{16,0},{24,8},{0,16},{8,24},{17,1},{25,9},{1,17},{9,25},{18,2},{26... | collective-permute-start | bytes 3145736 | tf_op jit(solution)/shard_map/ppermute | solution.py:647
  927.9 34.8 %collective-permute-start.55 = (bf16[128,2048]{1,0:T(8,128)(2,1)S(1)}, bf16[128,2048]{1,0:T(8,128)(2,1)S(1)}, u32[]{:S(2)}, u32[]{:S(2)}) collective-permute-start(bf16[128,2048]{1,0:T(8,128)(2,1)S(1)} %collective-permute-done.54), channel_id=1, source_target_pairs={{16,0},{24,8},{0,16},{8,24},{17,1},{25,9},{1,17},{9,25},{18,2},{26... | collective-permute-start | bytes 1572872 | tf_op jit(solution)/shard_map/ppermute | solution.py:647
  929.1 33.6 %collective-permute-start.57 = (bf16[128,2048]{1,0:T(8,128)(2,1)S(1)}, bf16[128,2048]{1,0:T(8,128)(2,1)S(1)}, u32[]{:S(2)}, u32[]{:S(2)}) collective-permute-start(bf16[128,2048]{1,0:T(8,128)(2,1)S(1)} %collective-permute-done.56), channel_id=1, source_target_pairs={{8,0},{0,8},{24,16},{16,24},{9,1},{1,9},{25,17},{17,25},{10,2},{2,... | collective-permute-start | bytes 1572872 | tf_op jit(solution)/shard_map/ppermute | solution.py:647
  965.5 14.3 %collective-permute-start.59 = (bf16[64,2048]{1,0:T(8,128)(2,1)S(1)}, bf16[64,2048]{1,0:T(8,128)(2,1)S(1)}, u32[]{:S(2)}, u32[]{:S(2)}) collective-permute-start(bf16[64,2048]{1,0:T(8,128)(2,1)S(1)} %get-tuple-element.202), channel_id=1, source_target_pairs={{1,0},{4,1},{7,2},{2,3},{5,4},{0,5},{3,6},{6,7},{9,8},{12,9},{15,1... | collective-permute-start | bytes 786440 | tf_op jit(solution)/shard_map/ppermute | solution.py:794
  965.6 15.1 %collective-permute-start.60 = (bf16[64,2048]{1,0:T(8,128)(2,1)S(1)}, bf16[64,2048]{1,0:T(8,128)(2,1)S(1)}, u32[]{:S(2)}, u32[]{:S(2)}) collective-permute-start(bf16[64,2048]{1,0:T(8,128)(2,1)S(1)} %get-tuple-element.201), channel_id=1, source_target_pairs={{2,0},{5,1},{0,2},{3,3},{6,4},{1,5},{4,6},{7,7},{10,8},{13,9},{8,1... | collective-permute-start | bytes 786440 | tf_op jit(solution)/shard_map/ppermute | solution.py:794
  (74 other events, 589.1 us)
Sparse Core Ops, SparseCore 0:
  12.8 93.2 all-gather.4
  107.7 81.8 all-gather.6
  466.2 55.3 reduce-scatter.4
  523.1 52.6 all-gather.8
  577.9 85.8 reduce-scatter.6
  685.5 64.7 reduce-scatter.8
  752.0 52.5 all-gather.10
  806.8 85.8 reduce-scatter.10

commit v5 on v4

--- a/solution.py
+++ b/solution.py
@@ -755,13 +755,14 @@
     return jnp.stack([own, from_x, from_y, jnp.concatenate([first, second], axis=0)])
 
 
-def butterfly(values):
-    for axis in ("group", "dp"):
-        size, bit = lax.axis_size(axis), 1
-        while bit < size:
-            values = values + lax.ppermute(values, axis, [(i, i ^ bit) for i in range(size)])
-            bit *= 2
-    return values
+def butterfly_steps():
+    return [
+        (axis, 1 << bit) for axis in ("dp", "group") for bit in range((lax.axis_size(axis) - 1).bit_length())
+    ]
+
+
+def partner(values, axis, bit):
+    return lax.ppermute(values, axis, [(i, i ^ bit) for i in range(lax.axis_size(axis))])
 
 
 def heads_aligned(unit):
@@ -1049,8 +1050,9 @@
                 jnp.sum(grad_y_float, axis=0),
             ]
         )
-        vector_grad = butterfly(vector_local)
-        return grad_hidden, vector_grad, *grads
+        for step in butterfly_steps()[:-1]:
+            vector_local = vector_local + partner(vector_local, *step)
+        return grad_hidden, vector_local, *grads
 
     def beside_last(gathered):
         return (lax.psum_scatter(after(kept[4], gathered), "group", scatter_dimension=0, tiled=True),)
@@ -1073,7 +1075,8 @@
     results, _, meanwhile, (branch,) = orthogonalize(
         owned, packed, source_rows.astype(jnp.int32), pieces, after_gram, beside_first, after_first_steps, after_first, beside_last
     )
-    grad_hidden, vector_grad, grad_in, grad_back, moment_in_new, moment_back_new = meanwhile
+    grad_hidden, vector_half, grad_in, grad_back, moment_in_new, moment_back_new = meanwhile
+    vector_grad = vector_half + partner(after(vector_half, results[0]), *butterfly_steps()[-1])
     block_out = (x_float + branch.astype(F32) + bias_out).astype(BF16)
     if fast:
         returned = by_distance(exchange_dp(*results))

time: 998 us -> 1000 us (level)
    ppermute x5, waiting for transfers between devices: 23.8 us -> 1.08 us  [partner(): lax.ppermute(values, axis, [(i, i ^ bit) for i in range(lax.axis_size(axi...]
    ppermute x6, waiting for transfers between devices: 10 us -> 21.5 us  [return_qkv(): lax.ppermute(lax.dynamic_index_in_dim(parts, (j - me) * inverse % 3, 0, k...]
    unnamed x145 -> x146, local copies, waits for them, and re-layouts: 26.8 us -> 29 us
  transfers between devices with their start and end apart: 69 -> 69, of which waited for: 26 -> 28; matrix products, arithmetic and copies ran while one was open for 16% -> 16% of each run, Pallas kernels for 36% -> 36%
where the time goes in v5:
time: 1000 us; the launch traced here: 998 us
  Pallas kernels  409 us (41%)
  waiting for transfers between devices  289 us (29%)
  starting transfers between devices  97.1 us (10%)
  other arithmetic  72.2 us (7%)
  local copies, waits for them, and re-layouts  65.7 us (7%)
  matrix products  48.7 us (5%)
  between operations  15.8 us (2%)
    ppermute x44, waiting for transfers between devices, hop(): return lax.ppermute(values, 'dp', [(t ^ bit, t) for t in targets])  112 us
    pallas_call x1, Pallas kernels, orthogonalize(): pl.pallas_call(functools.partial(second_body, 3), out_shape=[jax.ShapeDty...  110 us
    all_gather x2, waiting for transfers between devices, gram_sum(): lax.all_gather(after(part, *jax.tree.leaves(meanwhile)), 'group', axis=0,...  108 us
    pallas_call x1, Pallas kernels, orthogonalize(): pl.pallas_call(functools.partial(first_body, 2), out_shape=(x_shape, pack...  102 us
    ppermute x44, starting transfers between devices, hop(): return lax.ppermute(values, 'dp', [(t ^ bit, t) for t in targets])  58.2 us
    pallas_call x4, Pallas kernels, by_columns(): pl.pallas_call(body, grid=(steps,), in_specs=([] if scalar is None else [...  54.9 us
    pallas_call x4, Pallas kernels, by_rows(): pl.pallas_call(body, grid=(steps,), in_specs=[pl.BlockSpec((rows, one.sha...  51.3 us
    dot_general x4, matrix products, dot(): return jnp.dot(left, right, preferred_element_type=F32)  48.7 us
  transfers between devices with their start and end apart: 69, of which 28 were waited for; matrix products, arithmetic and copies ran while one was open for 16% of the time, Pallas kernels for 36%

profile of v5, /device:TPU:1, one launch (start us, length us, event | category | flops | bytes accessed | tf_op | source)
XLA Modules:
  0.0 997.6 jit_solution(970505969767118743)
XLA Ops:
  7.3 2.6 copy.128
  19.6 4.2 collective-permute-start.2
  25.7 4.4 collective-permute-start.1
  38.9 11.8 %collective-permute-done = bf16[64,2048]{1,0:T(8,128)(2,1)} collective-permute-done((bf16[64,2048]{1,0:T(8,128)(2,1)}, bf16[64,2048]{1,0:T(8,128)(2,1)}, u32[]{:S(2)}, u32[]{:S(2)}) %collective-permute-start) | collective-permute-done | bytes 262176 | tf_op jit(solution)/shard_map/ppermute | solution.py:777
  59.3 8.3 collective-permute-done.6
  69.1 3.3 pad_maximum_fusion.1.refs_2_
  72.5 10.9 %collective-permute-done.3.refs_0_.refs_3_.refs_1_ = bf16[192,2048]{1,0:T(8,128)(2,1)} collective-permute-done((bf16[192,2048]{1,0:T(8,128)(2,1)S(1)}, bf16[192,2048]{1,0:T(8,128)(2,1)}, u32[]{:S(2)}, u32[]{:S(2)}) %collective-permute-start.3) | collective-permute-done | bytes 786464 | tf_op jit(solution)/shard_map/ppermute | solution.py:647
  84.8 21.3 %all-gather.5.cloned.1.call-done.x_ref.refs_1_.r_ref = bf16[2048,2048]{1,0:T(8,128)(2,1)} async-done(((bf16[256,2048]{1,0:T(8,128)(2,1)}), bf16[2048,2048]{1,0:T(8,128)(2,1)}) %all-gather.5.cloned.1.call-update) | async-done | bytes 8388624 | tf_op jit(solution)/shard_map/all_gather | solution.py:885
  113.0 4.9 broadcast_multiply_fusion
  117.9 18.7 %up_forward.1 = (bf16[2048,1024]{1,0:T(8,128)(2,1)}, bf16[2048,1024]{1,0:T(8,128)(2,1)}) custom-call(bf16[2048,2048]{1,0:T(8,128)(2,1)} %all-gather.5.cloned.1.call-done.x_ref.refs_1_.r_ref, bf16[1024,2048]{1,0:T(8,128)(2,1)} %bitcast.204, f32[1,1024]{1,0:T(1,128)} %bitcast.255), custom_call_target="tpu_custom_call" | custom-call | tf_op jit(solution)/shard_map/up_forward/pallas_call | solution.py:77
  141.5 2.7 slice_bitcast_fusion.2.refs_0_
  156.8 11.6 %project_qkv.1.refs_3_.pre_ref = f32[2048,768]{1,0:T(8,128)} custom-call(bf16[2048,2048]{1,0:T(8,128)(2,1)} %all-gather.5.cloned.1.call-done.x_ref.refs_1_.r_ref, bf16[768,2048]{1,0:T(8,128)(2,1)} %bitcast.225, f32[1,768]{1,0:T(1,128)} %broadcast_in_dim_reshape.7.b_ref), custom_call_target="tpu_custom_call" | custom-call | tf_op jit(solution)/shard_map/project_qkv/pallas_call | solution.py:77
  175.7 11.7 %fusion.41.refs_6_ = f32[2048,2048]{1,0:T(8,128)} fusion(bf16[2048,1024]{1,0:T(8,128)(2,1)S(1)} %copy-done, bf16[1024,2048]{1,0:T(8,128)(2,1)S(1)} %bitcast.201), kind=kOutput, calls=%fused_computation.185 | convolution fusion | flops 8589934592 | bytes 25165824 | tf_op jit(solution)/shard_map/dot_general | solution.py:854
  189.6 14.3 %grad_down.1 = (bf16[256,2048]{1,0:T(8,128)(2,1)}, bf16[256,2048]{1,0:T(8,128)(2,1)}, bf16[256,2048]{1,0:T(8,128)(2,1)}, bf16[256,2048]{1,0:T(8,128)(2,1)}) custom-call(bf16[2048,1024]{1,0:T(8,128)(2,1)} %get-tuple-element.82.refs_1_.l_ref, bf16[2048,2048]{1,0:T(8,128)(2,1)} %after.36.r_ref.g_ref.x_ref.q_ref), custom_call_target="tpu_custom_call" | custom-call | tf_op jit(solution)/shard_map/grad_down/pallas_call | solution.py:95
  205.1 2.7 fusion.40
  209.8 6.6 collective-permute-start.24
  221.2 14.3 %up_backward.1.l_ref.refs_0_ = bf16[2048,1024]{1,0:T(8,128)(2,1)} custom-call(bf16[2048,2048]{1,0:T(8,128)(2,1)} %after.36.r_ref.g_ref.x_ref.q_ref, bf16[2048,1024]{1,0:T(8,128)(2,1)} %after.37.s_ref, bf16[1024,2048]{1,0:T(8,128)(2,1)} %bitcast.203), custom_call_target="tpu_custom_call" | custom-call | tf_op jit(solution)/shard_map/up_backward/pallas_call | solution.py:77
  235.5 14.5 %grad_up.1 = (bf16[256,2048]{1,0:T(8,128)(2,1)}, bf16[256,2048]{1,0:T(8,128)(2,1)}, bf16[256,2048]{1,0:T(8,128)(2,1)}, bf16[256,2048]{1,0:T(8,128)(2,1)}) custom-call(bf16[2048,1024]{1,0:T(8,128)(2,1)} %up_backward.1.l_ref.refs_0_, bf16[2048,2048]{1,0:T(8,128)(2,1)} %all-gather.5.cloned.1.call-done.x_ref.refs_1_.r_ref), custom_call_target="tpu_custom_call" | custom-call | tf_op jit(solution)/shard_map/grad_up/pallas_call | solution.py:95
  254.6 4.0 scatter_next.3
  262.2 6.7 project_grad.1.refs_0_
  271.2 22.4 %attention.2 = (bf16[2048,128]{1,0:T(8,128)(2,1)}, bf16[2048,384]{1,0:T(8,128)(2,1)}) custom-call(s32[8]{0:T(128)} %and_select_fusion.6.refs_5_.first_ref, f32[2048,768]{1,0:T(8,128)} %project_qkv.1.refs_3_.pre_ref, bf16[2048,256]{1,0:T(8,128)(2,1)} %after.39.grad_ref, s32[2048,1]{1,0:T(8,128)} %subtract_subtract_fusion.refs_6_.start_ref, ...), custom_call_target="tpu_custom_call" | custom-call | tf_op jit(solution)/shard_map/attention/pallas_call | solution.py:328
  293.6 2.7 copy.101.refs_0_
  296.3 4.0 scatter_next.4
  303.8 4.5 momentum.2
  308.4 13.0 %weight_grads_plus.2 = (bf16[384,2048]{1,0:T(8,128)(2,1)}, bf16[128,2048]{1,0:T(8,128)(2,1)}, bf16[192,2048]{1,0:T(8,128)(2,1)}, bf16[192,2048]{1,0:T(8,128)(2,1...) custom-call(s32[1]{0:T(128)} %bitcast.42.me_ref, bf16[2048,384]{1,0:T(8,128)(2,1)} %after.40.l_ref, ...), custom_call_target="tpu_custom_call" | custom-call | tf_op jit(solution)/shard_map/weight_grads_plus/pallas_call | solution.py:95
  324.5 4.5 momentum.3
  329.0 3.6 to_owners.1
  332.6 22.5 %attention.3 = (bf16[2048,128]{1,0:T(8,128)(2,1)}, bf16[2048,384]{1,0:T(8,128)(2,1)}) custom-call(s32[8]{0:T(128)} %and_select_fusion.6.refs_5_.first_ref, f32[2048,768]{1,0:T(8,128)} %project_qkv.1.refs_3_.pre_ref, bf16[2048,256]{1,0:T(8,128)(2,1)} %after.42.grad_ref, s32[2048,1]{1,0:T(8,128)} %subtract_subtract_fusion.refs_6_.start_ref, ...), custom_call_target="tpu_custom_call" | custom-call | tf_op jit(solution)/shard_map/attention/pallas_call | solution.py:328
  355.2 3.3 pad_maximum_fusion.7.refs_0_
  358.5 4.2 reduce_next.2
  362.8 13.1 %weight_grads_plus.3 = (bf16[384,2048]{1,0:T(8,128)(2,1)}, bf16[128,2048]{1,0:T(8,128)(2,1)}, bf16[192,2048]{1,0:T(8,128)(2,1)}, bf16[192,2048]{1,0:T(8,128)(2,1...) custom-call(s32[1]{0:T(128)} %bitcast.42.me_ref, bf16[2048,384]{1,0:T(8,128)(2,1)} %after.43.l_ref, ...), custom_call_target="tpu_custom_call" | custom-call | tf_op jit(solution)/shard_map/weight_grads_plus/pallas_call | solution.py:95
  376.0 6.0 collective-permute-start.32
  386.1 6.7 collective-permute-done.32
  392.8 4.3 collective-permute-start.28
  398.4 11.3 %collective-permute-done.37.refs_3_ = bf16[192,2048]{1,0:T(8,128)(2,1)} collective-permute-done((bf16[192,2048]{1,0:T(8,128)(2,1)}, bf16[192,2048]{1,0:T(8,128)(2,1)}, u32[]{:S(2)}, u32[]{:S(2)}) %collective-permute-start.37) | collective-permute-done | bytes 786464 | tf_op jit(solution)/shard_map/ppermute | solution.py:647
  409.7 5.0 collective-permute-start.34
  414.7 4.2 reduce_next.3
  421.1 8.3 collective-permute-done.33.refs_4_
  429.3 3.9 collective-permute-start.38
  435.9 13.4 %collective-permute-done.31.refs_3_ = bf16[128,2048]{1,0:T(8,128)(2,1)S(1)} collective-permute-done((bf16[128,2048]{1,0:T(8,128)(2,1)}, bf16[128,2048]{1,0:T(8,128)(2,1)S(1)}, u32[]{:S(2)}, u32[]{:S(2)}) %collective-permute-start.31) | collective-permute-done | bytes 524320 | tf_op jit(solution)/shard_map/ppermute | solution.py:647
  449.4 4.1 collective-permute-done.39.refs_12_
  454.4 13.0 %gram.1 = (bf16[1024,2048]{1,0:T(8,128)(2,1)}, bf16[9216,256]{1,0:T(8,128)(2,1)}) custom-call(s32[1]{0:T(128)} %bitcast.42.me_ref, bf16[256,2048]{1,0:T(8,128)(2,1)} %get-tuple-element.110.refs_0_, bf16[256,2048]{1,0:T(8,128)(2,1)} %copy-done.48, bf16[256,2048]{1,0:T(8,128)(2,1)} %collective-permute-done.27.refs_2_, bf16[128,2048]{1,0:T(8,128)(2,1)} %copy-done.55, ...), custom_call_target="tpu_custom_call" | custom-call | tf_op jit(solution)/shard_map/gram/pallas_call | solution.py:576
  482.5 11.9 %add_convert_fusion.1.refs_8_.refs_0_ = bf16[2048,2048]{1,0:T(8,128)(2,1)} fusion(f32[2048,2048]{1,0:T(8,128)} %fusion.41.refs_6_, bf16[2048,256]{1,0:T(8,128)(2,1)S(1)} %copy-done.24, bf16[256,2048]{1,0:T(8,128)(2,1)S(1)} %bitcast.219), kind=kOutput, calls=%fused_computation.1 | convolution fusion | flops 2155872256 | bytes 27262976 | tf_op jit(solution)/shard_map/dot_general | solution.py:854
  494.4 11.7 %fusion.42 = f32[2048,2048]{1,0:T(8,128)} fusion(bf16[2048,1024]{1,0:T(8,128)(2,1)S(1)} %copy-done.1, bf16[1024,2048]{1,0:T(8,128)(2,1)S(1)} %bitcast.205), kind=kOutput, calls=%fused_computation.186 | convolution fusion | flops 8589934592 | bytes 25165824 | tf_op jit(solution)/shard_map/dot_general | solution.py:854
  506.1 13.4 %add_convert_fusion.refs_1_.refs_0_ = bf16[2048,2048]{1,0:T(8,128)(2,1)} fusion(f32[2048,2048]{1,0:T(8,128)} %fusion.42, bf16[2048,768]{1,0:T(8,128)(2,1)S(1)} %copy-done.2, bf16[768,2048]{1,0:T(8,128)(2,1)} %bitcast.226), kind=kOutput, calls=%fused_computation | convolution fusion | flops 6450839552 | bytes 31457280 | tf_op jit(solution)/shard_map/dot_general | solution.py:854
  521.5 54.1 %all-gather.9.cloned.1.call-done.packed_ref.refs_1_ = bf16[9216,256]{1,0:T(8,128)(2,1)} async-done(((bf16[1152,256]{1,0:T(8,128)(2,1)}), bf16[9216,256]{1,0:T(8,128)(2,1)}) %all-gather.9.cloned.1.call-update) | async-done | bytes 4718608 | tf_op jit(solution)/shard_map/all_gather | solution.py:598
  578.2 101.7 %first_steps.1 = (bf16[1024,2048]{1,0:T(8,128)(2,1)}, bf16[9216,256]{1,0:T(8,128)(2,1)}) custom-call(bf16[9216,256]{1,0:T(8,128)(2,1)} %all-gather.9.cloned.1.call-done.packed_ref.refs_1_, bf16[1024,2048]{1,0:T(8,128)(2,1)} %get-tuple-element.132.x_ref), custom_call_target="tpu_custom_call" | custom-call | tf_op jit(solution)/shard_map/first_steps/pallas_call | solution.py:614
  681.2 4.0 scatter_next.5
  685.7 3.1 convert_reduce_fusion
  690.0 8.4 collective-permute-done.46
  710.5 3.3 collective-permute-start.50
  714.9 3.9 fusion.34
  721.1 7.4 collective-permute-done.48
  730.4 2.9 collective-permute-done.50
  733.6 5.2 fusion.35
  740.5 7.8 reduce-scatter.9.cloned.1.call-done.refs_0_
  748.4 54.2 %all-gather.11.cloned.1.call-done.refs_1_.packed_ref = bf16[9216,256]{1,0:T(8,128)(2,1)} async-done(((bf16[1152,256]{1,0:T(8,128)(2,1)}), bf16[9216,256]{1,0:T(8,128)(2,1)}) %all-gather.11.cloned.1.call-update) | async-done | bytes 4718608 | tf_op jit(solution)/shard_map/all_gather | solution.py:598
  803.2 4.5 maximum_add_fusion.1
  808.5 109.7 %last_steps.1 = (bf16[256,2048]{1,0:T(8,128)(2,1)}, bf16[256,2048]{1,0:T(8,128)(2,1)}, bf16[256,2048]{1,0:T(8,128)(2,1)}, bf16[128,2048]{1,0:T(8,128)(2,1)}, bf16[128,2048]{1,0:T(8,128)(2,1)}) custom-call(s32[16]{0:T(128)} %broadcast_select_fusion.1.from_ref, bf16[9216,256]{1,0:T(8,128)(2,1)} %all-gather.11.cloned.1.call-done.refs_1_.packed_ref, ...), custom_call_target="tpu_custom_call" | custom-call | tf_op jit(solution)/shard_map/last_steps/pallas_call | solution.py:629
  922.5 5.5 maximum_add_fusion
  928.1 4.5 collective-permute-done.53
  936.5 30.7 %collective-permute-done.54 = bf16[128,2048]{1,0:T(8,128)(2,1)S(1)} collective-permute-done((bf16[128,2048]{1,0:T(8,128)(2,1)S(1)}, bf16[128,2048]{1,0:T(8,128)(2,1)S(1)}, u32[]{:S(2)}, u32[]{:S(2)}) %collective-permute-start.54) | collective-permute-done | bytes 524320 | tf_op jit(solution)/shard_map/ppermute | solution.py:647
  970.6 3.2 collective-permute-start.59
  978.3 5.4 collective-permute-done.58
  (413 shorter events, 167.5 us)
Async XLA Ops:
  7.2 98.9 %all-gather.5.cloned.1.call-start = ((), (), s32[]{:S(2)}) async-start(), calls=%async_computation.4 | async-start | bytes 9437184 | tf_op jit(solution)/shard_map/all_gather | solution.py:885
  12.7 176.9 %all-gather.7.cloned.1.call-start = ((), (), s32[]{:S(2)}) async-start(), calls=%async_computation.5 | async-start | bytes 9437184 | tf_op jit(solution)/shard_map/all_gather | solution.py:889
  14.3 39.1 %collective-permute-start.5 = (bf16[256,2048]{1,0:T(8,128)(2,1)}, bf16[256,2048]{1,0:T(8,128)(2,1)S(1)}, u32[]{:S(2)}, u32[]{:S(2)}) collective-permute-start(bf16[256,2048]{1,0:T(8,128)(2,1)} %get-tuple-element.185), channel_id=1, source_target_pairs={{16,0},{24,8},{0,16},{8,24},{17,1},{25,9},{1,17},{9,25},{18,2},{26... | collective-permute-start | bytes 3145736 | tf_op jit(solution)/shard_map/ppermute | solution.py:647
  16.4 37.2 %collective-permute-start.4 = (bf16[256,2048]{1,0:T(8,128)(2,1)}, bf16[256,2048]{1,0:T(8,128)(2,1)}, u32[]{:S(2)}, u32[]{:S(2)}) collective-permute-start(bf16[256,2048]{1,0:T(8,128)(2,1)} %get-tuple-element.185), channel_id=1, source_target_pairs={{8,0},{0,8},{24,16},{16,24},{9,1},{1,9},{25,17},{17,25},{10,2},{2,... | collective-permute-start | bytes 3145736 | tf_op jit(solution)/shard_map/ppermute | solution.py:647
  19.6 19.3 %collective-permute-start.2 = (bf16[64,2048]{1,0:T(8,128)(2,1)}, bf16[64,2048]{1,0:T(8,128)(2,1)S(1)}, u32[]{:S(2)}, u32[]{:S(2)}) collective-permute-start(bf16[64,2048]{1,0:T(8,128)(2,1)} %get-tuple-element.183), channel_id=1, source_target_pairs={{0,2},{1,5},{2,0},{3,3},{4,6},{5,1},{6,4},{7,7},{8,10},{9,13},{10,... | collective-permute-start | bytes 786440 | tf_op jit(solution)/shard_map/ppermute | solution.py:777
  23.8 27.0 %collective-permute-start = (bf16[64,2048]{1,0:T(8,128)(2,1)}, bf16[64,2048]{1,0:T(8,128)(2,1)}, u32[]{:S(2)}, u32[]{:S(2)}) collective-permute-start(bf16[64,2048]{1,0:T(8,128)(2,1)} %get-tuple-element.181), channel_id=1, source_target_pairs={{0,0},{1,3},{2,6},{3,1},{4,4},{5,7},{6,2},{7,5},{8,8},{9,11},{10,1... | collective-permute-start | bytes 786440 | tf_op jit(solution)/shard_map/ppermute | solution.py:777
  25.7 26.6 %collective-permute-start.1 = (bf16[64,2048]{1,0:T(8,128)(2,1)}, bf16[64,2048]{1,0:T(8,128)(2,1)}, u32[]{:S(2)}, u32[]{:S(2)}) collective-permute-start(bf16[64,2048]{1,0:T(8,128)(2,1)} %get-tuple-element.182), channel_id=1, source_target_pairs={{0,1},{1,4},{2,7},{3,2},{4,5},{5,0},{6,3},{7,6},{8,9},{9,12},{10,1... | collective-permute-start | bytes 786440 | tf_op jit(solution)/shard_map/ppermute | solution.py:777
  53.5 14.1 %collective-permute-start.6 = (bf16[128,2048]{1,0:T(8,128)(2,1)S(1)}, bf16[128,2048]{1,0:T(8,128)(2,1)S(1)}, u32[]{:S(2)}, u32[]{:S(2)}) collective-permute-start(bf16[128,2048]{1,0:T(8,128)(2,1)S(1)} %slice.201), channel_id=1, source_target_pairs={{8,0},{0,8},{24,16},{16,24},{9,1},{1,9},{25,17},{17,25},{10,2},{2,... | collective-permute-start | bytes 1572872 | tf_op jit(solution)/shard_map/ppermute | solution.py:647
  54.9 14.1 %collective-permute-start.7 = (bf16[128,2048]{1,0:T(8,128)(2,1)S(1)}, bf16[128,2048]{1,0:T(8,128)(2,1)S(1)}, u32[]{:S(2)}, u32[]{:S(2)}) collective-permute-start(bf16[128,2048]{1,0:T(8,128)(2,1)S(1)} %slice.202), channel_id=1, source_target_pairs={{16,0},{24,8},{0,16},{8,24},{17,1},{25,9},{1,17},{9,25},{18,2},{26... | collective-permute-start | bytes 1572872 | tf_op jit(solution)/shard_map/ppermute | solution.py:647
  56.1 27.3 %collective-permute-start.3 = (bf16[192,2048]{1,0:T(8,128)(2,1)S(1)}, bf16[192,2048]{1,0:T(8,128)(2,1)}, u32[]{:S(2)}, u32[]{:S(2)}) collective-permute-start(bf16[192,2048]{1,0:T(8,128)(2,1)S(1)} %get-tuple-element.207), channel_id=1, source_target_pairs={{8,0},{0,8},{24,16},{16,24},{9,1},{1,9},{25,17},{17,25},{10,2},{2,... | collective-permute-start | bytes 2359304 | tf_op jit(solution)/shard_map/ppermute | solution.py:647
  57.3 27.5 %collective-permute-start.8 = (bf16[192,2048]{1,0:T(8,128)(2,1)S(1)}, bf16[192,2048]{1,0:T(8,128)(2,1)S(1)}, u32[]{:S(2)}, u32[]{:S(2)}) collective-permute-start(bf16[192,2048]{1,0:T(8,128)(2,1)S(1)} %get-tuple-element.207), channel_id=1, source_target_pairs={{16,0},{24,8},{0,16},{8,24},{17,1},{25,9},{1,17},{9,25},{18,2},{26... | collective-permute-start | bytes 2359304 | tf_op jit(solution)/shard_map/ppermute | solution.py:647
  106.2 415.3 %reduce-scatter.5.cloned.1.call-start = ((), (), s32[]{:S(2)}) async-start(), calls=%async_computation.6 | async-start | bytes 5308416 | tf_op jit(solution)/shard_map/reduce_scatter | solution.py:597
  109.6 34.6 %collective-permute-start.12 = (bf16[320,2048]{1,0:T(8,128)(2,1)}, bf16[320,2048]{1,0:T(8,128)(2,1)S(1)}, u32[]{:S(2)}, u32[]{:S(2)}) collective-permute-start(bf16[320,2048]{1,0:T(8,128)(2,1)} %after.33), channel_id=1, source_target_pairs={{16,0},{24,8},{0,16},{8,24},{17,1},{25,9},{1,17},{9,25},{18,2},{26... | collective-permute-start | bytes 3932168 | tf_op jit(solution)/shard_map/ppermute | solution.py:647
  110.4 36.7 %collective-permute-start.11 = (bf16[320,2048]{1,0:T(8,128)(2,1)}, bf16[320,2048]{1,0:T(8,128)(2,1)S(1)}, u32[]{:S(2)}, u32[]{:S(2)}) collective-permute-start(bf16[320,2048]{1,0:T(8,128)(2,1)} %after.33), channel_id=1, source_target_pairs={{8,0},{0,8},{24,16},{16,24},{9,1},{1,9},{25,17},{17,25},{10,2},{2,... | collective-permute-start | bytes 3932168 | tf_op jit(solution)/shard_map/ppermute | solution.py:647
  138.4 12.9 %collective-permute-start.10 = (bf16[96,2048]{1,0:T(8,128)(2,1)}, bf16[96,2048]{1,0:T(8,128)(2,1)}, u32[]{:S(2)}, u32[]{:S(2)}) collective-permute-start(bf16[96,2048]{1,0:T(8,128)(2,1)} %slice.204), channel_id=1, source_target_pairs={{16,0},{24,8},{0,16},{8,24},{17,1},{25,9},{1,17},{9,25},{18,2},{26... | collective-permute-start | bytes 1179656 | tf_op jit(solution)/shard_map/ppermute | solution.py:647
  146.4 22.0 %collective-permute-start.13 = (bf16[160,2048]{1,0:T(8,128)(2,1)S(1)}, bf16[160,2048]{1,0:T(8,128)(2,1)S(1)}, u32[]{:S(2)}, u32[]{:S(2)}) collective-permute-start(bf16[160,2048]{1,0:T(8,128)(2,1)S(1)} %slice.205), channel_id=1, source_target_pairs={{8,0},{0,8},{24,16},{16,24},{9,1},{1,9},{25,17},{17,25},{10,2},{2,... | collective-permute-start | bytes 1966088 | tf_op jit(solution)/shard_map/ppermute | solution.py:647
  150.3 18.1 %collective-permute-start.14 = (bf16[160,2048]{1,0:T(8,128)(2,1)}, bf16[160,2048]{1,0:T(8,128)(2,1)S(1)}, u32[]{:S(2)}, u32[]{:S(2)}) collective-permute-start(bf16[160,2048]{1,0:T(8,128)(2,1)} %slice.206), channel_id=1, source_target_pairs={{16,0},{24,8},{0,16},{8,24},{17,1},{25,9},{1,17},{9,25},{18,2},{26... | collective-permute-start | bytes 1966088 | tf_op jit(solution)/shard_map/ppermute | solution.py:647
  203.9 50.6 %collective-permute-start.15 = (bf16[256,2048]{1,0:T(8,128)(2,1)}, bf16[256,2048]{1,0:T(8,128)(2,1)}, u32[]{:S(2)}, u32[]{:S(2)}) collective-permute-start(bf16[256,2048]{1,0:T(8,128)(2,1)} %get-tuple-element.85.refs_1_), channel_id=1, source_target_pairs={{8,0},{0,8},{24,16},{16,24},{9,1},{1,9},{25,17},{17,25},{10,2},{2,... | collective-permute-start | bytes 3145736 | tf_op jit(solution)/shard_map/ppermute | solution.py:647
  207.9 42.1 %collective-permute-start.23 = (f32[64,2048]{1,0:T(8,128)}, f32[64,2048]{1,0:T(8,128)}, u32[]{:S(2)}, u32[]{:S(2)}) collective-permute-start(f32[64,2048]{1,0:T(8,128)} %get-tuple-element.189), channel_id=1, source_target_pairs={{0,0},{1,3},{2,6},{3,1},{4,4},{5,7},{6,2},{7,5},{8,8},{9,11},{10,1... | collective-permute-start | bytes 1572872 | tf_op jit(solution)/shard_map/ppermute | solution.py:777
  209.8 40.7 %collective-permute-start.24 = (f32[64,2048]{1,0:T(8,128)}, f32[64,2048]{1,0:T(8,128)}, u32[]{:S(2)}, u32[]{:S(2)}) collective-permute-start(f32[64,2048]{1,0:T(8,128)} %get-tuple-element.191), channel_id=1, source_target_pairs={{0,1},{1,4},{2,7},{3,2},{4,5},{5,0},{6,3},{7,6},{8,9},{9,12},{10,1... | collective-permute-start | bytes 1572872 | tf_op jit(solution)/shard_map/ppermute | solution.py:777
  216.4 36.6 %collective-permute-start.25 = (f32[64,2048]{1,0:T(8,128)}, f32[64,2048]{1,0:T(8,128)}, u32[]{:S(2)}, u32[]{:S(2)}) collective-permute-start(f32[64,2048]{1,0:T(8,128)} %get-tuple-element.190), channel_id=1, source_target_pairs={{0,2},{1,5},{2,0},{3,3},{4,6},{5,1},{6,4},{7,7},{8,10},{9,13},{10,... | collective-permute-start | bytes 1572872 | tf_op jit(solution)/shard_map/ppermute | solution.py:777
  218.8 35.8 %collective-permute-start.16 = (bf16[256,2048]{1,0:T(8,128)(2,1)}, bf16[256,2048]{1,0:T(8,128)(2,1)}, u32[]{:S(2)}, u32[]{:S(2)}) collective-permute-start(bf16[256,2048]{1,0:T(8,128)(2,1)} %get-tuple-element.87.refs_3_), channel_id=1, source_target_pairs={{16,0},{24,8},{0,16},{8,24},{17,1},{25,9},{1,17},{9,25},{18,2},{26... | collective-permute-start | bytes 3145736 | tf_op jit(solution)/shard_map/ppermute | solution.py:647
  250.0 46.4 %collective-permute-start.17 = (bf16[256,2048]{1,0:T(8,128)(2,1)}, bf16[256,2048]{1,0:T(8,128)(2,1)}, u32[]{:S(2)}, u32[]{:S(2)}) collective-permute-start(bf16[256,2048]{1,0:T(8,128)(2,1)} %get-tuple-element.88.refs_4_), channel_id=1, source_target_pairs={{8,0},{0,8},{24,16},{16,24},{9,1},{1,9},{25,17},{17,25},{10,2},{2,... | collective-permute-start | bytes 3145736 | tf_op jit(solution)/shard_map/ppermute | solution.py:647
  250.5 45.8 %collective-permute-start.18 = (bf16[256,2048]{1,0:T(8,128)(2,1)}, bf16[256,2048]{1,0:T(8,128)(2,1)}, u32[]{:S(2)}, u32[]{:S(2)}) collective-permute-start(bf16[256,2048]{1,0:T(8,128)(2,1)} %get-tuple-element.90.refs_6_), channel_id=1, source_target_pairs={{16,0},{24,8},{0,16},{8,24},{17,1},{25,9},{1,17},{9,25},{18,2},{26... | collective-permute-start | bytes 3145736 | tf_op jit(solution)/shard_map/ppermute | solution.py:647
  258.5 44.2 %collective-permute-start.21 = (bf16[128,2048]{1,0:T(8,128)(2,1)}, bf16[128,2048]{1,0:T(8,128)(2,1)S(1)}, u32[]{:S(2)}, u32[]{:S(2)}) collective-permute-start(bf16[128,2048]{1,0:T(8,128)(2,1)} %get-tuple-element.92.refs_1_), channel_id=1, source_target_pairs={{16,0},{24,8},{0,16},{8,24},{17,1},{25,9},{1,17},{9,25},{18,2},{26... | collective-permute-start | bytes 1572872 | tf_op jit(solution)/shard_map/ppermute | solution.py:647
  259.3 43.5 %collective-permute-start.22 = (bf16[128,2048]{1,0:T(8,128)(2,1)}, bf16[128,2048]{1,0:T(8,128)(2,1)S(1)}, u32[]{:S(2)}, u32[]{:S(2)}) collective-permute-start(bf16[128,2048]{1,0:T(8,128)(2,1)} %get-tuple-element.93.refs_2_), channel_id=1, source_target_pairs={{8,0},{0,8},{24,16},{16,24},{9,1},{1,9},{25,17},{17,25},{10,2},{2,... | collective-permute-start | bytes 1572872 | tf_op jit(solution)/shard_map/ppermute | solution.py:647
  300.3 24.2 %collective-permute-start.19 = (bf16[128,2048]{1,0:T(8,128)(2,1)}, bf16[128,2048]{1,0:T(8,128)(2,1)}, u32[]{:S(2)}, u32[]{:S(2)}) collective-permute-start(bf16[128,2048]{1,0:T(8,128)(2,1)} %get-tuple-element.96.refs_2_), channel_id=1, source_target_pairs={{16,0},{24,8},{0,16},{8,24},{17,1},{25,9},{1,17},{9,25},{18,2},{26... | collective-permute-start | bytes 1572872 | tf_op jit(solution)/shard_map/ppermute | solution.py:647
  302.8 21.7 %collective-permute-start.20 = (bf16[128,2048]{1,0:T(8,128)(2,1)}, bf16[128,2048]{1,0:T(8,128)(2,1)}, u32[]{:S(2)}, u32[]{:S(2)}) collective-permute-start(bf16[128,2048]{1,0:T(8,128)(2,1)} %get-tuple-element.98.refs_3_), channel_id=1, source_target_pairs={{8,0},{0,8},{24,16},{16,24},{9,1},{1,9},{25,17},{17,25},{10,2},{2,... | collective-permute-start | bytes 1572872 | tf_op jit(solution)/shard_map/ppermute | solution.py:647
  321.4 37.1 %collective-permute-start.29 = (bf16[192,2048]{1,0:T(8,128)(2,1)}, bf16[192,2048]{1,0:T(8,128)(2,1)}, u32[]{:S(2)}, u32[]{:S(2)}) collective-permute-start(bf16[192,2048]{1,0:T(8,128)(2,1)} %get-tuple-element.103.refs_5_), channel_id=1, source_target_pairs={{8,0},{0,8},{24,16},{16,24},{9,1},{1,9},{25,17},{17,25},{10,2},{2,... | collective-permute-start | bytes 2359304 | tf_op jit(solution)/shard_map/ppermute | solution.py:647
  322.9 35.6 %collective-permute-start.30 = (bf16[192,2048]{1,0:T(8,128)(2,1)}, bf16[192,2048]{1,0:T(8,128)(2,1)}, u32[]{:S(2)}, u32[]{:S(2)}) collective-permute-start(bf16[192,2048]{1,0:T(8,128)(2,1)} %get-tuple-element.114), channel_id=1, source_target_pairs={{16,0},{24,8},{0,16},{8,24},{17,1},{25,9},{1,17},{9,25},{18,2},{26... | collective-permute-start | bytes 2359304 | tf_op jit(solution)/shard_map/ppermute | solution.py:647
  375.9 21.2 %collective-permute-start.36 = (bf16[192,2048]{1,0:T(8,128)(2,1)}, bf16[192,2048]{1,0:T(8,128)(2,1)}, u32[]{:S(2)}, u32[]{:S(2)}) collective-permute-start(bf16[192,2048]{1,0:T(8,128)(2,1)} %get-tuple-element.117.refs_1_), channel_id=1, source_target_pairs={{8,0},{0,8},{24,16},{16,24},{9,1},{1,9},{25,17},{17,25},{10,2},{2,... | collective-permute-start | bytes 2359304 | tf_op jit(solution)/shard_map/ppermute | solution.py:647
  376.0 16.9 %collective-permute-start.32 = (bf16[128,2048]{1,0:T(8,128)(2,1)}, bf16[128,2048]{1,0:T(8,128)(2,1)}, u32[]{:S(2)}, u32[]{:S(2)}) collective-permute-start(bf16[128,2048]{1,0:T(8,128)(2,1)} %get-tuple-element.108.refs_4_), channel_id=1, source_target_pairs={{24,8},{0,16},{25,9},{1,17},{26,10},{2,18},{27,11},{3,19},{28,12},... | collective-permute-start | bytes 1572872 | tf_op jit(solution)/shard_map/ppermute | solution.py:647
  382.0 51.3 %collective-permute-start.26 = (bf16[256,2048]{1,0:T(8,128)(2,1)S(1)}, bf16[256,2048]{1,0:T(8,128)(2,1)S(1)}, u32[]{:S(2)}, u32[]{:S(2)}) collective-permute-start(bf16[256,2048]{1,0:T(8,128)(2,1)S(1)} %copy-done.43), channel_id=1, source_target_pairs={{8,0},{16,24},{9,1},{17,25},{10,2},{18,26},{11,3},{19,27},{12,4},{... | collective-permute-start | bytes 3145736 | tf_op jit(solution)/shard_map/ppermute | solution.py:647
  383.3 26.4 %collective-permute-start.37 = (bf16[192,2048]{1,0:T(8,128)(2,1)}, bf16[192,2048]{1,0:T(8,128)(2,1)}, u32[]{:S(2)}, u32[]{:S(2)}) collective-permute-start(bf16[192,2048]{1,0:T(8,128)(2,1)} %get-tuple-element.122), channel_id=1, source_target_pairs={{16,0},{24,8},{0,16},{8,24},{17,1},{25,9},{1,17},{9,25},{18,2},{26... | collective-permute-start | bytes 2359304 | tf_op jit(solution)/shard_map/ppermute | solution.py:647
  384.8 49.8 %collective-permute-start.27 = (bf16[256,2048]{1,0:T(8,128)(2,1)S(1)}, bf16[256,2048]{1,0:T(8,128)(2,1)}, u32[]{:S(2)}, u32[]{:S(2)}) collective-permute-start(bf16[256,2048]{1,0:T(8,128)(2,1)S(1)} %copy-done.42), channel_id=1, source_target_pairs={{16,0},{8,24},{17,1},{9,25},{18,2},{10,26},{19,3},{11,27},{20,4},{... | collective-permute-start | bytes 3145736 | tf_op jit(solution)/shard_map/ppermute | solution.py:647
  392.8 26.1 %collective-permute-start.28 = (bf16[128,2048]{1,0:T(8,128)(2,1)S(1)}, bf16[128,2048]{1,0:T(8,128)(2,1)}, u32[]{:S(2)}, u32[]{:S(2)}) collective-permute-start(bf16[128,2048]{1,0:T(8,128)(2,1)S(1)} %copy-done.50), channel_id=1, source_target_pairs={{24,16},{0,8},{25,17},{1,9},{26,18},{2,10},{27,19},{3,11},{28,20},... | collective-permute-start | bytes 1572872 | tf_op jit(solution)/shard_map/ppermute | solution.py:647
  397.1 32.2 %collective-permute-start.33 = (bf16[128,2048]{1,0:T(8,128)(2,1)}, bf16[128,2048]{1,0:T(8,128)(2,1)}, u32[]{:S(2)}, u32[]{:S(2)}) collective-permute-start(bf16[128,2048]{1,0:T(8,128)(2,1)} %collective-permute-done.32), channel_id=1, source_target_pairs={{8,0},{16,24},{9,1},{17,25},{10,2},{18,26},{11,3},{19,27},{12,4},{... | collective-permute-start | bytes 1572872 | tf_op jit(solution)/shard_map/ppermute | solution.py:647
  409.7 39.6 %collective-permute-start.34 = (bf16[192,2048]{1,0:T(8,128)(2,1)}, bf16[192,2048]{1,0:T(8,128)(2,1)}, u32[]{:S(2)}, u32[]{:S(2)}) collective-permute-start(bf16[192,2048]{1,0:T(8,128)(2,1)} %get-tuple-element.115.refs_1_), channel_id=1, source_target_pairs={{24,8},{0,16},{25,9},{1,17},{26,10},{2,18},{27,11},{3,19},{28,12},... | collective-permute-start | bytes 2359304 | tf_op jit(solution)/shard_map/ppermute | solution.py:647
  418.9 30.4 %collective-permute-start.35 = (bf16[192,2048]{1,0:T(8,128)(2,1)}, bf16[192,2048]{1,0:T(8,128)(2,1)}, u32[]{:S(2)}, u32[]{:S(2)}) collective-permute-start(bf16[192,2048]{1,0:T(8,128)(2,1)} %get-tuple-element.116.refs_2_), channel_id=1, source_target_pairs={{0,8},{24,16},{1,9},{25,17},{2,10},{26,18},{3,11},{27,19},{4,12},{... | collective-permute-start | bytes 2359304 | tf_op jit(solution)/shard_map/ppermute | solution.py:647
  429.3 20.0 %collective-permute-start.38 = (bf16[192,2048]{1,0:T(8,128)(2,1)}, bf16[192,2048]{1,0:T(8,128)(2,1)}, u32[]{:S(2)}, u32[]{:S(2)}) collective-permute-start(bf16[192,2048]{1,0:T(8,128)(2,1)} %get-tuple-element.124), channel_id=1, source_target_pairs={{24,8},{0,16},{25,9},{1,17},{26,10},{2,18},{27,11},{3,19},{28,12},... | collective-permute-start | bytes 2359304 | tf_op jit(solution)/shard_map/ppermute | solution.py:647
  433.3 20.2 %collective-permute-start.39 = (bf16[192,2048]{1,0:T(8,128)(2,1)}, bf16[192,2048]{1,0:T(8,128)(2,1)S(1)}, u32[]{:S(2)}, u32[]{:S(2)}) collective-permute-start(bf16[192,2048]{1,0:T(8,128)(2,1)} %get-tuple-element.126), channel_id=1, source_target_pairs={{0,8},{24,16},{1,9},{25,17},{2,10},{26,18},{3,11},{27,19},{4,12},{... | collective-permute-start | bytes 2359304 | tf_op jit(solution)/shard_map/ppermute | solution.py:647
  434.6 14.7 %collective-permute-start.31 = (bf16[128,2048]{1,0:T(8,128)(2,1)}, bf16[128,2048]{1,0:T(8,128)(2,1)S(1)}, u32[]{:S(2)}, u32[]{:S(2)}) collective-permute-start(bf16[128,2048]{1,0:T(8,128)(2,1)} %after.44), channel_id=1, source_target_pairs={{16,0},{8,24},{17,1},{9,25},{18,2},{10,26},{19,3},{11,27},{20,4},{... | collective-permute-start | bytes 1572872 | tf_op jit(solution)/shard_map/ppermute | solution.py:647
  467.4 108.3 %all-gather.9.cloned.1.call-start = ((), (), s32[]{:S(2)}) async-start(), calls=%async_computation.7 | async-start | bytes 5308416 | tf_op jit(solution)/shard_map/all_gather | solution.py:598
  521.5 163.7 %reduce-scatter.7.cloned.1.call-start = ((), (), s32[]{:S(2)}) async-start(), calls=%async_computation.8 | async-start | bytes 9437184 | tf_op jit(solution)/shard_map/reduce_scatter | solution.py:1016
  575.6 172.7 %reduce-scatter.9.cloned.1.call-start = ((), (), s32[]{:S(2)}) async-start(), calls=%async_computation.9 | async-start | bytes 5308416 | tf_op jit(solution)/shard_map/reduce_scatter | solution.py:597
  575.7 104.2 %collective-permute-start.41 = (bf16[256,2048]{1,0:T(8,128)(2,1)}, bf16[256,2048]{1,0:T(8,128)(2,1)S(1)}, u32[]{:S(2)}, u32[]{:S(2)}) collective-permute-start(bf16[256,2048]{1,0:T(8,128)(2,1)} %after.55), channel_id=1, source_target_pairs={{16,0},{24,8},{0,16},{8,24},{17,1},{25,9},{1,17},{9,25},{18,2},{26... | collective-permute-start | bytes 3145736 | tf_op jit(solution)/shard_map/ppermute | solution.py:647
  577.0 102.9 %collective-permute-start.40 = (bf16[256,2048]{1,0:T(8,128)(2,1)}, bf16[256,2048]{1,0:T(8,128)(2,1)S(1)}, u32[]{:S(2)}, u32[]{:S(2)}) collective-permute-start(bf16[256,2048]{1,0:T(8,128)(2,1)} %after.53), channel_id=1, source_target_pairs={{8,0},{0,8},{24,16},{16,24},{9,1},{1,9},{25,17},{17,25},{10,2},{2,... | collective-permute-start | bytes 3145736 | tf_op jit(solution)/shard_map/ppermute | solution.py:647
  685.2 117.4 %all-gather.11.cloned.1.call-start = ((), (), s32[]{:S(2)}) async-start(), calls=%async_computation.10 | async-start | bytes 5308416 | tf_op jit(solution)/shard_map/all_gather | solution.py:598
  685.3 13.0 %collective-permute-start.46 = (bf16[128,2048]{1,0:T(8,128)(2,1)}, bf16[128,2048]{1,0:T(8,128)(2,1)}, u32[]{:S(2)}, u32[]{:S(2)}) collective-permute-start(bf16[128,2048]{1,0:T(8,128)(2,1)} %get-tuple-element.134.refs_2_), channel_id=1, source_target_pairs={{16,0},{24,8},{0,16},{8,24},{17,1},{25,9},{1,17},{9,25},{18,2},{26... | collective-permute-start | bytes 1572872 | tf_op jit(solution)/shard_map/ppermute | solution.py:647
  689.3 12.7 %collective-permute-start.47 = (bf16[128,2048]{1,0:T(8,128)(2,1)}, bf16[128,2048]{1,0:T(8,128)(2,1)S(1)}, u32[]{:S(2)}, u32[]{:S(2)}) collective-permute-start(bf16[128,2048]{1,0:T(8,128)(2,1)} %get-tuple-element.135.refs_3_), channel_id=1, source_target_pairs={{8,0},{0,8},{24,16},{16,24},{9,1},{1,9},{25,17},{17,25},{10,2},{2,... | collective-permute-start | bytes 1572872 | tf_op jit(solution)/shard_map/ppermute | solution.py:647
  707.6 20.9 %collective-permute-start.48 = (bf16[64,2048]{1,0:T(8,128)(2,1)S(1)}, bf16[64,2048]{1,0:T(8,128)(2,1)S(1)}, u32[]{:S(2)}, u32[]{:S(2)}) collective-permute-start(bf16[64,2048]{1,0:T(8,128)(2,1)S(1)} %get-tuple-element.203), channel_id=1, source_target_pairs={{0,0},{3,1},{6,2},{1,3},{4,4},{7,5},{2,6},{5,7},{8,8},{11,9},{14,1... | collective-permute-start | bytes 786440 | tf_op jit(solution)/shard_map/ppermute | solution.py:795
  709.5 20.9 %collective-permute-start.49 = (bf16[64,2048]{1,0:T(8,128)(2,1)S(1)}, bf16[64,2048]{1,0:T(8,128)(2,1)S(1)}, u32[]{:S(2)}, u32[]{:S(2)}) collective-permute-start(bf16[64,2048]{1,0:T(8,128)(2,1)S(1)} %get-tuple-element.205), channel_id=1, source_target_pairs={{1,0},{4,1},{7,2},{2,3},{5,4},{0,5},{3,6},{6,7},{9,8},{12,9},{15,1... | collective-permute-start | bytes 786440 | tf_op jit(solution)/shard_map/ppermute | solution.py:795
  710.5 22.8 %collective-permute-start.50 = (bf16[64,2048]{1,0:T(8,128)(2,1)S(1)}, bf16[64,2048]{1,0:T(8,128)(2,1)S(1)}, u32[]{:S(2)}, u32[]{:S(2)}) collective-permute-start(bf16[64,2048]{1,0:T(8,128)(2,1)S(1)} %get-tuple-element.204), channel_id=1, source_target_pairs={{2,0},{5,1},{0,2},{3,3},{6,4},{1,5},{4,6},{7,7},{10,8},{13,9},{8,1... | collective-permute-start | bytes 786440 | tf_op jit(solution)/shard_map/ppermute | solution.py:795
  718.7 14.8 %collective-permute-start.44 = (f32[20480]{0:T(1024)S(1)}, f32[20480]{0:T(1024)S(1)}, u32[]{:S(2)}, u32[]{:S(2)}) collective-permute-start(f32[20480]{0:T(1024)S(1)} %add.242), channel_id=1, source_target_pairs={{0,1},{1,0},{2,3},{3,2},{4,5},{5,4},{6,7},{7,6},{8,9},{9,8},{10,11... | collective-permute-start | bytes 245768 | tf_op jit(solution)/shard_map/ppermute | solution.py:765
  748.3 239.4 %reduce-scatter.11.cloned.1.call-start = ((), (), s32[]{:S(2)}) async-start(), calls=%async_computation.11 | async-start | bytes 9437184 | tf_op jit(solution)/shard_map/reduce_scatter | solution.py:1058
  918.2 17.0 %collective-permute-start.60 = (f32[20480]{0:T(1024)}, f32[20480]{0:T(1024)S(1)}, u32[]{:S(2)}, u32[]{:S(2)}) collective-permute-start(f32[20480]{0:T(1024)} %after.59), channel_id=1, source_target_pairs={{0,4},{1,5},{2,6},{3,7},{4,0},{5,1},{6,2},{7,3},{8,12},{9,13},{10,... | collective-permute-start | bytes 245768 | tf_op jit(solution)/shard_map/ppermute | solution.py:765
  919.6 13.0 %collective-permute-start.53 = (bf16[128,2048]{1,0:T(8,128)(2,1)}, bf16[128,2048]{1,0:T(8,128)(2,1)S(1)}, u32[]{:S(2)}, u32[]{:S(2)}) collective-permute-start(bf16[128,2048]{1,0:T(8,128)(2,1)} %get-tuple-element.148), channel_id=1, source_target_pairs={{8,0},{0,8},{24,16},{16,24},{9,1},{1,9},{25,17},{17,25},{10,2},{2,... | collective-permute-start | bytes 1572872 | tf_op jit(solution)/shard_map/ppermute | solution.py:647
  920.8 13.1 %collective-permute-start.55 = (bf16[128,2048]{1,0:T(8,128)(2,1)}, bf16[128,2048]{1,0:T(8,128)(2,1)S(1)}, u32[]{:S(2)}, u32[]{:S(2)}) collective-permute-start(bf16[128,2048]{1,0:T(8,128)(2,1)} %get-tuple-element.149), channel_id=1, source_target_pairs={{16,0},{24,8},{0,16},{8,24},{17,1},{25,9},{1,17},{9,25},{18,2},{26... | collective-permute-start | bytes 1572872 | tf_op jit(solution)/shard_map/ppermute | solution.py:647
  922.1 45.3 %collective-permute-start.51 = (bf16[256,2048]{1,0:T(8,128)(2,1)}, bf16[256,2048]{1,0:T(8,128)(2,1)S(1)}, u32[]{:S(2)}, u32[]{:S(2)}) collective-permute-start(bf16[256,2048]{1,0:T(8,128)(2,1)} %get-tuple-element.146), channel_id=1, source_target_pairs={{8,0},{0,8},{24,16},{16,24},{9,1},{1,9},{25,17},{17,25},{10,2},{2,... | collective-permute-start | bytes 3145736 | tf_op jit(solution)/shard_map/ppermute | solution.py:647
  922.2 45.1 %collective-permute-start.52 = (bf16[256,2048]{1,0:T(8,128)(2,1)}, bf16[256,2048]{1,0:T(8,128)(2,1)S(1)}, u32[]{:S(2)}, u32[]{:S(2)}) collective-permute-start(bf16[256,2048]{1,0:T(8,128)(2,1)} %get-tuple-element.147), channel_id=1, source_target_pairs={{16,0},{24,8},{0,16},{8,24},{17,1},{25,9},{1,17},{9,25},{18,2},{26... | collective-permute-start | bytes 3145736 | tf_op jit(solution)/shard_map/ppermute | solution.py:647
  932.6 34.7 %collective-permute-start.54 = (bf16[128,2048]{1,0:T(8,128)(2,1)S(1)}, bf16[128,2048]{1,0:T(8,128)(2,1)S(1)}, u32[]{:S(2)}, u32[]{:S(2)}) collective-permute-start(bf16[128,2048]{1,0:T(8,128)(2,1)S(1)} %collective-permute-done.53), channel_id=1, source_target_pairs={{16,0},{24,8},{0,16},{8,24},{17,1},{25,9},{1,17},{9,25},{18,2},{26... | collective-permute-start | bytes 1572872 | tf_op jit(solution)/shard_map/ppermute | solution.py:647
  933.9 33.4 %collective-permute-start.56 = (bf16[128,2048]{1,0:T(8,128)(2,1)S(1)}, bf16[128,2048]{1,0:T(8,128)(2,1)S(1)}, u32[]{:S(2)}, u32[]{:S(2)}) collective-permute-start(bf16[128,2048]{1,0:T(8,128)(2,1)S(1)} %collective-permute-done.55), channel_id=1, source_target_pairs={{8,0},{0,8},{24,16},{16,24},{9,1},{1,9},{25,17},{17,25},{10,2},{2,... | collective-permute-start | bytes 1572872 | tf_op jit(solution)/shard_map/ppermute | solution.py:647
  970.1 13.7 %collective-permute-start.58 = (bf16[64,2048]{1,0:T(8,128)(2,1)S(1)}, bf16[64,2048]{1,0:T(8,128)(2,1)S(1)}, u32[]{:S(2)}, u32[]{:S(2)}) collective-permute-start(bf16[64,2048]{1,0:T(8,128)(2,1)S(1)} %get-tuple-element.202), channel_id=1, source_target_pairs={{1,0},{4,1},{7,2},{2,3},{5,4},{0,5},{3,6},{6,7},{9,8},{12,9},{15,1... | collective-permute-start | bytes 786440 | tf_op jit(solution)/shard_map/ppermute | solution.py:795
  970.6 14.7 %collective-permute-start.59 = (bf16[64,2048]{1,0:T(8,128)(2,1)S(1)}, bf16[64,2048]{1,0:T(8,128)(2,1)S(1)}, u32[]{:S(2)}, u32[]{:S(2)}) collective-permute-start(bf16[64,2048]{1,0:T(8,128)(2,1)S(1)} %get-tuple-element.201), channel_id=1, source_target_pairs={{2,0},{5,1},{0,2},{3,3},{6,4},{1,5},{4,6},{7,7},{10,8},{13,9},{8,1... | collective-permute-start | bytes 786440 | tf_op jit(solution)/shard_map/ppermute | solution.py:795
  (74 other events, 597.8 us)
Sparse Core Ops, SparseCore 0:
  12.8 93.2 all-gather.4
  107.7 81.8 all-gather.6
  467.5 53.9 reduce-scatter.4
  523.0 52.6 all-gather.8
  577.8 85.8 reduce-scatter.6
  685.3 62.9 reduce-scatter.8
  749.9 52.5 all-gather.10
  804.9 85.8 reduce-scatter.10
